TPU v7x, 128 devices: a whole 4x4x4 slice. The times are simulated.
128 devices in a mesh: gx: 8 (over y_hi, x), gy: 16 (over y_lo, z, core).
Axes of the slice: x: 4, y: 4 (y_hi: 2, y_lo: 2; y = y_hi * 2 + y_lo), z: 4, core: 2. Of those that a mesh axis runs over, the one named last changes fastest.
Arguments:
- right_side: float32 [8, 32, 64, 128], P('gx', 'gy'), may hold values from -6 to 6
- initial: float32 [8, 32, 64, 128], P('gx', 'gy'), may hold values from -30 to 30
- elem_blocks: bfloat16 [8, 32, 64, 1024], P('gx', 'gy'), may hold values from -1 to 3
- face_blocks: bfloat16 [6, 8, 32, 64, 1024], P(None, 'gx', 'gy'), may hold values from -0.25 to 0.25
- fault_blocks: bfloat16 [8, 16, 64, 8192], P('gx', 'gy'), may hold values from -0.3125 to 0.3125
- faults: int32 [3, 8, 16, 128], P(None, 'gx', 'gy'), may hold values from 0 to 31, as said below
- fault_count: int32 [8, 16], P('gx', 'gy'), may hold values from 96 to 128, as said below
Outputs:
- solution: float32 [8, 32, 64, 128], P('gx', 'gy')
Inputs may be any that keep to these rules, and one draw needn't show every extreme that they name: `faults`: among the first fault_count pairs of a device, at most 16 name the same partner device, and on every device some partner device is named by exactly 16 of them; all entries, active or not, are valid element and device numbers. `fault_count`: some device has 128 active pairs.
All inputs are finite; a program needn't handle non-finite values.
Results may differ from a plain program's by a relative error of at most 0.04.
Values may be sent and summed in bfloat16 or wider, within the bound.
No kernel may reach another device: no remote copies, remote signals or barrier semaphores. Data moves between devices by JAX's collectives and lax.ppermute only.
A program may use at most 64 MiB of HBM per device.

v0:
```python
import jax
import jax.numpy as jnp
from jax import lax
from jax.experimental import pallas as pl
from jax.experimental.pallas import tpu as pltpu
from jax.sharding import PartitionSpec as P

NODES = 64
RHS = 8
LZ = 16
SWEEPS = 2
DEGREE = 4
ROWS = LZ * RHS
ELEMS = 2 * LZ
PAIRS = 128
CHIPS = 8

spectrum_low = 0.6
spectrum_high = 3.0

BF = jnp.bfloat16
F32 = jnp.float32
NT = (((1,), (1,)), ((), ()))


def dot(a, b):
    return jnp.dot(a, b, preferred_element_type=F32)


def dot_t(a, b):
    return lax.dot_general(a, b, NT, preferred_element_type=F32)


def iota(shape, dim):
    return lax.broadcasted_iota(jnp.int32, shape, dim)


def coefficients():
    centre_point = (spectrum_high + spectrum_low) / 2.0
    half_width = (spectrum_high - spectrum_low) / 2.0
    sigma_ratio = centre_point / half_width
    steps = []
    rho_prev = 1.0 / sigma_ratio
    for _ in range(1, DEGREE):
        rho_next = 1.0 / (2.0 * sigma_ratio - rho_prev)
        steps.append((rho_next * rho_prev, 2.0 * rho_next / half_width))
        rho_prev = rho_next
    return centre_point, steps


def write_field(field, spread_ref, packed_ref, rows_ref):
    packed_ref[...] = jnp.concatenate([field[:ROWS], field[ROWS:]], axis=1).astype(BF)
    rows_ref[...] = field
    pieces = [rows_ref[pl.ds(r, ELEMS, stride=RHS), :] for r in range(RHS)]
    spread = jnp.concatenate(pieces, axis=1).astype(BF)
    for chip in range(CHIPS):
        spread_ref[chip] = spread


def first_kernel(initial_ref, spread_ref, packed_ref, solution_ref, rows_ref):
    field = jnp.concatenate([initial_ref[0, 0].T, initial_ref[0, 1].T], axis=0)
    solution_ref[...] = field
    write_field(field, spread_ref, packed_ref, rows_ref)


def setup_kernel(place_ref, right_ref, faults_ref, right_out, pick_ref, land_ref, expand_ref, mask_ref):
    right_out[...] = jnp.concatenate([right_ref[0, 0].T, right_ref[0, 1].T], axis=0)
    own = faults_ref[0, 0]
    device = faults_ref[1, 0]
    column = (
        jnp.where(device % 2 == place_ref[0] % 2, 0, CHIPS * ELEMS) + (device // 2) * ELEMS + faults_ref[2, 0]
    )
    hit = iota((2 * CHIPS * ELEMS, PAIRS), 0) == column
    pick_ref[...] = jnp.where(hit, 1.0, 0.0).T.astype(BF)
    lands = (iota((ELEMS * RHS, PAIRS), 0) // RHS == own) & (iota((ELEMS * RHS, PAIRS), 1) < place_ref[2])
    land_ref[...] = jnp.where(lands, 1.0, 0.0).astype(BF)
    source = iota((2 * NODES, 2 * NODES * LZ), 0)
    target = iota((2 * NODES, 2 * NODES * LZ), 1) // LZ
    expand_ref[...] = jnp.where(source == target, 1.0, 0.0).astype(BF)
    shift = iota((ROWS, 128), 1) % LZ - iota((ROWS, 128), 0) // RHS
    for k in range(3):
        mask_ref[k] = jnp.where(shift == k - 1, 1.0, 0.0).astype(BF)


def masked(expanded, mask):
    return expanded * jnp.concatenate([mask] * (NODES * LZ // 128), axis=1)


def local_kernel(place_ref, own_ref, even_ref, odd_ref, elem_ref, face_ref, expand_ref, mask_ref, out_ref):
    at = place_ref[1]
    is_even = at % 2 == 0
    low = jnp.where(is_even, odd_ref[...], even_ref[...])
    high = jnp.where(is_even, even_ref[...], odd_ref[...])
    low = jnp.where(at > 0, low, jnp.zeros_like(low))
    high = jnp.where(at < 7, high, jnp.zeros_like(high))
    down, same, up = mask_ref[0], mask_ref[1], mask_ref[2]
    zero = jnp.zeros((RHS, NODES), F32)
    width = NODES * LZ
    sums = [None, None]

    def add(ly, value):
        sums[ly] = value if sums[ly] is None else sums[ly] + value

    for ly in range(2):
        wide = dot(own_ref[...], expand_ref[:, ly * width : (ly + 1) * width]).astype(BF)
        here = masked(wide, same)
        add(ly, dot_t(here, elem_ref[0, ly]))
        add(1 - ly, dot_t(here, face_ref[2 + ly, 0, 1 - ly]))
        lower = dot_t(masked(wide, up), face_ref[4, 0, ly])
        add(ly, jnp.concatenate([zero, lower[:-RHS]], axis=0))
        upper = dot_t(masked(wide, down), face_ref[5, 0, ly])
        add(ly, jnp.concatenate([upper[RHS:], zero], axis=0))
        for direction, field in enumerate((low, high)):
            wide = dot(field, expand_ref[:, ly * width : (ly + 1) * width]).astype(BF)
            add(ly, dot_t(masked(wide, same), face_ref[direction, 0, ly]))
    out_ref[:ROWS] = sums[0]
    out_ref[ROWS:] = sums[1]


def make_final_kernel(turn, last):
    centre_point, steps = coefficients()

    def final_kernel(
        place_ref, local_ref, mine_ref, other_ref, pick_ref, land_ref, expand_ref, mask_ref, face_ref, fault_ref,
        *refs,
    ):
        if turn == 0:
            right_ref, solution_ref = refs[:2]
            outs = refs[2:]
        else:
            solution_ref, residual_ref, step_ref, correction_ref = refs[:4]
            outs = refs[4:]
        rows_ref, values_ref, plane_ref = outs[-3:]
        outs = outs[:-3]
        half = CHIPS * ELEMS
        picked = dot(pick_ref[:, :half], mine_ref[...].reshape(half, RHS * NODES)) + dot(
            pick_ref[:, half:], other_ref[...].reshape(half, RHS * NODES)
        )
        values_ref[...] = picked.T
        at = place_ref[0]
        chip = at // 2
        is_even = at % 2 == 0
        low_chip = jnp.where(is_even, jnp.maximum(chip - 1, 0), chip)
        high_chip = jnp.where(is_even, chip, jnp.minimum(chip + 1, CHIPS - 1))
        same = mask_ref[1]
        sums = []
        for ly in range(2):
            if ly == 0:
                plane = other_ref[low_chip, LZ:].astype(F32)
                plane = jnp.where(at > 0, plane, jnp.zeros_like(plane))
            else:
                plane = other_ref[high_chip, :LZ].astype(F32)
                plane = jnp.where(at < 2 * CHIPS - 1, plane, jnp.zeros_like(plane))
            for r in range(RHS):
                plane_ref[ly, pl.ds(r, LZ, stride=RHS), :] = plane[:, r * NODES : (r + 1) * NODES]
            wide = dot(plane_ref[ly].astype(BF), expand_ref[:NODES, : NODES * LZ]).astype(BF)
            sums.append(dot_t(masked(wide, same), face_ref[2 + ly, 0, ly]))
        total = local_ref[...] + jnp.concatenate(sums, axis=0)
        land = land_ref[...].reshape(ELEMS // 2, 2 * RHS, PAIRS)
        group = 4
        for start in range(0, NODES, group):
            parts = []
            for m in range(start, start + group):
                value = values_ref[pl.ds(m, RHS, stride=NODES), :]
                value = jnp.concatenate([value, value], axis=0).astype(BF)
                parts.append((land * value[None]).reshape(ELEMS * RHS, PAIRS))
            total = total + dot_t(
                jnp.concatenate(parts, axis=1), fault_ref[0, 0, :, start * PAIRS : (start + group) * PAIRS]
            )
        if turn == 0:
            residual = right_ref[...] - total
            step = residual / centre_point
            correction = step
        else:
            residual = residual_ref[...]
            old, new = steps[turn - 1]
            step = old * step_ref[...] + new * (residual - total)
            correction = correction_ref[...] + step
        if last:
            result = solution_ref[...] + correction
            outs[0][0, 0] = result[:ROWS].T
            outs[0][0, 1] = result[ROWS:].T
            return
        if turn == DEGREE - 1:
            result = solution_ref[...] + correction
            outs[2][...] = result
            write_field(result, outs[0], outs[1], rows_ref)
        else:
            outs[2][...] = residual
            outs[3][...] = step
            outs[4][...] = correction
            write_field(correction, outs[0], outs[1], rows_ref)

    return final_kernel


def call(kernel, out_shape, n_smem, n_in, scratch=(), flops=0):
    vmem = pl.BlockSpec(memory_space=pltpu.VMEM)
    smem = pl.BlockSpec(memory_space=pltpu.SMEM)
    single = not isinstance(out_shape, (list, tuple))
    return pl.pallas_call(
        kernel,
        out_shape=out_shape,
        in_specs=[smem] * n_smem + [vmem] * n_in,
        out_specs=vmem if single else [vmem] * len(out_shape),
        scratch_shapes=list(scratch),
        compiler_params=pltpu.CompilerParams(vmem_limit_bytes=32 * 1024 * 1024),
        cost_estimate=pl.CostEstimate(flops=flops, bytes_accessed=2 << 20, transcendentals=0),
    )


def shape(dims, dtype):
    return jax.ShapeDtypeStruct(dims, dtype)


def swap(value, axis, pairs):
    return lax.ppermute(value, axis, pairs + [(b, a) for a, b in pairs])


def shards(right_side, initial, elem_blocks, face_blocks, fault_blocks, faults, fault_count):
    place = jnp.stack([lax.axis_index("gy"), lax.axis_index("gx"), fault_count[0, 0]]).astype(jnp.int32)
    same_core = [list(range(core, 2 * CHIPS, 2)) for core in range(2)]
    field_rows = ELEMS * RHS
    state = shape((field_rows, NODES), F32)
    spread_shape = shape((CHIPS, ELEMS, RHS * NODES), BF)
    packed_shape = shape((ROWS, 2 * NODES), BF)
    rows_scratch = pltpu.VMEM((field_rows, NODES), F32)

    spread, packed, total = call(first_kernel, [spread_shape, packed_shape, state], 0, 1, [rows_scratch])(initial)
    right, pick, land, expand, mask = call(
        setup_kernel,
        [
            state,
            shape((PAIRS, 2 * CHIPS * ELEMS), BF),
            shape((field_rows, PAIRS), BF),
            shape((2 * NODES, 2 * NODES * LZ), BF),
            shape((3, ROWS, 128), BF),
        ],
        1,
        2,
    )(place, right_side, faults[:, 0])

    residual = step = correction = None
    for sweep in range(SWEEPS):
        for turn in range(DEGREE):
            mine = lax.all_to_all(spread, "gy", 0, 0, axis_index_groups=same_core)
            even = swap(packed, "gx", [(0, 1), (2, 3), (4, 5), (6, 7)])
            odd = swap(packed, "gx", [(1, 2), (3, 4), (5, 6), (7, 0)])
            local = call(local_kernel, state, 1, 7, flops=4 << 30)(
                place, packed, even, odd, elem_blocks, face_blocks, expand, mask
            )
            other = swap(mine, "gy", [(2 * chip, 2 * chip + 1) for chip in range(CHIPS)])
            last = sweep == SWEEPS - 1 and turn == DEGREE - 1
            if last:
                outs = shape((1, 2, NODES, ROWS), F32)
            elif turn == DEGREE - 1:
                outs = [spread_shape, packed_shape, state]
            else:
                outs = [spread_shape, packed_shape, state, state, state]
            extra = [right, total] if turn == 0 else [total, residual, step, correction]
            results = call(
                make_final_kernel(turn, last),
                outs,
                1,
                9 + len(extra),
                [
                    rows_scratch,
                    pltpu.VMEM((RHS * NODES, PAIRS), F32),
                    pltpu.VMEM((2, ROWS, NODES), F32),
                ],
                flops=4 << 30,
            )(place, local, mine, other, pick, land, expand, mask, face_blocks, fault_blocks, *extra)
            if last:
                return results
            if turn == DEGREE - 1:
                spread, packed, total = results
            else:
                spread, packed, residual, step, correction = results


def solution(mesh):
    in_specs = (
        P("gx", "gy", None, None),
        P("gx", "gy", None, None),
        P("gx", "gy", None, None),
        P(None, "gx", "gy", None, None),
        P("gx", "gy", None, None),
        P(None, "gx", "gy", None),
        P("gx", "gy"),
    )
    out_specs = P("gx", "gy", None, None)
    return jax.shard_map(shards, mesh=mesh, in_specs=in_specs, out_specs=out_specs, check_vma=False)
```

profile of v0, /device:TPU:1, one launch (start us, length us, event | category | flops | bytes accessed | tf_op | source)
XLA Modules:
  0.0 198.8 jit_solution(12647166152997544912)
XLA Ops:
  2.4 6.9 %all-to-all-start = ((bf16[8,32,512]{2,1,0:T(8,128)(2,1)}), bf16[8,32,512]{2,1,0:T(8,128)(2,1)S(1)}, u32[]{:S(2)}, u32[]{:S(2)}) async-start(bf16[8,32,512]{2,1,0:T(8,128)(2,1)} %get-tuple-element.49), calls=%async_computation | async-start | bytes 524288 | tf_op jit(solution)/shard_map/all_to_all | solution.py:246
  9.3 4.8 %collective-permute-start.1 = (bf16[128,128]{1,0:T(8,128)(2,1)S(1)}, bf16[128,128]{1,0:T(8,128)(2,1)S(1)}, u32[]{:S(2)}, u32[]{:S(2)}) collective-permute-start(bf16[128,128]{1,0:T(8,128)(2,1)S(1)} %get-tuple-element.46.own_ref), channel_id=1, source_target_pairs={{16,32},{48,64},{80,96},{112,0},{32,16},{64,48},{96,80},{0,112},{1... | collective-permute-start | bytes 98312 | tf_op jit(solution)/shard_map/ppermute | solution.py:217
  19.0 1.2 collective-permute-start.2
  21.4 1.4 copy-done.3
  27.0 2.0 %shard_map.75.local_ref = f32[256,64]{1,0:T(8,128)S(1)} custom-call(s32[3]{0:T(128)S(1)} %pad_add_fusion.place_ref, bf16[128,128]{1,0:T(8,128)(2,1)S(1)} %copy-done.41, bf16[128,128]{1,0:T(8,128)(2,1)S(1)} %copy-done.45, bf16[128,128]{1,0:T(8,128)(2,1)S(1)} %copy-done.43, bf16[1,2,64,1024]{3,2,1,0:T(8,128)(2,1)S(1)} %copy-done.6, ...), custom_call_target="tpu_custom_call" | custom-call | flops 4294967296 | bytes 2097152 | tf_op jit(solution)/shard_map/pallas_call | solution.py:249
  29.1 3.0 %shard_map.76 = (bf16[8,32,512]{2,1,0:T(8,128)(2,1)}, bf16[128,128]{1,0:T(8,128)(2,1)S(1)}, f32[256,64]{1,0:T(8,128)S(1)}, f32[256,64]{1,0:T(8,128)S(1)}, f32[256,64]{1,0:T(8,128)S(1)}) custom-call(s32[3]{0:T(128)S(1)} %pad_add_fusion.place_ref, f32[256,64]{1,0:T(8,128)S(1)} %shard_map.75.local_ref, bf16[8,32,512]{2,1,0:T(8,128)(2,1)S(1)} %all-to-all-done.mine_ref, ...), custom_call_target="tpu_custom_call" | custom-call | flops 4294967296 | bytes 2097152 | tf_op jit(solution)/shard_map/pallas_call | solution.py:261
  34.7 4.8 %all-to-all-start.1 = ((bf16[8,32,512]{2,1,0:T(8,128)(2,1)}), bf16[8,32,512]{2,1,0:T(8,128)(2,1)S(1)}, u32[]{:S(2)}, u32[]{:S(2)}) async-start(bf16[8,32,512]{2,1,0:T(8,128)(2,1)} %get-tuple-element.55), calls=%async_computation.1 | async-start | bytes 524288 | tf_op jit(solution)/shard_map/all_to_all | solution.py:246
  39.5 1.7 collective-permute-start.4
  41.3 4.3 %all-to-all-done.1.mine_ref = bf16[8,32,512]{2,1,0:T(8,128)(2,1)S(1)} async-done(((bf16[8,32,512]{2,1,0:T(8,128)(2,1)}), bf16[8,32,512]{2,1,0:T(8,128)(2,1)S(1)}, u32[]{:S(2)}, u32[]{:S(2)}) %all-to-all-start.1) | async-done | bytes 262176 | tf_op jit(solution)/shard_map/all_to_all | solution.py:246
  45.6 1.9 collective-permute-start.5
  50.1 2.4 %shard_map.77.local_ref = f32[256,64]{1,0:T(8,128)S(1)} custom-call(s32[3]{0:T(128)S(1)} %pad_add_fusion.place_ref, bf16[128,128]{1,0:T(8,128)(2,1)S(1)} %copy-done.59, bf16[128,128]{1,0:T(8,128)(2,1)} %collective-permute-done.3.even_ref, bf16[128,128]{1,0:T(8,128)(2,1)} %collective-permute-done.4.odd_ref, bf16[1,2,64,1024]{3,2,1,0:T(8,128)(2,1)S(1)} %copy-done.7, ...), custom_call_target="tpu_custom_call" | custom-call | flops 4294967296 | bytes 2097152 | tf_op jit(solution)/shard_map/pallas_call | solution.py:249
  52.6 3.0 %shard_map.78 = (bf16[8,32,512]{2,1,0:T(8,128)(2,1)}, bf16[128,128]{1,0:T(8,128)(2,1)S(1)}, f32[256,64]{1,0:T(8,128)S(1)}, f32[256,64]{1,0:T(8,128)S(1)}, f32[256,64]{1,0:T(8,128)S(1)}) custom-call(s32[3]{0:T(128)S(1)} %pad_add_fusion.place_ref, f32[256,64]{1,0:T(8,128)S(1)} %shard_map.77.local_ref, bf16[8,32,512]{2,1,0:T(8,128)(2,1)S(1)} %all-to-all-done.1.mine_ref, ...), custom_call_target="tpu_custom_call" | custom-call | flops 4294967296 | bytes 2097152 | tf_op jit(solution)/shard_map/pallas_call | solution.py:261
  58.2 3.8 %all-to-all-start.2 = ((bf16[8,32,512]{2,1,0:T(8,128)(2,1)}), bf16[8,32,512]{2,1,0:T(8,128)(2,1)S(1)}, u32[]{:S(2)}, u32[]{:S(2)}) async-start(bf16[8,32,512]{2,1,0:T(8,128)(2,1)} %get-tuple-element.60), calls=%async_computation.2 | async-start | bytes 524288 | tf_op jit(solution)/shard_map/all_to_all | solution.py:246
  62.0 2.4 %collective-permute-start.7 = (bf16[128,128]{1,0:T(8,128)(2,1)}, bf16[128,128]{1,0:T(8,128)(2,1)}, u32[]{:S(2)}, u32[]{:S(2)}) collective-permute-start(bf16[128,128]{1,0:T(8,128)(2,1)} %copy-done.46), channel_id=1, source_target_pairs={{16,32},{48,64},{80,96},{112,0},{32,16},{64,48},{96,80},{0,112},{1... | collective-permute-start | bytes 98312 | tf_op jit(solution)/shard_map/ppermute | solution.py:217
  64.3 3.7 %all-to-all-done.2.mine_ref = bf16[8,32,512]{2,1,0:T(8,128)(2,1)S(1)} async-done(((bf16[8,32,512]{2,1,0:T(8,128)(2,1)}), bf16[8,32,512]{2,1,0:T(8,128)(2,1)S(1)}, u32[]{:S(2)}, u32[]{:S(2)}) %all-to-all-start.2) | async-done | bytes 262176 | tf_op jit(solution)/shard_map/all_to_all | solution.py:246
  68.0 3.2 %collective-permute-start.8 = (bf16[8,32,512]{2,1,0:T(8,128)(2,1)S(1)}, bf16[8,32,512]{2,1,0:T(8,128)(2,1)S(1)}, u32[]{:S(2)}, u32[]{:S(2)}) collective-permute-start(bf16[8,32,512]{2,1,0:T(8,128)(2,1)S(1)} %all-to-all-done.2.mine_ref), channel_id=1, source_target_pairs={{0,1},{2,3},{4,5},{6,7},{8,9},{10,11},{12,13},{14,15},{1,0},{3,2},... | collective-permute-start | bytes 786440 | tf_op jit(solution)/shard_map/ppermute | solution.py:217
  73.9 2.3 %shard_map.79.local_ref = f32[256,64]{1,0:T(8,128)S(1)} custom-call(s32[3]{0:T(128)S(1)} %pad_add_fusion.place_ref, bf16[128,128]{1,0:T(8,128)(2,1)S(1)} %copy-done.47, bf16[128,128]{1,0:T(8,128)(2,1)} %collective-permute-done.6.even_ref, bf16[128,128]{1,0:T(8,128)(2,1)} %collective-permute-done.7.odd_ref, bf16[1,2,64,1024]{3,2,1,0:T(8,128)(2,1)S(1)} %copy-done.8, ...), custom_call_target="tpu_custom_call" | custom-call | flops 4294967296 | bytes 2097152 | tf_op jit(solution)/shard_map/pallas_call | solution.py:249
  76.3 3.0 %shard_map.80 = (bf16[8,32,512]{2,1,0:T(8,128)(2,1)}, bf16[128,128]{1,0:T(8,128)(2,1)S(1)}, f32[256,64]{1,0:T(8,128)S(1)}, f32[256,64]{1,0:T(8,128)S(1)}, f32[256,64]{1,0:T(8,128)S(1)}) custom-call(s32[3]{0:T(128)S(1)} %pad_add_fusion.place_ref, f32[256,64]{1,0:T(8,128)S(1)} %shard_map.79.local_ref, bf16[8,32,512]{2,1,0:T(8,128)(2,1)S(1)} %all-to-all-done.2.mine_ref, ...), custom_call_target="tpu_custom_call" | custom-call | flops 4294967296 | bytes 2097152 | tf_op jit(solution)/shard_map/pallas_call | solution.py:261
  81.9 3.4 %all-to-all-start.3 = ((bf16[8,32,512]{2,1,0:T(8,128)(2,1)}), bf16[8,32,512]{2,1,0:T(8,128)(2,1)S(1)}, u32[]{:S(2)}, u32[]{:S(2)}) async-start(bf16[8,32,512]{2,1,0:T(8,128)(2,1)} %get-tuple-element.65), calls=%async_computation.3 | async-start | bytes 524288 | tf_op jit(solution)/shard_map/all_to_all | solution.py:246
  85.3 3.3 %collective-permute-start.10 = (bf16[128,128]{1,0:T(8,128)(2,1)}, bf16[128,128]{1,0:T(8,128)(2,1)}, u32[]{:S(2)}, u32[]{:S(2)}) collective-permute-start(bf16[128,128]{1,0:T(8,128)(2,1)} %copy-done.48), channel_id=1, source_target_pairs={{16,32},{48,64},{80,96},{112,0},{32,16},{64,48},{96,80},{0,112},{1... | collective-permute-start | bytes 98312 | tf_op jit(solution)/shard_map/ppermute | solution.py:217
  88.6 2.7 %all-to-all-done.3.mine_ref = bf16[8,32,512]{2,1,0:T(8,128)(2,1)S(1)} async-done(((bf16[8,32,512]{2,1,0:T(8,128)(2,1)}), bf16[8,32,512]{2,1,0:T(8,128)(2,1)S(1)}, u32[]{:S(2)}, u32[]{:S(2)}) %all-to-all-start.3) | async-done | bytes 262176 | tf_op jit(solution)/shard_map/all_to_all | solution.py:246
  91.3 4.1 %collective-permute-start.11 = (bf16[8,32,512]{2,1,0:T(8,128)(2,1)S(1)}, bf16[8,32,512]{2,1,0:T(8,128)(2,1)S(1)}, u32[]{:S(2)}, u32[]{:S(2)}) collective-permute-start(bf16[8,32,512]{2,1,0:T(8,128)(2,1)S(1)} %all-to-all-done.3.mine_ref), channel_id=1, source_target_pairs={{0,1},{2,3},{4,5},{6,7},{8,9},{10,11},{12,13},{14,15},{1,0},{3,2},... | collective-permute-start | bytes 786440 | tf_op jit(solution)/shard_map/ppermute | solution.py:217
  98.0 2.3 %shard_map.81.local_ref = f32[256,64]{1,0:T(8,128)S(1)} custom-call(s32[3]{0:T(128)S(1)} %pad_add_fusion.place_ref, bf16[128,128]{1,0:T(8,128)(2,1)S(1)} %copy-done.49, bf16[128,128]{1,0:T(8,128)(2,1)} %collective-permute-done.9.even_ref, bf16[128,128]{1,0:T(8,128)(2,1)} %collective-permute-done.10.odd_ref, bf16[1,2,64,1024]{3,2,1,0:T(8,128)(2,1)S(1)} %copy-done.9, ...), custom_call_target="tpu_custom_call" | custom-call | flops 4294967296 | bytes 2097152 | tf_op jit(solution)/shard_map/pallas_call | solution.py:249
  100.4 3.0 %shard_map.82 = (bf16[8,32,512]{2,1,0:T(8,128)(2,1)}, bf16[128,128]{1,0:T(8,128)(2,1)S(1)}, f32[256,64]{1,0:T(8,128)S(1)}) custom-call(s32[3]{0:T(128)S(1)} %pad_add_fusion.place_ref, f32[256,64]{1,0:T(8,128)S(1)} %shard_map.81.local_ref, bf16[8,32,512]{2,1,0:T(8,128)(2,1)S(1)} %all-to-all-done.3.mine_ref, ...), custom_call_target="tpu_custom_call" | custom-call | flops 4294967296 | bytes 2097152 | tf_op jit(solution)/shard_map/pallas_call | solution.py:261
  104.7 3.4 %all-to-all-start.4 = ((bf16[8,32,512]{2,1,0:T(8,128)(2,1)}), bf16[8,32,512]{2,1,0:T(8,128)(2,1)S(1)}, u32[]{:S(2)}, u32[]{:S(2)}) async-start(bf16[8,32,512]{2,1,0:T(8,128)(2,1)} %get-tuple-element.70), calls=%async_computation.4 | async-start | bytes 524288 | tf_op jit(solution)/shard_map/all_to_all | solution.py:246
  108.1 3.0 %collective-permute-start.13 = (bf16[128,128]{1,0:T(8,128)(2,1)}, bf16[128,128]{1,0:T(8,128)(2,1)}, u32[]{:S(2)}, u32[]{:S(2)}) collective-permute-start(bf16[128,128]{1,0:T(8,128)(2,1)} %copy-done.54), channel_id=1, source_target_pairs={{16,32},{48,64},{80,96},{112,0},{32,16},{64,48},{96,80},{0,112},{1... | collective-permute-start | bytes 98312 | tf_op jit(solution)/shard_map/ppermute | solution.py:217
  111.2 3.0 %all-to-all-done.4.mine_ref = bf16[8,32,512]{2,1,0:T(8,128)(2,1)S(1)} async-done(((bf16[8,32,512]{2,1,0:T(8,128)(2,1)}), bf16[8,32,512]{2,1,0:T(8,128)(2,1)S(1)}, u32[]{:S(2)}, u32[]{:S(2)}) %all-to-all-start.4) | async-done | bytes 262176 | tf_op jit(solution)/shard_map/all_to_all | solution.py:246
  114.1 4.2 %collective-permute-start.14 = (bf16[8,32,512]{2,1,0:T(8,128)(2,1)S(1)}, bf16[8,32,512]{2,1,0:T(8,128)(2,1)S(1)}, u32[]{:S(2)}, u32[]{:S(2)}) collective-permute-start(bf16[8,32,512]{2,1,0:T(8,128)(2,1)S(1)} %all-to-all-done.4.mine_ref), channel_id=1, source_target_pairs={{0,1},{2,3},{4,5},{6,7},{8,9},{10,11},{12,13},{14,15},{1,0},{3,2},... | collective-permute-start | bytes 786440 | tf_op jit(solution)/shard_map/ppermute | solution.py:217
  120.9 2.3 %shard_map.83.local_ref = f32[256,64]{1,0:T(8,128)S(1)} custom-call(s32[3]{0:T(128)S(1)} %pad_add_fusion.place_ref, bf16[128,128]{1,0:T(8,128)(2,1)S(1)} %copy-done.55, bf16[128,128]{1,0:T(8,128)(2,1)} %collective-permute-done.12.even_ref, bf16[128,128]{1,0:T(8,128)(2,1)} %collective-permute-done.13.odd_ref, bf16[1,2,64,1024]{3,2,1,0:T(8,128)(2,1)S(1)} %copy-done.10, ...), custom_call_target="tpu_custom_call" | custom-call | flops 4294967296 | bytes 2097152 | tf_op jit(solution)/shard_map/pallas_call | solution.py:249
  123.3 3.0 %shard_map.84 = (bf16[8,32,512]{2,1,0:T(8,128)(2,1)}, bf16[128,128]{1,0:T(8,128)(2,1)S(1)}, f32[256,64]{1,0:T(8,128)S(1)}, f32[256,64]{1,0:T(8,128)S(1)}, f32[256,64]{1,0:T(8,128)S(1)}) custom-call(s32[3]{0:T(128)S(1)} %pad_add_fusion.place_ref, f32[256,64]{1,0:T(8,128)S(1)} %shard_map.83.local_ref, bf16[8,32,512]{2,1,0:T(8,128)(2,1)S(1)} %all-to-all-done.4.mine_ref, ...), custom_call_target="tpu_custom_call" | custom-call | flops 4294967296 | bytes 2097152 | tf_op jit(solution)/shard_map/pallas_call | solution.py:261
  128.9 3.4 %all-to-all-start.5 = ((bf16[8,32,512]{2,1,0:T(8,128)(2,1)}), bf16[8,32,512]{2,1,0:T(8,128)(2,1)S(1)}, u32[]{:S(2)}, u32[]{:S(2)}) async-start(bf16[8,32,512]{2,1,0:T(8,128)(2,1)} %get-tuple-element.73), calls=%async_computation.5 | async-start | bytes 524288 | tf_op jit(solution)/shard_map/all_to_all | solution.py:246
  132.3 3.0 %collective-permute-start.16 = (bf16[128,128]{1,0:T(8,128)(2,1)}, bf16[128,128]{1,0:T(8,128)(2,1)}, u32[]{:S(2)}, u32[]{:S(2)}) collective-permute-start(bf16[128,128]{1,0:T(8,128)(2,1)} %copy-done.56), channel_id=1, source_target_pairs={{16,32},{48,64},{80,96},{112,0},{32,16},{64,48},{96,80},{0,112},{1... | collective-permute-start | bytes 98312 | tf_op jit(solution)/shard_map/ppermute | solution.py:217
  135.3 3.0 %all-to-all-done.5.mine_ref = bf16[8,32,512]{2,1,0:T(8,128)(2,1)S(1)} async-done(((bf16[8,32,512]{2,1,0:T(8,128)(2,1)}), bf16[8,32,512]{2,1,0:T(8,128)(2,1)S(1)}, u32[]{:S(2)}, u32[]{:S(2)}) %all-to-all-start.5) | async-done | bytes 262176 | tf_op jit(solution)/shard_map/all_to_all | solution.py:246
  138.3 4.1 %collective-permute-start.17 = (bf16[8,32,512]{2,1,0:T(8,128)(2,1)S(1)}, bf16[8,32,512]{2,1,0:T(8,128)(2,1)S(1)}, u32[]{:S(2)}, u32[]{:S(2)}) collective-permute-start(bf16[8,32,512]{2,1,0:T(8,128)(2,1)S(1)} %all-to-all-done.5.mine_ref), channel_id=1, source_target_pairs={{0,1},{2,3},{4,5},{6,7},{8,9},{10,11},{12,13},{14,15},{1,0},{3,2},... | collective-permute-start | bytes 786440 | tf_op jit(solution)/shard_map/ppermute | solution.py:217
  145.0 2.3 %shard_map.85.local_ref = f32[256,64]{1,0:T(8,128)S(1)} custom-call(s32[3]{0:T(128)S(1)} %pad_add_fusion.place_ref, bf16[128,128]{1,0:T(8,128)(2,1)S(1)} %copy-done.57, bf16[128,128]{1,0:T(8,128)(2,1)} %collective-permute-done.15.even_ref, bf16[128,128]{1,0:T(8,128)(2,1)} %collective-permute-done.16.odd_ref, bf16[1,2,64,1024]{3,2,1,0:T(8,128)(2,1)S(1)} %copy-done.11, ...), custom_call_target="tpu_custom_call" | custom-call | flops 4294967296 | bytes 2097152 | tf_op jit(solution)/shard_map/pallas_call | solution.py:249
  147.5 3.0 %shard_map.86 = (bf16[8,32,512]{2,1,0:T(8,128)(2,1)}, bf16[128,128]{1,0:T(8,128)(2,1)S(1)}, f32[256,64]{1,0:T(8,128)S(1)}, f32[256,64]{1,0:T(8,128)S(1)}, f32[256,64]{1,0:T(8,128)S(1)}) custom-call(s32[3]{0:T(128)S(1)} %pad_add_fusion.place_ref, f32[256,64]{1,0:T(8,128)S(1)} %shard_map.85.local_ref, bf16[8,32,512]{2,1,0:T(8,128)(2,1)S(1)} %all-to-all-done.5.mine_ref, ...), custom_call_target="tpu_custom_call" | custom-call | flops 4294967296 | bytes 2097152 | tf_op jit(solution)/shard_map/pallas_call | solution.py:261
  153.1 3.4 %all-to-all-start.6 = ((bf16[8,32,512]{2,1,0:T(8,128)(2,1)}), bf16[8,32,512]{2,1,0:T(8,128)(2,1)S(1)}, u32[]{:S(2)}, u32[]{:S(2)}) async-start(bf16[8,32,512]{2,1,0:T(8,128)(2,1)} %get-tuple-element.78), calls=%async_computation.6 | async-start | bytes 524288 | tf_op jit(solution)/shard_map/all_to_all | solution.py:246
  156.5 3.0 %collective-permute-start.19 = (bf16[128,128]{1,0:T(8,128)(2,1)}, bf16[128,128]{1,0:T(8,128)(2,1)}, u32[]{:S(2)}, u32[]{:S(2)}) collective-permute-start(bf16[128,128]{1,0:T(8,128)(2,1)} %copy-done.50), channel_id=1, source_target_pairs={{16,32},{48,64},{80,96},{112,0},{32,16},{64,48},{96,80},{0,112},{1... | collective-permute-start | bytes 98312 | tf_op jit(solution)/shard_map/ppermute | solution.py:217
  159.5 3.0 %all-to-all-done.6.mine_ref = bf16[8,32,512]{2,1,0:T(8,128)(2,1)S(1)} async-done(((bf16[8,32,512]{2,1,0:T(8,128)(2,1)}), bf16[8,32,512]{2,1,0:T(8,128)(2,1)S(1)}, u32[]{:S(2)}, u32[]{:S(2)}) %all-to-all-start.6) | async-done | bytes 262176 | tf_op jit(solution)/shard_map/all_to_all | solution.py:246
  162.5 4.1 %collective-permute-start.20 = (bf16[8,32,512]{2,1,0:T(8,128)(2,1)S(1)}, bf16[8,32,512]{2,1,0:T(8,128)(2,1)S(1)}, u32[]{:S(2)}, u32[]{:S(2)}) collective-permute-start(bf16[8,32,512]{2,1,0:T(8,128)(2,1)S(1)} %all-to-all-done.6.mine_ref), channel_id=1, source_target_pairs={{0,1},{2,3},{4,5},{6,7},{8,9},{10,11},{12,13},{14,15},{1,0},{3,2},... | collective-permute-start | bytes 786440 | tf_op jit(solution)/shard_map/ppermute | solution.py:217
  169.2 2.3 %shard_map.87.local_ref = f32[256,64]{1,0:T(8,128)S(1)} custom-call(s32[3]{0:T(128)S(1)} %pad_add_fusion.place_ref, bf16[128,128]{1,0:T(8,128)(2,1)S(1)} %copy-done.51, bf16[128,128]{1,0:T(8,128)(2,1)} %collective-permute-done.18.even_ref, bf16[128,128]{1,0:T(8,128)(2,1)} %collective-permute-done.19.odd_ref, bf16[1,2,64,1024]{3,2,1,0:T(8,128)(2,1)S(1)} %copy-done.12, ...), custom_call_target="tpu_custom_call" | custom-call | flops 4294967296 | bytes 2097152 | tf_op jit(solution)/shard_map/pallas_call | solution.py:249
  171.7 3.0 %shard_map.88 = (bf16[8,32,512]{2,1,0:T(8,128)(2,1)}, bf16[128,128]{1,0:T(8,128)(2,1)S(1)}, f32[256,64]{1,0:T(8,128)S(1)}, f32[256,64]{1,0:T(8,128)S(1)}, f32[256,64]{1,0:T(8,128)S(1)}) custom-call(s32[3]{0:T(128)S(1)} %pad_add_fusion.place_ref, f32[256,64]{1,0:T(8,128)S(1)} %shard_map.87.local_ref, bf16[8,32,512]{2,1,0:T(8,128)(2,1)S(1)} %all-to-all-done.6.mine_ref, ...), custom_call_target="tpu_custom_call" | custom-call | flops 4294967296 | bytes 2097152 | tf_op jit(solution)/shard_map/pallas_call | solution.py:261
  177.3 3.4 %all-to-all-start.7 = ((bf16[8,32,512]{2,1,0:T(8,128)(2,1)}), bf16[8,32,512]{2,1,0:T(8,128)(2,1)S(1)}, u32[]{:S(2)}, u32[]{:S(2)}) async-start(bf16[8,32,512]{2,1,0:T(8,128)(2,1)} %get-tuple-element.83), calls=%async_computation.7 | async-start | bytes 524288 | tf_op jit(solution)/shard_map/all_to_all | solution.py:246
  180.7 3.0 %collective-permute-start.22 = (bf16[128,128]{1,0:T(8,128)(2,1)}, bf16[128,128]{1,0:T(8,128)(2,1)}, u32[]{:S(2)}, u32[]{:S(2)}) collective-permute-start(bf16[128,128]{1,0:T(8,128)(2,1)} %copy-done.52), channel_id=1, source_target_pairs={{16,32},{48,64},{80,96},{112,0},{32,16},{64,48},{96,80},{0,112},{1... | collective-permute-start | bytes 98312 | tf_op jit(solution)/shard_map/ppermute | solution.py:217
  183.7 3.0 %all-to-all-done.7.mine_ref = bf16[8,32,512]{2,1,0:T(8,128)(2,1)S(1)} async-done(((bf16[8,32,512]{2,1,0:T(8,128)(2,1)}), bf16[8,32,512]{2,1,0:T(8,128)(2,1)S(1)}, u32[]{:S(2)}, u32[]{:S(2)}) %all-to-all-start.7) | async-done | bytes 262176 | tf_op jit(solution)/shard_map/all_to_all | solution.py:246
  186.7 4.1 %collective-permute-start.23 = (bf16[8,32,512]{2,1,0:T(8,128)(2,1)S(1)}, bf16[8,32,512]{2,1,0:T(8,128)(2,1)S(1)}, u32[]{:S(2)}, u32[]{:S(2)}) collective-permute-start(bf16[8,32,512]{2,1,0:T(8,128)(2,1)S(1)} %all-to-all-done.7.mine_ref), channel_id=1, source_target_pairs={{0,1},{2,3},{4,5},{6,7},{8,9},{10,11},{12,13},{14,15},{1,0},{3,2},... | collective-permute-start | bytes 786440 | tf_op jit(solution)/shard_map/ppermute | solution.py:217
  193.4 2.3 %shard_map.89.local_ref = f32[256,64]{1,0:T(8,128)S(1)} custom-call(s32[3]{0:T(128)S(1)} %pad_add_fusion.place_ref, bf16[128,128]{1,0:T(8,128)(2,1)S(1)} %copy-done.53, bf16[128,128]{1,0:T(8,128)(2,1)} %collective-permute-done.21.even_ref, bf16[128,128]{1,0:T(8,128)(2,1)} %collective-permute-done.22.odd_ref, bf16[1,2,64,1024]{3,2,1,0:T(8,128)(2,1)S(1)} %copy-done.13, ...), custom_call_target="tpu_custom_call" | custom-call | flops 4294967296 | bytes 2097152 | tf_op jit(solution)/shard_map/pallas_call | solution.py:249
  195.8 2.9 %shard_map.90 = f32[1,2,64,128]{3,2,1,0:T(8,128)} custom-call(s32[3]{0:T(128)S(1)} %pad_add_fusion.place_ref, f32[256,64]{1,0:T(8,128)S(1)} %shard_map.89.local_ref, bf16[8,32,512]{2,1,0:T(8,128)(2,1)S(1)} %all-to-all-done.7.mine_ref, bf16[8,32,512]{2,1,0:T(8,128)(2,1)S(1)} %collective-permute-done.23.other_ref, ...), custom_call_target="tpu_custom_call" | custom-call | flops 4294967296 | bytes 2097152 | tf_op jit(solution)/shard_map/pallas_call | solution.py:261
  (237 shorter events, 47.0 us)
Async XLA Ops:
  2.4 19.0 %copy-start.40 = (bf16[128,128]{1,0:T(8,128)(2,1)}, bf16[128,128]{1,0:T(8,128)(2,1)S(1)}, u32[]{:S(2)}) copy-start(bf16[128,128]{1,0:T(8,128)(2,1)S(1)} %get-tuple-element.46.own_ref) | copy-start | bytes 98308
  2.4 16.6 %all-to-all-start = ((bf16[8,32,512]{2,1,0:T(8,128)(2,1)}), bf16[8,32,512]{2,1,0:T(8,128)(2,1)S(1)}, u32[]{:S(2)}, u32[]{:S(2)}) async-start(bf16[8,32,512]{2,1,0:T(8,128)(2,1)} %get-tuple-element.49), calls=%async_computation | async-start | bytes 524288 | tf_op jit(solution)/shard_map/all_to_all | solution.py:246
  9.3 10.9 %collective-permute-start.1 = (bf16[128,128]{1,0:T(8,128)(2,1)S(1)}, bf16[128,128]{1,0:T(8,128)(2,1)S(1)}, u32[]{:S(2)}, u32[]{:S(2)}) collective-permute-start(bf16[128,128]{1,0:T(8,128)(2,1)S(1)} %get-tuple-element.46.own_ref), channel_id=1, source_target_pairs={{16,32},{48,64},{80,96},{112,0},{32,16},{64,48},{96,80},{0,112},{1... | collective-permute-start | bytes 98312 | tf_op jit(solution)/shard_map/ppermute | solution.py:217
  14.1 6.7 %collective-permute-start = (bf16[128,128]{1,0:T(8,128)(2,1)S(1)}, bf16[128,128]{1,0:T(8,128)(2,1)S(1)}, u32[]{:S(2)}, u32[]{:S(2)}) collective-permute-start(bf16[128,128]{1,0:T(8,128)(2,1)S(1)} %get-tuple-element.46.own_ref), channel_id=1, source_target_pairs={{0,16},{32,48},{64,80},{96,112},{16,0},{48,32},{80,64},{112,96},{1... | collective-permute-start | bytes 98312 | tf_op jit(solution)/shard_map/ppermute | solution.py:217
  19.0 10.1 %collective-permute-start.2 = (bf16[8,32,512]{2,1,0:T(8,128)(2,1)S(1)}, bf16[8,32,512]{2,1,0:T(8,128)(2,1)S(1)}, u32[]{:S(2)}, u32[]{:S(2)}) collective-permute-start(bf16[8,32,512]{2,1,0:T(8,128)(2,1)S(1)} %all-to-all-done.mine_ref), channel_id=1, source_target_pairs={{0,1},{2,3},{4,5},{6,7},{8,9},{10,11},{12,13},{14,15},{1,0},{3,2},... | collective-permute-start | bytes 786440 | tf_op jit(solution)/shard_map/ppermute | solution.py:217
  34.7 10.9 %all-to-all-start.1 = ((bf16[8,32,512]{2,1,0:T(8,128)(2,1)}), bf16[8,32,512]{2,1,0:T(8,128)(2,1)S(1)}, u32[]{:S(2)}, u32[]{:S(2)}) async-start(bf16[8,32,512]{2,1,0:T(8,128)(2,1)} %get-tuple-element.55), calls=%async_computation.1 | async-start | bytes 524288 | tf_op jit(solution)/shard_map/all_to_all | solution.py:246
  39.5 8.0 %collective-permute-start.4 = (bf16[128,128]{1,0:T(8,128)(2,1)}, bf16[128,128]{1,0:T(8,128)(2,1)}, u32[]{:S(2)}, u32[]{:S(2)}) collective-permute-start(bf16[128,128]{1,0:T(8,128)(2,1)} %copy-done.58), channel_id=1, source_target_pairs={{16,32},{48,64},{80,96},{112,0},{32,16},{64,48},{96,80},{0,112},{1... | collective-permute-start | bytes 98312 | tf_op jit(solution)/shard_map/ppermute | solution.py:217
  41.2 6.3 %collective-permute-start.3 = (bf16[128,128]{1,0:T(8,128)(2,1)}, bf16[128,128]{1,0:T(8,128)(2,1)}, u32[]{:S(2)}, u32[]{:S(2)}) collective-permute-start(bf16[128,128]{1,0:T(8,128)(2,1)} %copy-done.58), channel_id=1, source_target_pairs={{0,16},{32,48},{64,80},{96,112},{16,0},{48,32},{80,64},{112,96},{1... | collective-permute-start | bytes 98312 | tf_op jit(solution)/shard_map/ppermute | solution.py:217
  45.6 6.9 %collective-permute-start.5 = (bf16[8,32,512]{2,1,0:T(8,128)(2,1)S(1)}, bf16[8,32,512]{2,1,0:T(8,128)(2,1)S(1)}, u32[]{:S(2)}, u32[]{:S(2)}) collective-permute-start(bf16[8,32,512]{2,1,0:T(8,128)(2,1)S(1)} %all-to-all-done.1.mine_ref), channel_id=1, source_target_pairs={{0,1},{2,3},{4,5},{6,7},{8,9},{10,11},{12,13},{14,15},{1,0},{3,2},... | collective-permute-start | bytes 786440 | tf_op jit(solution)/shard_map/ppermute | solution.py:217
  50.1 2.4 %copy-start.33 = (bf16[256,128]{1,0:T(8,128)(2,1)S(1)}, bf16[256,128]{1,0:T(8,128)(2,1)}, u32[]{:S(2)}) copy-start(bf16[256,128]{1,0:T(8,128)(2,1)} %copy-done.31) | copy-start | bytes 196612
  50.1 2.4 %copy-start.96 = (f32[256,64]{1,0:T(8,128)S(1)}, f32[256,64]{1,0:T(8,128)}, u32[]{:S(2)}) copy-start(f32[256,64]{1,0:T(8,128)} %copy-done.95) | copy-start | bytes 196612
  50.1 2.4 %copy-start.98 = (f32[256,64]{1,0:T(8,128)S(1)}, f32[256,64]{1,0:T(8,128)}, u32[]{:S(2)}) copy-start(f32[256,64]{1,0:T(8,128)} %copy-done.97) | copy-start | bytes 196612
  50.1 2.4 %copy-start.100 = (f32[256,64]{1,0:T(8,128)S(1)}, f32[256,64]{1,0:T(8,128)}, u32[]{:S(2)}) copy-start(f32[256,64]{1,0:T(8,128)} %copy-done.99) | copy-start | bytes 196612
  58.2 9.9 %all-to-all-start.2 = ((bf16[8,32,512]{2,1,0:T(8,128)(2,1)}), bf16[8,32,512]{2,1,0:T(8,128)(2,1)S(1)}, u32[]{:S(2)}, u32[]{:S(2)}) async-start(bf16[8,32,512]{2,1,0:T(8,128)(2,1)} %get-tuple-element.60), calls=%async_computation.2 | async-start | bytes 524288 | tf_op jit(solution)/shard_map/all_to_all | solution.py:246
  62.0 9.3 %collective-permute-start.7 = (bf16[128,128]{1,0:T(8,128)(2,1)}, bf16[128,128]{1,0:T(8,128)(2,1)}, u32[]{:S(2)}, u32[]{:S(2)}) collective-permute-start(bf16[128,128]{1,0:T(8,128)(2,1)} %copy-done.46), channel_id=1, source_target_pairs={{16,32},{48,64},{80,96},{112,0},{32,16},{64,48},{96,80},{0,112},{1... | collective-permute-start | bytes 98312 | tf_op jit(solution)/shard_map/ppermute | solution.py:217
  64.3 6.9 %collective-permute-start.6 = (bf16[128,128]{1,0:T(8,128)(2,1)}, bf16[128,128]{1,0:T(8,128)(2,1)}, u32[]{:S(2)}, u32[]{:S(2)}) collective-permute-start(bf16[128,128]{1,0:T(8,128)(2,1)} %copy-done.46), channel_id=1, source_target_pairs={{0,16},{32,48},{64,80},{96,112},{16,0},{48,32},{80,64},{112,96},{1... | collective-permute-start | bytes 98312 | tf_op jit(solution)/shard_map/ppermute | solution.py:217
  68.0 8.2 %collective-permute-start.8 = (bf16[8,32,512]{2,1,0:T(8,128)(2,1)S(1)}, bf16[8,32,512]{2,1,0:T(8,128)(2,1)S(1)}, u32[]{:S(2)}, u32[]{:S(2)}) collective-permute-start(bf16[8,32,512]{2,1,0:T(8,128)(2,1)S(1)} %all-to-all-done.2.mine_ref), channel_id=1, source_target_pairs={{0,1},{2,3},{4,5},{6,7},{8,9},{10,11},{12,13},{14,15},{1,0},{3,2},... | collective-permute-start | bytes 786440 | tf_op jit(solution)/shard_map/ppermute | solution.py:217
  73.9 2.4 %copy-start.74 = (f32[256,64]{1,0:T(8,128)S(1)}, f32[256,64]{1,0:T(8,128)}, u32[]{:S(2)}) copy-start(f32[256,64]{1,0:T(8,128)} %copy-done.73) | copy-start | bytes 196612
  73.9 2.4 %copy-start.76 = (f32[256,64]{1,0:T(8,128)S(1)}, f32[256,64]{1,0:T(8,128)}, u32[]{:S(2)}) copy-start(f32[256,64]{1,0:T(8,128)} %copy-done.75) | copy-start | bytes 196612
  81.9 9.4 %all-to-all-start.3 = ((bf16[8,32,512]{2,1,0:T(8,128)(2,1)}), bf16[8,32,512]{2,1,0:T(8,128)(2,1)S(1)}, u32[]{:S(2)}, u32[]{:S(2)}) async-start(bf16[8,32,512]{2,1,0:T(8,128)(2,1)} %get-tuple-element.65), calls=%async_computation.3 | async-start | bytes 524288 | tf_op jit(solution)/shard_map/all_to_all | solution.py:246
  85.3 10.1 %collective-permute-start.10 = (bf16[128,128]{1,0:T(8,128)(2,1)}, bf16[128,128]{1,0:T(8,128)(2,1)}, u32[]{:S(2)}, u32[]{:S(2)}) collective-permute-start(bf16[128,128]{1,0:T(8,128)(2,1)} %copy-done.48), channel_id=1, source_target_pairs={{16,32},{48,64},{80,96},{112,0},{32,16},{64,48},{96,80},{0,112},{1... | collective-permute-start | bytes 98312 | tf_op jit(solution)/shard_map/ppermute | solution.py:217
  88.6 6.7 %collective-permute-start.9 = (bf16[128,128]{1,0:T(8,128)(2,1)}, bf16[128,128]{1,0:T(8,128)(2,1)}, u32[]{:S(2)}, u32[]{:S(2)}) collective-permute-start(bf16[128,128]{1,0:T(8,128)(2,1)} %copy-done.48), channel_id=1, source_target_pairs={{0,16},{32,48},{64,80},{96,112},{16,0},{48,32},{80,64},{112,96},{1... | collective-permute-start | bytes 98312 | tf_op jit(solution)/shard_map/ppermute | solution.py:217
  91.3 9.1 %collective-permute-start.11 = (bf16[8,32,512]{2,1,0:T(8,128)(2,1)S(1)}, bf16[8,32,512]{2,1,0:T(8,128)(2,1)S(1)}, u32[]{:S(2)}, u32[]{:S(2)}) collective-permute-start(bf16[8,32,512]{2,1,0:T(8,128)(2,1)S(1)} %all-to-all-done.3.mine_ref), channel_id=1, source_target_pairs={{0,1},{2,3},{4,5},{6,7},{8,9},{10,11},{12,13},{14,15},{1,0},{3,2},... | collective-permute-start | bytes 786440 | tf_op jit(solution)/shard_map/ppermute | solution.py:217
  98.0 2.4 %copy-start.84 = (f32[256,64]{1,0:T(8,128)S(1)}, f32[256,64]{1,0:T(8,128)}, u32[]{:S(2)}) copy-start(f32[256,64]{1,0:T(8,128)} %copy-done.83) | copy-start | bytes 196612
  98.0 2.4 %copy-start.86 = (f32[256,64]{1,0:T(8,128)S(1)}, f32[256,64]{1,0:T(8,128)}, u32[]{:S(2)}) copy-start(f32[256,64]{1,0:T(8,128)} %copy-done.85) | copy-start | bytes 196612
  98.0 2.4 %copy-start.88 = (f32[256,64]{1,0:T(8,128)S(1)}, f32[256,64]{1,0:T(8,128)}, u32[]{:S(2)}) copy-start(f32[256,64]{1,0:T(8,128)} %copy-done.87) | copy-start | bytes 196612
  104.7 9.4 %all-to-all-start.4 = ((bf16[8,32,512]{2,1,0:T(8,128)(2,1)}), bf16[8,32,512]{2,1,0:T(8,128)(2,1)S(1)}, u32[]{:S(2)}, u32[]{:S(2)}) async-start(bf16[8,32,512]{2,1,0:T(8,128)(2,1)} %get-tuple-element.70), calls=%async_computation.4 | async-start | bytes 524288 | tf_op jit(solution)/shard_map/all_to_all | solution.py:246
  108.1 10.2 %collective-permute-start.13 = (bf16[128,128]{1,0:T(8,128)(2,1)}, bf16[128,128]{1,0:T(8,128)(2,1)}, u32[]{:S(2)}, u32[]{:S(2)}) collective-permute-start(bf16[128,128]{1,0:T(8,128)(2,1)} %copy-done.54), channel_id=1, source_target_pairs={{16,32},{48,64},{80,96},{112,0},{32,16},{64,48},{96,80},{0,112},{1... | collective-permute-start | bytes 98312 | tf_op jit(solution)/shard_map/ppermute | solution.py:217
  111.2 7.1 %collective-permute-start.12 = (bf16[128,128]{1,0:T(8,128)(2,1)}, bf16[128,128]{1,0:T(8,128)(2,1)}, u32[]{:S(2)}, u32[]{:S(2)}) collective-permute-start(bf16[128,128]{1,0:T(8,128)(2,1)} %copy-done.54), channel_id=1, source_target_pairs={{0,16},{32,48},{64,80},{96,112},{16,0},{48,32},{80,64},{112,96},{1... | collective-permute-start | bytes 98312 | tf_op jit(solution)/shard_map/ppermute | solution.py:217
  114.1 9.1 %collective-permute-start.14 = (bf16[8,32,512]{2,1,0:T(8,128)(2,1)S(1)}, bf16[8,32,512]{2,1,0:T(8,128)(2,1)S(1)}, u32[]{:S(2)}, u32[]{:S(2)}) collective-permute-start(bf16[8,32,512]{2,1,0:T(8,128)(2,1)S(1)} %all-to-all-done.4.mine_ref), channel_id=1, source_target_pairs={{0,1},{2,3},{4,5},{6,7},{8,9},{10,11},{12,13},{14,15},{1,0},{3,2},... | collective-permute-start | bytes 786440 | tf_op jit(solution)/shard_map/ppermute | solution.py:217
  128.9 9.4 %all-to-all-start.5 = ((bf16[8,32,512]{2,1,0:T(8,128)(2,1)}), bf16[8,32,512]{2,1,0:T(8,128)(2,1)S(1)}, u32[]{:S(2)}, u32[]{:S(2)}) async-start(bf16[8,32,512]{2,1,0:T(8,128)(2,1)} %get-tuple-element.73), calls=%async_computation.5 | async-start | bytes 524288 | tf_op jit(solution)/shard_map/all_to_all | solution.py:246
  132.3 10.1 %collective-permute-start.16 = (bf16[128,128]{1,0:T(8,128)(2,1)}, bf16[128,128]{1,0:T(8,128)(2,1)}, u32[]{:S(2)}, u32[]{:S(2)}) collective-permute-start(bf16[128,128]{1,0:T(8,128)(2,1)} %copy-done.56), channel_id=1, source_target_pairs={{16,32},{48,64},{80,96},{112,0},{32,16},{64,48},{96,80},{0,112},{1... | collective-permute-start | bytes 98312 | tf_op jit(solution)/shard_map/ppermute | solution.py:217
  135.3 7.1 %collective-permute-start.15 = (bf16[128,128]{1,0:T(8,128)(2,1)}, bf16[128,128]{1,0:T(8,128)(2,1)}, u32[]{:S(2)}, u32[]{:S(2)}) collective-permute-start(bf16[128,128]{1,0:T(8,128)(2,1)} %copy-done.56), channel_id=1, source_target_pairs={{0,16},{32,48},{64,80},{96,112},{16,0},{48,32},{80,64},{112,96},{1... | collective-permute-start | bytes 98312 | tf_op jit(solution)/shard_map/ppermute | solution.py:217
  138.3 9.1 %collective-permute-start.17 = (bf16[8,32,512]{2,1,0:T(8,128)(2,1)S(1)}, bf16[8,32,512]{2,1,0:T(8,128)(2,1)S(1)}, u32[]{:S(2)}, u32[]{:S(2)}) collective-permute-start(bf16[8,32,512]{2,1,0:T(8,128)(2,1)S(1)} %all-to-all-done.5.mine_ref), channel_id=1, source_target_pairs={{0,1},{2,3},{4,5},{6,7},{8,9},{10,11},{12,13},{14,15},{1,0},{3,2},... | collective-permute-start | bytes 786440 | tf_op jit(solution)/shard_map/ppermute | solution.py:217
  145.0 2.4 %copy-start.92 = (f32[256,64]{1,0:T(8,128)S(1)}, f32[256,64]{1,0:T(8,128)}, u32[]{:S(2)}) copy-start(f32[256,64]{1,0:T(8,128)} %copy-done.91) | copy-start | bytes 196612
  145.0 2.4 %copy-start.94 = (f32[256,64]{1,0:T(8,128)S(1)}, f32[256,64]{1,0:T(8,128)}, u32[]{:S(2)}) copy-start(f32[256,64]{1,0:T(8,128)} %copy-done.93) | copy-start | bytes 196612
  153.1 9.4 %all-to-all-start.6 = ((bf16[8,32,512]{2,1,0:T(8,128)(2,1)}), bf16[8,32,512]{2,1,0:T(8,128)(2,1)S(1)}, u32[]{:S(2)}, u32[]{:S(2)}) async-start(bf16[8,32,512]{2,1,0:T(8,128)(2,1)} %get-tuple-element.78), calls=%async_computation.6 | async-start | bytes 524288 | tf_op jit(solution)/shard_map/all_to_all | solution.py:246
  156.5 10.1 %collective-permute-start.19 = (bf16[128,128]{1,0:T(8,128)(2,1)}, bf16[128,128]{1,0:T(8,128)(2,1)}, u32[]{:S(2)}, u32[]{:S(2)}) collective-permute-start(bf16[128,128]{1,0:T(8,128)(2,1)} %copy-done.50), channel_id=1, source_target_pairs={{16,32},{48,64},{80,96},{112,0},{32,16},{64,48},{96,80},{0,112},{1... | collective-permute-start | bytes 98312 | tf_op jit(solution)/shard_map/ppermute | solution.py:217
  159.5 7.1 %collective-permute-start.18 = (bf16[128,128]{1,0:T(8,128)(2,1)}, bf16[128,128]{1,0:T(8,128)(2,1)}, u32[]{:S(2)}, u32[]{:S(2)}) collective-permute-start(bf16[128,128]{1,0:T(8,128)(2,1)} %copy-done.50), channel_id=1, source_target_pairs={{0,16},{32,48},{64,80},{96,112},{16,0},{48,32},{80,64},{112,96},{1... | collective-permute-start | bytes 98312 | tf_op jit(solution)/shard_map/ppermute | solution.py:217
  162.5 9.1 %collective-permute-start.20 = (bf16[8,32,512]{2,1,0:T(8,128)(2,1)S(1)}, bf16[8,32,512]{2,1,0:T(8,128)(2,1)S(1)}, u32[]{:S(2)}, u32[]{:S(2)}) collective-permute-start(bf16[8,32,512]{2,1,0:T(8,128)(2,1)S(1)} %all-to-all-done.6.mine_ref), channel_id=1, source_target_pairs={{0,1},{2,3},{4,5},{6,7},{8,9},{10,11},{12,13},{14,15},{1,0},{3,2},... | collective-permute-start | bytes 786440 | tf_op jit(solution)/shard_map/ppermute | solution.py:217
  169.2 2.4 %copy-start.80 = (f32[256,64]{1,0:T(8,128)S(1)}, f32[256,64]{1,0:T(8,128)}, u32[]{:S(2)}) copy-start(f32[256,64]{1,0:T(8,128)} %copy-done.79) | copy-start | bytes 196612
  169.2 2.4 %copy-start.82 = (f32[256,64]{1,0:T(8,128)S(1)}, f32[256,64]{1,0:T(8,128)}, u32[]{:S(2)}) copy-start(f32[256,64]{1,0:T(8,128)} %copy-done.81) | copy-start | bytes 196612
  177.3 9.4 %all-to-all-start.7 = ((bf16[8,32,512]{2,1,0:T(8,128)(2,1)}), bf16[8,32,512]{2,1,0:T(8,128)(2,1)S(1)}, u32[]{:S(2)}, u32[]{:S(2)}) async-start(bf16[8,32,512]{2,1,0:T(8,128)(2,1)} %get-tuple-element.83), calls=%async_computation.7 | async-start | bytes 524288 | tf_op jit(solution)/shard_map/all_to_all | solution.py:246
  180.7 10.1 %collective-permute-start.22 = (bf16[128,128]{1,0:T(8,128)(2,1)}, bf16[128,128]{1,0:T(8,128)(2,1)}, u32[]{:S(2)}, u32[]{:S(2)}) collective-permute-start(bf16[128,128]{1,0:T(8,128)(2,1)} %copy-done.52), channel_id=1, source_target_pairs={{16,32},{48,64},{80,96},{112,0},{32,16},{64,48},{96,80},{0,112},{1... | collective-permute-start | bytes 98312 | tf_op jit(solution)/shard_map/ppermute | solution.py:217
  183.7 7.1 %collective-permute-start.21 = (bf16[128,128]{1,0:T(8,128)(2,1)}, bf16[128,128]{1,0:T(8,128)(2,1)}, u32[]{:S(2)}, u32[]{:S(2)}) collective-permute-start(bf16[128,128]{1,0:T(8,128)(2,1)} %copy-done.52), channel_id=1, source_target_pairs={{0,16},{32,48},{64,80},{96,112},{16,0},{48,32},{80,64},{112,96},{1... | collective-permute-start | bytes 98312 | tf_op jit(solution)/shard_map/ppermute | solution.py:217
  186.7 9.1 %collective-permute-start.23 = (bf16[8,32,512]{2,1,0:T(8,128)(2,1)S(1)}, bf16[8,32,512]{2,1,0:T(8,128)(2,1)S(1)}, u32[]{:S(2)}, u32[]{:S(2)}) collective-permute-start(bf16[8,32,512]{2,1,0:T(8,128)(2,1)S(1)} %all-to-all-done.7.mine_ref), channel_id=1, source_target_pairs={{0,1},{2,3},{4,5},{6,7},{8,9},{10,11},{12,13},{14,15},{1,0},{3,2},... | collective-permute-start | bytes 786440 | tf_op jit(solution)/shard_map/ppermute | solution.py:217
  193.4 2.4 %copy-start.68 = (f32[256,64]{1,0:T(8,128)S(1)}, f32[256,64]{1,0:T(8,128)}, u32[]{:S(2)}) copy-start(f32[256,64]{1,0:T(8,128)} %copy-done.67) | copy-start | bytes 196612
  193.4 2.4 %copy-start.70 = (f32[256,64]{1,0:T(8,128)S(1)}, f32[256,64]{1,0:T(8,128)}, u32[]{:S(2)}) copy-start(f32[256,64]{1,0:T(8,128)} %copy-done.69) | copy-start | bytes 196612
  (85 other events, 99.9 us)
where the time goes:
time: 201 us; the launch traced here: 199 us
  starting transfers between devices  84 us (42%)
  local copies, waits for them, and re-layouts  46.5 us (23%)
  Pallas kernels  44.3 us (22%)
  waiting for transfers between devices  22.6 us (11%)
    ppermute x24, starting transfers between devices, swap(): return lax.ppermute(value, axis, pairs + [(b, a) for a, b in pairs])  51.4 us
    unnamed x202, local copies, waits for them, and re-layouts  46.5 us
    all_to_all x8, starting transfers between devices, shards(): mine = lax.all_to_all(spread, 'gy', 0, 0, axis_index_groups=same_core)  32.5 us
    pallas_call x8, Pallas kernels, shards(): call(make_final_kernel(turn, last), outs, 1, 9 + len(extra), [rows_scratc...  24.2 us
    all_to_all x8, waiting for transfers between devices, shards(): mine = lax.all_to_all(spread, 'gy', 0, 0, axis_index_groups=same_core)  22.5 us
    pallas_call x8, Pallas kernels, shards(): call(local_kernel, state, 1, 7, flops=4 << 30)  18.4 us
  transfers between devices with their start and end apart: 32, of which 7 were waited for; matrix products, arithmetic and copies ran while one was open for 0% of the time, Pallas kernels for 10%

commit v1 on v0

v1 whole, which is shorter than its diff:
```python
import jax
import jax.numpy as jnp
from jax import lax
from jax.experimental import pallas as pl
from jax.experimental.pallas import tpu as pltpu
from jax.sharding import PartitionSpec as P

NODES = 64
RHS = 8
LZ = 16
SWEEPS = 2
DEGREE = 4
ROWS = LZ * RHS
ELEMS = 2 * LZ
PAIRS = 128
CHIPS = 8
ROOM = 14
LOCAL_ROOM = 14
STATE_ROWS = 8192

spectrum_low = 0.6
spectrum_high = 3.0

BF = jnp.bfloat16
F32 = jnp.float32
NT = (((1,), (1,)), ((), ()))


def dot(a, b):
    return jnp.dot(a, b, preferred_element_type=F32)


def dot_t(a, b):
    return lax.dot_general(a, b, NT, preferred_element_type=F32)


def iota(shape, dim):
    return lax.broadcasted_iota(jnp.int32, shape, dim)


def coefficients():
    centre_point = (spectrum_high + spectrum_low) / 2.0
    half_width = (spectrum_high - spectrum_low) / 2.0
    sigma_ratio = centre_point / half_width
    steps = []
    rho_prev = 1.0 / sigma_ratio
    for _ in range(1, DEGREE):
        rho_next = 1.0 / (2.0 * sigma_ratio - rho_prev)
        steps.append((rho_next * rho_prev, 2.0 * rho_next / half_width))
        rho_prev = rho_next
    return centre_point, steps


def send_field(field, spread_out, packed_out, scratch):
    rows_ref, spread_ref, packed_ref, sems = scratch
    rows_ref[...] = field
    pieces = [rows_ref[pl.ds(r, ELEMS, stride=RHS), :] for r in range(RHS)]
    spread_ref[...] = jnp.concatenate(pieces, axis=1).astype(BF)
    copies = [pltpu.make_async_copy(spread_ref, spread_out.at[chip], sems.at[chip]) for chip in range(CHIPS)]
    for copy in copies:
        copy.start()
    packed_ref[...] = jnp.concatenate([field[:ROWS], field[ROWS:]], axis=1).astype(BF)
    copies.append(pltpu.make_async_copy(packed_ref, packed_out, sems.at[CHIPS]))
    copies[-1].start()
    return copies


def send_states(states, outs, state_ref, sems):
    copies = []
    for k, value in enumerate(states):
        state_ref[k] = value
        copies.append(
            pltpu.make_async_copy(state_ref.at[k], outs[k].at[pl.ds(0, ELEMS * RHS)], sems.at[CHIPS + 1 + k])
        )
        copies[-1].start()
    return copies


def first_kernel(initial_ref, spread_out, packed_out, solution_out, state_ref, *scratch):
    field = jnp.concatenate([initial_ref[0, 0].T, initial_ref[0, 1].T], axis=0)
    copies = send_states((field,), (solution_out,), state_ref, scratch[-1])
    copies += send_field(field, spread_out, packed_out, scratch)
    for copy in copies:
        copy.wait()


def setup_kernel(count_ref, right_ref, faults_ref, right_out, index_out):
    right_out[...] = jnp.concatenate([right_ref[0, 0].T, right_ref[0, 1].T], axis=0)
    device = faults_ref[1]
    column = (
        jnp.where(device % 2 == lax.axis_index("gy") % 2, 0, CHIPS * ELEMS)
        + (device // 2) * ELEMS
        + faults_ref[2]
    )
    owner = jnp.where(iota((1, PAIRS), 1) < count_ref[0, 0], faults_ref[0], -1)
    index_out[...] = jnp.concatenate([column, owner, jnp.zeros((6, PAIRS), jnp.int32)], axis=0)


def one_hot(hit):
    return jnp.where(hit, 1.0, 0.0).astype(BF)


def expander():
    return one_hot(iota((NODES, NODES * LZ), 1) // LZ == iota((NODES, NODES * LZ), 0))


def layer_mask(shift):
    return one_hot(iota((ROWS, 128), 1) % LZ - iota((ROWS, 128), 0) // RHS == shift)


def masked(expanded, mask):
    return expanded * jnp.concatenate([mask] * (NODES * LZ // 128), axis=1)


def gathered(index_ref, half, blocks_ref):
    rows = CHIPS * ELEMS
    hit = iota((rows, PAIRS), 0) + half * rows == index_ref[0:1, :]
    return dot(blocks_ref[...].reshape(rows, RHS * NODES).T, one_hot(hit))


def local_kernel(own_ref, elem_hbm, face_hbm, out_ref, elem_ref, side_ref, layer_ref, sems):
    copies = [
        pltpu.make_async_copy(elem_hbm.at[0], elem_ref, sems.at[0]),
        pltpu.make_async_copy(face_hbm.at[2, 0, 1], side_ref.at[0], sems.at[1]),
        pltpu.make_async_copy(face_hbm.at[3, 0, 0], side_ref.at[1], sems.at[2]),
        pltpu.make_async_copy(face_hbm.at[pl.ds(4, 2), 0], layer_ref, sems.at[3]),
    ]
    for copy in copies:
        copy.start()
    expand = expander()
    wide = [dot(own_ref[:, ly * NODES : (ly + 1) * NODES], expand).astype(BF) for ly in range(2)]
    same, up, down = layer_mask(0), layer_mask(1), layer_mask(-1)
    zero = jnp.zeros((RHS, NODES), F32)
    here = [masked(wide[ly], same) for ly in range(2)]
    for copy in copies[:3]:
        copy.wait()
    sums = [dot_t(here[ly], elem_ref[ly]) + dot_t(here[1 - ly], side_ref[1 - ly]) for ly in range(2)]
    copies[3].wait()
    for ly in range(2):
        lower = dot_t(masked(wide[ly], up), layer_ref[0, ly])
        upper = dot_t(masked(wide[ly], down), layer_ref[1, ly])
        sums[ly] += jnp.concatenate([zero, lower[:-RHS]], axis=0) + jnp.concatenate([upper[RHS:], zero], axis=0)
    out_ref[...] = jnp.concatenate(sums, axis=0)


def make_stage_kernel(turn):
    _, steps = coefficients()
    n_states = 1 if turn == 0 else 2
    n_late = min(turn, 1) + (turn == DEGREE - 1)

    def stage_kernel(mine_ref, even_ref, odd_ref, index_ref, face_hbm, fault_hbm, local_hbm, *refs):
        states, refs = refs[:n_states], refs[n_states:]
        late, refs = refs[:n_late], refs[n_late:]
        fault_ref, sides_ref, index_out, base_ref, half_ref, *refs = refs
        late_refs, refs = refs[:n_late], refs[n_late:]
        face_ref, local_ref, state_ref, sems = refs
        field_rows = pl.ds(0, ELEMS * RHS)
        first = [
            pltpu.make_async_copy(face_hbm.at[pl.ds(0, 2), 0], face_ref, sems.at[0]),
            pltpu.make_async_copy(local_hbm, local_ref, sems.at[1]),
        ]
        first += [
            pltpu.make_async_copy(a.at[field_rows], state_ref.at[k], sems.at[2 + k]) for k, a in enumerate(states)
        ]
        later = [
            pltpu.make_async_copy(fault_hbm.at[0, 0], fault_ref, sems.at[4]),
            pltpu.make_async_copy(face_hbm.at[2, 0, 0], sides_ref.at[0], sems.at[5]),
            pltpu.make_async_copy(face_hbm.at[3, 0, 1], sides_ref.at[1], sems.at[6]),
        ]
        later += [
            pltpu.make_async_copy(a.at[field_rows], b, sems.at[7 + k]) for k, (a, b) in enumerate(zip(late, late_refs))
        ]
        for copy in first + later:
            copy.start()
        index_out[...] = index_ref[...]
        half_ref[...] = gathered(index_ref, 0, mine_ref)
        at = lax.axis_index("gx")
        is_even = at % 2 == 0
        low = jnp.where(is_even, odd_ref[...], even_ref[...])
        high = jnp.where(is_even, even_ref[...], odd_ref[...])
        low = jnp.where(at > 0, low, jnp.zeros_like(low))
        high = jnp.where(at < 7, high, jnp.zeros_like(high))
        expand, same = expander(), layer_mask(0)
        wide = [
            [masked(dot(field[:, ly * NODES : (ly + 1) * NODES], expand).astype(BF), same) for field in (low, high)]
            for ly in range(2)
        ]
        for copy in first:
            copy.wait()
        sums = [dot_t(wide[ly][0], face_ref[0, ly]) + dot_t(wide[ly][1], face_ref[1, ly]) for ly in range(2)]
        local = local_ref[...] + jnp.concatenate(sums, axis=0)
        if turn == 0:
            base_ref[...] = state_ref[0] - local
        else:
            old, new = steps[turn - 1]
            base_ref[...] = old * state_ref[1] + new * (state_ref[0] - local)
        for copy in later:
            copy.wait()

    return stage_kernel


def make_final_kernel(turn, last):
    centre_point, steps = coefficients()
    n_late = min(turn, 1) + (turn == DEGREE - 1)

    def final_kernel(other_ref, fault_ref, sides_ref, index_ref, base_ref, half_ref, *refs):
        held, refs = refs[:n_late], refs[n_late:]
        n_outs = 1 if last else 3 if turn == DEGREE - 1 else 4
        outs, refs = refs[:n_outs], refs[n_outs:]
        values_ref, plane_ref, state_ref, *scratch = refs
        values_ref[...] = half_ref[...] + gathered(index_ref, 1, other_ref)
        at = lax.axis_index("gy")
        chip = at // 2
        is_even = at % 2 == 0
        low_chip = jnp.where(is_even, jnp.maximum(chip - 1, 0), chip)
        high_chip = jnp.where(is_even, chip, jnp.minimum(chip + 1, CHIPS - 1))
        expand, same = expander(), layer_mask(0)
        sums = []
        for ly in range(2):
            if ly == 0:
                plane = other_ref[low_chip, LZ:].astype(F32)
                plane = jnp.where(at > 0, plane, jnp.zeros_like(plane))
            else:
                plane = other_ref[high_chip, :LZ].astype(F32)
                plane = jnp.where(at < 2 * CHIPS - 1, plane, jnp.zeros_like(plane))
            for r in range(RHS):
                plane_ref[ly, pl.ds(r, LZ, stride=RHS), :] = plane[:, r * NODES : (r + 1) * NODES]
            wide = dot(plane_ref[ly].astype(BF), expand).astype(BF)
            sums.append(dot_t(masked(wide, same), sides_ref[ly]))
        total = jnp.concatenate(sums, axis=0)
        land = one_hot(iota((ELEMS * RHS, PAIRS), 0) // RHS == index_ref[1:2, :])
        land = land.reshape(ELEMS // 2, 2 * RHS, PAIRS)
        group = 4
        for start in range(0, NODES, group):
            parts = []
            for m in range(start, start + group):
                value = values_ref[pl.ds(m, RHS, stride=NODES), :]
                value = jnp.concatenate([value, value], axis=0).astype(BF)
                parts.append((land * value[None]).reshape(ELEMS * RHS, PAIRS))
            total = total + dot_t(
                jnp.concatenate(parts, axis=1), fault_ref[:, start * PAIRS : (start + group) * PAIRS]
            )
        if turn == 0:
            residual = base_ref[...] - total
            step = residual / centre_point
            states = (residual, step)
        else:
            step = base_ref[...] - steps[turn - 1][1] * total
            correction = held[0][...] + step
            states = (step, correction)
        if turn == DEGREE - 1:
            states = (held[1][...] + correction,)
        if last:
            outs[0][0, 0] = states[0][:ROWS].T
            outs[0][0, 1] = states[0][ROWS:].T
            return
        copies = send_states(states, outs[2:], state_ref, scratch[-1])
        copies += send_field(states[-1], outs[0], outs[1], scratch)
        for copy in copies:
            copy.wait()

    return final_kernel


VMEM = pl.BlockSpec(memory_space=pltpu.VMEM)
SMEM = pl.BlockSpec(memory_space=pltpu.SMEM)
HBM = pl.BlockSpec(memory_space=pltpu.HBM)
ANY = pl.BlockSpec(memory_space=pl.ANY)


def call(kernel, in_specs, out_shape, out_specs, scratch=(), flops=0, room=2):
    return pl.pallas_call(
        kernel,
        out_shape=out_shape,
        in_specs=in_specs,
        out_specs=out_specs,
        scratch_shapes=list(scratch),
        compiler_params=pltpu.CompilerParams(vmem_limit_bytes=(64 - room) * 1024 * 1024),
        cost_estimate=pl.CostEstimate(flops=flops, bytes_accessed=2 << 20, transcendentals=0),
    )


def shape(dims, dtype):
    return jax.ShapeDtypeStruct(dims, dtype)


def swap(value, axis, pairs):
    return lax.ppermute(value, axis, pairs + [(b, a) for a, b in pairs])


def shards(right_side, initial, elem_blocks, face_blocks, fault_blocks, faults, fault_count):
    same_core = [list(range(core, 2 * CHIPS, 2)) for core in range(2)]
    field_rows = ELEMS * RHS
    state = shape((field_rows, NODES), F32)
    big_state = shape((STATE_ROWS, NODES), F32)
    spread_shape = shape((CHIPS, ELEMS, RHS * NODES), BF)
    packed_shape = shape((ROWS, 2 * NODES), BF)
    send_scratch = [
        pltpu.VMEM((2, field_rows, NODES), F32),
        pltpu.VMEM((field_rows, NODES), F32),
        pltpu.VMEM((ELEMS, RHS * NODES), BF),
        pltpu.VMEM((ROWS, 2 * NODES), BF),
        pltpu.SemaphoreType.DMA((CHIPS + 3,)),
    ]
    final_scratch = [pltpu.VMEM((RHS * NODES, PAIRS), F32), pltpu.VMEM((2, ROWS, NODES), F32)]
    block = (NODES, NODES * LZ)

    spread, packed, total = call(
        first_kernel, [VMEM], [spread_shape, packed_shape, big_state], [HBM] * 3, send_scratch
    )(initial)
    right, index = call(
        setup_kernel, [SMEM, VMEM, VMEM], [state, shape((8, PAIRS), jnp.int32)], [pl.BlockSpec()] * 2
    )(fault_count, right_side, faults[:, 0])

    residual = step = correction = None
    for sweep in range(SWEEPS):
        for turn in range(DEGREE):
            mine = lax.all_to_all(spread, "gy", 0, 0, axis_index_groups=same_core)
            even = swap(packed, "gx", [(0, 1), (2, 3), (4, 5), (6, 7)])
            odd = swap(packed, "gx", [(1, 2), (3, 4), (5, 6), (7, 0)])
            local = call(
                local_kernel,
                [VMEM, ANY, ANY],
                state,
                pl.BlockSpec(),
                [
                    pltpu.VMEM((2, *block), BF),
                    pltpu.VMEM((2, *block), BF),
                    pltpu.VMEM((2, 2, *block), BF),
                    pltpu.SemaphoreType.DMA((4,)),
                ],
                room=LOCAL_ROOM,
            )(packed, elem_blocks, face_blocks)
            mine, local, even, odd = lax.optimization_barrier((mine, local, even, odd))
            other = swap(mine, "gy", [(2 * chip, 2 * chip + 1) for chip in range(CHIPS)])
            last = sweep == SWEEPS - 1 and turn == DEGREE - 1
            states = [right] if turn == 0 else [residual, step]
            late = ([correction] if turn > 0 else []) + ([total] if turn == DEGREE - 1 else [])
            staged_shapes = [
                shape((NODES, NODES * PAIRS), BF),
                shape((2, *block), BF),
                shape((8, PAIRS), jnp.int32),
                state,
                shape((RHS * NODES, PAIRS), F32),
            ] + [state] * len(late)
            staged = call(
                make_stage_kernel(turn),
                [VMEM] * 4 + [ANY] * (3 + len(states) + len(late)),
                staged_shapes,
                [VMEM] * len(staged_shapes),
                [
                    pltpu.VMEM((2, 2, *block), BF),
                    pltpu.VMEM((field_rows, NODES), F32),
                    pltpu.VMEM((2, field_rows, NODES), F32),
                    pltpu.SemaphoreType.DMA((9,)),
                ],
                room=ROOM,
            )(mine, even, odd, index, face_blocks, fault_blocks, local, *states, *late)
            if last:
                outs, out_specs = [shape((1, 2, NODES, ROWS), F32)], [pl.BlockSpec()]
            else:
                outs = [spread_shape, packed_shape] + [big_state] * (1 if turn == DEGREE - 1 else 2)
                out_specs = [HBM] * len(outs)
            results = call(
                make_final_kernel(turn, last),
                [VMEM] * (1 + len(staged_shapes)),
                outs,
                out_specs,
                final_scratch + send_scratch,
                flops=4 << 30,
                room=ROOM,
            )(other, *staged)
            if last:
                return results[0]
            if turn == DEGREE - 1:
                spread, packed, total = results
            elif turn == 0:
                spread, packed, residual, step = results
                correction = step
            else:
                spread, packed, step, correction = results


def solution(mesh):
    in_specs = (
        P("gx", "gy", None, None),
        P("gx", "gy", None, None),
        P("gx", "gy", None, None),
        P(None, "gx", "gy", None, None),
        P("gx", "gy", None, None),
        P(None, "gx", "gy", None),
        P("gx", "gy"),
    )
    out_specs = P("gx", "gy", None, None)
    return jax.shard_map(shards, mesh=mesh, in_specs=in_specs, out_specs=out_specs, check_vma=False)
```

time: 201 us -> 153 us (0.76)
  local copies, waits for them, and re-layouts: 46.5 us -> 6 us
  waiting for transfers between devices: 22.6 us -> 10.9 us
  Pallas kernels: 44.3 us -> 49.6 us
    unnamed x202 -> x34, local copies, waits for them, and re-layouts: 46.5 us -> 6 us
    all_to_all x8, waiting for transfers between devices: 22.5 us -> 0.08 us  [shards(): mine = lax.all_to_all(spread, 'gy', 0, 0, axis_index_groups=same_core)]
    ppermute x24, starting transfers between devices: 51.4 us -> 40.6 us  [swap(): return lax.ppermute(value, axis, pairs + [(b, a) for a, b in pairs])]
    ppermute x24, waiting for transfers between devices: 0.06 us -> 10.8 us  [swap(): return lax.ppermute(value, axis, pairs + [(b, a) for a, b in pairs])]
    all_to_all x8, starting transfers between devices: 32.5 us -> 43.2 us  [shards(): mine = lax.all_to_all(spread, 'gy', 0, 0, axis_index_groups=same_core)]
    pallas_call x18 -> x26, Pallas kernels: 44.3 us -> 49.6 us  [the longest x8 20.8 us: shards(): call(make_final_kernel(turn, last), [VMEM] * (1 + len(staged_shapes)), ou...]
  transfers between devices with their start and end apart: 32 -> 32, of which waited for: 7 -> 7; matrix products, arithmetic and copies ran while one was open for 0% -> 0% of each run, Pallas kernels for 10% -> 18%
where the time goes in v1:
time: 153 us; the launch traced here: 151 us
  starting transfers between devices  83.8 us (55%)
  Pallas kernels  49.6 us (32%)
  waiting for transfers between devices  10.9 us (7%)
  local copies, waits for them, and re-layouts  6 us (4%)
    all_to_all x8, starting transfers between devices, shards(): mine = lax.all_to_all(spread, 'gy', 0, 0, axis_index_groups=same_core)  43.2 us
    ppermute x24, starting transfers between devices, swap(): return lax.ppermute(value, axis, pairs + [(b, a) for a, b in pairs])  40.6 us
    pallas_call x8, Pallas kernels, shards(): call(make_final_kernel(turn, last), [VMEM] * (1 + len(staged_shapes)), ou...  20.8 us
    pallas_call x8, Pallas kernels, shards(): call(make_stage_kernel(turn), [VMEM] * 4 + [ANY] * (3 + len(states) + len...  13 us
    pallas_call x8, Pallas kernels, shards(): call(local_kernel, [VMEM, ANY, ANY], state, pl.BlockSpec(), [pltpu.VMEM((...  12.4 us
    ppermute x24, waiting for transfers between devices, swap(): return lax.ppermute(value, axis, pairs + [(b, a) for a, b in pairs])  10.8 us
    unnamed x34, local copies, waits for them, and re-layouts  6 us
  transfers between devices with their start and end apart: 32, of which 7 were waited for; matrix products, arithmetic and copies ran while one was open for 0% of the time, Pallas kernels for 18%

profile of v1, /device:TPU:1, one launch (start us, length us, event | category | flops | bytes accessed | tf_op | source)
XLA Modules:
  0.0 151.5 jit_solution(1886798521843221800)
XLA Ops:
  0.0 1.9 %shard_map.73 = (bf16[8,32,512]{2,1,0:T(8,128)(2,1)}, bf16[128,128]{1,0:T(8,128)(2,1)}, f32[8192,64]{1,0:T(8,128)}) custom-call(f32[1,2,64,128]{3,2,1,0:T(8,128)} %initial_ref.1), custom_call_target="tpu_custom_call" | custom-call | bytes 2097152 | tf_op jit(solution)/shard_map/pallas_call | solution.py:309
  1.9 6.9 %all-to-all-start = ((bf16[8,32,512]{2,1,0:T(8,128)(2,1)}), bf16[8,32,512]{2,1,0:T(8,128)(2,1)S(1)}, u32[]{:S(2)}, u32[]{:S(2)}) async-start(bf16[8,32,512]{2,1,0:T(8,128)(2,1)} %get-tuple-element.117), calls=%async_computation | async-start | bytes 524288 | tf_op jit(solution)/shard_map/all_to_all | solution.py:319
  8.8 4.8 %collective-permute-start.1 = (bf16[128,128]{1,0:T(8,128)(2,1)}, bf16[128,128]{1,0:T(8,128)(2,1)S(1)}, u32[]{:S(2)}, u32[]{:S(2)}) collective-permute-start(bf16[128,128]{1,0:T(8,128)(2,1)} %get-tuple-element.118.own_ref), channel_id=1, source_target_pairs={{16,32},{48,64},{80,96},{112,0},{32,16},{64,48},{96,80},{0,112},{1... | collective-permute-start | bytes 98312 | tf_op jit(solution)/shard_map/ppermute | solution.py:289
  16.7 1.5 %shard_map.74.local_hbm = f32[256,64]{1,0:T(8,128)S(1)} custom-call(bf16[128,128]{1,0:T(8,128)(2,1)S(1)} %copy-done.16, bf16[1,2,64,1024]{3,2,1,0:T(8,128)(2,1)S(1)} %copy-done.10, bf16[6,1,2,64,1024]{4,3,2,1,0:T(8,128)(2,1)S(1)} %copy-done), custom_call_target="tpu_custom_call" | custom-call | bytes 2097152 | tf_op jit(solution)/shard_map/pallas_call | solution.py:322
  20.2 1.6 %shard_map.75 = (f32[256,64]{1,0:T(8,128)}, s32[8,128]{1,0:T(8,128)}) custom-call(s32[1,1]{1,0:T(1,128)S(6)} %copy.8.count_ref, f32[1,2,64,128]{3,2,1,0:T(8,128)} %right_ref.1, s32[3,1,128]{2,1,0:T(1,128)} %bitcast.1), custom_call_target="tpu_custom_call" | custom-call | bytes 2097152 | tf_op jit(solution)/shard_map/pallas_call | solution.py:312
  24.6 1.6 %shard_map.76 = (bf16[64,8192]{1,0:T(8,128)(2,1)S(1)}, bf16[2,64,1024]{2,1,0:T(8,128)(2,1)S(1)}, s32[8,128]{1,0:T(8,128)S(1)}, f32[256,64]{1,0:T(8,128)S(1)}, f32[512,128]{1,0:T(8,128)S(1)}) custom-call(bf16[8,32,512]{2,1,0:T(8,128)(2,1)S(1)} %all-to-all-done.mine_ref, bf16[128,128]{1,0:T(8,128)(2,1)S(1)} %collective-permute-done.even_ref, ...), custom_call_target="tpu_custom_call" | custom-call | bytes 2097152 | tf_op jit(solution)/shard_map/pallas_call | solution.py:347
  26.3 2.6 %shard_map.77 = (bf16[8,32,512]{2,1,0:T(8,128)(2,1)}, bf16[128,128]{1,0:T(8,128)(2,1)S(1)}, f32[8192,64]{1,0:T(8,128)}, f32[8192,64]{1,0:T(8,128)}) custom-call(bf16[8,32,512]{2,1,0:T(8,128)(2,1)S(1)} %collective-permute-done.2.other_ref, bf16[64,8192]{1,0:T(8,128)(2,1)S(1)} %get-tuple-element.125.fault_ref, ...), custom_call_target="tpu_custom_call" | custom-call | flops 4294967296 | bytes 2097152 | tf_op jit(solution)/shard_map/pallas_call | solution.py:365
  28.9 4.8 %all-to-all-start.1 = ((bf16[8,32,512]{2,1,0:T(8,128)(2,1)}), bf16[8,32,512]{2,1,0:T(8,128)(2,1)S(1)}, u32[]{:S(2)}, u32[]{:S(2)}) async-start(bf16[8,32,512]{2,1,0:T(8,128)(2,1)} %get-tuple-element.130), calls=%async_computation.1 | async-start | bytes 524288 | tf_op jit(solution)/shard_map/all_to_all | solution.py:319
  33.7 3.3 %collective-permute-start.4 = (bf16[128,128]{1,0:T(8,128)(2,1)S(1)}, bf16[128,128]{1,0:T(8,128)(2,1)S(1)}, u32[]{:S(2)}, u32[]{:S(2)}) collective-permute-start(bf16[128,128]{1,0:T(8,128)(2,1)S(1)} %get-tuple-element.131.own_ref), channel_id=1, source_target_pairs={{16,32},{48,64},{80,96},{112,0},{32,16},{64,48},{96,80},{0,112},{1... | collective-permute-start | bytes 98312 | tf_op jit(solution)/shard_map/ppermute | solution.py:289
  37.0 1.6 %shard_map.78.local_hbm = f32[256,64]{1,0:T(8,128)S(1)} custom-call(bf16[128,128]{1,0:T(8,128)(2,1)S(1)} %get-tuple-element.131.own_ref, bf16[1,2,64,1024]{3,2,1,0:T(8,128)(2,1)S(1)} %copy-done.11, bf16[6,1,2,64,1024]{4,3,2,1,0:T(8,128)(2,1)S(1)} %copy-done.1), custom_call_target="tpu_custom_call" | custom-call | bytes 2097152 | tf_op jit(solution)/shard_map/pallas_call | solution.py:322
  40.1 1.6 %collective-permute-start.5 = (bf16[8,32,512]{2,1,0:T(8,128)(2,1)S(1)}, bf16[8,32,512]{2,1,0:T(8,128)(2,1)S(1)}, u32[]{:S(2)}, u32[]{:S(2)}) collective-permute-start(bf16[8,32,512]{2,1,0:T(8,128)(2,1)S(1)} %all-to-all-done.1.mine_ref), channel_id=1, source_target_pairs={{0,1},{2,3},{4,5},{6,7},{8,9},{10,11},{12,13},{14,15},{1,0},{3,2},... | collective-permute-start | bytes 786440 | tf_op jit(solution)/shard_map/ppermute | solution.py:289
  41.7 1.7 %shard_map.79 = (bf16[64,8192]{1,0:T(8,128)(2,1)S(1)}, bf16[2,64,1024]{2,1,0:T(8,128)(2,1)S(1)}, s32[8,128]{1,0:T(8,128)S(1)}, f32[256,64]{1,0:T(8,128)S(1)}, f3...) custom-call(bf16[8,32,512]{2,1,0:T(8,128)(2,1)S(1)} %all-to-all-done.1.mine_ref, ...), custom_call_target="tpu_custom_call" | custom-call | bytes 2097152 | tf_op jit(solution)/shard_map/pallas_call | solution.py:347
  43.4 2.6 %shard_map.80 = (bf16[8,32,512]{2,1,0:T(8,128)(2,1)}, bf16[128,128]{1,0:T(8,128)(2,1)S(1)}, f32[8192,64]{1,0:T(8,128)}, f32[8192,64]{1,0:T(8,128)}) custom-call(bf16[8,32,512]{2,1,0:T(8,128)(2,1)S(1)} %collective-permute-done.5.other_ref, bf16[64,8192]{1,0:T(8,128)(2,1)S(1)} %get-tuple-element.138.fault_ref, ...), custom_call_target="tpu_custom_call" | custom-call | flops 4294967296 | bytes 2097152 | tf_op jit(solution)/shard_map/pallas_call | solution.py:365
  46.0 5.2 %all-to-all-start.2 = ((bf16[8,32,512]{2,1,0:T(8,128)(2,1)}), bf16[8,32,512]{2,1,0:T(8,128)(2,1)S(1)}, u32[]{:S(2)}, u32[]{:S(2)}) async-start(bf16[8,32,512]{2,1,0:T(8,128)(2,1)} %get-tuple-element.144), calls=%async_computation.2 | async-start | bytes 524288 | tf_op jit(solution)/shard_map/all_to_all | solution.py:319
  51.3 3.3 %collective-permute-start.7 = (bf16[128,128]{1,0:T(8,128)(2,1)S(1)}, bf16[128,128]{1,0:T(8,128)(2,1)S(1)}, u32[]{:S(2)}, u32[]{:S(2)}) collective-permute-start(bf16[128,128]{1,0:T(8,128)(2,1)S(1)} %get-tuple-element.145.own_ref), channel_id=1, source_target_pairs={{16,32},{48,64},{80,96},{112,0},{32,16},{64,48},{96,80},{0,112},{1... | collective-permute-start | bytes 98312 | tf_op jit(solution)/shard_map/ppermute | solution.py:289
  56.1 1.5 %collective-permute-done.7.odd_ref = bf16[128,128]{1,0:T(8,128)(2,1)S(1)} collective-permute-done((bf16[128,128]{1,0:T(8,128)(2,1)S(1)}, bf16[128,128]{1,0:T(8,128)(2,1)S(1)}, u32[]{:S(2)}, u32[]{:S(2)}) %collective-permute-start.7) | collective-permute-done | bytes 32800 | tf_op jit(solution)/shard_map/ppermute | solution.py:289
  57.7 1.7 %collective-permute-start.8 = (bf16[8,32,512]{2,1,0:T(8,128)(2,1)S(1)}, bf16[8,32,512]{2,1,0:T(8,128)(2,1)S(1)}, u32[]{:S(2)}, u32[]{:S(2)}) collective-permute-start(bf16[8,32,512]{2,1,0:T(8,128)(2,1)S(1)} %all-to-all-done.2.mine_ref), channel_id=1, source_target_pairs={{0,1},{2,3},{4,5},{6,7},{8,9},{10,11},{12,13},{14,15},{1,0},{3,2},... | collective-permute-start | bytes 786440 | tf_op jit(solution)/shard_map/ppermute | solution.py:289
  59.3 1.6 %shard_map.82 = (bf16[64,8192]{1,0:T(8,128)(2,1)S(1)}, bf16[2,64,1024]{2,1,0:T(8,128)(2,1)S(1)}, s32[8,128]{1,0:T(8,128)S(1)}, f32[256,64]{1,0:T(8,128)S(1)}, f3...) custom-call(bf16[8,32,512]{2,1,0:T(8,128)(2,1)S(1)} %all-to-all-done.2.mine_ref, ...), custom_call_target="tpu_custom_call" | custom-call | bytes 2097152 | tf_op jit(solution)/shard_map/pallas_call | solution.py:347
  61.0 2.6 %shard_map.83 = (bf16[8,32,512]{2,1,0:T(8,128)(2,1)}, bf16[128,128]{1,0:T(8,128)(2,1)S(1)}, f32[8192,64]{1,0:T(8,128)}, f32[8192,64]{1,0:T(8,128)}) custom-call(bf16[8,32,512]{2,1,0:T(8,128)(2,1)S(1)} %collective-permute-done.8.other_ref, bf16[64,8192]{1,0:T(8,128)(2,1)S(1)} %get-tuple-element.152.fault_ref, ...), custom_call_target="tpu_custom_call" | custom-call | flops 4294967296 | bytes 2097152 | tf_op jit(solution)/shard_map/pallas_call | solution.py:365
  63.6 5.2 %all-to-all-start.3 = ((bf16[8,32,512]{2,1,0:T(8,128)(2,1)}), bf16[8,32,512]{2,1,0:T(8,128)(2,1)S(1)}, u32[]{:S(2)}, u32[]{:S(2)}) async-start(bf16[8,32,512]{2,1,0:T(8,128)(2,1)} %get-tuple-element.158), calls=%async_computation.3 | async-start | bytes 524288 | tf_op jit(solution)/shard_map/all_to_all | solution.py:319
  68.9 3.3 %collective-permute-start.10 = (bf16[128,128]{1,0:T(8,128)(2,1)S(1)}, bf16[128,128]{1,0:T(8,128)(2,1)S(1)}, u32[]{:S(2)}, u32[]{:S(2)}) collective-permute-start(bf16[128,128]{1,0:T(8,128)(2,1)S(1)} %get-tuple-element.159.own_ref), channel_id=1, source_target_pairs={{16,32},{48,64},{80,96},{112,0},{32,16},{64,48},{96,80},{0,112},{1... | collective-permute-start | bytes 98312 | tf_op jit(solution)/shard_map/ppermute | solution.py:289
  72.2 1.5 %shard_map.84.local_hbm = f32[256,64]{1,0:T(8,128)S(1)} custom-call(bf16[128,128]{1,0:T(8,128)(2,1)S(1)} %get-tuple-element.159.own_ref, bf16[1,2,64,1024]{3,2,1,0:T(8,128)(2,1)S(1)} %copy-done.11, bf16[6,1,2,64,1024]{4,3,2,1,0:T(8,128)(2,1)S(1)} %copy-done.3), custom_call_target="tpu_custom_call" | custom-call | bytes 2097152 | tf_op jit(solution)/shard_map/pallas_call | solution.py:322
  75.3 1.7 %collective-permute-start.11 = (bf16[8,32,512]{2,1,0:T(8,128)(2,1)S(1)}, bf16[8,32,512]{2,1,0:T(8,128)(2,1)S(1)}, u32[]{:S(2)}, u32[]{:S(2)}) collective-permute-start(bf16[8,32,512]{2,1,0:T(8,128)(2,1)S(1)} %all-to-all-done.3.mine_ref), channel_id=1, source_target_pairs={{0,1},{2,3},{4,5},{6,7},{8,9},{10,11},{12,13},{14,15},{1,0},{3,2},... | collective-permute-start | bytes 786440 | tf_op jit(solution)/shard_map/ppermute | solution.py:289
  76.9 1.6 %shard_map.85 = (bf16[64,8192]{1,0:T(8,128)(2,1)S(1)}, bf16[2,64,1024]{2,1,0:T(8,128)(2,1)S(1)}, s32[8,128]{1,0:T(8,128)S(1)}, f32[256,64]{1,0:T(8,128)S(1)}, f3...) custom-call(bf16[8,32,512]{2,1,0:T(8,128)(2,1)S(1)} %all-to-all-done.3.mine_ref, ...), custom_call_target="tpu_custom_call" | custom-call | bytes 2097152 | tf_op jit(solution)/shard_map/pallas_call | solution.py:347
  78.6 2.6 %shard_map.86 = (bf16[8,32,512]{2,1,0:T(8,128)(2,1)}, bf16[128,128]{1,0:T(8,128)(2,1)S(1)}, f32[8192,64]{1,0:T(8,128)}) custom-call(bf16[8,32,512]{2,1,0:T(8,128)(2,1)S(1)} %collective-permute-done.11.other_ref, bf16[64,8192]{1,0:T(8,128)(2,1)S(1)} %get-tuple-element.167.fault_ref, bf16[2,64,1024]{2,1,0:T(8,128)(2,1)S(1)} %get-tuple-element.168.sides_ref, ...), custom_call_target="tpu_custom_call" | custom-call | flops 4294967296 | bytes 2097152 | tf_op jit(solution)/shard_map/pallas_call | solution.py:365
  81.2 5.2 %all-to-all-start.4 = ((bf16[8,32,512]{2,1,0:T(8,128)(2,1)}), bf16[8,32,512]{2,1,0:T(8,128)(2,1)S(1)}, u32[]{:S(2)}, u32[]{:S(2)}) async-start(bf16[8,32,512]{2,1,0:T(8,128)(2,1)} %get-tuple-element.174), calls=%async_computation.4 | async-start | bytes 524288 | tf_op jit(solution)/shard_map/all_to_all | solution.py:319
  86.5 3.3 %collective-permute-start.13 = (bf16[128,128]{1,0:T(8,128)(2,1)S(1)}, bf16[128,128]{1,0:T(8,128)(2,1)S(1)}, u32[]{:S(2)}, u32[]{:S(2)}) collective-permute-start(bf16[128,128]{1,0:T(8,128)(2,1)S(1)} %get-tuple-element.175.own_ref), channel_id=1, source_target_pairs={{16,32},{48,64},{80,96},{112,0},{32,16},{64,48},{96,80},{0,112},{1... | collective-permute-start | bytes 98312 | tf_op jit(solution)/shard_map/ppermute | solution.py:289
  89.7 1.5 %shard_map.87.local_hbm = f32[256,64]{1,0:T(8,128)S(1)} custom-call(bf16[128,128]{1,0:T(8,128)(2,1)S(1)} %get-tuple-element.175.own_ref, bf16[1,2,64,1024]{3,2,1,0:T(8,128)(2,1)S(1)} %copy-done.11, bf16[6,1,2,64,1024]{4,3,2,1,0:T(8,128)(2,1)S(1)} %copy-done.4), custom_call_target="tpu_custom_call" | custom-call | bytes 2097152 | tf_op jit(solution)/shard_map/pallas_call | solution.py:322
  92.9 1.7 %collective-permute-start.14 = (bf16[8,32,512]{2,1,0:T(8,128)(2,1)S(1)}, bf16[8,32,512]{2,1,0:T(8,128)(2,1)S(1)}, u32[]{:S(2)}, u32[]{:S(2)}) collective-permute-start(bf16[8,32,512]{2,1,0:T(8,128)(2,1)S(1)} %all-to-all-done.4.mine_ref), channel_id=1, source_target_pairs={{0,1},{2,3},{4,5},{6,7},{8,9},{10,11},{12,13},{14,15},{1,0},{3,2},... | collective-permute-start | bytes 786440 | tf_op jit(solution)/shard_map/ppermute | solution.py:289
  94.5 1.6 %shard_map.88 = (bf16[64,8192]{1,0:T(8,128)(2,1)S(1)}, bf16[2,64,1024]{2,1,0:T(8,128)(2,1)S(1)}, s32[8,128]{1,0:T(8,128)S(1)}, f32[256,64]{1,0:T(8,128)S(1)}, f32[512,128]{1,0:T(8,128)S(1)}) custom-call(bf16[8,32,512]{2,1,0:T(8,128)(2,1)S(1)} %all-to-all-done.4.mine_ref, bf16[128,128]{1,0:T(8,128)(2,1)S(1)} %collective-permute-done.12.even_ref, ...), custom_call_target="tpu_custom_call" | custom-call | bytes 2097152 | tf_op jit(solution)/shard_map/pallas_call | solution.py:347
  96.1 2.6 %shard_map.89 = (bf16[8,32,512]{2,1,0:T(8,128)(2,1)}, bf16[128,128]{1,0:T(8,128)(2,1)S(1)}, f32[8192,64]{1,0:T(8,128)}, f32[8192,64]{1,0:T(8,128)}) custom-call(bf16[8,32,512]{2,1,0:T(8,128)(2,1)S(1)} %collective-permute-done.14.other_ref, bf16[64,8192]{1,0:T(8,128)(2,1)S(1)} %get-tuple-element.180.fault_ref, ...), custom_call_target="tpu_custom_call" | custom-call | flops 4294967296 | bytes 2097152 | tf_op jit(solution)/shard_map/pallas_call | solution.py:365
  98.7 5.2 %all-to-all-start.5 = ((bf16[8,32,512]{2,1,0:T(8,128)(2,1)}), bf16[8,32,512]{2,1,0:T(8,128)(2,1)S(1)}, u32[]{:S(2)}, u32[]{:S(2)}) async-start(bf16[8,32,512]{2,1,0:T(8,128)(2,1)} %get-tuple-element.185), calls=%async_computation.5 | async-start | bytes 524288 | tf_op jit(solution)/shard_map/all_to_all | solution.py:319
  104.0 3.3 %collective-permute-start.16 = (bf16[128,128]{1,0:T(8,128)(2,1)S(1)}, bf16[128,128]{1,0:T(8,128)(2,1)S(1)}, u32[]{:S(2)}, u32[]{:S(2)}) collective-permute-start(bf16[128,128]{1,0:T(8,128)(2,1)S(1)} %get-tuple-element.186.own_ref), channel_id=1, source_target_pairs={{16,32},{48,64},{80,96},{112,0},{32,16},{64,48},{96,80},{0,112},{1... | collective-permute-start | bytes 98312 | tf_op jit(solution)/shard_map/ppermute | solution.py:289
  107.2 1.5 %shard_map.90.local_hbm = f32[256,64]{1,0:T(8,128)S(1)} custom-call(bf16[128,128]{1,0:T(8,128)(2,1)S(1)} %get-tuple-element.186.own_ref, bf16[1,2,64,1024]{3,2,1,0:T(8,128)(2,1)S(1)} %copy-done.11, bf16[6,1,2,64,1024]{4,3,2,1,0:T(8,128)(2,1)S(1)} %copy-done.5), custom_call_target="tpu_custom_call" | custom-call | bytes 2097152 | tf_op jit(solution)/shard_map/pallas_call | solution.py:322
  110.4 1.6 %collective-permute-start.17 = (bf16[8,32,512]{2,1,0:T(8,128)(2,1)S(1)}, bf16[8,32,512]{2,1,0:T(8,128)(2,1)S(1)}, u32[]{:S(2)}, u32[]{:S(2)}) collective-permute-start(bf16[8,32,512]{2,1,0:T(8,128)(2,1)S(1)} %all-to-all-done.5.mine_ref), channel_id=1, source_target_pairs={{0,1},{2,3},{4,5},{6,7},{8,9},{10,11},{12,13},{14,15},{1,0},{3,2},... | collective-permute-start | bytes 786440 | tf_op jit(solution)/shard_map/ppermute | solution.py:289
  112.0 1.6 %shard_map.91 = (bf16[64,8192]{1,0:T(8,128)(2,1)S(1)}, bf16[2,64,1024]{2,1,0:T(8,128)(2,1)S(1)}, s32[8,128]{1,0:T(8,128)S(1)}, f32[256,64]{1,0:T(8,128)S(1)}, f3...) custom-call(bf16[8,32,512]{2,1,0:T(8,128)(2,1)S(1)} %all-to-all-done.5.mine_ref, ...), custom_call_target="tpu_custom_call" | custom-call | bytes 2097152 | tf_op jit(solution)/shard_map/pallas_call | solution.py:347
  113.7 2.6 %shard_map.92 = (bf16[8,32,512]{2,1,0:T(8,128)(2,1)}, bf16[128,128]{1,0:T(8,128)(2,1)S(1)}, f32[8192,64]{1,0:T(8,128)}, f32[8192,64]{1,0:T(8,128)}) custom-call(bf16[8,32,512]{2,1,0:T(8,128)(2,1)S(1)} %collective-permute-done.17.other_ref, bf16[64,8192]{1,0:T(8,128)(2,1)S(1)} %get-tuple-element.193.fault_ref, ...), custom_call_target="tpu_custom_call" | custom-call | flops 4294967296 | bytes 2097152 | tf_op jit(solution)/shard_map/pallas_call | solution.py:365
  116.3 5.2 %all-to-all-start.6 = ((bf16[8,32,512]{2,1,0:T(8,128)(2,1)}), bf16[8,32,512]{2,1,0:T(8,128)(2,1)S(1)}, u32[]{:S(2)}, u32[]{:S(2)}) async-start(bf16[8,32,512]{2,1,0:T(8,128)(2,1)} %get-tuple-element.199), calls=%async_computation.6 | async-start | bytes 524288 | tf_op jit(solution)/shard_map/all_to_all | solution.py:319
  121.5 3.3 %collective-permute-start.19 = (bf16[128,128]{1,0:T(8,128)(2,1)S(1)}, bf16[128,128]{1,0:T(8,128)(2,1)S(1)}, u32[]{:S(2)}, u32[]{:S(2)}) collective-permute-start(bf16[128,128]{1,0:T(8,128)(2,1)S(1)} %get-tuple-element.200.own_ref), channel_id=1, source_target_pairs={{16,32},{48,64},{80,96},{112,0},{32,16},{64,48},{96,80},{0,112},{1... | collective-permute-start | bytes 98312 | tf_op jit(solution)/shard_map/ppermute | solution.py:289
  127.9 1.7 %collective-permute-start.20 = (bf16[8,32,512]{2,1,0:T(8,128)(2,1)S(1)}, bf16[8,32,512]{2,1,0:T(8,128)(2,1)S(1)}, u32[]{:S(2)}, u32[]{:S(2)}) collective-permute-start(bf16[8,32,512]{2,1,0:T(8,128)(2,1)S(1)} %all-to-all-done.6.mine_ref), channel_id=1, source_target_pairs={{0,1},{2,3},{4,5},{6,7},{8,9},{10,11},{12,13},{14,15},{1,0},{3,2},... | collective-permute-start | bytes 786440 | tf_op jit(solution)/shard_map/ppermute | solution.py:289
  129.6 1.6 %shard_map.94 = (bf16[64,8192]{1,0:T(8,128)(2,1)S(1)}, bf16[2,64,1024]{2,1,0:T(8,128)(2,1)S(1)}, s32[8,128]{1,0:T(8,128)S(1)}, f32[256,64]{1,0:T(8,128)S(1)}, f3...) custom-call(bf16[8,32,512]{2,1,0:T(8,128)(2,1)S(1)} %all-to-all-done.6.mine_ref, ...), custom_call_target="tpu_custom_call" | custom-call | bytes 2097152 | tf_op jit(solution)/shard_map/pallas_call | solution.py:347
  131.2 2.6 %shard_map.95 = (bf16[8,32,512]{2,1,0:T(8,128)(2,1)}, bf16[128,128]{1,0:T(8,128)(2,1)S(1)}, f32[8192,64]{1,0:T(8,128)}, f32[8192,64]{1,0:T(8,128)}) custom-call(bf16[8,32,512]{2,1,0:T(8,128)(2,1)S(1)} %collective-permute-done.20.other_ref, bf16[64,8192]{1,0:T(8,128)(2,1)S(1)} %get-tuple-element.207.fault_ref, ...), custom_call_target="tpu_custom_call" | custom-call | flops 4294967296 | bytes 2097152 | tf_op jit(solution)/shard_map/pallas_call | solution.py:365
  133.9 5.2 %all-to-all-start.7 = ((bf16[8,32,512]{2,1,0:T(8,128)(2,1)}), bf16[8,32,512]{2,1,0:T(8,128)(2,1)S(1)}, u32[]{:S(2)}, u32[]{:S(2)}) async-start(bf16[8,32,512]{2,1,0:T(8,128)(2,1)} %get-tuple-element.213), calls=%async_computation.7 | async-start | bytes 524288 | tf_op jit(solution)/shard_map/all_to_all | solution.py:319
  139.1 3.3 %collective-permute-start.22 = (bf16[128,128]{1,0:T(8,128)(2,1)S(1)}, bf16[128,128]{1,0:T(8,128)(2,1)S(1)}, u32[]{:S(2)}, u32[]{:S(2)}) collective-permute-start(bf16[128,128]{1,0:T(8,128)(2,1)S(1)} %get-tuple-element.214.own_ref), channel_id=1, source_target_pairs={{16,32},{48,64},{80,96},{112,0},{32,16},{64,48},{96,80},{0,112},{1... | collective-permute-start | bytes 98312 | tf_op jit(solution)/shard_map/ppermute | solution.py:289
  143.9 1.5 %collective-permute-done.22.odd_ref = bf16[128,128]{1,0:T(8,128)(2,1)S(1)} collective-permute-done((bf16[128,128]{1,0:T(8,128)(2,1)S(1)}, bf16[128,128]{1,0:T(8,128)(2,1)S(1)}, u32[]{:S(2)}, u32[]{:S(2)}) %collective-permute-start.22) | collective-permute-done | bytes 32800 | tf_op jit(solution)/shard_map/ppermute | solution.py:289
  145.5 1.7 %collective-permute-start.23 = (bf16[8,32,512]{2,1,0:T(8,128)(2,1)S(1)}, bf16[8,32,512]{2,1,0:T(8,128)(2,1)S(1)}, u32[]{:S(2)}, u32[]{:S(2)}) collective-permute-start(bf16[8,32,512]{2,1,0:T(8,128)(2,1)S(1)} %all-to-all-done.7.mine_ref), channel_id=1, source_target_pairs={{0,1},{2,3},{4,5},{6,7},{8,9},{10,11},{12,13},{14,15},{1,0},{3,2},... | collective-permute-start | bytes 786440 | tf_op jit(solution)/shard_map/ppermute | solution.py:289
  147.1 1.6 %shard_map.97 = (bf16[64,8192]{1,0:T(8,128)(2,1)S(1)}, bf16[2,64,1024]{2,1,0:T(8,128)(2,1)S(1)}, s32[8,128]{1,0:T(8,128)S(1)}, f32[256,64]{1,0:T(8,128)S(1)}, f3...) custom-call(bf16[8,32,512]{2,1,0:T(8,128)(2,1)S(1)} %all-to-all-done.7.mine_ref, ...), custom_call_target="tpu_custom_call" | custom-call | bytes 2097152 | tf_op jit(solution)/shard_map/pallas_call | solution.py:347
  148.8 2.5 %shard_map.98 = f32[1,2,64,128]{3,2,1,0:T(8,128)} custom-call(bf16[8,32,512]{2,1,0:T(8,128)(2,1)S(1)} %collective-permute-done.23.other_ref, bf16[64,8192]{1,0:T(8,128)(2,1)S(1)} %get-tuple-element.222.fault_ref, bf16[2,64,1024]{2,1,0:T(8,128)(2,1)S(1)} %get-tuple-element.223.sides_ref, s32[8,128]{1,0:T(8,128)S(1)} %get-tuple-element.224.index_ref, ...), custom_call_target="tpu_custom_call" | custom-call | flops 4294967296 | bytes 2097152 | tf_op jit(solution)/shard_map/pallas_call | solution.py:365
  (76 shorter events, 19.8 us)
Async XLA Ops:
  1.9 16.4 %all-to-all-start = ((bf16[8,32,512]{2,1,0:T(8,128)(2,1)}), bf16[8,32,512]{2,1,0:T(8,128)(2,1)S(1)}, u32[]{:S(2)}, u32[]{:S(2)}) async-start(bf16[8,32,512]{2,1,0:T(8,128)(2,1)} %get-tuple-element.117), calls=%async_computation | async-start | bytes 524288 | tf_op jit(solution)/shard_map/all_to_all | solution.py:319
  8.8 9.5 %collective-permute-start.1 = (bf16[128,128]{1,0:T(8,128)(2,1)}, bf16[128,128]{1,0:T(8,128)(2,1)S(1)}, u32[]{:S(2)}, u32[]{:S(2)}) collective-permute-start(bf16[128,128]{1,0:T(8,128)(2,1)} %get-tuple-element.118.own_ref), channel_id=1, source_target_pairs={{16,32},{48,64},{80,96},{112,0},{32,16},{64,48},{96,80},{0,112},{1... | collective-permute-start | bytes 98312 | tf_op jit(solution)/shard_map/ppermute | solution.py:289
  13.6 4.7 %collective-permute-start = (bf16[128,128]{1,0:T(8,128)(2,1)}, bf16[128,128]{1,0:T(8,128)(2,1)S(1)}, u32[]{:S(2)}, u32[]{:S(2)}) collective-permute-start(bf16[128,128]{1,0:T(8,128)(2,1)} %get-tuple-element.118.own_ref), channel_id=1, source_target_pairs={{0,16},{32,48},{64,80},{96,112},{16,0},{48,32},{80,64},{112,96},{1... | collective-permute-start | bytes 98312 | tf_op jit(solution)/shard_map/ppermute | solution.py:289
  13.6 1.4 copy-start
  15.0 0.9 copy-start.10
  15.9 0.8 copy-start.16
  18.3 7.9 %collective-permute-start.2 = (bf16[8,32,512]{2,1,0:T(8,128)(2,1)S(1)}, bf16[8,32,512]{2,1,0:T(8,128)(2,1)S(1)}, u32[]{:S(2)}, u32[]{:S(2)}) collective-permute-start(bf16[8,32,512]{2,1,0:T(8,128)(2,1)S(1)} %all-to-all-done.mine_ref), channel_id=1, source_target_pairs={{0,1},{2,3},{4,5},{6,7},{8,9},{10,11},{12,13},{14,15},{1,0},{3,2},... | collective-permute-start | bytes 786440 | tf_op jit(solution)/shard_map/ppermute | solution.py:289
  21.8 1.2 copy-start.8
  23.1 0.9 copy-start.12
  26.2 10.8 %copy-start.1 = (bf16[6,1,2,64,1024]{4,3,2,1,0:T(8,128)(2,1)S(1)}, bf16[6,1,2,64,1024]{4,3,2,1,0:T(8,128)(2,1)}, u32[]{:S(2)}) copy-start(bf16[6,1,2,64,1024]{4,3,2,1,0:T(8,128)(2,1)} %face_hbm.31) | copy-start | bytes 4718596
  26.2 10.8 %copy-start.11 = (bf16[1,2,64,1024]{3,2,1,0:T(8,128)(2,1)S(1)}, bf16[1,2,64,1024]{3,2,1,0:T(8,128)(2,1)}, u32[]{:S(2)}) copy-start(bf16[1,2,64,1024]{3,2,1,0:T(8,128)(2,1)} %elem_hbm.15) | copy-start | bytes 786436
  26.2 15.5 %copy-start.9 = (bf16[1,1,64,8192]{3,2,1,0:T(8,128)(2,1)S(1)}, bf16[1,1,64,8192]{3,2,1,0:T(8,128)(2,1)}, u32[]{:S(2)}) copy-start(bf16[1,1,64,8192]{3,2,1,0:T(8,128)(2,1)} %fault_hbm.15) | copy-start | bytes 3145732
  26.3 15.5 %copy-start.15 = (s32[8,128]{1,0:T(8,128)S(1)}, s32[8,128]{1,0:T(8,128)}, u32[]{:S(2)}) copy-start(s32[8,128]{1,0:T(8,128)} %get-tuple-element.122.index_ref) | copy-start | bytes 12292
  28.9 11.2 %all-to-all-start.1 = ((bf16[8,32,512]{2,1,0:T(8,128)(2,1)}), bf16[8,32,512]{2,1,0:T(8,128)(2,1)S(1)}, u32[]{:S(2)}, u32[]{:S(2)}) async-start(bf16[8,32,512]{2,1,0:T(8,128)(2,1)} %get-tuple-element.130), calls=%async_computation.1 | async-start | bytes 524288 | tf_op jit(solution)/shard_map/all_to_all | solution.py:319
  33.7 6.4 %collective-permute-start.4 = (bf16[128,128]{1,0:T(8,128)(2,1)S(1)}, bf16[128,128]{1,0:T(8,128)(2,1)S(1)}, u32[]{:S(2)}, u32[]{:S(2)}) collective-permute-start(bf16[128,128]{1,0:T(8,128)(2,1)S(1)} %get-tuple-element.131.own_ref), channel_id=1, source_target_pairs={{16,32},{48,64},{80,96},{112,0},{32,16},{64,48},{96,80},{0,112},{1... | collective-permute-start | bytes 98312 | tf_op jit(solution)/shard_map/ppermute | solution.py:289
  37.0 3.1 %collective-permute-start.3 = (bf16[128,128]{1,0:T(8,128)(2,1)S(1)}, bf16[128,128]{1,0:T(8,128)(2,1)S(1)}, u32[]{:S(2)}, u32[]{:S(2)}) collective-permute-start(bf16[128,128]{1,0:T(8,128)(2,1)S(1)} %get-tuple-element.131.own_ref), channel_id=1, source_target_pairs={{0,16},{32,48},{64,80},{96,112},{16,0},{48,32},{80,64},{112,96},{1... | collective-permute-start | bytes 98312 | tf_op jit(solution)/shard_map/ppermute | solution.py:289
  40.1 3.3 %collective-permute-start.5 = (bf16[8,32,512]{2,1,0:T(8,128)(2,1)S(1)}, bf16[8,32,512]{2,1,0:T(8,128)(2,1)S(1)}, u32[]{:S(2)}, u32[]{:S(2)}) collective-permute-start(bf16[8,32,512]{2,1,0:T(8,128)(2,1)S(1)} %all-to-all-done.1.mine_ref), channel_id=1, source_target_pairs={{0,1},{2,3},{4,5},{6,7},{8,9},{10,11},{12,13},{14,15},{1,0},{3,2},... | collective-permute-start | bytes 786440 | tf_op jit(solution)/shard_map/ppermute | solution.py:289
  43.4 11.2 %copy-start.2 = (bf16[6,1,2,64,1024]{4,3,2,1,0:T(8,128)(2,1)S(1)}, bf16[6,1,2,64,1024]{4,3,2,1,0:T(8,128)(2,1)}, u32[]{:S(2)}) copy-start(bf16[6,1,2,64,1024]{4,3,2,1,0:T(8,128)(2,1)} %face_hbm.31) | copy-start | bytes 4718596
  46.0 11.6 %all-to-all-start.2 = ((bf16[8,32,512]{2,1,0:T(8,128)(2,1)}), bf16[8,32,512]{2,1,0:T(8,128)(2,1)S(1)}, u32[]{:S(2)}, u32[]{:S(2)}) async-start(bf16[8,32,512]{2,1,0:T(8,128)(2,1)} %get-tuple-element.144), calls=%async_computation.2 | async-start | bytes 524288 | tf_op jit(solution)/shard_map/all_to_all | solution.py:319
  51.3 6.4 %collective-permute-start.7 = (bf16[128,128]{1,0:T(8,128)(2,1)S(1)}, bf16[128,128]{1,0:T(8,128)(2,1)S(1)}, u32[]{:S(2)}, u32[]{:S(2)}) collective-permute-start(bf16[128,128]{1,0:T(8,128)(2,1)S(1)} %get-tuple-element.145.own_ref), channel_id=1, source_target_pairs={{16,32},{48,64},{80,96},{112,0},{32,16},{64,48},{96,80},{0,112},{1... | collective-permute-start | bytes 98312 | tf_op jit(solution)/shard_map/ppermute | solution.py:289
  54.6 3.1 %collective-permute-start.6 = (bf16[128,128]{1,0:T(8,128)(2,1)S(1)}, bf16[128,128]{1,0:T(8,128)(2,1)S(1)}, u32[]{:S(2)}, u32[]{:S(2)}) collective-permute-start(bf16[128,128]{1,0:T(8,128)(2,1)S(1)} %get-tuple-element.145.own_ref), channel_id=1, source_target_pairs={{0,16},{32,48},{64,80},{96,112},{16,0},{48,32},{80,64},{112,96},{1... | collective-permute-start | bytes 98312 | tf_op jit(solution)/shard_map/ppermute | solution.py:289
  57.7 3.3 %collective-permute-start.8 = (bf16[8,32,512]{2,1,0:T(8,128)(2,1)S(1)}, bf16[8,32,512]{2,1,0:T(8,128)(2,1)S(1)}, u32[]{:S(2)}, u32[]{:S(2)}) collective-permute-start(bf16[8,32,512]{2,1,0:T(8,128)(2,1)S(1)} %all-to-all-done.2.mine_ref), channel_id=1, source_target_pairs={{0,1},{2,3},{4,5},{6,7},{8,9},{10,11},{12,13},{14,15},{1,0},{3,2},... | collective-permute-start | bytes 786440 | tf_op jit(solution)/shard_map/ppermute | solution.py:289
  61.0 11.2 %copy-start.3 = (bf16[6,1,2,64,1024]{4,3,2,1,0:T(8,128)(2,1)S(1)}, bf16[6,1,2,64,1024]{4,3,2,1,0:T(8,128)(2,1)}, u32[]{:S(2)}) copy-start(bf16[6,1,2,64,1024]{4,3,2,1,0:T(8,128)(2,1)} %face_hbm.31) | copy-start | bytes 4718596
  63.6 11.6 %all-to-all-start.3 = ((bf16[8,32,512]{2,1,0:T(8,128)(2,1)}), bf16[8,32,512]{2,1,0:T(8,128)(2,1)S(1)}, u32[]{:S(2)}, u32[]{:S(2)}) async-start(bf16[8,32,512]{2,1,0:T(8,128)(2,1)} %get-tuple-element.158), calls=%async_computation.3 | async-start | bytes 524288 | tf_op jit(solution)/shard_map/all_to_all | solution.py:319
  68.9 6.4 %collective-permute-start.10 = (bf16[128,128]{1,0:T(8,128)(2,1)S(1)}, bf16[128,128]{1,0:T(8,128)(2,1)S(1)}, u32[]{:S(2)}, u32[]{:S(2)}) collective-permute-start(bf16[128,128]{1,0:T(8,128)(2,1)S(1)} %get-tuple-element.159.own_ref), channel_id=1, source_target_pairs={{16,32},{48,64},{80,96},{112,0},{32,16},{64,48},{96,80},{0,112},{1... | collective-permute-start | bytes 98312 | tf_op jit(solution)/shard_map/ppermute | solution.py:289
  72.1 3.1 %collective-permute-start.9 = (bf16[128,128]{1,0:T(8,128)(2,1)S(1)}, bf16[128,128]{1,0:T(8,128)(2,1)S(1)}, u32[]{:S(2)}, u32[]{:S(2)}) collective-permute-start(bf16[128,128]{1,0:T(8,128)(2,1)S(1)} %get-tuple-element.159.own_ref), channel_id=1, source_target_pairs={{0,16},{32,48},{64,80},{96,112},{16,0},{48,32},{80,64},{112,96},{1... | collective-permute-start | bytes 98312 | tf_op jit(solution)/shard_map/ppermute | solution.py:289
  75.3 3.3 %collective-permute-start.11 = (bf16[8,32,512]{2,1,0:T(8,128)(2,1)S(1)}, bf16[8,32,512]{2,1,0:T(8,128)(2,1)S(1)}, u32[]{:S(2)}, u32[]{:S(2)}) collective-permute-start(bf16[8,32,512]{2,1,0:T(8,128)(2,1)S(1)} %all-to-all-done.3.mine_ref), channel_id=1, source_target_pairs={{0,1},{2,3},{4,5},{6,7},{8,9},{10,11},{12,13},{14,15},{1,0},{3,2},... | collective-permute-start | bytes 786440 | tf_op jit(solution)/shard_map/ppermute | solution.py:289
  78.6 11.2 %copy-start.4 = (bf16[6,1,2,64,1024]{4,3,2,1,0:T(8,128)(2,1)S(1)}, bf16[6,1,2,64,1024]{4,3,2,1,0:T(8,128)(2,1)}, u32[]{:S(2)}) copy-start(bf16[6,1,2,64,1024]{4,3,2,1,0:T(8,128)(2,1)} %face_hbm.31) | copy-start | bytes 4718596
  78.6 15.9 %copy-start.13 = (f32[256,64]{1,0:T(8,128)S(1)}, f32[256,64]{1,0:T(8,128)}, u32[]{:S(2)}) copy-start(f32[256,64]{1,0:T(8,128)} %get-tuple-element.124.refs_0_) | copy-start | bytes 196612
  81.2 11.6 %all-to-all-start.4 = ((bf16[8,32,512]{2,1,0:T(8,128)(2,1)}), bf16[8,32,512]{2,1,0:T(8,128)(2,1)S(1)}, u32[]{:S(2)}, u32[]{:S(2)}) async-start(bf16[8,32,512]{2,1,0:T(8,128)(2,1)} %get-tuple-element.174), calls=%async_computation.4 | async-start | bytes 524288 | tf_op jit(solution)/shard_map/all_to_all | solution.py:319
  86.5 6.4 %collective-permute-start.13 = (bf16[128,128]{1,0:T(8,128)(2,1)S(1)}, bf16[128,128]{1,0:T(8,128)(2,1)S(1)}, u32[]{:S(2)}, u32[]{:S(2)}) collective-permute-start(bf16[128,128]{1,0:T(8,128)(2,1)S(1)} %get-tuple-element.175.own_ref), channel_id=1, source_target_pairs={{16,32},{48,64},{80,96},{112,0},{32,16},{64,48},{96,80},{0,112},{1... | collective-permute-start | bytes 98312 | tf_op jit(solution)/shard_map/ppermute | solution.py:289
  89.7 3.1 %collective-permute-start.12 = (bf16[128,128]{1,0:T(8,128)(2,1)S(1)}, bf16[128,128]{1,0:T(8,128)(2,1)S(1)}, u32[]{:S(2)}, u32[]{:S(2)}) collective-permute-start(bf16[128,128]{1,0:T(8,128)(2,1)S(1)} %get-tuple-element.175.own_ref), channel_id=1, source_target_pairs={{0,16},{32,48},{64,80},{96,112},{16,0},{48,32},{80,64},{112,96},{1... | collective-permute-start | bytes 98312 | tf_op jit(solution)/shard_map/ppermute | solution.py:289
  92.9 3.2 %collective-permute-start.14 = (bf16[8,32,512]{2,1,0:T(8,128)(2,1)S(1)}, bf16[8,32,512]{2,1,0:T(8,128)(2,1)S(1)}, u32[]{:S(2)}, u32[]{:S(2)}) collective-permute-start(bf16[8,32,512]{2,1,0:T(8,128)(2,1)S(1)} %all-to-all-done.4.mine_ref), channel_id=1, source_target_pairs={{0,1},{2,3},{4,5},{6,7},{8,9},{10,11},{12,13},{14,15},{1,0},{3,2},... | collective-permute-start | bytes 786440 | tf_op jit(solution)/shard_map/ppermute | solution.py:289
  96.1 11.2 %copy-start.5 = (bf16[6,1,2,64,1024]{4,3,2,1,0:T(8,128)(2,1)S(1)}, bf16[6,1,2,64,1024]{4,3,2,1,0:T(8,128)(2,1)}, u32[]{:S(2)}) copy-start(bf16[6,1,2,64,1024]{4,3,2,1,0:T(8,128)(2,1)} %face_hbm.31) | copy-start | bytes 4718596
  98.7 11.7 %all-to-all-start.5 = ((bf16[8,32,512]{2,1,0:T(8,128)(2,1)}), bf16[8,32,512]{2,1,0:T(8,128)(2,1)S(1)}, u32[]{:S(2)}, u32[]{:S(2)}) async-start(bf16[8,32,512]{2,1,0:T(8,128)(2,1)} %get-tuple-element.185), calls=%async_computation.5 | async-start | bytes 524288 | tf_op jit(solution)/shard_map/all_to_all | solution.py:319
  104.0 6.4 %collective-permute-start.16 = (bf16[128,128]{1,0:T(8,128)(2,1)S(1)}, bf16[128,128]{1,0:T(8,128)(2,1)S(1)}, u32[]{:S(2)}, u32[]{:S(2)}) collective-permute-start(bf16[128,128]{1,0:T(8,128)(2,1)S(1)} %get-tuple-element.186.own_ref), channel_id=1, source_target_pairs={{16,32},{48,64},{80,96},{112,0},{32,16},{64,48},{96,80},{0,112},{1... | collective-permute-start | bytes 98312 | tf_op jit(solution)/shard_map/ppermute | solution.py:289
  107.2 3.1 %collective-permute-start.15 = (bf16[128,128]{1,0:T(8,128)(2,1)S(1)}, bf16[128,128]{1,0:T(8,128)(2,1)S(1)}, u32[]{:S(2)}, u32[]{:S(2)}) collective-permute-start(bf16[128,128]{1,0:T(8,128)(2,1)S(1)} %get-tuple-element.186.own_ref), channel_id=1, source_target_pairs={{0,16},{32,48},{64,80},{96,112},{16,0},{48,32},{80,64},{112,96},{1... | collective-permute-start | bytes 98312 | tf_op jit(solution)/shard_map/ppermute | solution.py:289
  110.4 3.3 %collective-permute-start.17 = (bf16[8,32,512]{2,1,0:T(8,128)(2,1)S(1)}, bf16[8,32,512]{2,1,0:T(8,128)(2,1)S(1)}, u32[]{:S(2)}, u32[]{:S(2)}) collective-permute-start(bf16[8,32,512]{2,1,0:T(8,128)(2,1)S(1)} %all-to-all-done.5.mine_ref), channel_id=1, source_target_pairs={{0,1},{2,3},{4,5},{6,7},{8,9},{10,11},{12,13},{14,15},{1,0},{3,2},... | collective-permute-start | bytes 786440 | tf_op jit(solution)/shard_map/ppermute | solution.py:289
  113.6 11.2 %copy-start.6 = (bf16[6,1,2,64,1024]{4,3,2,1,0:T(8,128)(2,1)S(1)}, bf16[6,1,2,64,1024]{4,3,2,1,0:T(8,128)(2,1)}, u32[]{:S(2)}) copy-start(bf16[6,1,2,64,1024]{4,3,2,1,0:T(8,128)(2,1)} %face_hbm.31) | copy-start | bytes 4718596
  116.3 11.6 %all-to-all-start.6 = ((bf16[8,32,512]{2,1,0:T(8,128)(2,1)}), bf16[8,32,512]{2,1,0:T(8,128)(2,1)S(1)}, u32[]{:S(2)}, u32[]{:S(2)}) async-start(bf16[8,32,512]{2,1,0:T(8,128)(2,1)} %get-tuple-element.199), calls=%async_computation.6 | async-start | bytes 524288 | tf_op jit(solution)/shard_map/all_to_all | solution.py:319
  121.5 6.4 %collective-permute-start.19 = (bf16[128,128]{1,0:T(8,128)(2,1)S(1)}, bf16[128,128]{1,0:T(8,128)(2,1)S(1)}, u32[]{:S(2)}, u32[]{:S(2)}) collective-permute-start(bf16[128,128]{1,0:T(8,128)(2,1)S(1)} %get-tuple-element.200.own_ref), channel_id=1, source_target_pairs={{16,32},{48,64},{80,96},{112,0},{32,16},{64,48},{96,80},{0,112},{1... | collective-permute-start | bytes 98312 | tf_op jit(solution)/shard_map/ppermute | solution.py:289
  124.8 3.1 %collective-permute-start.18 = (bf16[128,128]{1,0:T(8,128)(2,1)S(1)}, bf16[128,128]{1,0:T(8,128)(2,1)S(1)}, u32[]{:S(2)}, u32[]{:S(2)}) collective-permute-start(bf16[128,128]{1,0:T(8,128)(2,1)S(1)} %get-tuple-element.200.own_ref), channel_id=1, source_target_pairs={{0,16},{32,48},{64,80},{96,112},{16,0},{48,32},{80,64},{112,96},{1... | collective-permute-start | bytes 98312 | tf_op jit(solution)/shard_map/ppermute | solution.py:289
  127.9 3.3 %collective-permute-start.20 = (bf16[8,32,512]{2,1,0:T(8,128)(2,1)S(1)}, bf16[8,32,512]{2,1,0:T(8,128)(2,1)S(1)}, u32[]{:S(2)}, u32[]{:S(2)}) collective-permute-start(bf16[8,32,512]{2,1,0:T(8,128)(2,1)S(1)} %all-to-all-done.6.mine_ref), channel_id=1, source_target_pairs={{0,1},{2,3},{4,5},{6,7},{8,9},{10,11},{12,13},{14,15},{1,0},{3,2},... | collective-permute-start | bytes 786440 | tf_op jit(solution)/shard_map/ppermute | solution.py:289
  131.2 11.2 %copy-start.7 = (bf16[6,1,2,64,1024]{4,3,2,1,0:T(8,128)(2,1)S(1)}, bf16[6,1,2,64,1024]{4,3,2,1,0:T(8,128)(2,1)}, u32[]{:S(2)}) copy-start(bf16[6,1,2,64,1024]{4,3,2,1,0:T(8,128)(2,1)} %face_hbm.31) | copy-start | bytes 4718596
  133.9 11.6 %all-to-all-start.7 = ((bf16[8,32,512]{2,1,0:T(8,128)(2,1)}), bf16[8,32,512]{2,1,0:T(8,128)(2,1)S(1)}, u32[]{:S(2)}, u32[]{:S(2)}) async-start(bf16[8,32,512]{2,1,0:T(8,128)(2,1)} %get-tuple-element.213), calls=%async_computation.7 | async-start | bytes 524288 | tf_op jit(solution)/shard_map/all_to_all | solution.py:319
  139.1 6.4 %collective-permute-start.22 = (bf16[128,128]{1,0:T(8,128)(2,1)S(1)}, bf16[128,128]{1,0:T(8,128)(2,1)S(1)}, u32[]{:S(2)}, u32[]{:S(2)}) collective-permute-start(bf16[128,128]{1,0:T(8,128)(2,1)S(1)} %get-tuple-element.214.own_ref), channel_id=1, source_target_pairs={{16,32},{48,64},{80,96},{112,0},{32,16},{64,48},{96,80},{0,112},{1... | collective-permute-start | bytes 98312 | tf_op jit(solution)/shard_map/ppermute | solution.py:289
  142.4 3.1 %collective-permute-start.21 = (bf16[128,128]{1,0:T(8,128)(2,1)S(1)}, bf16[128,128]{1,0:T(8,128)(2,1)S(1)}, u32[]{:S(2)}, u32[]{:S(2)}) collective-permute-start(bf16[128,128]{1,0:T(8,128)(2,1)S(1)} %get-tuple-element.214.own_ref), channel_id=1, source_target_pairs={{0,16},{32,48},{64,80},{96,112},{16,0},{48,32},{80,64},{112,96},{1... | collective-permute-start | bytes 98312 | tf_op jit(solution)/shard_map/ppermute | solution.py:289
  145.5 3.3 %collective-permute-start.23 = (bf16[8,32,512]{2,1,0:T(8,128)(2,1)S(1)}, bf16[8,32,512]{2,1,0:T(8,128)(2,1)S(1)}, u32[]{:S(2)}, u32[]{:S(2)}) collective-permute-start(bf16[8,32,512]{2,1,0:T(8,128)(2,1)S(1)} %all-to-all-done.7.mine_ref), channel_id=1, source_target_pairs={{0,1},{2,3},{4,5},{6,7},{8,9},{10,11},{12,13},{14,15},{1,0},{3,2},... | collective-permute-start | bytes 786440 | tf_op jit(solution)/shard_map/ppermute | solution.py:289
  (1 other events, 0.7 us)

commit v2 on v1

v2 whole, which is shorter than its diff:
```python
import jax
import jax.numpy as jnp
from jax import lax
from jax.experimental import pallas as pl
from jax.experimental.pallas import tpu as pltpu
from jax.sharding import PartitionSpec as P

NODES = 64
RHS = 8
LZ = 16
SWEEPS = 2
DEGREE = 4
ROWS = LZ * RHS
ELEMS = 2 * LZ
PAIRS = 128
CHIPS = 8
ROOM = 14

spectrum_low = 0.6
spectrum_high = 3.0

BF = jnp.bfloat16
F32 = jnp.float32
NT = (((1,), (1,)), ((), ()))


def dot(a, b):
    return jnp.dot(a, b, preferred_element_type=F32)


def dot_t(a, b):
    return lax.dot_general(a, b, NT, preferred_element_type=F32)


def iota(shape, dim):
    return lax.broadcasted_iota(jnp.int32, shape, dim)


def coefficients():
    centre_point = (spectrum_high + spectrum_low) / 2.0
    half_width = (spectrum_high - spectrum_low) / 2.0
    sigma_ratio = centre_point / half_width
    steps = []
    rho_prev = 1.0 / sigma_ratio
    for _ in range(1, DEGREE):
        rho_next = 1.0 / (2.0 * sigma_ratio - rho_prev)
        steps.append((rho_next * rho_prev, 2.0 * rho_next / half_width))
        rho_prev = rho_next
    return centre_point, steps


def send_field(field, spread_hbm, packed_out, scratch):
    rows_ref, spread_ref, sem = scratch
    rows_ref[...] = field
    pieces = [rows_ref[pl.ds(r, ELEMS, stride=RHS), :] for r in range(RHS)]
    spread = jnp.concatenate(pieces, axis=1).astype(BF)
    for chip in range(CHIPS):
        spread_ref[chip] = spread
    copy = pltpu.make_async_copy(spread_ref, spread_hbm, sem)
    copy.start()
    packed_out[...] = jnp.concatenate([field[:ROWS], field[ROWS:]], axis=1).astype(BF)
    return copy


def first_kernel(
    count_ref, initial_ref, right_ref, faults_ref, spread_out, packed_out, solution_out, right_out, index_out, *scratch
):
    field = jnp.concatenate([initial_ref[0, 0].T, initial_ref[0, 1].T], axis=0)
    copy = send_field(field, spread_out, packed_out, scratch)
    solution_out[...] = field
    right_out[...] = jnp.concatenate([right_ref[0, 0].T, right_ref[0, 1].T], axis=0)
    device = faults_ref[1, 0]
    column = (
        jnp.where(device % 2 == lax.axis_index("gy") % 2, 0, CHIPS * ELEMS)
        + (device // 2) * ELEMS
        + faults_ref[2, 0]
    )
    owner = jnp.where(iota((1, PAIRS), 1) < count_ref[0, 0], faults_ref[0, 0], -1)
    index_out[...] = jnp.concatenate([column, owner, jnp.zeros((6, PAIRS), jnp.int32)], axis=0)
    copy.wait()


def one_hot(hit):
    return jnp.where(hit, 1.0, 0.0).astype(BF)


def expander():
    return one_hot(iota((NODES, NODES * LZ), 1) // LZ == iota((NODES, NODES * LZ), 0))


def layer_mask(shift):
    return one_hot(iota((ROWS, 128), 1) % LZ - iota((ROWS, 128), 0) // RHS == shift)


def masked(expanded, mask):
    return expanded * jnp.concatenate([mask] * (NODES * LZ // 128), axis=1)


def gathered(index_ref, half, blocks_ref):
    rows = CHIPS * ELEMS
    hit = iota((rows, PAIRS), 0) + half * rows == index_ref[0:1, :]
    return dot(blocks_ref[...].reshape(rows, RHS * NODES).T, one_hot(hit))


def local_kernel(own_ref, elem_ref, face_ref, out_ref):
    expand = expander()
    wide = [dot(own_ref[:, ly * NODES : (ly + 1) * NODES], expand).astype(BF) for ly in range(2)]
    same, up, down = layer_mask(0), layer_mask(1), layer_mask(-1)
    zero = jnp.zeros((RHS, NODES), F32)
    here = [masked(wide[ly], same) for ly in range(2)]
    sums = [
        dot_t(here[ly], elem_ref[0, ly]) + dot_t(here[1 - ly], face_ref[3 - ly, 0, ly]) for ly in range(2)
    ]
    for ly in range(2):
        lower = dot_t(masked(wide[ly], up), face_ref[4, 0, ly])
        upper = dot_t(masked(wide[ly], down), face_ref[5, 0, ly])
        sums[ly] += jnp.concatenate([zero, lower[:-RHS]], axis=0) + jnp.concatenate([upper[RHS:], zero], axis=0)
    out_ref[...] = jnp.concatenate(sums, axis=0)


def make_stage_kernel(turn):
    _, steps = coefficients()

    def stage_kernel(mine_ref, even_ref, odd_ref, index_ref, face_ref, local_ref, *refs):
        states, (base_ref, half_ref) = refs[:-2], refs[-2:]
        half_ref[...] = gathered(index_ref, 0, mine_ref)
        at = lax.axis_index("gx")
        is_even = at % 2 == 0
        low = jnp.where(is_even, odd_ref[...], even_ref[...])
        high = jnp.where(is_even, even_ref[...], odd_ref[...])
        low = jnp.where(at > 0, low, jnp.zeros_like(low))
        high = jnp.where(at < 7, high, jnp.zeros_like(high))
        expand, same = expander(), layer_mask(0)
        wide = [
            [masked(dot(field[:, ly * NODES : (ly + 1) * NODES], expand).astype(BF), same) for field in (low, high)]
            for ly in range(2)
        ]
        sums = [dot_t(wide[ly][0], face_ref[0, 0, ly]) + dot_t(wide[ly][1], face_ref[1, 0, ly]) for ly in range(2)]
        local = local_ref[...] + jnp.concatenate(sums, axis=0)
        if turn == 0:
            base_ref[...] = states[0][...] - local
        else:
            old, new = steps[turn - 1]
            base_ref[...] = old * states[1][...] + new * (states[0][...] - local)

    return stage_kernel


def make_final_kernel(turn, last):
    centre_point, steps = coefficients()
    n_late = min(turn, 1) + (turn == DEGREE - 1)

    def final_kernel(fault_ref, face_ref, index_ref, other_ref, base_ref, half_ref, *refs):
        held, refs = refs[:n_late], refs[n_late:]
        n_outs = 1 if last else 3 if turn == DEGREE - 1 else 4
        outs, refs = refs[:n_outs], refs[n_outs:]
        values_ref, plane_ref, *scratch = refs
        values_ref[...] = half_ref[...] + gathered(index_ref, 1, other_ref)
        at = lax.axis_index("gy")
        chip = at // 2
        is_even = at % 2 == 0
        low_chip = jnp.where(is_even, jnp.maximum(chip - 1, 0), chip)
        high_chip = jnp.where(is_even, chip, jnp.minimum(chip + 1, CHIPS - 1))
        expand, same = expander(), layer_mask(0)
        sums = []
        for ly in range(2):
            if ly == 0:
                plane = other_ref[low_chip, LZ:].astype(F32)
                plane = jnp.where(at > 0, plane, jnp.zeros_like(plane))
            else:
                plane = other_ref[high_chip, :LZ].astype(F32)
                plane = jnp.where(at < 2 * CHIPS - 1, plane, jnp.zeros_like(plane))
            for r in range(RHS):
                plane_ref[ly, pl.ds(r, LZ, stride=RHS), :] = plane[:, r * NODES : (r + 1) * NODES]
            wide = dot(plane_ref[ly].astype(BF), expand).astype(BF)
            sums.append(dot_t(masked(wide, same), face_ref[2 + ly, 0, ly]))
        total = jnp.concatenate(sums, axis=0)
        land = one_hot(iota((ELEMS * RHS, PAIRS), 0) // RHS == index_ref[1:2, :])
        land = land.reshape(ELEMS // 2, 2 * RHS, PAIRS)
        group = 4
        for start in range(0, NODES, group):
            parts = []
            for m in range(start, start + group):
                value = values_ref[pl.ds(m, RHS, stride=NODES), :]
                value = jnp.concatenate([value, value], axis=0).astype(BF)
                parts.append((land * value[None]).reshape(ELEMS * RHS, PAIRS))
            total = total + dot_t(
                jnp.concatenate(parts, axis=1), fault_ref[0, 0, :, start * PAIRS : (start + group) * PAIRS]
            )
        if turn == 0:
            residual = base_ref[...] - total
            step = residual / centre_point
            states = (residual, step)
        else:
            step = base_ref[...] - steps[turn - 1][1] * total
            correction = held[0][...] + step
            states = (step, correction)
        if turn == DEGREE - 1:
            states = (held[1][...] + correction,)
        if last:
            outs[0][0, 0] = states[0][:ROWS].T
            outs[0][0, 1] = states[0][ROWS:].T
            return
        copy = send_field(states[-1], outs[0], outs[1], scratch)
        for out, value in zip(outs[2:], states):
            out[...] = value
        copy.wait()

    return final_kernel


VMEM = pl.BlockSpec(memory_space=pltpu.VMEM)
SMEM = pl.BlockSpec(memory_space=pltpu.SMEM)
HBM = pl.BlockSpec(memory_space=pltpu.HBM)


def call(kernel, in_specs, out_shape, out_specs, scratch=(), flops=0, room=2):
    return pl.pallas_call(
        kernel,
        out_shape=out_shape,
        in_specs=in_specs,
        out_specs=out_specs,
        scratch_shapes=list(scratch),
        compiler_params=pltpu.CompilerParams(vmem_limit_bytes=(64 - room) * 1024 * 1024),
        cost_estimate=pl.CostEstimate(flops=flops, bytes_accessed=2 << 20, transcendentals=0),
    )


def shape(dims, dtype):
    return jax.ShapeDtypeStruct(dims, dtype)


def swap(value, axis, pairs):
    return lax.ppermute(value, axis, pairs + [(b, a) for a, b in pairs])


def shards(right_side, initial, elem_blocks, face_blocks, fault_blocks, faults, fault_count):
    odd_pairs = [(2 * CHIPS * a + j, 2 * CHIPS * (a + 1) + j) for a in (1, 3, 5) for j in range(2 * CHIPS)]
    odd_pairs += [(2 * CHIPS * a + j, 2 * CHIPS * a + j + 1) for a in (0, 7) for j in range(0, 2 * CHIPS, 2)]
    same_core = [list(range(core, 2 * CHIPS, 2)) for core in range(2)]
    field_rows = ELEMS * RHS
    state = shape((field_rows, NODES), F32)
    spread_shape = shape((CHIPS, ELEMS, RHS * NODES), BF)
    packed_shape = shape((ROWS, 2 * NODES), BF)
    send_scratch = [
        pltpu.VMEM((field_rows, NODES), F32),
        pltpu.VMEM((CHIPS, ELEMS, RHS * NODES), BF),
        pltpu.SemaphoreType.DMA(()),
    ]
    final_scratch = [pltpu.VMEM((RHS * NODES, PAIRS), F32), pltpu.VMEM((2, ROWS, NODES), F32)]

    spread, packed, total, right, index = call(
        first_kernel,
        [SMEM] + [pl.BlockSpec()] * 3,
        [spread_shape, packed_shape, state, state, shape((8, PAIRS), jnp.int32)],
        [HBM] + [VMEM] * 4,
        send_scratch,
        room=ROOM,
    )(fault_count, initial, right_side, faults)
    residual = step = correction = None
    for sweep in range(SWEEPS):
        for turn in range(DEGREE):
            mine = lax.all_to_all(spread, "gy", 0, 0, axis_index_groups=same_core)
            even = swap(packed, "gx", [(0, 1), (2, 3), (4, 5), (6, 7)])
            odd = swap(packed, ("gx", "gy"), odd_pairs)
            local = call(local_kernel, [VMEM] * 3, state, VMEM, room=ROOM)(packed, elem_blocks, face_blocks)
            mine, local, even, odd = lax.optimization_barrier((mine, local, even, odd))
            other = swap(mine, "gy", [(2 * chip, 2 * chip + 1) for chip in range(CHIPS)])
            last = sweep == SWEEPS - 1 and turn == DEGREE - 1
            states = [right] if turn == 0 else [residual, step]
            late = ([correction] if turn > 0 else []) + ([total] if turn == DEGREE - 1 else [])
            base, half = call(
                make_stage_kernel(turn),
                [VMEM] * (6 + len(states)),
                [state, shape((RHS * NODES, PAIRS), F32)],
                [VMEM] * 2,
                room=ROOM,
            )(mine, even, odd, index, face_blocks, local, *states)
            if last:
                outs, out_specs = [shape((1, 2, NODES, ROWS), F32)], [pl.BlockSpec()]
            else:
                outs = [spread_shape, packed_shape] + [state] * (1 if turn == DEGREE - 1 else 2)
                out_specs = [HBM] + [VMEM] * (len(outs) - 1)
            results = call(
                make_final_kernel(turn, last),
                [VMEM] * (6 + len(late)),
                outs,
                out_specs,
                final_scratch + send_scratch,
                flops=4 << 30,
                room=ROOM,
            )(fault_blocks, face_blocks, index, other, base, half, *late)
            if last:
                return results[0]
            if turn == DEGREE - 1:
                spread, packed, total = results
            elif turn == 0:
                spread, packed, residual, step = results
                correction = step
            else:
                spread, packed, step, correction = results


def solution(mesh):
    in_specs = (
        P("gx", "gy", None, None),
        P("gx", "gy", None, None),
        P("gx", "gy", None, None),
        P(None, "gx", "gy", None, None),
        P("gx", "gy", None, None),
        P(None, "gx", "gy", None),
        P("gx", "gy"),
    )
    out_specs = P("gx", "gy", None, None)
    return jax.shard_map(shards, mesh=mesh, in_specs=in_specs, out_specs=out_specs, check_vma=False)
```

time: 153 us -> 149 us (0.974)
  the two profiles are of different devices: /device:TPU:1 before, /device:TPU:17 now
where the time goes in v2:
time: 149 us; the launch traced here: 147 us
  starting transfers between devices  79.5 us (53%)
  Pallas kernels  34.1 us (23%)
  waiting for transfers between devices  24.3 us (16%)
  local copies, waits for them, and re-layouts  8.41 us (6%)
    all_to_all x8, starting transfers between devices, shards(): mine = lax.all_to_all(spread, 'gy', 0, 0, axis_index_groups=same_core)  43.8 us
    ppermute x24, starting transfers between devices, swap(): return lax.ppermute(value, axis, pairs + [(b, a) for a, b in pairs])  35.7 us
    ppermute x24, waiting for transfers between devices, swap(): return lax.ppermute(value, axis, pairs + [(b, a) for a, b in pairs])  24.3 us
    pallas_call x8, Pallas kernels, shards(): call(make_final_kernel(turn, last), [VMEM] * (6 + len(late)), outs, out_s...  20 us
    unnamed x30, local copies, waits for them, and re-layouts  8.41 us
    pallas_call x8, Pallas kernels, shards(): call(local_kernel, [VMEM] * 3, state, VMEM, room=ROOM)  6.86 us
    pallas_call x8, Pallas kernels, shards(): call(make_stage_kernel(turn), [VMEM] * (6 + len(states)), [state, shape((...  6.32 us
  transfers between devices with their start and end apart: 32, of which 16 were waited for; matrix products, arithmetic and copies ran while one was open for 0% of the time, Pallas kernels for 9%

profile of v2, /device:TPU:17, one launch (start us, length us, event | category | flops | bytes accessed | tf_op | source)
XLA Modules:
  0.0 147.5 jit_solution(6554298170516062629)
XLA Ops:
  3.0 0.9 shard_map.73
  3.9 5.8 %all-to-all-start = ((bf16[8,32,512]{2,1,0:T(8,128)(2,1)}), bf16[8,32,512]{2,1,0:T(8,128)(2,1)S(1)}, u32[]{:S(2)}, u32[]{:S(2)}) async-start(bf16[8,32,512]{2,1,0:T(8,128)(2,1)} %get-tuple-element.86), calls=%async_computation | async-start | bytes 524288 | tf_op jit(solution)/shard_map/all_to_all | solution.py:263
  9.7 2.5 %collective-permute-start.1 = (bf16[128,128]{1,0:T(8,128)(2,1)S(1)}, bf16[128,128]{1,0:T(8,128)(2,1)S(1)}, u32[]{:S(2)}, u32[]{:S(2)}) collective-permute-start(bf16[128,128]{1,0:T(8,128)(2,1)S(1)} %get-tuple-element.87.own_ref), channel_id=1, source_target_pairs={{16,32},{17,33},{18,34},{19,35},{20,36},{21,37},{22,38},{23,39},{2... | collective-permute-start | bytes 98312 | tf_op jit(solution)/shard_map/ppermute | solution.py:234
  12.3 1.4 copy-done
  13.7 0.9 copy-done.2
  16.1 2.1 %collective-permute-start.2 = (bf16[8,32,512]{2,1,0:T(8,128)(2,1)S(1)}, bf16[8,32,512]{2,1,0:T(8,128)(2,1)S(1)}, u32[]{:S(2)}, u32[]{:S(2)}) collective-permute-start(bf16[8,32,512]{2,1,0:T(8,128)(2,1)S(1)} %all-to-all-done.mine_ref), channel_id=1, source_target_pairs={{0,1},{2,3},{4,5},{6,7},{8,9},{10,11},{12,13},{14,15},{1,0},{3,2},... | collective-permute-start | bytes 786440 | tf_op jit(solution)/shard_map/ppermute | solution.py:234
  19.4 1.2 copy-done.7
  20.6 2.5 %shard_map.76 = (bf16[8,32,512]{2,1,0:T(8,128)(2,1)}, bf16[128,128]{1,0:T(8,128)(2,1)S(1)}, f32[256,64]{1,0:T(8,128)S(1)}, f32[256,64]{1,0:T(8,128)S(1)}) custom-call(bf16[1,1,64,8192]{3,2,1,0:T(8,128)(2,1)S(1)} %copy-done.7, bf16[6,1,2,64,1024]{4,3,2,1,0:T(8,128)(2,1)S(1)} %copy-done.1, s32[8,128]{1,0:T(8,128)S(1)} %get-tuple-element.85.index_ref, ...), custom_call_target="tpu_custom_call" | custom-call | flops 4294967296 | bytes 2097152 | tf_op jit(solution)/shard_map/pallas_call | solution.py:284
  23.1 5.4 %all-to-all-start.1 = ((bf16[8,32,512]{2,1,0:T(8,128)(2,1)}), bf16[8,32,512]{2,1,0:T(8,128)(2,1)S(1)}, u32[]{:S(2)}, u32[]{:S(2)}) async-start(bf16[8,32,512]{2,1,0:T(8,128)(2,1)} %get-tuple-element.95), calls=%async_computation.1 | async-start | bytes 524288 | tf_op jit(solution)/shard_map/all_to_all | solution.py:263
  28.6 2.5 %collective-permute-start.4 = (bf16[128,128]{1,0:T(8,128)(2,1)S(1)}, bf16[128,128]{1,0:T(8,128)(2,1)S(1)}, u32[]{:S(2)}, u32[]{:S(2)}) collective-permute-start(bf16[128,128]{1,0:T(8,128)(2,1)S(1)} %get-tuple-element.96.own_ref), channel_id=1, source_target_pairs={{16,32},{17,33},{18,34},{19,35},{20,36},{21,37},{22,38},{23,39},{2... | collective-permute-start | bytes 98312 | tf_op jit(solution)/shard_map/ppermute | solution.py:234
  31.1 0.9 shard_map.77.local_ref
  32.0 3.0 %collective-permute-done.4.odd_ref = bf16[128,128]{1,0:T(8,128)(2,1)S(1)} collective-permute-done((bf16[128,128]{1,0:T(8,128)(2,1)S(1)}, bf16[128,128]{1,0:T(8,128)(2,1)S(1)}, u32[]{:S(2)}, u32[]{:S(2)}) %collective-permute-start.4) | collective-permute-done | bytes 32800 | tf_op jit(solution)/shard_map/ppermute | solution.py:234
  34.9 1.9 %collective-permute-start.5 = (bf16[8,32,512]{2,1,0:T(8,128)(2,1)S(1)}, bf16[8,32,512]{2,1,0:T(8,128)(2,1)S(1)}, u32[]{:S(2)}, u32[]{:S(2)}) collective-permute-start(bf16[8,32,512]{2,1,0:T(8,128)(2,1)S(1)} %all-to-all-done.1.mine_ref), channel_id=1, source_target_pairs={{0,1},{2,3},{4,5},{6,7},{8,9},{10,11},{12,13},{14,15},{1,0},{3,2},... | collective-permute-start | bytes 786440 | tf_op jit(solution)/shard_map/ppermute | solution.py:234
  38.0 2.5 %shard_map.79 = (bf16[8,32,512]{2,1,0:T(8,128)(2,1)}, bf16[128,128]{1,0:T(8,128)(2,1)S(1)}, f32[256,64]{1,0:T(8,128)S(1)}, f32[256,64]{1,0:T(8,128)S(1)}) custom-call(bf16[1,1,64,8192]{3,2,1,0:T(8,128)(2,1)S(1)} %copy-done.8, bf16[6,1,2,64,1024]{4,3,2,1,0:T(8,128)(2,1)S(1)} %copy-done.1, s32[8,128]{1,0:T(8,128)S(1)} %get-tuple-element.85.index_ref, ...), custom_call_target="tpu_custom_call" | custom-call | flops 4294967296 | bytes 2097152 | tf_op jit(solution)/shard_map/pallas_call | solution.py:284
  40.5 5.4 %all-to-all-start.2 = ((bf16[8,32,512]{2,1,0:T(8,128)(2,1)}), bf16[8,32,512]{2,1,0:T(8,128)(2,1)S(1)}, u32[]{:S(2)}, u32[]{:S(2)}) async-start(bf16[8,32,512]{2,1,0:T(8,128)(2,1)} %get-tuple-element.105), calls=%async_computation.2 | async-start | bytes 524288 | tf_op jit(solution)/shard_map/all_to_all | solution.py:263
  46.0 2.5 %collective-permute-start.7 = (bf16[128,128]{1,0:T(8,128)(2,1)S(1)}, bf16[128,128]{1,0:T(8,128)(2,1)S(1)}, u32[]{:S(2)}, u32[]{:S(2)}) collective-permute-start(bf16[128,128]{1,0:T(8,128)(2,1)S(1)} %get-tuple-element.106.own_ref), channel_id=1, source_target_pairs={{16,32},{17,33},{18,34},{19,35},{20,36},{21,37},{22,38},{23,39},{2... | collective-permute-start | bytes 98312 | tf_op jit(solution)/shard_map/ppermute | solution.py:234
  49.4 3.0 %collective-permute-done.7.odd_ref = bf16[128,128]{1,0:T(8,128)(2,1)S(1)} collective-permute-done((bf16[128,128]{1,0:T(8,128)(2,1)S(1)}, bf16[128,128]{1,0:T(8,128)(2,1)S(1)}, u32[]{:S(2)}, u32[]{:S(2)}) %collective-permute-start.7) | collective-permute-done | bytes 32800 | tf_op jit(solution)/shard_map/ppermute | solution.py:234
  52.3 1.9 %collective-permute-start.8 = (bf16[8,32,512]{2,1,0:T(8,128)(2,1)S(1)}, bf16[8,32,512]{2,1,0:T(8,128)(2,1)S(1)}, u32[]{:S(2)}, u32[]{:S(2)}) collective-permute-start(bf16[8,32,512]{2,1,0:T(8,128)(2,1)S(1)} %all-to-all-done.2.mine_ref), channel_id=1, source_target_pairs={{0,1},{2,3},{4,5},{6,7},{8,9},{10,11},{12,13},{14,15},{1,0},{3,2},... | collective-permute-start | bytes 786440 | tf_op jit(solution)/shard_map/ppermute | solution.py:234
  55.4 2.5 %shard_map.82 = (bf16[8,32,512]{2,1,0:T(8,128)(2,1)}, bf16[128,128]{1,0:T(8,128)(2,1)S(1)}, f32[256,64]{1,0:T(8,128)S(1)}, f32[256,64]{1,0:T(8,128)S(1)}) custom-call(bf16[1,1,64,8192]{3,2,1,0:T(8,128)(2,1)S(1)} %copy-done.9, bf16[6,1,2,64,1024]{4,3,2,1,0:T(8,128)(2,1)S(1)} %copy-done.1, s32[8,128]{1,0:T(8,128)S(1)} %get-tuple-element.85.index_ref, ...), custom_call_target="tpu_custom_call" | custom-call | flops 4294967296 | bytes 2097152 | tf_op jit(solution)/shard_map/pallas_call | solution.py:284
  57.9 5.4 %all-to-all-start.3 = ((bf16[8,32,512]{2,1,0:T(8,128)(2,1)}), bf16[8,32,512]{2,1,0:T(8,128)(2,1)S(1)}, u32[]{:S(2)}, u32[]{:S(2)}) async-start(bf16[8,32,512]{2,1,0:T(8,128)(2,1)} %get-tuple-element.115), calls=%async_computation.3 | async-start | bytes 524288 | tf_op jit(solution)/shard_map/all_to_all | solution.py:263
  63.3 2.5 %collective-permute-start.10 = (bf16[128,128]{1,0:T(8,128)(2,1)S(1)}, bf16[128,128]{1,0:T(8,128)(2,1)S(1)}, u32[]{:S(2)}, u32[]{:S(2)}) collective-permute-start(bf16[128,128]{1,0:T(8,128)(2,1)S(1)} %get-tuple-element.116.own_ref), channel_id=1, source_target_pairs={{16,32},{17,33},{18,34},{19,35},{20,36},{21,37},{22,38},{23,39},{2... | collective-permute-start | bytes 98312 | tf_op jit(solution)/shard_map/ppermute | solution.py:234
  66.8 3.0 %collective-permute-done.10.odd_ref = bf16[128,128]{1,0:T(8,128)(2,1)S(1)} collective-permute-done((bf16[128,128]{1,0:T(8,128)(2,1)S(1)}, bf16[128,128]{1,0:T(8,128)(2,1)S(1)}, u32[]{:S(2)}, u32[]{:S(2)}) %collective-permute-start.10) | collective-permute-done | bytes 32800 | tf_op jit(solution)/shard_map/ppermute | solution.py:234
  69.7 1.9 %collective-permute-start.11 = (bf16[8,32,512]{2,1,0:T(8,128)(2,1)S(1)}, bf16[8,32,512]{2,1,0:T(8,128)(2,1)S(1)}, u32[]{:S(2)}, u32[]{:S(2)}) collective-permute-start(bf16[8,32,512]{2,1,0:T(8,128)(2,1)S(1)} %all-to-all-done.3.mine_ref), channel_id=1, source_target_pairs={{0,1},{2,3},{4,5},{6,7},{8,9},{10,11},{12,13},{14,15},{1,0},{3,2},... | collective-permute-start | bytes 786440 | tf_op jit(solution)/shard_map/ppermute | solution.py:234
  72.8 2.5 %shard_map.85 = (bf16[8,32,512]{2,1,0:T(8,128)(2,1)}, bf16[128,128]{1,0:T(8,128)(2,1)S(1)}, f32[256,64]{1,0:T(8,128)S(1)}) custom-call(bf16[1,1,64,8192]{3,2,1,0:T(8,128)(2,1)S(1)} %copy-done.10, bf16[6,1,2,64,1024]{4,3,2,1,0:T(8,128)(2,1)S(1)} %copy-done.1, s32[8,128]{1,0:T(8,128)S(1)} %get-tuple-element.85.index_ref, ...), custom_call_target="tpu_custom_call" | custom-call | flops 4294967296 | bytes 2097152 | tf_op jit(solution)/shard_map/pallas_call | solution.py:284
  75.3 5.4 %all-to-all-start.4 = ((bf16[8,32,512]{2,1,0:T(8,128)(2,1)}), bf16[8,32,512]{2,1,0:T(8,128)(2,1)S(1)}, u32[]{:S(2)}, u32[]{:S(2)}) async-start(bf16[8,32,512]{2,1,0:T(8,128)(2,1)} %get-tuple-element.126), calls=%async_computation.4 | async-start | bytes 524288 | tf_op jit(solution)/shard_map/all_to_all | solution.py:263
  80.7 2.5 %collective-permute-start.13 = (bf16[128,128]{1,0:T(8,128)(2,1)S(1)}, bf16[128,128]{1,0:T(8,128)(2,1)S(1)}, u32[]{:S(2)}, u32[]{:S(2)}) collective-permute-start(bf16[128,128]{1,0:T(8,128)(2,1)S(1)} %get-tuple-element.127.own_ref), channel_id=1, source_target_pairs={{16,32},{17,33},{18,34},{19,35},{20,36},{21,37},{22,38},{23,39},{2... | collective-permute-start | bytes 98312 | tf_op jit(solution)/shard_map/ppermute | solution.py:234
  84.2 3.0 %collective-permute-done.13.odd_ref = bf16[128,128]{1,0:T(8,128)(2,1)S(1)} collective-permute-done((bf16[128,128]{1,0:T(8,128)(2,1)S(1)}, bf16[128,128]{1,0:T(8,128)(2,1)S(1)}, u32[]{:S(2)}, u32[]{:S(2)}) %collective-permute-start.13) | collective-permute-done | bytes 32800 | tf_op jit(solution)/shard_map/ppermute | solution.py:234
  87.1 1.8 %collective-permute-start.14 = (bf16[8,32,512]{2,1,0:T(8,128)(2,1)S(1)}, bf16[8,32,512]{2,1,0:T(8,128)(2,1)S(1)}, u32[]{:S(2)}, u32[]{:S(2)}) collective-permute-start(bf16[8,32,512]{2,1,0:T(8,128)(2,1)S(1)} %all-to-all-done.4.mine_ref), channel_id=1, source_target_pairs={{0,1},{2,3},{4,5},{6,7},{8,9},{10,11},{12,13},{14,15},{1,0},{3,2},... | collective-permute-start | bytes 786440 | tf_op jit(solution)/shard_map/ppermute | solution.py:234
  90.1 1.2 copy-done.11
  91.3 2.5 %shard_map.88 = (bf16[8,32,512]{2,1,0:T(8,128)(2,1)}, bf16[128,128]{1,0:T(8,128)(2,1)S(1)}, f32[256,64]{1,0:T(8,128)S(1)}, f32[256,64]{1,0:T(8,128)S(1)}) custom-call(bf16[1,1,64,8192]{3,2,1,0:T(8,128)(2,1)S(1)} %copy-done.11, bf16[6,1,2,64,1024]{4,3,2,1,0:T(8,128)(2,1)S(1)} %copy-done.1, s32[8,128]{1,0:T(8,128)S(1)} %get-tuple-element.85.index_ref, ...), custom_call_target="tpu_custom_call" | custom-call | flops 4294967296 | bytes 2097152 | tf_op jit(solution)/shard_map/pallas_call | solution.py:284
  93.8 5.4 %all-to-all-start.5 = ((bf16[8,32,512]{2,1,0:T(8,128)(2,1)}), bf16[8,32,512]{2,1,0:T(8,128)(2,1)S(1)}, u32[]{:S(2)}, u32[]{:S(2)}) async-start(bf16[8,32,512]{2,1,0:T(8,128)(2,1)} %get-tuple-element.134), calls=%async_computation.5 | async-start | bytes 524288 | tf_op jit(solution)/shard_map/all_to_all | solution.py:263
  99.3 2.5 %collective-permute-start.16 = (bf16[128,128]{1,0:T(8,128)(2,1)S(1)}, bf16[128,128]{1,0:T(8,128)(2,1)S(1)}, u32[]{:S(2)}, u32[]{:S(2)}) collective-permute-start(bf16[128,128]{1,0:T(8,128)(2,1)S(1)} %get-tuple-element.135.own_ref), channel_id=1, source_target_pairs={{16,32},{17,33},{18,34},{19,35},{20,36},{21,37},{22,38},{23,39},{2... | collective-permute-start | bytes 98312 | tf_op jit(solution)/shard_map/ppermute | solution.py:234
  101.8 0.9 shard_map.89.local_ref
  102.7 3.0 %collective-permute-done.16.odd_ref = bf16[128,128]{1,0:T(8,128)(2,1)S(1)} collective-permute-done((bf16[128,128]{1,0:T(8,128)(2,1)S(1)}, bf16[128,128]{1,0:T(8,128)(2,1)S(1)}, u32[]{:S(2)}, u32[]{:S(2)}) %collective-permute-start.16) | collective-permute-done | bytes 32800 | tf_op jit(solution)/shard_map/ppermute | solution.py:234
  105.7 1.9 %collective-permute-start.17 = (bf16[8,32,512]{2,1,0:T(8,128)(2,1)S(1)}, bf16[8,32,512]{2,1,0:T(8,128)(2,1)S(1)}, u32[]{:S(2)}, u32[]{:S(2)}) collective-permute-start(bf16[8,32,512]{2,1,0:T(8,128)(2,1)S(1)} %all-to-all-done.5.mine_ref), channel_id=1, source_target_pairs={{0,1},{2,3},{4,5},{6,7},{8,9},{10,11},{12,13},{14,15},{1,0},{3,2},... | collective-permute-start | bytes 786440 | tf_op jit(solution)/shard_map/ppermute | solution.py:234
  108.7 2.5 %shard_map.91 = (bf16[8,32,512]{2,1,0:T(8,128)(2,1)}, bf16[128,128]{1,0:T(8,128)(2,1)S(1)}, f32[256,64]{1,0:T(8,128)S(1)}, f32[256,64]{1,0:T(8,128)S(1)}) custom-call(bf16[1,1,64,8192]{3,2,1,0:T(8,128)(2,1)S(1)} %copy-done.12, bf16[6,1,2,64,1024]{4,3,2,1,0:T(8,128)(2,1)S(1)} %copy-done.1, s32[8,128]{1,0:T(8,128)S(1)} %get-tuple-element.85.index_ref, ...), custom_call_target="tpu_custom_call" | custom-call | flops 4294967296 | bytes 2097152 | tf_op jit(solution)/shard_map/pallas_call | solution.py:284
  111.2 5.4 %all-to-all-start.6 = ((bf16[8,32,512]{2,1,0:T(8,128)(2,1)}), bf16[8,32,512]{2,1,0:T(8,128)(2,1)S(1)}, u32[]{:S(2)}, u32[]{:S(2)}) async-start(bf16[8,32,512]{2,1,0:T(8,128)(2,1)} %get-tuple-element.144), calls=%async_computation.6 | async-start | bytes 524288 | tf_op jit(solution)/shard_map/all_to_all | solution.py:263
  116.7 2.5 %collective-permute-start.19 = (bf16[128,128]{1,0:T(8,128)(2,1)S(1)}, bf16[128,128]{1,0:T(8,128)(2,1)S(1)}, u32[]{:S(2)}, u32[]{:S(2)}) collective-permute-start(bf16[128,128]{1,0:T(8,128)(2,1)S(1)} %get-tuple-element.145.own_ref), channel_id=1, source_target_pairs={{16,32},{17,33},{18,34},{19,35},{20,36},{21,37},{22,38},{23,39},{2... | collective-permute-start | bytes 98312 | tf_op jit(solution)/shard_map/ppermute | solution.py:234
  120.1 3.0 %collective-permute-done.19.odd_ref = bf16[128,128]{1,0:T(8,128)(2,1)S(1)} collective-permute-done((bf16[128,128]{1,0:T(8,128)(2,1)S(1)}, bf16[128,128]{1,0:T(8,128)(2,1)S(1)}, u32[]{:S(2)}, u32[]{:S(2)}) %collective-permute-start.19) | collective-permute-done | bytes 32800 | tf_op jit(solution)/shard_map/ppermute | solution.py:234
  123.1 2.1 %collective-permute-start.20 = (bf16[8,32,512]{2,1,0:T(8,128)(2,1)S(1)}, bf16[8,32,512]{2,1,0:T(8,128)(2,1)S(1)}, u32[]{:S(2)}, u32[]{:S(2)}) collective-permute-start(bf16[8,32,512]{2,1,0:T(8,128)(2,1)S(1)} %all-to-all-done.6.mine_ref), channel_id=1, source_target_pairs={{0,1},{2,3},{4,5},{6,7},{8,9},{10,11},{12,13},{14,15},{1,0},{3,2},... | collective-permute-start | bytes 786440 | tf_op jit(solution)/shard_map/ppermute | solution.py:234
  126.3 2.5 %shard_map.94 = (bf16[8,32,512]{2,1,0:T(8,128)(2,1)}, bf16[128,128]{1,0:T(8,128)(2,1)S(1)}, f32[256,64]{1,0:T(8,128)S(1)}, f32[256,64]{1,0:T(8,128)S(1)}) custom-call(bf16[1,1,64,8192]{3,2,1,0:T(8,128)(2,1)S(1)} %copy-done.13, bf16[6,1,2,64,1024]{4,3,2,1,0:T(8,128)(2,1)S(1)} %copy-done.1, s32[8,128]{1,0:T(8,128)S(1)} %get-tuple-element.85.index_ref, ...), custom_call_target="tpu_custom_call" | custom-call | flops 4294967296 | bytes 2097152 | tf_op jit(solution)/shard_map/pallas_call | solution.py:284
  128.9 5.4 %all-to-all-start.7 = ((bf16[8,32,512]{2,1,0:T(8,128)(2,1)}), bf16[8,32,512]{2,1,0:T(8,128)(2,1)S(1)}, u32[]{:S(2)}, u32[]{:S(2)}) async-start(bf16[8,32,512]{2,1,0:T(8,128)(2,1)} %get-tuple-element.154), calls=%async_computation.7 | async-start | bytes 524288 | tf_op jit(solution)/shard_map/all_to_all | solution.py:263
  134.3 2.5 %collective-permute-start.22 = (bf16[128,128]{1,0:T(8,128)(2,1)S(1)}, bf16[128,128]{1,0:T(8,128)(2,1)S(1)}, u32[]{:S(2)}, u32[]{:S(2)}) collective-permute-start(bf16[128,128]{1,0:T(8,128)(2,1)S(1)} %get-tuple-element.155.own_ref), channel_id=1, source_target_pairs={{16,32},{17,33},{18,34},{19,35},{20,36},{21,37},{22,38},{23,39},{2... | collective-permute-start | bytes 98312 | tf_op jit(solution)/shard_map/ppermute | solution.py:234
  136.8 0.9 shard_map.95.local_ref
  137.7 3.0 %collective-permute-done.22.odd_ref = bf16[128,128]{1,0:T(8,128)(2,1)S(1)} collective-permute-done((bf16[128,128]{1,0:T(8,128)(2,1)S(1)}, bf16[128,128]{1,0:T(8,128)(2,1)S(1)}, u32[]{:S(2)}, u32[]{:S(2)}) %collective-permute-start.22) | collective-permute-done | bytes 32800 | tf_op jit(solution)/shard_map/ppermute | solution.py:234
  140.7 1.8 %collective-permute-start.23 = (bf16[8,32,512]{2,1,0:T(8,128)(2,1)S(1)}, bf16[8,32,512]{2,1,0:T(8,128)(2,1)S(1)}, u32[]{:S(2)}, u32[]{:S(2)}) collective-permute-start(bf16[8,32,512]{2,1,0:T(8,128)(2,1)S(1)} %all-to-all-done.7.mine_ref), channel_id=1, source_target_pairs={{0,1},{2,3},{4,5},{6,7},{8,9},{10,11},{12,13},{14,15},{1,0},{3,2},... | collective-permute-start | bytes 786440 | tf_op jit(solution)/shard_map/ppermute | solution.py:234
  143.7 1.2 copy-done.14
  144.9 2.4 %shard_map.97 = f32[1,2,64,128]{3,2,1,0:T(8,128)} custom-call(bf16[1,1,64,8192]{3,2,1,0:T(8,128)(2,1)S(1)} %copy-done.14, bf16[6,1,2,64,1024]{4,3,2,1,0:T(8,128)(2,1)S(1)} %copy-done.1, s32[8,128]{1,0:T(8,128)S(1)} %get-tuple-element.85.index_ref, bf16[8,32,512]{2,1,0:T(8,128)(2,1)S(1)} %collective-permute-done.23.other_ref, ...), custom_call_target="tpu_custom_call" | custom-call | flops 4294967296 | bytes 2097152 | tf_op jit(solution)/shard_map/pallas_call | solution.py:284
  (71 shorter events, 16.6 us)
Async XLA Ops:
  0.7 0.8 copy-start.4
  1.5 0.8 copy-start.5
  2.3 0.7 copy-start.6
  3.9 12.2 %all-to-all-start = ((bf16[8,32,512]{2,1,0:T(8,128)(2,1)}), bf16[8,32,512]{2,1,0:T(8,128)(2,1)S(1)}, u32[]{:S(2)}, u32[]{:S(2)}) async-start(bf16[8,32,512]{2,1,0:T(8,128)(2,1)} %get-tuple-element.86), calls=%async_computation | async-start | bytes 524288 | tf_op jit(solution)/shard_map/all_to_all | solution.py:263
  9.7 6.4 %collective-permute-start.1 = (bf16[128,128]{1,0:T(8,128)(2,1)S(1)}, bf16[128,128]{1,0:T(8,128)(2,1)S(1)}, u32[]{:S(2)}, u32[]{:S(2)}) collective-permute-start(bf16[128,128]{1,0:T(8,128)(2,1)S(1)} %get-tuple-element.87.own_ref), channel_id=1, source_target_pairs={{16,32},{17,33},{18,34},{19,35},{20,36},{21,37},{22,38},{23,39},{2... | collective-permute-start | bytes 98312 | tf_op jit(solution)/shard_map/ppermute | solution.py:234
  12.2 3.8 %collective-permute-start = (bf16[128,128]{1,0:T(8,128)(2,1)S(1)}, bf16[128,128]{1,0:T(8,128)(2,1)S(1)}, u32[]{:S(2)}, u32[]{:S(2)}) collective-permute-start(bf16[128,128]{1,0:T(8,128)(2,1)S(1)} %get-tuple-element.87.own_ref), channel_id=1, source_target_pairs={{0,16},{32,48},{64,80},{96,112},{16,0},{48,32},{80,64},{112,96},{1... | collective-permute-start | bytes 98312 | tf_op jit(solution)/shard_map/ppermute | solution.py:234
  12.3 1.4 copy-start
  13.7 0.9 copy-start.2
  14.6 3.6 %copy-start.1 = (bf16[6,1,2,64,1024]{4,3,2,1,0:T(8,128)(2,1)S(1)}, bf16[6,1,2,64,1024]{4,3,2,1,0:T(8,128)(2,1)}, u32[]{:S(2)}) copy-start(bf16[6,1,2,64,1024]{4,3,2,1,0:T(8,128)(2,1)} %face_ref.47) | copy-start | bytes 4718596
  16.1 3.3 %collective-permute-start.2 = (bf16[8,32,512]{2,1,0:T(8,128)(2,1)S(1)}, bf16[8,32,512]{2,1,0:T(8,128)(2,1)S(1)}, u32[]{:S(2)}, u32[]{:S(2)}) collective-permute-start(bf16[8,32,512]{2,1,0:T(8,128)(2,1)S(1)} %all-to-all-done.mine_ref), channel_id=1, source_target_pairs={{0,1},{2,3},{4,5},{6,7},{8,9},{10,11},{12,13},{14,15},{1,0},{3,2},... | collective-permute-start | bytes 786440 | tf_op jit(solution)/shard_map/ppermute | solution.py:234
  19.4 1.2 copy-start.7
  20.6 10.5 %copy-start.3 = (bf16[1,2,64,1024]{3,2,1,0:T(8,128)(2,1)S(1)}, bf16[1,2,64,1024]{3,2,1,0:T(8,128)(2,1)}, u32[]{:S(2)}) copy-start(bf16[1,2,64,1024]{3,2,1,0:T(8,128)(2,1)} %elem_ref.15) | copy-start | bytes 786436
  23.1 11.8 %all-to-all-start.1 = ((bf16[8,32,512]{2,1,0:T(8,128)(2,1)}), bf16[8,32,512]{2,1,0:T(8,128)(2,1)S(1)}, u32[]{:S(2)}, u32[]{:S(2)}) async-start(bf16[8,32,512]{2,1,0:T(8,128)(2,1)} %get-tuple-element.95), calls=%async_computation.1 | async-start | bytes 524288 | tf_op jit(solution)/shard_map/all_to_all | solution.py:263
  28.6 6.4 %collective-permute-start.4 = (bf16[128,128]{1,0:T(8,128)(2,1)S(1)}, bf16[128,128]{1,0:T(8,128)(2,1)S(1)}, u32[]{:S(2)}, u32[]{:S(2)}) collective-permute-start(bf16[128,128]{1,0:T(8,128)(2,1)S(1)} %get-tuple-element.96.own_ref), channel_id=1, source_target_pairs={{16,32},{17,33},{18,34},{19,35},{20,36},{21,37},{22,38},{23,39},{2... | collective-permute-start | bytes 98312 | tf_op jit(solution)/shard_map/ppermute | solution.py:234
  31.1 3.8 %collective-permute-start.3 = (bf16[128,128]{1,0:T(8,128)(2,1)S(1)}, bf16[128,128]{1,0:T(8,128)(2,1)S(1)}, u32[]{:S(2)}, u32[]{:S(2)}) collective-permute-start(bf16[128,128]{1,0:T(8,128)(2,1)S(1)} %get-tuple-element.96.own_ref), channel_id=1, source_target_pairs={{0,16},{32,48},{64,80},{96,112},{16,0},{48,32},{80,64},{112,96},{1... | collective-permute-start | bytes 98312 | tf_op jit(solution)/shard_map/ppermute | solution.py:234
  34.9 3.1 %copy-start.8 = (bf16[1,1,64,8192]{3,2,1,0:T(8,128)(2,1)S(1)}, bf16[1,1,64,8192]{3,2,1,0:T(8,128)(2,1)}, u32[]{:S(2)}) copy-start(bf16[1,1,64,8192]{3,2,1,0:T(8,128)(2,1)} %fault_ref.15) | copy-start | bytes 3145732
  34.9 3.0 %collective-permute-start.5 = (bf16[8,32,512]{2,1,0:T(8,128)(2,1)S(1)}, bf16[8,32,512]{2,1,0:T(8,128)(2,1)S(1)}, u32[]{:S(2)}, u32[]{:S(2)}) collective-permute-start(bf16[8,32,512]{2,1,0:T(8,128)(2,1)S(1)} %all-to-all-done.1.mine_ref), channel_id=1, source_target_pairs={{0,1},{2,3},{4,5},{6,7},{8,9},{10,11},{12,13},{14,15},{1,0},{3,2},... | collective-permute-start | bytes 786440 | tf_op jit(solution)/shard_map/ppermute | solution.py:234
  40.5 11.8 %all-to-all-start.2 = ((bf16[8,32,512]{2,1,0:T(8,128)(2,1)}), bf16[8,32,512]{2,1,0:T(8,128)(2,1)S(1)}, u32[]{:S(2)}, u32[]{:S(2)}) async-start(bf16[8,32,512]{2,1,0:T(8,128)(2,1)} %get-tuple-element.105), calls=%async_computation.2 | async-start | bytes 524288 | tf_op jit(solution)/shard_map/all_to_all | solution.py:263
  46.0 6.4 %collective-permute-start.7 = (bf16[128,128]{1,0:T(8,128)(2,1)S(1)}, bf16[128,128]{1,0:T(8,128)(2,1)S(1)}, u32[]{:S(2)}, u32[]{:S(2)}) collective-permute-start(bf16[128,128]{1,0:T(8,128)(2,1)S(1)} %get-tuple-element.106.own_ref), channel_id=1, source_target_pairs={{16,32},{17,33},{18,34},{19,35},{20,36},{21,37},{22,38},{23,39},{2... | collective-permute-start | bytes 98312 | tf_op jit(solution)/shard_map/ppermute | solution.py:234
  48.5 3.8 %collective-permute-start.6 = (bf16[128,128]{1,0:T(8,128)(2,1)S(1)}, bf16[128,128]{1,0:T(8,128)(2,1)S(1)}, u32[]{:S(2)}, u32[]{:S(2)}) collective-permute-start(bf16[128,128]{1,0:T(8,128)(2,1)S(1)} %get-tuple-element.106.own_ref), channel_id=1, source_target_pairs={{0,16},{32,48},{64,80},{96,112},{16,0},{48,32},{80,64},{112,96},{1... | collective-permute-start | bytes 98312 | tf_op jit(solution)/shard_map/ppermute | solution.py:234
  52.3 3.1 %copy-start.9 = (bf16[1,1,64,8192]{3,2,1,0:T(8,128)(2,1)S(1)}, bf16[1,1,64,8192]{3,2,1,0:T(8,128)(2,1)}, u32[]{:S(2)}) copy-start(bf16[1,1,64,8192]{3,2,1,0:T(8,128)(2,1)} %fault_ref.15) | copy-start | bytes 3145732
  52.3 3.0 %collective-permute-start.8 = (bf16[8,32,512]{2,1,0:T(8,128)(2,1)S(1)}, bf16[8,32,512]{2,1,0:T(8,128)(2,1)S(1)}, u32[]{:S(2)}, u32[]{:S(2)}) collective-permute-start(bf16[8,32,512]{2,1,0:T(8,128)(2,1)S(1)} %all-to-all-done.2.mine_ref), channel_id=1, source_target_pairs={{0,1},{2,3},{4,5},{6,7},{8,9},{10,11},{12,13},{14,15},{1,0},{3,2},... | collective-permute-start | bytes 786440 | tf_op jit(solution)/shard_map/ppermute | solution.py:234
  57.9 11.8 %all-to-all-start.3 = ((bf16[8,32,512]{2,1,0:T(8,128)(2,1)}), bf16[8,32,512]{2,1,0:T(8,128)(2,1)S(1)}, u32[]{:S(2)}, u32[]{:S(2)}) async-start(bf16[8,32,512]{2,1,0:T(8,128)(2,1)} %get-tuple-element.115), calls=%async_computation.3 | async-start | bytes 524288 | tf_op jit(solution)/shard_map/all_to_all | solution.py:263
  63.3 6.4 %collective-permute-start.10 = (bf16[128,128]{1,0:T(8,128)(2,1)S(1)}, bf16[128,128]{1,0:T(8,128)(2,1)S(1)}, u32[]{:S(2)}, u32[]{:S(2)}) collective-permute-start(bf16[128,128]{1,0:T(8,128)(2,1)S(1)} %get-tuple-element.116.own_ref), channel_id=1, source_target_pairs={{16,32},{17,33},{18,34},{19,35},{20,36},{21,37},{22,38},{23,39},{2... | collective-permute-start | bytes 98312 | tf_op jit(solution)/shard_map/ppermute | solution.py:234
  65.9 3.8 %collective-permute-start.9 = (bf16[128,128]{1,0:T(8,128)(2,1)S(1)}, bf16[128,128]{1,0:T(8,128)(2,1)S(1)}, u32[]{:S(2)}, u32[]{:S(2)}) collective-permute-start(bf16[128,128]{1,0:T(8,128)(2,1)S(1)} %get-tuple-element.116.own_ref), channel_id=1, source_target_pairs={{0,16},{32,48},{64,80},{96,112},{16,0},{48,32},{80,64},{112,96},{1... | collective-permute-start | bytes 98312 | tf_op jit(solution)/shard_map/ppermute | solution.py:234
  69.7 3.1 %copy-start.10 = (bf16[1,1,64,8192]{3,2,1,0:T(8,128)(2,1)S(1)}, bf16[1,1,64,8192]{3,2,1,0:T(8,128)(2,1)}, u32[]{:S(2)}) copy-start(bf16[1,1,64,8192]{3,2,1,0:T(8,128)(2,1)} %fault_ref.15) | copy-start | bytes 3145732
  69.7 3.0 %collective-permute-start.11 = (bf16[8,32,512]{2,1,0:T(8,128)(2,1)S(1)}, bf16[8,32,512]{2,1,0:T(8,128)(2,1)S(1)}, u32[]{:S(2)}, u32[]{:S(2)}) collective-permute-start(bf16[8,32,512]{2,1,0:T(8,128)(2,1)S(1)} %all-to-all-done.3.mine_ref), channel_id=1, source_target_pairs={{0,1},{2,3},{4,5},{6,7},{8,9},{10,11},{12,13},{14,15},{1,0},{3,2},... | collective-permute-start | bytes 786440 | tf_op jit(solution)/shard_map/ppermute | solution.py:234
  75.3 11.8 %all-to-all-start.4 = ((bf16[8,32,512]{2,1,0:T(8,128)(2,1)}), bf16[8,32,512]{2,1,0:T(8,128)(2,1)S(1)}, u32[]{:S(2)}, u32[]{:S(2)}) async-start(bf16[8,32,512]{2,1,0:T(8,128)(2,1)} %get-tuple-element.126), calls=%async_computation.4 | async-start | bytes 524288 | tf_op jit(solution)/shard_map/all_to_all | solution.py:263
  80.7 6.4 %collective-permute-start.13 = (bf16[128,128]{1,0:T(8,128)(2,1)S(1)}, bf16[128,128]{1,0:T(8,128)(2,1)S(1)}, u32[]{:S(2)}, u32[]{:S(2)}) collective-permute-start(bf16[128,128]{1,0:T(8,128)(2,1)S(1)} %get-tuple-element.127.own_ref), channel_id=1, source_target_pairs={{16,32},{17,33},{18,34},{19,35},{20,36},{21,37},{22,38},{23,39},{2... | collective-permute-start | bytes 98312 | tf_op jit(solution)/shard_map/ppermute | solution.py:234
  83.3 3.8 %collective-permute-start.12 = (bf16[128,128]{1,0:T(8,128)(2,1)S(1)}, bf16[128,128]{1,0:T(8,128)(2,1)S(1)}, u32[]{:S(2)}, u32[]{:S(2)}) collective-permute-start(bf16[128,128]{1,0:T(8,128)(2,1)S(1)} %get-tuple-element.127.own_ref), channel_id=1, source_target_pairs={{0,16},{32,48},{64,80},{96,112},{16,0},{48,32},{80,64},{112,96},{1... | collective-permute-start | bytes 98312 | tf_op jit(solution)/shard_map/ppermute | solution.py:234
  87.1 3.0 %collective-permute-start.14 = (bf16[8,32,512]{2,1,0:T(8,128)(2,1)S(1)}, bf16[8,32,512]{2,1,0:T(8,128)(2,1)S(1)}, u32[]{:S(2)}, u32[]{:S(2)}) collective-permute-start(bf16[8,32,512]{2,1,0:T(8,128)(2,1)S(1)} %all-to-all-done.4.mine_ref), channel_id=1, source_target_pairs={{0,1},{2,3},{4,5},{6,7},{8,9},{10,11},{12,13},{14,15},{1,0},{3,2},... | collective-permute-start | bytes 786440 | tf_op jit(solution)/shard_map/ppermute | solution.py:234
  90.1 1.2 copy-start.11
  93.8 11.8 %all-to-all-start.5 = ((bf16[8,32,512]{2,1,0:T(8,128)(2,1)}), bf16[8,32,512]{2,1,0:T(8,128)(2,1)S(1)}, u32[]{:S(2)}, u32[]{:S(2)}) async-start(bf16[8,32,512]{2,1,0:T(8,128)(2,1)} %get-tuple-element.134), calls=%async_computation.5 | async-start | bytes 524288 | tf_op jit(solution)/shard_map/all_to_all | solution.py:263
  99.3 6.4 %collective-permute-start.16 = (bf16[128,128]{1,0:T(8,128)(2,1)S(1)}, bf16[128,128]{1,0:T(8,128)(2,1)S(1)}, u32[]{:S(2)}, u32[]{:S(2)}) collective-permute-start(bf16[128,128]{1,0:T(8,128)(2,1)S(1)} %get-tuple-element.135.own_ref), channel_id=1, source_target_pairs={{16,32},{17,33},{18,34},{19,35},{20,36},{21,37},{22,38},{23,39},{2... | collective-permute-start | bytes 98312 | tf_op jit(solution)/shard_map/ppermute | solution.py:234
  101.8 3.8 %collective-permute-start.15 = (bf16[128,128]{1,0:T(8,128)(2,1)S(1)}, bf16[128,128]{1,0:T(8,128)(2,1)S(1)}, u32[]{:S(2)}, u32[]{:S(2)}) collective-permute-start(bf16[128,128]{1,0:T(8,128)(2,1)S(1)} %get-tuple-element.135.own_ref), channel_id=1, source_target_pairs={{0,16},{32,48},{64,80},{96,112},{16,0},{48,32},{80,64},{112,96},{1... | collective-permute-start | bytes 98312 | tf_op jit(solution)/shard_map/ppermute | solution.py:234
  105.7 3.1 %copy-start.12 = (bf16[1,1,64,8192]{3,2,1,0:T(8,128)(2,1)S(1)}, bf16[1,1,64,8192]{3,2,1,0:T(8,128)(2,1)}, u32[]{:S(2)}) copy-start(bf16[1,1,64,8192]{3,2,1,0:T(8,128)(2,1)} %fault_ref.15) | copy-start | bytes 3145732
  105.7 3.0 %collective-permute-start.17 = (bf16[8,32,512]{2,1,0:T(8,128)(2,1)S(1)}, bf16[8,32,512]{2,1,0:T(8,128)(2,1)S(1)}, u32[]{:S(2)}, u32[]{:S(2)}) collective-permute-start(bf16[8,32,512]{2,1,0:T(8,128)(2,1)S(1)} %all-to-all-done.5.mine_ref), channel_id=1, source_target_pairs={{0,1},{2,3},{4,5},{6,7},{8,9},{10,11},{12,13},{14,15},{1,0},{3,2},... | collective-permute-start | bytes 786440 | tf_op jit(solution)/shard_map/ppermute | solution.py:234
  111.2 11.8 %all-to-all-start.6 = ((bf16[8,32,512]{2,1,0:T(8,128)(2,1)}), bf16[8,32,512]{2,1,0:T(8,128)(2,1)S(1)}, u32[]{:S(2)}, u32[]{:S(2)}) async-start(bf16[8,32,512]{2,1,0:T(8,128)(2,1)} %get-tuple-element.144), calls=%async_computation.6 | async-start | bytes 524288 | tf_op jit(solution)/shard_map/all_to_all | solution.py:263
  116.7 6.4 %collective-permute-start.19 = (bf16[128,128]{1,0:T(8,128)(2,1)S(1)}, bf16[128,128]{1,0:T(8,128)(2,1)S(1)}, u32[]{:S(2)}, u32[]{:S(2)}) collective-permute-start(bf16[128,128]{1,0:T(8,128)(2,1)S(1)} %get-tuple-element.145.own_ref), channel_id=1, source_target_pairs={{16,32},{17,33},{18,34},{19,35},{20,36},{21,37},{22,38},{23,39},{2... | collective-permute-start | bytes 98312 | tf_op jit(solution)/shard_map/ppermute | solution.py:234
  119.2 3.8 %collective-permute-start.18 = (bf16[128,128]{1,0:T(8,128)(2,1)S(1)}, bf16[128,128]{1,0:T(8,128)(2,1)S(1)}, u32[]{:S(2)}, u32[]{:S(2)}) collective-permute-start(bf16[128,128]{1,0:T(8,128)(2,1)S(1)} %get-tuple-element.145.own_ref), channel_id=1, source_target_pairs={{0,16},{32,48},{64,80},{96,112},{16,0},{48,32},{80,64},{112,96},{1... | collective-permute-start | bytes 98312 | tf_op jit(solution)/shard_map/ppermute | solution.py:234
  123.1 3.3 %copy-start.13 = (bf16[1,1,64,8192]{3,2,1,0:T(8,128)(2,1)S(1)}, bf16[1,1,64,8192]{3,2,1,0:T(8,128)(2,1)}, u32[]{:S(2)}) copy-start(bf16[1,1,64,8192]{3,2,1,0:T(8,128)(2,1)} %fault_ref.15) | copy-start | bytes 3145732
  123.1 3.3 %collective-permute-start.20 = (bf16[8,32,512]{2,1,0:T(8,128)(2,1)S(1)}, bf16[8,32,512]{2,1,0:T(8,128)(2,1)S(1)}, u32[]{:S(2)}, u32[]{:S(2)}) collective-permute-start(bf16[8,32,512]{2,1,0:T(8,128)(2,1)S(1)} %all-to-all-done.6.mine_ref), channel_id=1, source_target_pairs={{0,1},{2,3},{4,5},{6,7},{8,9},{10,11},{12,13},{14,15},{1,0},{3,2},... | collective-permute-start | bytes 786440 | tf_op jit(solution)/shard_map/ppermute | solution.py:234
  128.9 11.8 %all-to-all-start.7 = ((bf16[8,32,512]{2,1,0:T(8,128)(2,1)}), bf16[8,32,512]{2,1,0:T(8,128)(2,1)S(1)}, u32[]{:S(2)}, u32[]{:S(2)}) async-start(bf16[8,32,512]{2,1,0:T(8,128)(2,1)} %get-tuple-element.154), calls=%async_computation.7 | async-start | bytes 524288 | tf_op jit(solution)/shard_map/all_to_all | solution.py:263
  134.3 6.4 %collective-permute-start.22 = (bf16[128,128]{1,0:T(8,128)(2,1)S(1)}, bf16[128,128]{1,0:T(8,128)(2,1)S(1)}, u32[]{:S(2)}, u32[]{:S(2)}) collective-permute-start(bf16[128,128]{1,0:T(8,128)(2,1)S(1)} %get-tuple-element.155.own_ref), channel_id=1, source_target_pairs={{16,32},{17,33},{18,34},{19,35},{20,36},{21,37},{22,38},{23,39},{2... | collective-permute-start | bytes 98312 | tf_op jit(solution)/shard_map/ppermute | solution.py:234
  136.8 3.8 %collective-permute-start.21 = (bf16[128,128]{1,0:T(8,128)(2,1)S(1)}, bf16[128,128]{1,0:T(8,128)(2,1)S(1)}, u32[]{:S(2)}, u32[]{:S(2)}) collective-permute-start(bf16[128,128]{1,0:T(8,128)(2,1)S(1)} %get-tuple-element.155.own_ref), channel_id=1, source_target_pairs={{0,16},{32,48},{64,80},{96,112},{16,0},{48,32},{80,64},{112,96},{1... | collective-permute-start | bytes 98312 | tf_op jit(solution)/shard_map/ppermute | solution.py:234
  140.7 3.0 %collective-permute-start.23 = (bf16[8,32,512]{2,1,0:T(8,128)(2,1)S(1)}, bf16[8,32,512]{2,1,0:T(8,128)(2,1)S(1)}, u32[]{:S(2)}, u32[]{:S(2)}) collective-permute-start(bf16[8,32,512]{2,1,0:T(8,128)(2,1)S(1)} %all-to-all-done.7.mine_ref), channel_id=1, source_target_pairs={{0,1},{2,3},{4,5},{6,7},{8,9},{10,11},{12,13},{14,15},{1,0},{3,2},... | collective-permute-start | bytes 786440 | tf_op jit(solution)/shard_map/ppermute | solution.py:234
  143.7 1.2 copy-start.14

commit v3 on v2

--- a/solution.py
+++ b/solution.py
@@ -15,6 +15,7 @@
 PAIRS = 128
 CHIPS = 8
 ROOM = 14
+FAR_FLOPS = 100 << 30
 
 spectrum_low = 0.6
 spectrum_high = 3.0
@@ -118,25 +119,33 @@
     out_ref[...] = jnp.concatenate(sums, axis=0)
 
 
+def side_sum(packed_ref, face_ref, from_high):
+    expand, same = expander(), layer_mask(0)
+    side = jnp.where(from_high, 1, 0)
+    wide = [dot(packed_ref[:, ly * NODES : (ly + 1) * NODES], expand).astype(BF) for ly in range(2)]
+    return jnp.concatenate([dot_t(masked(wide[ly], same), face_ref[side, 0, ly]) for ly in range(2)], axis=0)
+
+
+def make_far_kernel(turn):
+    _, steps = coefficients()
+    scale = 1.0 if turn == 0 else steps[turn - 1][1]
+
+    def far_kernel(odd_ref, face_ref, base_ref, out_ref):
+        column = lax.axis_index("gx")
+        far = side_sum(odd_ref, face_ref, column % 2 == 1)
+        inner = (column > 0) & (column < 7)
+        out_ref[...] = base_ref[...] - scale * jnp.where(inner, far, jnp.zeros_like(far))
+
+    return far_kernel
+
+
 def make_stage_kernel(turn):
     _, steps = coefficients()
 
-    def stage_kernel(mine_ref, even_ref, odd_ref, index_ref, face_ref, local_ref, *refs):
+    def stage_kernel(mine_ref, even_ref, index_ref, face_ref, local_ref, *refs):
         states, (base_ref, half_ref) = refs[:-2], refs[-2:]
         half_ref[...] = gathered(index_ref, 0, mine_ref)
-        at = lax.axis_index("gx")
-        is_even = at % 2 == 0
-        low = jnp.where(is_even, odd_ref[...], even_ref[...])
-        high = jnp.where(is_even, even_ref[...], odd_ref[...])
-        low = jnp.where(at > 0, low, jnp.zeros_like(low))
-        high = jnp.where(at < 7, high, jnp.zeros_like(high))
-        expand, same = expander(), layer_mask(0)
-        wide = [
-            [masked(dot(field[:, ly * NODES : (ly + 1) * NODES], expand).astype(BF), same) for field in (low, high)]
-            for ly in range(2)
-        ]
-        sums = [dot_t(wide[ly][0], face_ref[0, 0, ly]) + dot_t(wide[ly][1], face_ref[1, 0, ly]) for ly in range(2)]
-        local = local_ref[...] + jnp.concatenate(sums, axis=0)
+        local = local_ref[...] + side_sum(even_ref, face_ref, lax.axis_index("gx") % 2 == 0)
         if turn == 0:
             base_ref[...] = states[0][...] - local
         else:
@@ -264,18 +273,19 @@
             even = swap(packed, "gx", [(0, 1), (2, 3), (4, 5), (6, 7)])
             odd = swap(packed, ("gx", "gy"), odd_pairs)
             local = call(local_kernel, [VMEM] * 3, state, VMEM, room=ROOM)(packed, elem_blocks, face_blocks)
-            mine, local, even, odd = lax.optimization_barrier((mine, local, even, odd))
+            mine, local = lax.optimization_barrier((mine, local))
             other = swap(mine, "gy", [(2 * chip, 2 * chip + 1) for chip in range(CHIPS)])
             last = sweep == SWEEPS - 1 and turn == DEGREE - 1
             states = [right] if turn == 0 else [residual, step]
             late = ([correction] if turn > 0 else []) + ([total] if turn == DEGREE - 1 else [])
             base, half = call(
                 make_stage_kernel(turn),
-                [VMEM] * (6 + len(states)),
+                [VMEM] * (5 + len(states)),
                 [state, shape((RHS * NODES, PAIRS), F32)],
                 [VMEM] * 2,
                 room=ROOM,
-            )(mine, even, odd, index, face_blocks, local, *states)
+            )(mine, even, index, face_blocks, local, *states)
+            base = call(make_far_kernel(turn), [VMEM] * 3, state, VMEM, flops=FAR_FLOPS, room=ROOM)(odd, face_blocks, base)
             if last:
                 outs, out_specs = [shape((1, 2, NODES, ROWS), F32)], [pl.BlockSpec()]
             else:

time: 149 us -> 144 us (0.966)
  starting transfers between devices: 79.5 us -> 73.7 us
  Pallas kernels: 34.1 us -> 35.6 us
  waiting for transfers between devices: 24.3 us -> 22.8 us
    ppermute x24, waiting for transfers between devices: 24.3 us -> 1.28 us  [swap(): return lax.ppermute(value, axis, pairs + [(b, a) for a, b in pairs])]
    all_to_all x8, waiting for transfers between devices: 0.02 us -> 21.5 us  [shards(): mine = lax.all_to_all(spread, 'gy', 0, 0, axis_index_groups=same_core)]
    all_to_all x8, starting transfers between devices: 43.8 us -> 32.2 us  [shards(): mine = lax.all_to_all(spread, 'gy', 0, 0, axis_index_groups=same_core)]
    ppermute x24, starting transfers between devices: 35.7 us -> 41.5 us  [swap(): return lax.ppermute(value, axis, pairs + [(b, a) for a, b in pairs])]
    pallas_call x8 -> x16, Pallas kernels: 6.32 us -> 7.75 us  [the longest x8 4.04 us: shards(): call(make_stage_kernel(turn), [VMEM] * (5 + len(states)), [state, shape((...]
    unnamed x30 -> x34, local copies, waits for them, and re-layouts: 8.41 us -> 9.47 us
  transfers between devices with their start and end apart: 32 -> 32, of which waited for: 16 -> 15; matrix products, arithmetic and copies ran while one was open for 0% -> 0% of each run, Pallas kernels for 9% -> 10%
where the time goes in v3:
time: 144 us; the launch traced here: 143 us
  starting transfers between devices  73.7 us (51%)
  Pallas kernels  35.6 us (25%)
  waiting for transfers between devices  22.8 us (16%)
  local copies, waits for them, and re-layouts  9.47 us (7%)
    ppermute x24, starting transfers between devices, swap(): return lax.ppermute(value, axis, pairs + [(b, a) for a, b in pairs])  41.5 us
    all_to_all x8, starting transfers between devices, shards(): mine = lax.all_to_all(spread, 'gy', 0, 0, axis_index_groups=same_core)  32.2 us
    all_to_all x8, waiting for transfers between devices, shards(): mine = lax.all_to_all(spread, 'gy', 0, 0, axis_index_groups=same_core)  21.5 us
    pallas_call x8, Pallas kernels, shards(): call(make_final_kernel(turn, last), [VMEM] * (6 + len(late)), outs, out_s...  20 us
    unnamed x34, local copies, waits for them, and re-layouts  9.47 us
    pallas_call x8, Pallas kernels, shards(): call(local_kernel, [VMEM] * 3, state, VMEM, room=ROOM)  6.86 us
    pallas_call x8, Pallas kernels, shards(): call(make_stage_kernel(turn), [VMEM] * (5 + len(states)), [state, shape((...  4.04 us
    pallas_call x8, Pallas kernels, shards(): call(make_far_kernel(turn), [VMEM] * 3, state, VMEM, flops=FAR_FLOPS, roo...  3.71 us
  transfers between devices with their start and end apart: 32, of which 15 were waited for; matrix products, arithmetic and copies ran while one was open for 0% of the time, Pallas kernels for 10%

profile of v3, /device:TPU:17, one launch (start us, length us, event | category | flops | bytes accessed | tf_op | source)
XLA Modules:
  0.0 142.9 jit_solution(5580255940238639274)
XLA Ops:
  3.0 0.9 shard_map.73
  4.0 5.8 %all-to-all-start = ((bf16[8,32,512]{2,1,0:T(8,128)(2,1)}), bf16[8,32,512]{2,1,0:T(8,128)(2,1)S(1)}, u32[]{:S(2)}, u32[]{:S(2)}) async-start(bf16[8,32,512]{2,1,0:T(8,128)(2,1)} %get-tuple-element.70), calls=%async_computation | async-start | bytes 524288 | tf_op jit(solution)/shard_map/all_to_all | solution.py:272
  9.7 1.2 collective-permute-start.2
  10.9 1.9 %collective-permute-start.1 = (bf16[128,128]{1,0:T(8,128)(2,1)S(1)}, bf16[128,128]{1,0:T(8,128)(2,1)S(1)}, u32[]{:S(2)}, u32[]{:S(2)}) collective-permute-start(bf16[128,128]{1,0:T(8,128)(2,1)S(1)} %get-tuple-element.71.own_ref), channel_id=1, source_target_pairs={{16,32},{17,33},{18,34},{19,35},{20,36},{21,37},{22,38},{23,39},{2... | collective-permute-start | bytes 98312 | tf_op jit(solution)/shard_map/ppermute | solution.py:243
  12.8 1.4 copy-done
  14.2 0.9 copy-done.2
  15.2 0.9 shard_map.74.local_ref
  16.1 1.9 %collective-permute-start = (bf16[8,32,512]{2,1,0:T(8,128)(2,1)S(1)}, bf16[8,32,512]{2,1,0:T(8,128)(2,1)S(1)}, u32[]{:S(2)}, u32[]{:S(2)}) collective-permute-start(bf16[8,32,512]{2,1,0:T(8,128)(2,1)S(1)} %all-to-all-done.mine_ref), channel_id=1, source_target_pairs={{0,1},{2,3},{4,5},{6,7},{8,9},{10,11},{12,13},{14,15},{1,0},{3,2},... | collective-permute-start | bytes 786440 | tf_op jit(solution)/shard_map/ppermute | solution.py:243
  19.7 2.5 %shard_map.77 = (bf16[8,32,512]{2,1,0:T(8,128)(2,1)}, bf16[128,128]{1,0:T(8,128)(2,1)S(1)}, f32[256,64]{1,0:T(8,128)S(1)}, f32[256,64]{1,0:T(8,128)S(1)}) custom-call(bf16[1,1,64,8192]{3,2,1,0:T(8,128)(2,1)S(1)} %copy-done.9, bf16[6,1,2,64,1024]{4,3,2,1,0:T(8,128)(2,1)S(1)} %copy-done.1, s32[8,128]{1,0:T(8,128)S(1)} %get-tuple-element.69.index_ref, ...), custom_call_target="tpu_custom_call" | custom-call | flops 4294967296 | bytes 2097152 | tf_op jit(solution)/shard_map/pallas_call | solution.py:294
  22.2 5.8 %all-to-all-start.1 = ((bf16[8,32,512]{2,1,0:T(8,128)(2,1)}), bf16[8,32,512]{2,1,0:T(8,128)(2,1)S(1)}, u32[]{:S(2)}, u32[]{:S(2)}) async-start(bf16[8,32,512]{2,1,0:T(8,128)(2,1)} %get-tuple-element.77), calls=%async_computation.1 | async-start | bytes 524288 | tf_op jit(solution)/shard_map/all_to_all | solution.py:272
  28.0 2.1 %collective-permute-start.4 = (bf16[128,128]{1,0:T(8,128)(2,1)S(1)}, bf16[128,128]{1,0:T(8,128)(2,1)S(1)}, u32[]{:S(2)}, u32[]{:S(2)}) collective-permute-start(bf16[128,128]{1,0:T(8,128)(2,1)S(1)} %get-tuple-element.78.own_ref), channel_id=1, source_target_pairs={{16,32},{17,33},{18,34},{19,35},{20,36},{21,37},{22,38},{23,39},{2... | collective-permute-start | bytes 98312 | tf_op jit(solution)/shard_map/ppermute | solution.py:243
  30.1 0.9 shard_map.78.local_ref
  30.9 3.2 %all-to-all-done.1.mine_ref = bf16[8,32,512]{2,1,0:T(8,128)(2,1)S(1)} async-done(((bf16[8,32,512]{2,1,0:T(8,128)(2,1)}), bf16[8,32,512]{2,1,0:T(8,128)(2,1)S(1)}, u32[]{:S(2)}, u32[]{:S(2)}) %all-to-all-start.1) | async-done | bytes 262176 | tf_op jit(solution)/shard_map/all_to_all | solution.py:272
  34.1 2.3 %collective-permute-start.3 = (bf16[8,32,512]{2,1,0:T(8,128)(2,1)S(1)}, bf16[8,32,512]{2,1,0:T(8,128)(2,1)S(1)}, u32[]{:S(2)}, u32[]{:S(2)}) collective-permute-start(bf16[8,32,512]{2,1,0:T(8,128)(2,1)S(1)} %all-to-all-done.1.mine_ref), channel_id=1, source_target_pairs={{0,1},{2,3},{4,5},{6,7},{8,9},{10,11},{12,13},{14,15},{1,0},{3,2},... | collective-permute-start | bytes 786440 | tf_op jit(solution)/shard_map/ppermute | solution.py:243
  38.2 2.5 %shard_map.81 = (bf16[8,32,512]{2,1,0:T(8,128)(2,1)}, bf16[128,128]{1,0:T(8,128)(2,1)S(1)}, f32[256,64]{1,0:T(8,128)S(1)}, f32[256,64]{1,0:T(8,128)S(1)}) custom-call(bf16[1,1,64,8192]{3,2,1,0:T(8,128)(2,1)S(1)} %copy-done.10, bf16[6,1,2,64,1024]{4,3,2,1,0:T(8,128)(2,1)S(1)} %copy-done.1, s32[8,128]{1,0:T(8,128)S(1)} %get-tuple-element.69.index_ref, ...), custom_call_target="tpu_custom_call" | custom-call | flops 4294967296 | bytes 2097152 | tf_op jit(solution)/shard_map/pallas_call | solution.py:294
  40.7 3.4 %all-to-all-start.2 = ((bf16[8,32,512]{2,1,0:T(8,128)(2,1)}), bf16[8,32,512]{2,1,0:T(8,128)(2,1)S(1)}, u32[]{:S(2)}, u32[]{:S(2)}) async-start(bf16[8,32,512]{2,1,0:T(8,128)(2,1)} %get-tuple-element.85), calls=%async_computation.2 | async-start | bytes 524288 | tf_op jit(solution)/shard_map/all_to_all | solution.py:272
  44.2 2.0 %collective-permute-start.7 = (bf16[128,128]{1,0:T(8,128)(2,1)S(1)}, bf16[128,128]{1,0:T(8,128)(2,1)S(1)}, u32[]{:S(2)}, u32[]{:S(2)}) collective-permute-start(bf16[128,128]{1,0:T(8,128)(2,1)S(1)} %get-tuple-element.86.own_ref), channel_id=1, source_target_pairs={{16,32},{17,33},{18,34},{19,35},{20,36},{21,37},{22,38},{23,39},{2... | collective-permute-start | bytes 98312 | tf_op jit(solution)/shard_map/ppermute | solution.py:243
  47.0 3.1 %all-to-all-done.2.mine_ref = bf16[8,32,512]{2,1,0:T(8,128)(2,1)S(1)} async-done(((bf16[8,32,512]{2,1,0:T(8,128)(2,1)}), bf16[8,32,512]{2,1,0:T(8,128)(2,1)S(1)}, u32[]{:S(2)}, u32[]{:S(2)}) %all-to-all-start.2) | async-done | bytes 262176 | tf_op jit(solution)/shard_map/all_to_all | solution.py:272
  50.1 3.3 %collective-permute-start.6 = (bf16[8,32,512]{2,1,0:T(8,128)(2,1)S(1)}, bf16[8,32,512]{2,1,0:T(8,128)(2,1)S(1)}, u32[]{:S(2)}, u32[]{:S(2)}) collective-permute-start(bf16[8,32,512]{2,1,0:T(8,128)(2,1)S(1)} %all-to-all-done.2.mine_ref), channel_id=1, source_target_pairs={{0,1},{2,3},{4,5},{6,7},{8,9},{10,11},{12,13},{14,15},{1,0},{3,2},... | collective-permute-start | bytes 786440 | tf_op jit(solution)/shard_map/ppermute | solution.py:243
  55.2 2.5 %shard_map.85 = (bf16[8,32,512]{2,1,0:T(8,128)(2,1)}, bf16[128,128]{1,0:T(8,128)(2,1)S(1)}, f32[256,64]{1,0:T(8,128)S(1)}, f32[256,64]{1,0:T(8,128)S(1)}) custom-call(bf16[1,1,64,8192]{3,2,1,0:T(8,128)(2,1)S(1)} %copy-done.11, bf16[6,1,2,64,1024]{4,3,2,1,0:T(8,128)(2,1)S(1)} %copy-done.1, s32[8,128]{1,0:T(8,128)S(1)} %get-tuple-element.69.index_ref, ...), custom_call_target="tpu_custom_call" | custom-call | flops 4294967296 | bytes 2097152 | tf_op jit(solution)/shard_map/pallas_call | solution.py:294
  57.7 3.4 %all-to-all-start.3 = ((bf16[8,32,512]{2,1,0:T(8,128)(2,1)}), bf16[8,32,512]{2,1,0:T(8,128)(2,1)S(1)}, u32[]{:S(2)}, u32[]{:S(2)}) async-start(bf16[8,32,512]{2,1,0:T(8,128)(2,1)} %get-tuple-element.93), calls=%async_computation.3 | async-start | bytes 524288 | tf_op jit(solution)/shard_map/all_to_all | solution.py:272
  61.2 2.1 %collective-permute-start.10 = (bf16[128,128]{1,0:T(8,128)(2,1)S(1)}, bf16[128,128]{1,0:T(8,128)(2,1)S(1)}, u32[]{:S(2)}, u32[]{:S(2)}) collective-permute-start(bf16[128,128]{1,0:T(8,128)(2,1)S(1)} %get-tuple-element.94.own_ref), channel_id=1, source_target_pairs={{16,32},{17,33},{18,34},{19,35},{20,36},{21,37},{22,38},{23,39},{2... | collective-permute-start | bytes 98312 | tf_op jit(solution)/shard_map/ppermute | solution.py:243
  64.2 2.9 %all-to-all-done.3.mine_ref = bf16[8,32,512]{2,1,0:T(8,128)(2,1)S(1)} async-done(((bf16[8,32,512]{2,1,0:T(8,128)(2,1)}), bf16[8,32,512]{2,1,0:T(8,128)(2,1)S(1)}, u32[]{:S(2)}, u32[]{:S(2)}) %all-to-all-start.3) | async-done | bytes 262176 | tf_op jit(solution)/shard_map/all_to_all | solution.py:272
  67.1 3.3 %collective-permute-start.9 = (bf16[8,32,512]{2,1,0:T(8,128)(2,1)S(1)}, bf16[8,32,512]{2,1,0:T(8,128)(2,1)S(1)}, u32[]{:S(2)}, u32[]{:S(2)}) collective-permute-start(bf16[8,32,512]{2,1,0:T(8,128)(2,1)S(1)} %all-to-all-done.3.mine_ref), channel_id=1, source_target_pairs={{0,1},{2,3},{4,5},{6,7},{8,9},{10,11},{12,13},{14,15},{1,0},{3,2},... | collective-permute-start | bytes 786440 | tf_op jit(solution)/shard_map/ppermute | solution.py:243
  72.2 2.5 %shard_map.89 = (bf16[8,32,512]{2,1,0:T(8,128)(2,1)}, bf16[128,128]{1,0:T(8,128)(2,1)S(1)}, f32[256,64]{1,0:T(8,128)S(1)}) custom-call(bf16[1,1,64,8192]{3,2,1,0:T(8,128)(2,1)S(1)} %copy-done.12, bf16[6,1,2,64,1024]{4,3,2,1,0:T(8,128)(2,1)S(1)} %copy-done.1, s32[8,128]{1,0:T(8,128)S(1)} %get-tuple-element.69.index_ref, ...), custom_call_target="tpu_custom_call" | custom-call | flops 4294967296 | bytes 2097152 | tf_op jit(solution)/shard_map/pallas_call | solution.py:294
  74.7 3.6 %all-to-all-start.4 = ((bf16[8,32,512]{2,1,0:T(8,128)(2,1)}), bf16[8,32,512]{2,1,0:T(8,128)(2,1)S(1)}, u32[]{:S(2)}, u32[]{:S(2)}) async-start(bf16[8,32,512]{2,1,0:T(8,128)(2,1)} %get-tuple-element.102), calls=%async_computation.4 | async-start | bytes 524288 | tf_op jit(solution)/shard_map/all_to_all | solution.py:272
  78.3 2.0 %collective-permute-start.13 = (bf16[128,128]{1,0:T(8,128)(2,1)S(1)}, bf16[128,128]{1,0:T(8,128)(2,1)S(1)}, u32[]{:S(2)}, u32[]{:S(2)}) collective-permute-start(bf16[128,128]{1,0:T(8,128)(2,1)S(1)} %get-tuple-element.103.own_ref), channel_id=1, source_target_pairs={{16,32},{17,33},{18,34},{19,35},{20,36},{21,37},{22,38},{23,39},{2... | collective-permute-start | bytes 98312 | tf_op jit(solution)/shard_map/ppermute | solution.py:243
  80.3 0.9 shard_map.90.local_ref
  81.2 3.1 %all-to-all-done.4.mine_ref = bf16[8,32,512]{2,1,0:T(8,128)(2,1)S(1)} async-done(((bf16[8,32,512]{2,1,0:T(8,128)(2,1)}), bf16[8,32,512]{2,1,0:T(8,128)(2,1)S(1)}, u32[]{:S(2)}, u32[]{:S(2)}) %all-to-all-start.4) | async-done | bytes 262176 | tf_op jit(solution)/shard_map/all_to_all | solution.py:272
  84.3 3.3 %collective-permute-start.12 = (bf16[8,32,512]{2,1,0:T(8,128)(2,1)S(1)}, bf16[8,32,512]{2,1,0:T(8,128)(2,1)S(1)}, u32[]{:S(2)}, u32[]{:S(2)}) collective-permute-start(bf16[8,32,512]{2,1,0:T(8,128)(2,1)S(1)} %all-to-all-done.4.mine_ref), channel_id=1, source_target_pairs={{0,1},{2,3},{4,5},{6,7},{8,9},{10,11},{12,13},{14,15},{1,0},{3,2},... | collective-permute-start | bytes 786440 | tf_op jit(solution)/shard_map/ppermute | solution.py:243
  89.3 2.5 %shard_map.93 = (bf16[8,32,512]{2,1,0:T(8,128)(2,1)}, bf16[128,128]{1,0:T(8,128)(2,1)S(1)}, f32[256,64]{1,0:T(8,128)S(1)}, f32[256,64]{1,0:T(8,128)S(1)}) custom-call(bf16[1,1,64,8192]{3,2,1,0:T(8,128)(2,1)S(1)} %copy-done.13, bf16[6,1,2,64,1024]{4,3,2,1,0:T(8,128)(2,1)S(1)} %copy-done.1, s32[8,128]{1,0:T(8,128)S(1)} %get-tuple-element.69.index_ref, ...), custom_call_target="tpu_custom_call" | custom-call | flops 4294967296 | bytes 2097152 | tf_op jit(solution)/shard_map/pallas_call | solution.py:294
  91.8 3.4 %all-to-all-start.5 = ((bf16[8,32,512]{2,1,0:T(8,128)(2,1)}), bf16[8,32,512]{2,1,0:T(8,128)(2,1)S(1)}, u32[]{:S(2)}, u32[]{:S(2)}) async-start(bf16[8,32,512]{2,1,0:T(8,128)(2,1)} %get-tuple-element.108), calls=%async_computation.5 | async-start | bytes 524288 | tf_op jit(solution)/shard_map/all_to_all | solution.py:272
  95.3 2.0 %collective-permute-start.16 = (bf16[128,128]{1,0:T(8,128)(2,1)S(1)}, bf16[128,128]{1,0:T(8,128)(2,1)S(1)}, u32[]{:S(2)}, u32[]{:S(2)}) collective-permute-start(bf16[128,128]{1,0:T(8,128)(2,1)S(1)} %get-tuple-element.109.own_ref), channel_id=1, source_target_pairs={{16,32},{17,33},{18,34},{19,35},{20,36},{21,37},{22,38},{23,39},{2... | collective-permute-start | bytes 98312 | tf_op jit(solution)/shard_map/ppermute | solution.py:243
  97.3 0.9 shard_map.94.local_ref
  98.2 3.1 %all-to-all-done.5.mine_ref = bf16[8,32,512]{2,1,0:T(8,128)(2,1)S(1)} async-done(((bf16[8,32,512]{2,1,0:T(8,128)(2,1)}), bf16[8,32,512]{2,1,0:T(8,128)(2,1)S(1)}, u32[]{:S(2)}, u32[]{:S(2)}) %all-to-all-start.5) | async-done | bytes 262176 | tf_op jit(solution)/shard_map/all_to_all | solution.py:272
  101.3 3.3 %collective-permute-start.15 = (bf16[8,32,512]{2,1,0:T(8,128)(2,1)S(1)}, bf16[8,32,512]{2,1,0:T(8,128)(2,1)S(1)}, u32[]{:S(2)}, u32[]{:S(2)}) collective-permute-start(bf16[8,32,512]{2,1,0:T(8,128)(2,1)S(1)} %all-to-all-done.5.mine_ref), channel_id=1, source_target_pairs={{0,1},{2,3},{4,5},{6,7},{8,9},{10,11},{12,13},{14,15},{1,0},{3,2},... | collective-permute-start | bytes 786440 | tf_op jit(solution)/shard_map/ppermute | solution.py:243
  106.3 2.5 %shard_map.97 = (bf16[8,32,512]{2,1,0:T(8,128)(2,1)}, bf16[128,128]{1,0:T(8,128)(2,1)S(1)}, f32[256,64]{1,0:T(8,128)S(1)}, f32[256,64]{1,0:T(8,128)S(1)}) custom-call(bf16[1,1,64,8192]{3,2,1,0:T(8,128)(2,1)S(1)} %copy-done.14, bf16[6,1,2,64,1024]{4,3,2,1,0:T(8,128)(2,1)S(1)} %copy-done.1, s32[8,128]{1,0:T(8,128)S(1)} %get-tuple-element.69.index_ref, ...), custom_call_target="tpu_custom_call" | custom-call | flops 4294967296 | bytes 2097152 | tf_op jit(solution)/shard_map/pallas_call | solution.py:294
  108.8 3.4 %all-to-all-start.6 = ((bf16[8,32,512]{2,1,0:T(8,128)(2,1)}), bf16[8,32,512]{2,1,0:T(8,128)(2,1)S(1)}, u32[]{:S(2)}, u32[]{:S(2)}) async-start(bf16[8,32,512]{2,1,0:T(8,128)(2,1)} %get-tuple-element.116), calls=%async_computation.6 | async-start | bytes 524288 | tf_op jit(solution)/shard_map/all_to_all | solution.py:272
  112.3 2.0 %collective-permute-start.19 = (bf16[128,128]{1,0:T(8,128)(2,1)S(1)}, bf16[128,128]{1,0:T(8,128)(2,1)S(1)}, u32[]{:S(2)}, u32[]{:S(2)}) collective-permute-start(bf16[128,128]{1,0:T(8,128)(2,1)S(1)} %get-tuple-element.117.own_ref), channel_id=1, source_target_pairs={{16,32},{17,33},{18,34},{19,35},{20,36},{21,37},{22,38},{23,39},{2... | collective-permute-start | bytes 98312 | tf_op jit(solution)/shard_map/ppermute | solution.py:243
  114.3 0.9 shard_map.98.local_ref
  115.2 3.1 %all-to-all-done.6.mine_ref = bf16[8,32,512]{2,1,0:T(8,128)(2,1)S(1)} async-done(((bf16[8,32,512]{2,1,0:T(8,128)(2,1)}), bf16[8,32,512]{2,1,0:T(8,128)(2,1)S(1)}, u32[]{:S(2)}, u32[]{:S(2)}) %all-to-all-start.6) | async-done | bytes 262176 | tf_op jit(solution)/shard_map/all_to_all | solution.py:272
  118.3 3.3 %collective-permute-start.18 = (bf16[8,32,512]{2,1,0:T(8,128)(2,1)S(1)}, bf16[8,32,512]{2,1,0:T(8,128)(2,1)S(1)}, u32[]{:S(2)}, u32[]{:S(2)}) collective-permute-start(bf16[8,32,512]{2,1,0:T(8,128)(2,1)S(1)} %all-to-all-done.6.mine_ref), channel_id=1, source_target_pairs={{0,1},{2,3},{4,5},{6,7},{8,9},{10,11},{12,13},{14,15},{1,0},{3,2},... | collective-permute-start | bytes 786440 | tf_op jit(solution)/shard_map/ppermute | solution.py:243
  123.3 2.5 %shard_map.101 = (bf16[8,32,512]{2,1,0:T(8,128)(2,1)}, bf16[128,128]{1,0:T(8,128)(2,1)S(1)}, f32[256,64]{1,0:T(8,128)S(1)}, f32[256,64]{1,0:T(8,128)S(1)}) custom-call(bf16[1,1,64,8192]{3,2,1,0:T(8,128)(2,1)S(1)} %copy-done.15, bf16[6,1,2,64,1024]{4,3,2,1,0:T(8,128)(2,1)S(1)} %copy-done.1, s32[8,128]{1,0:T(8,128)S(1)} %get-tuple-element.69.index_ref, ...), custom_call_target="tpu_custom_call" | custom-call | flops 4294967296 | bytes 2097152 | tf_op jit(solution)/shard_map/pallas_call | solution.py:294
  125.8 3.4 %all-to-all-start.7 = ((bf16[8,32,512]{2,1,0:T(8,128)(2,1)}), bf16[8,32,512]{2,1,0:T(8,128)(2,1)S(1)}, u32[]{:S(2)}, u32[]{:S(2)}) async-start(bf16[8,32,512]{2,1,0:T(8,128)(2,1)} %get-tuple-element.124), calls=%async_computation.7 | async-start | bytes 524288 | tf_op jit(solution)/shard_map/all_to_all | solution.py:272
  129.4 2.0 %collective-permute-start.22 = (bf16[128,128]{1,0:T(8,128)(2,1)S(1)}, bf16[128,128]{1,0:T(8,128)(2,1)S(1)}, u32[]{:S(2)}, u32[]{:S(2)}) collective-permute-start(bf16[128,128]{1,0:T(8,128)(2,1)S(1)} %get-tuple-element.125.own_ref), channel_id=1, source_target_pairs={{16,32},{17,33},{18,34},{19,35},{20,36},{21,37},{22,38},{23,39},{2... | collective-permute-start | bytes 98312 | tf_op jit(solution)/shard_map/ppermute | solution.py:243
  132.2 3.1 %all-to-all-done.7.mine_ref = bf16[8,32,512]{2,1,0:T(8,128)(2,1)S(1)} async-done(((bf16[8,32,512]{2,1,0:T(8,128)(2,1)}), bf16[8,32,512]{2,1,0:T(8,128)(2,1)S(1)}, u32[]{:S(2)}, u32[]{:S(2)}) %all-to-all-start.7) | async-done | bytes 262176 | tf_op jit(solution)/shard_map/all_to_all | solution.py:272
  135.3 3.3 %collective-permute-start.21 = (bf16[8,32,512]{2,1,0:T(8,128)(2,1)S(1)}, bf16[8,32,512]{2,1,0:T(8,128)(2,1)S(1)}, u32[]{:S(2)}, u32[]{:S(2)}) collective-permute-start(bf16[8,32,512]{2,1,0:T(8,128)(2,1)S(1)} %all-to-all-done.7.mine_ref), channel_id=1, source_target_pairs={{0,1},{2,3},{4,5},{6,7},{8,9},{10,11},{12,13},{14,15},{1,0},{3,2},... | collective-permute-start | bytes 786440 | tf_op jit(solution)/shard_map/ppermute | solution.py:243
  140.3 2.4 %shard_map.105 = f32[1,2,64,128]{3,2,1,0:T(8,128)} custom-call(bf16[1,1,64,8192]{3,2,1,0:T(8,128)(2,1)S(1)} %copy-done.16, bf16[6,1,2,64,1024]{4,3,2,1,0:T(8,128)(2,1)S(1)} %copy-done.1, s32[8,128]{1,0:T(8,128)S(1)} %get-tuple-element.69.index_ref, bf16[8,32,512]{2,1,0:T(8,128)(2,1)S(1)} %collective-permute-done.21.other_ref, ...), custom_call_target="tpu_custom_call" | custom-call | flops 4294967296 | bytes 2097152 | tf_op jit(solution)/shard_map/pallas_call | solution.py:294
  (83 shorter events, 19.2 us)
Async XLA Ops:
  0.7 0.8 copy-start.6
  1.5 0.8 copy-start.7
  3.9 14.5 %copy-start.4 = (f32[256,64]{1,0:T(8,128)}, f32[256,64]{1,0:T(8,128)S(1)}, u32[]{:S(2)}) copy-start(f32[256,64]{1,0:T(8,128)S(1)} %get-tuple-element.74.refs_0_) | copy-start | bytes 196612
  4.0 12.1 %all-to-all-start = ((bf16[8,32,512]{2,1,0:T(8,128)(2,1)}), bf16[8,32,512]{2,1,0:T(8,128)(2,1)S(1)}, u32[]{:S(2)}, u32[]{:S(2)}) async-start(bf16[8,32,512]{2,1,0:T(8,128)(2,1)} %get-tuple-element.70), calls=%async_computation | async-start | bytes 524288 | tf_op jit(solution)/shard_map/all_to_all | solution.py:272
  9.7 8.2 %collective-permute-start.2 = (bf16[128,128]{1,0:T(8,128)(2,1)S(1)}, bf16[128,128]{1,0:T(8,128)(2,1)S(1)}, u32[]{:S(2)}, u32[]{:S(2)}) collective-permute-start(bf16[128,128]{1,0:T(8,128)(2,1)S(1)} %get-tuple-element.71.own_ref), channel_id=1, source_target_pairs={{0,16},{32,48},{64,80},{96,112},{16,0},{48,32},{80,64},{112,96},{1... | collective-permute-start | bytes 98312 | tf_op jit(solution)/shard_map/ppermute | solution.py:243
  10.9 7.5 %collective-permute-start.1 = (bf16[128,128]{1,0:T(8,128)(2,1)S(1)}, bf16[128,128]{1,0:T(8,128)(2,1)S(1)}, u32[]{:S(2)}, u32[]{:S(2)}) collective-permute-start(bf16[128,128]{1,0:T(8,128)(2,1)S(1)} %get-tuple-element.71.own_ref), channel_id=1, source_target_pairs={{16,32},{17,33},{18,34},{19,35},{20,36},{21,37},{22,38},{23,39},{2... | collective-permute-start | bytes 98312 | tf_op jit(solution)/shard_map/ppermute | solution.py:243
  12.8 1.4 copy-start
  14.2 0.9 copy-start.2
  15.2 2.7 %copy-start.1 = (bf16[6,1,2,64,1024]{4,3,2,1,0:T(8,128)(2,1)S(1)}, bf16[6,1,2,64,1024]{4,3,2,1,0:T(8,128)(2,1)}, u32[]{:S(2)}) copy-start(bf16[6,1,2,64,1024]{4,3,2,1,0:T(8,128)(2,1)} %face_ref.63) | copy-start | bytes 4718596
  16.1 3.0 %collective-permute-start = (bf16[8,32,512]{2,1,0:T(8,128)(2,1)S(1)}, bf16[8,32,512]{2,1,0:T(8,128)(2,1)S(1)}, u32[]{:S(2)}, u32[]{:S(2)}) collective-permute-start(bf16[8,32,512]{2,1,0:T(8,128)(2,1)S(1)} %all-to-all-done.mine_ref), channel_id=1, source_target_pairs={{0,1},{2,3},{4,5},{6,7},{8,9},{10,11},{12,13},{14,15},{1,0},{3,2},... | collective-permute-start | bytes 786440 | tf_op jit(solution)/shard_map/ppermute | solution.py:243
  18.4 1.2 copy-start.9
  19.7 10.4 %copy-start.3 = (bf16[1,2,64,1024]{3,2,1,0:T(8,128)(2,1)S(1)}, bf16[1,2,64,1024]{3,2,1,0:T(8,128)(2,1)}, u32[]{:S(2)}) copy-start(bf16[1,2,64,1024]{3,2,1,0:T(8,128)(2,1)} %elem_ref.15) | copy-start | bytes 786436
  22.2 11.9 %all-to-all-start.1 = ((bf16[8,32,512]{2,1,0:T(8,128)(2,1)}), bf16[8,32,512]{2,1,0:T(8,128)(2,1)S(1)}, u32[]{:S(2)}, u32[]{:S(2)}) async-start(bf16[8,32,512]{2,1,0:T(8,128)(2,1)} %get-tuple-element.77), calls=%async_computation.1 | async-start | bytes 524288 | tf_op jit(solution)/shard_map/all_to_all | solution.py:272
  28.0 8.4 %collective-permute-start.5 = (bf16[128,128]{1,0:T(8,128)(2,1)S(1)}, bf16[128,128]{1,0:T(8,128)(2,1)S(1)}, u32[]{:S(2)}, u32[]{:S(2)}) collective-permute-start(bf16[128,128]{1,0:T(8,128)(2,1)S(1)} %get-tuple-element.78.own_ref), channel_id=1, source_target_pairs={{0,16},{32,48},{64,80},{96,112},{16,0},{48,32},{80,64},{112,96},{1... | collective-permute-start | bytes 98312 | tf_op jit(solution)/shard_map/ppermute | solution.py:243
  28.0 8.9 %collective-permute-start.4 = (bf16[128,128]{1,0:T(8,128)(2,1)S(1)}, bf16[128,128]{1,0:T(8,128)(2,1)S(1)}, u32[]{:S(2)}, u32[]{:S(2)}) collective-permute-start(bf16[128,128]{1,0:T(8,128)(2,1)S(1)} %get-tuple-element.78.own_ref), channel_id=1, source_target_pairs={{16,32},{17,33},{18,34},{19,35},{20,36},{21,37},{22,38},{23,39},{2... | collective-permute-start | bytes 98312 | tf_op jit(solution)/shard_map/ppermute | solution.py:243
  34.1 3.5 %collective-permute-start.3 = (bf16[8,32,512]{2,1,0:T(8,128)(2,1)S(1)}, bf16[8,32,512]{2,1,0:T(8,128)(2,1)S(1)}, u32[]{:S(2)}, u32[]{:S(2)}) collective-permute-start(bf16[8,32,512]{2,1,0:T(8,128)(2,1)S(1)} %all-to-all-done.1.mine_ref), channel_id=1, source_target_pairs={{0,1},{2,3},{4,5},{6,7},{8,9},{10,11},{12,13},{14,15},{1,0},{3,2},... | collective-permute-start | bytes 786440 | tf_op jit(solution)/shard_map/ppermute | solution.py:243
  36.9 1.2 copy-start.10
  40.7 9.4 %all-to-all-start.2 = ((bf16[8,32,512]{2,1,0:T(8,128)(2,1)}), bf16[8,32,512]{2,1,0:T(8,128)(2,1)S(1)}, u32[]{:S(2)}, u32[]{:S(2)}) async-start(bf16[8,32,512]{2,1,0:T(8,128)(2,1)} %get-tuple-element.85), calls=%async_computation.2 | async-start | bytes 524288 | tf_op jit(solution)/shard_map/all_to_all | solution.py:272
  44.1 9.3 %collective-permute-start.8 = (bf16[128,128]{1,0:T(8,128)(2,1)S(1)}, bf16[128,128]{1,0:T(8,128)(2,1)S(1)}, u32[]{:S(2)}, u32[]{:S(2)}) collective-permute-start(bf16[128,128]{1,0:T(8,128)(2,1)S(1)} %get-tuple-element.86.own_ref), channel_id=1, source_target_pairs={{0,16},{32,48},{64,80},{96,112},{16,0},{48,32},{80,64},{112,96},{1... | collective-permute-start | bytes 98312 | tf_op jit(solution)/shard_map/ppermute | solution.py:243
  44.2 9.7 %collective-permute-start.7 = (bf16[128,128]{1,0:T(8,128)(2,1)S(1)}, bf16[128,128]{1,0:T(8,128)(2,1)S(1)}, u32[]{:S(2)}, u32[]{:S(2)}) collective-permute-start(bf16[128,128]{1,0:T(8,128)(2,1)S(1)} %get-tuple-element.86.own_ref), channel_id=1, source_target_pairs={{16,32},{17,33},{18,34},{19,35},{20,36},{21,37},{22,38},{23,39},{2... | collective-permute-start | bytes 98312 | tf_op jit(solution)/shard_map/ppermute | solution.py:243
  50.1 4.5 %collective-permute-start.6 = (bf16[8,32,512]{2,1,0:T(8,128)(2,1)S(1)}, bf16[8,32,512]{2,1,0:T(8,128)(2,1)S(1)}, u32[]{:S(2)}, u32[]{:S(2)}) collective-permute-start(bf16[8,32,512]{2,1,0:T(8,128)(2,1)S(1)} %all-to-all-done.2.mine_ref), channel_id=1, source_target_pairs={{0,1},{2,3},{4,5},{6,7},{8,9},{10,11},{12,13},{14,15},{1,0},{3,2},... | collective-permute-start | bytes 786440 | tf_op jit(solution)/shard_map/ppermute | solution.py:243
  53.9 1.2 copy-start.11
  57.7 9.4 %all-to-all-start.3 = ((bf16[8,32,512]{2,1,0:T(8,128)(2,1)}), bf16[8,32,512]{2,1,0:T(8,128)(2,1)S(1)}, u32[]{:S(2)}, u32[]{:S(2)}) async-start(bf16[8,32,512]{2,1,0:T(8,128)(2,1)} %get-tuple-element.93), calls=%async_computation.3 | async-start | bytes 524288 | tf_op jit(solution)/shard_map/all_to_all | solution.py:272
  61.1 9.3 %collective-permute-start.11 = (bf16[128,128]{1,0:T(8,128)(2,1)S(1)}, bf16[128,128]{1,0:T(8,128)(2,1)S(1)}, u32[]{:S(2)}, u32[]{:S(2)}) collective-permute-start(bf16[128,128]{1,0:T(8,128)(2,1)S(1)} %get-tuple-element.94.own_ref), channel_id=1, source_target_pairs={{0,16},{32,48},{64,80},{96,112},{16,0},{48,32},{80,64},{112,96},{1... | collective-permute-start | bytes 98312 | tf_op jit(solution)/shard_map/ppermute | solution.py:243
  61.2 9.7 %collective-permute-start.10 = (bf16[128,128]{1,0:T(8,128)(2,1)S(1)}, bf16[128,128]{1,0:T(8,128)(2,1)S(1)}, u32[]{:S(2)}, u32[]{:S(2)}) collective-permute-start(bf16[128,128]{1,0:T(8,128)(2,1)S(1)} %get-tuple-element.94.own_ref), channel_id=1, source_target_pairs={{16,32},{17,33},{18,34},{19,35},{20,36},{21,37},{22,38},{23,39},{2... | collective-permute-start | bytes 98312 | tf_op jit(solution)/shard_map/ppermute | solution.py:243
  67.1 4.4 %collective-permute-start.9 = (bf16[8,32,512]{2,1,0:T(8,128)(2,1)S(1)}, bf16[8,32,512]{2,1,0:T(8,128)(2,1)S(1)}, u32[]{:S(2)}, u32[]{:S(2)}) collective-permute-start(bf16[8,32,512]{2,1,0:T(8,128)(2,1)S(1)} %all-to-all-done.3.mine_ref), channel_id=1, source_target_pairs={{0,1},{2,3},{4,5},{6,7},{8,9},{10,11},{12,13},{14,15},{1,0},{3,2},... | collective-permute-start | bytes 786440 | tf_op jit(solution)/shard_map/ppermute | solution.py:243
  70.9 1.2 copy-start.12
  74.7 12.9 %copy-start.5 = (f32[256,64]{1,0:T(8,128)S(1)}, f32[256,64]{1,0:T(8,128)}, u32[]{:S(2)}) copy-start(f32[256,64]{1,0:T(8,128)} %copy-done.4) | copy-start | bytes 196612
  74.7 9.6 %all-to-all-start.4 = ((bf16[8,32,512]{2,1,0:T(8,128)(2,1)}), bf16[8,32,512]{2,1,0:T(8,128)(2,1)S(1)}, u32[]{:S(2)}, u32[]{:S(2)}) async-start(bf16[8,32,512]{2,1,0:T(8,128)(2,1)} %get-tuple-element.102), calls=%async_computation.4 | async-start | bytes 524288 | tf_op jit(solution)/shard_map/all_to_all | solution.py:272
  78.3 9.3 %collective-permute-start.14 = (bf16[128,128]{1,0:T(8,128)(2,1)S(1)}, bf16[128,128]{1,0:T(8,128)(2,1)S(1)}, u32[]{:S(2)}, u32[]{:S(2)}) collective-permute-start(bf16[128,128]{1,0:T(8,128)(2,1)S(1)} %get-tuple-element.103.own_ref), channel_id=1, source_target_pairs={{0,16},{32,48},{64,80},{96,112},{16,0},{48,32},{80,64},{112,96},{1... | collective-permute-start | bytes 98312 | tf_op jit(solution)/shard_map/ppermute | solution.py:243
  78.3 9.7 %collective-permute-start.13 = (bf16[128,128]{1,0:T(8,128)(2,1)S(1)}, bf16[128,128]{1,0:T(8,128)(2,1)S(1)}, u32[]{:S(2)}, u32[]{:S(2)}) collective-permute-start(bf16[128,128]{1,0:T(8,128)(2,1)S(1)} %get-tuple-element.103.own_ref), channel_id=1, source_target_pairs={{16,32},{17,33},{18,34},{19,35},{20,36},{21,37},{22,38},{23,39},{2... | collective-permute-start | bytes 98312 | tf_op jit(solution)/shard_map/ppermute | solution.py:243
  84.3 4.5 %collective-permute-start.12 = (bf16[8,32,512]{2,1,0:T(8,128)(2,1)S(1)}, bf16[8,32,512]{2,1,0:T(8,128)(2,1)S(1)}, u32[]{:S(2)}, u32[]{:S(2)}) collective-permute-start(bf16[8,32,512]{2,1,0:T(8,128)(2,1)S(1)} %all-to-all-done.4.mine_ref), channel_id=1, source_target_pairs={{0,1},{2,3},{4,5},{6,7},{8,9},{10,11},{12,13},{14,15},{1,0},{3,2},... | collective-permute-start | bytes 786440 | tf_op jit(solution)/shard_map/ppermute | solution.py:243
  88.1 1.2 copy-start.13
  91.8 9.4 %all-to-all-start.5 = ((bf16[8,32,512]{2,1,0:T(8,128)(2,1)}), bf16[8,32,512]{2,1,0:T(8,128)(2,1)S(1)}, u32[]{:S(2)}, u32[]{:S(2)}) async-start(bf16[8,32,512]{2,1,0:T(8,128)(2,1)} %get-tuple-element.108), calls=%async_computation.5 | async-start | bytes 524288 | tf_op jit(solution)/shard_map/all_to_all | solution.py:272
  95.3 9.3 %collective-permute-start.17 = (bf16[128,128]{1,0:T(8,128)(2,1)S(1)}, bf16[128,128]{1,0:T(8,128)(2,1)S(1)}, u32[]{:S(2)}, u32[]{:S(2)}) collective-permute-start(bf16[128,128]{1,0:T(8,128)(2,1)S(1)} %get-tuple-element.109.own_ref), channel_id=1, source_target_pairs={{0,16},{32,48},{64,80},{96,112},{16,0},{48,32},{80,64},{112,96},{1... | collective-permute-start | bytes 98312 | tf_op jit(solution)/shard_map/ppermute | solution.py:243
  95.3 9.7 %collective-permute-start.16 = (bf16[128,128]{1,0:T(8,128)(2,1)S(1)}, bf16[128,128]{1,0:T(8,128)(2,1)S(1)}, u32[]{:S(2)}, u32[]{:S(2)}) collective-permute-start(bf16[128,128]{1,0:T(8,128)(2,1)S(1)} %get-tuple-element.109.own_ref), channel_id=1, source_target_pairs={{16,32},{17,33},{18,34},{19,35},{20,36},{21,37},{22,38},{23,39},{2... | collective-permute-start | bytes 98312 | tf_op jit(solution)/shard_map/ppermute | solution.py:243
  101.3 4.5 %collective-permute-start.15 = (bf16[8,32,512]{2,1,0:T(8,128)(2,1)S(1)}, bf16[8,32,512]{2,1,0:T(8,128)(2,1)S(1)}, u32[]{:S(2)}, u32[]{:S(2)}) collective-permute-start(bf16[8,32,512]{2,1,0:T(8,128)(2,1)S(1)} %all-to-all-done.5.mine_ref), channel_id=1, source_target_pairs={{0,1},{2,3},{4,5},{6,7},{8,9},{10,11},{12,13},{14,15},{1,0},{3,2},... | collective-permute-start | bytes 786440 | tf_op jit(solution)/shard_map/ppermute | solution.py:243
  105.1 1.2 copy-start.14
  108.8 9.4 %all-to-all-start.6 = ((bf16[8,32,512]{2,1,0:T(8,128)(2,1)}), bf16[8,32,512]{2,1,0:T(8,128)(2,1)S(1)}, u32[]{:S(2)}, u32[]{:S(2)}) async-start(bf16[8,32,512]{2,1,0:T(8,128)(2,1)} %get-tuple-element.116), calls=%async_computation.6 | async-start | bytes 524288 | tf_op jit(solution)/shard_map/all_to_all | solution.py:272
  112.3 9.3 %collective-permute-start.20 = (bf16[128,128]{1,0:T(8,128)(2,1)S(1)}, bf16[128,128]{1,0:T(8,128)(2,1)S(1)}, u32[]{:S(2)}, u32[]{:S(2)}) collective-permute-start(bf16[128,128]{1,0:T(8,128)(2,1)S(1)} %get-tuple-element.117.own_ref), channel_id=1, source_target_pairs={{0,16},{32,48},{64,80},{96,112},{16,0},{48,32},{80,64},{112,96},{1... | collective-permute-start | bytes 98312 | tf_op jit(solution)/shard_map/ppermute | solution.py:243
  112.3 9.7 %collective-permute-start.19 = (bf16[128,128]{1,0:T(8,128)(2,1)S(1)}, bf16[128,128]{1,0:T(8,128)(2,1)S(1)}, u32[]{:S(2)}, u32[]{:S(2)}) collective-permute-start(bf16[128,128]{1,0:T(8,128)(2,1)S(1)} %get-tuple-element.117.own_ref), channel_id=1, source_target_pairs={{16,32},{17,33},{18,34},{19,35},{20,36},{21,37},{22,38},{23,39},{2... | collective-permute-start | bytes 98312 | tf_op jit(solution)/shard_map/ppermute | solution.py:243
  118.3 4.5 %collective-permute-start.18 = (bf16[8,32,512]{2,1,0:T(8,128)(2,1)S(1)}, bf16[8,32,512]{2,1,0:T(8,128)(2,1)S(1)}, u32[]{:S(2)}, u32[]{:S(2)}) collective-permute-start(bf16[8,32,512]{2,1,0:T(8,128)(2,1)S(1)} %all-to-all-done.6.mine_ref), channel_id=1, source_target_pairs={{0,1},{2,3},{4,5},{6,7},{8,9},{10,11},{12,13},{14,15},{1,0},{3,2},... | collective-permute-start | bytes 786440 | tf_op jit(solution)/shard_map/ppermute | solution.py:243
  122.1 1.2 copy-start.15
  125.8 9.4 %all-to-all-start.7 = ((bf16[8,32,512]{2,1,0:T(8,128)(2,1)}), bf16[8,32,512]{2,1,0:T(8,128)(2,1)S(1)}, u32[]{:S(2)}, u32[]{:S(2)}) async-start(bf16[8,32,512]{2,1,0:T(8,128)(2,1)} %get-tuple-element.124), calls=%async_computation.7 | async-start | bytes 524288 | tf_op jit(solution)/shard_map/all_to_all | solution.py:272
  129.3 9.3 %collective-permute-start.23 = (bf16[128,128]{1,0:T(8,128)(2,1)S(1)}, bf16[128,128]{1,0:T(8,128)(2,1)S(1)}, u32[]{:S(2)}, u32[]{:S(2)}) collective-permute-start(bf16[128,128]{1,0:T(8,128)(2,1)S(1)} %get-tuple-element.125.own_ref), channel_id=1, source_target_pairs={{0,16},{32,48},{64,80},{96,112},{16,0},{48,32},{80,64},{112,96},{1... | collective-permute-start | bytes 98312 | tf_op jit(solution)/shard_map/ppermute | solution.py:243
  129.4 9.7 %collective-permute-start.22 = (bf16[128,128]{1,0:T(8,128)(2,1)S(1)}, bf16[128,128]{1,0:T(8,128)(2,1)S(1)}, u32[]{:S(2)}, u32[]{:S(2)}) collective-permute-start(bf16[128,128]{1,0:T(8,128)(2,1)S(1)} %get-tuple-element.125.own_ref), channel_id=1, source_target_pairs={{16,32},{17,33},{18,34},{19,35},{20,36},{21,37},{22,38},{23,39},{2... | collective-permute-start | bytes 98312 | tf_op jit(solution)/shard_map/ppermute | solution.py:243
  135.3 4.4 %collective-permute-start.21 = (bf16[8,32,512]{2,1,0:T(8,128)(2,1)S(1)}, bf16[8,32,512]{2,1,0:T(8,128)(2,1)S(1)}, u32[]{:S(2)}, u32[]{:S(2)}) collective-permute-start(bf16[8,32,512]{2,1,0:T(8,128)(2,1)S(1)} %all-to-all-done.7.mine_ref), channel_id=1, source_target_pairs={{0,1},{2,3},{4,5},{6,7},{8,9},{10,11},{12,13},{14,15},{1,0},{3,2},... | collective-permute-start | bytes 786440 | tf_op jit(solution)/shard_map/ppermute | solution.py:243
  139.1 1.2 copy-start.16
  (1 other events, 0.7 us)

commit v4 on v3

--- a/solution.py
+++ b/solution.py
@@ -15,7 +15,7 @@
 PAIRS = 128
 CHIPS = 8
 ROOM = 14
-FAR_FLOPS = 100 << 30
+FAR_FLOPS = 8 << 30
 
 spectrum_low = 0.6
 spectrum_high = 3.0
@@ -52,24 +52,25 @@
 
 def send_field(field, spread_hbm, packed_out, scratch):
     rows_ref, spread_ref, sem = scratch
-    rows_ref[...] = field
+    rows_ref[:ROWS] = field[:, :NODES]
+    rows_ref[ROWS:] = field[:, NODES:]
     pieces = [rows_ref[pl.ds(r, ELEMS, stride=RHS), :] for r in range(RHS)]
     spread = jnp.concatenate(pieces, axis=1).astype(BF)
     for chip in range(CHIPS):
         spread_ref[chip] = spread
     copy = pltpu.make_async_copy(spread_ref, spread_hbm, sem)
     copy.start()
-    packed_out[...] = jnp.concatenate([field[:ROWS], field[ROWS:]], axis=1).astype(BF)
+    packed_out[...] = field.astype(BF)
     return copy
 
 
 def first_kernel(
     count_ref, initial_ref, right_ref, faults_ref, spread_out, packed_out, solution_out, right_out, index_out, *scratch
 ):
-    field = jnp.concatenate([initial_ref[0, 0].T, initial_ref[0, 1].T], axis=0)
+    field = initial_ref[0].reshape(2 * NODES, ROWS).T
     copy = send_field(field, spread_out, packed_out, scratch)
     solution_out[...] = field
-    right_out[...] = jnp.concatenate([right_ref[0, 0].T, right_ref[0, 1].T], axis=0)
+    right_out[...] = right_ref[0].reshape(2 * NODES, ROWS).T
     device = faults_ref[1, 0]
     column = (
         jnp.where(device % 2 == lax.axis_index("gy") % 2, 0, CHIPS * ELEMS)
@@ -116,14 +117,14 @@
         lower = dot_t(masked(wide[ly], up), face_ref[4, 0, ly])
         upper = dot_t(masked(wide[ly], down), face_ref[5, 0, ly])
         sums[ly] += jnp.concatenate([zero, lower[:-RHS]], axis=0) + jnp.concatenate([upper[RHS:], zero], axis=0)
-    out_ref[...] = jnp.concatenate(sums, axis=0)
+    out_ref[...] = jnp.concatenate(sums, axis=1)
 
 
 def side_sum(packed_ref, face_ref, from_high):
     expand, same = expander(), layer_mask(0)
     side = jnp.where(from_high, 1, 0)
     wide = [dot(packed_ref[:, ly * NODES : (ly + 1) * NODES], expand).astype(BF) for ly in range(2)]
-    return jnp.concatenate([dot_t(masked(wide[ly], same), face_ref[side, 0, ly]) for ly in range(2)], axis=0)
+    return jnp.concatenate([dot_t(masked(wide[ly], same), face_ref[side, 0, ly]) for ly in range(2)], axis=1)
 
 
 def make_far_kernel(turn):
@@ -196,6 +197,7 @@
             total = total + dot_t(
                 jnp.concatenate(parts, axis=1), fault_ref[0, 0, :, start * PAIRS : (start + group) * PAIRS]
             )
+        total = jnp.concatenate([total[:ROWS], total[ROWS:]], axis=1)
         if turn == 0:
             residual = base_ref[...] - total
             step = residual / centre_point
@@ -207,8 +209,7 @@
         if turn == DEGREE - 1:
             states = (held[1][...] + correction,)
         if last:
-            outs[0][0, 0] = states[0][:ROWS].T
-            outs[0][0, 1] = states[0][ROWS:].T
+            outs[0][0] = states[0].T.reshape(2, NODES, ROWS)
             return
         copy = send_field(states[-1], outs[0], outs[1], scratch)
         for out, value in zip(outs[2:], states):
@@ -248,7 +249,7 @@
     odd_pairs += [(2 * CHIPS * a + j, 2 * CHIPS * a + j + 1) for a in (0, 7) for j in range(0, 2 * CHIPS, 2)]
     same_core = [list(range(core, 2 * CHIPS, 2)) for core in range(2)]
     field_rows = ELEMS * RHS
-    state = shape((field_rows, NODES), F32)
+    state = shape((ROWS, 2 * NODES), F32)
     spread_shape = shape((CHIPS, ELEMS, RHS * NODES), BF)
     packed_shape = shape((ROWS, 2 * NODES), BF)
     send_scratch = [

time: 144 us -> 142 us (0.986)
  local copies, waits for them, and re-layouts: 9.47 us -> 6.59 us
  Pallas kernels: 35.6 us -> 38.2 us
  waiting for transfers between devices: 22.8 us -> 21.3 us
    unnamed x34 -> x40, local copies, waits for them, and re-layouts: 9.47 us -> 6.59 us
  transfers between devices with their start and end apart: 32 -> 32, of which waited for: 15 -> 7; matrix products, arithmetic and copies ran while one was open for 0% -> 0% of each run, Pallas kernels for 10% -> 11%
where the time goes in v4:
time: 142 us; the launch traced here: 141 us
  starting transfers between devices  73.4 us (52%)
  Pallas kernels  38.2 us (27%)
  waiting for transfers between devices  21.3 us (15%)
  local copies, waits for them, and re-layouts  6.59 us (5%)
  between operations  1.47 us (1%)
    ppermute x24, starting transfers between devices, swap(): return lax.ppermute(value, axis, pairs + [(b, a) for a, b in pairs])  41.3 us
    all_to_all x8, starting transfers between devices, shards(): mine = lax.all_to_all(spread, 'gy', 0, 0, axis_index_groups=same_core)  32.1 us
    all_to_all x8, waiting for transfers between devices, shards(): mine = lax.all_to_all(spread, 'gy', 0, 0, axis_index_groups=same_core)  21.2 us
    pallas_call x8, Pallas kernels, shards(): call(make_final_kernel(turn, last), [VMEM] * (6 + len(late)), outs, out_s...  21 us
    pallas_call x8, Pallas kernels, shards(): call(local_kernel, [VMEM] * 3, state, VMEM, room=ROOM)  7.11 us
    unnamed x40, local copies, waits for them, and re-layouts  6.59 us
    pallas_call x8, Pallas kernels, shards(): call(make_stage_kernel(turn), [VMEM] * (5 + len(states)), [state, shape((...  4.8 us
    pallas_call x8, Pallas kernels, shards(): call(make_far_kernel(turn), [VMEM] * 3, state, VMEM, flops=FAR_FLOPS, roo...  4.28 us
  transfers between devices with their start and end apart: 32, of which 7 were waited for; matrix products, arithmetic and copies ran while one was open for 0% of the time, Pallas kernels for 11%

profile of v4, /device:TPU:17, one launch (start us, length us, event | category | flops | bytes accessed | tf_op | source)
XLA Modules:
  0.0 141.0 jit_solution(2013701660703115105)
XLA Ops:
  3.0 1.0 shard_map.73
  4.0 5.8 %all-to-all-start = ((bf16[8,32,512]{2,1,0:T(8,128)(2,1)}), bf16[8,32,512]{2,1,0:T(8,128)(2,1)S(1)}, u32[]{:S(2)}, u32[]{:S(2)}) async-start(bf16[8,32,512]{2,1,0:T(8,128)(2,1)} %get-tuple-element.70), calls=%async_computation | async-start | bytes 524288 | tf_op jit(solution)/shard_map/all_to_all | solution.py:273
  9.8 1.3 collective-permute-start.2
  11.1 1.9 %collective-permute-start.1 = (bf16[128,128]{1,0:T(8,128)(2,1)S(1)}, bf16[128,128]{1,0:T(8,128)(2,1)S(1)}, u32[]{:S(2)}, u32[]{:S(2)}) collective-permute-start(bf16[128,128]{1,0:T(8,128)(2,1)S(1)} %get-tuple-element.71.own_ref), channel_id=1, source_target_pairs={{16,32},{17,33},{18,34},{19,35},{20,36},{21,37},{22,38},{23,39},{2... | collective-permute-start | bytes 98312 | tf_op jit(solution)/shard_map/ppermute | solution.py:244
  13.0 1.4 copy-done
  14.4 0.9 copy-done.2
  15.3 0.9 shard_map.74.local_ref
  16.2 1.7 %collective-permute-start = (bf16[8,32,512]{2,1,0:T(8,128)(2,1)S(1)}, bf16[8,32,512]{2,1,0:T(8,128)(2,1)S(1)}, u32[]{:S(2)}, u32[]{:S(2)}) collective-permute-start(bf16[8,32,512]{2,1,0:T(8,128)(2,1)S(1)} %all-to-all-done.mine_ref), channel_id=1, source_target_pairs={{0,1},{2,3},{4,5},{6,7},{8,9},{10,11},{12,13},{14,15},{1,0},{3,2},... | collective-permute-start | bytes 786440 | tf_op jit(solution)/shard_map/ppermute | solution.py:244
  19.8 2.6 %shard_map.77 = (bf16[8,32,512]{2,1,0:T(8,128)(2,1)}, bf16[128,128]{1,0:T(8,128)(2,1)S(1)}, f32[128,128]{1,0:T(8,128)S(1)}, f32[128,128]{1,0:T(8,128)S(1)}) custom-call(bf16[1,1,64,8192]{3,2,1,0:T(8,128)(2,1)S(1)} %copy-done.7, bf16[6,1,2,64,1024]{4,3,2,1,0:T(8,128)(2,1)S(1)} %copy-done.1, s32[8,128]{1,0:T(8,128)S(1)} %get-tuple-element.69.index_ref, ...), custom_call_target="tpu_custom_call" | custom-call | flops 4294967296 | bytes 2097152 | tf_op jit(solution)/shard_map/pallas_call | solution.py:295
  22.5 5.8 %all-to-all-start.1 = ((bf16[8,32,512]{2,1,0:T(8,128)(2,1)}), bf16[8,32,512]{2,1,0:T(8,128)(2,1)S(1)}, u32[]{:S(2)}, u32[]{:S(2)}) async-start(bf16[8,32,512]{2,1,0:T(8,128)(2,1)} %get-tuple-element.77), calls=%async_computation.1 | async-start | bytes 524288 | tf_op jit(solution)/shard_map/all_to_all | solution.py:273
  28.3 2.1 %collective-permute-start.4 = (bf16[128,128]{1,0:T(8,128)(2,1)S(1)}, bf16[128,128]{1,0:T(8,128)(2,1)S(1)}, u32[]{:S(2)}, u32[]{:S(2)}) collective-permute-start(bf16[128,128]{1,0:T(8,128)(2,1)S(1)} %get-tuple-element.78.own_ref), channel_id=1, source_target_pairs={{16,32},{17,33},{18,34},{19,35},{20,36},{21,37},{22,38},{23,39},{2... | collective-permute-start | bytes 98312 | tf_op jit(solution)/shard_map/ppermute | solution.py:244
  30.4 0.9 shard_map.78.local_ref
  31.3 3.1 %all-to-all-done.1.mine_ref = bf16[8,32,512]{2,1,0:T(8,128)(2,1)S(1)} async-done(((bf16[8,32,512]{2,1,0:T(8,128)(2,1)}), bf16[8,32,512]{2,1,0:T(8,128)(2,1)S(1)}, u32[]{:S(2)}, u32[]{:S(2)}) %all-to-all-start.1) | async-done | bytes 262176 | tf_op jit(solution)/shard_map/all_to_all | solution.py:273
  34.4 2.2 %collective-permute-start.3 = (bf16[8,32,512]{2,1,0:T(8,128)(2,1)S(1)}, bf16[8,32,512]{2,1,0:T(8,128)(2,1)S(1)}, u32[]{:S(2)}, u32[]{:S(2)}) collective-permute-start(bf16[8,32,512]{2,1,0:T(8,128)(2,1)S(1)} %all-to-all-done.1.mine_ref), channel_id=1, source_target_pairs={{0,1},{2,3},{4,5},{6,7},{8,9},{10,11},{12,13},{14,15},{1,0},{3,2},... | collective-permute-start | bytes 786440 | tf_op jit(solution)/shard_map/ppermute | solution.py:244
  37.7 2.7 %shard_map.81 = (bf16[8,32,512]{2,1,0:T(8,128)(2,1)}, bf16[128,128]{1,0:T(8,128)(2,1)S(1)}, f32[128,128]{1,0:T(8,128)S(1)}, f32[128,128]{1,0:T(8,128)S(1)}) custom-call(bf16[1,1,64,8192]{3,2,1,0:T(8,128)(2,1)S(1)} %copy-done.7, bf16[6,1,2,64,1024]{4,3,2,1,0:T(8,128)(2,1)S(1)} %copy-done.1, s32[8,128]{1,0:T(8,128)S(1)} %get-tuple-element.69.index_ref, ...), custom_call_target="tpu_custom_call" | custom-call | flops 4294967296 | bytes 2097152 | tf_op jit(solution)/shard_map/pallas_call | solution.py:295
  40.4 3.4 %all-to-all-start.2 = ((bf16[8,32,512]{2,1,0:T(8,128)(2,1)}), bf16[8,32,512]{2,1,0:T(8,128)(2,1)S(1)}, u32[]{:S(2)}, u32[]{:S(2)}) async-start(bf16[8,32,512]{2,1,0:T(8,128)(2,1)} %get-tuple-element.85), calls=%async_computation.2 | async-start | bytes 524288 | tf_op jit(solution)/shard_map/all_to_all | solution.py:273
  44.0 2.0 %collective-permute-start.7 = (bf16[128,128]{1,0:T(8,128)(2,1)S(1)}, bf16[128,128]{1,0:T(8,128)(2,1)S(1)}, u32[]{:S(2)}, u32[]{:S(2)}) collective-permute-start(bf16[128,128]{1,0:T(8,128)(2,1)S(1)} %get-tuple-element.86.own_ref), channel_id=1, source_target_pairs={{16,32},{17,33},{18,34},{19,35},{20,36},{21,37},{22,38},{23,39},{2... | collective-permute-start | bytes 98312 | tf_op jit(solution)/shard_map/ppermute | solution.py:244
  45.9 0.9 shard_map.82.local_ref
  46.8 3.0 %all-to-all-done.2.mine_ref = bf16[8,32,512]{2,1,0:T(8,128)(2,1)S(1)} async-done(((bf16[8,32,512]{2,1,0:T(8,128)(2,1)}), bf16[8,32,512]{2,1,0:T(8,128)(2,1)S(1)}, u32[]{:S(2)}, u32[]{:S(2)}) %all-to-all-start.2) | async-done | bytes 262176 | tf_op jit(solution)/shard_map/all_to_all | solution.py:273
  49.9 3.2 %collective-permute-start.6 = (bf16[8,32,512]{2,1,0:T(8,128)(2,1)S(1)}, bf16[8,32,512]{2,1,0:T(8,128)(2,1)S(1)}, u32[]{:S(2)}, u32[]{:S(2)}) collective-permute-start(bf16[8,32,512]{2,1,0:T(8,128)(2,1)S(1)} %all-to-all-done.2.mine_ref), channel_id=1, source_target_pairs={{0,1},{2,3},{4,5},{6,7},{8,9},{10,11},{12,13},{14,15},{1,0},{3,2},... | collective-permute-start | bytes 786440 | tf_op jit(solution)/shard_map/ppermute | solution.py:244
  54.5 2.6 %shard_map.85 = (bf16[8,32,512]{2,1,0:T(8,128)(2,1)}, bf16[128,128]{1,0:T(8,128)(2,1)S(1)}, f32[128,128]{1,0:T(8,128)S(1)}, f32[128,128]{1,0:T(8,128)S(1)}) custom-call(bf16[1,1,64,8192]{3,2,1,0:T(8,128)(2,1)S(1)} %copy-done.7, bf16[6,1,2,64,1024]{4,3,2,1,0:T(8,128)(2,1)S(1)} %copy-done.1, s32[8,128]{1,0:T(8,128)S(1)} %get-tuple-element.69.index_ref, ...), custom_call_target="tpu_custom_call" | custom-call | flops 4294967296 | bytes 2097152 | tf_op jit(solution)/shard_map/pallas_call | solution.py:295
  57.2 3.4 %all-to-all-start.3 = ((bf16[8,32,512]{2,1,0:T(8,128)(2,1)}), bf16[8,32,512]{2,1,0:T(8,128)(2,1)S(1)}, u32[]{:S(2)}, u32[]{:S(2)}) async-start(bf16[8,32,512]{2,1,0:T(8,128)(2,1)} %get-tuple-element.93), calls=%async_computation.3 | async-start | bytes 524288 | tf_op jit(solution)/shard_map/all_to_all | solution.py:273
  60.7 2.1 %collective-permute-start.10 = (bf16[128,128]{1,0:T(8,128)(2,1)S(1)}, bf16[128,128]{1,0:T(8,128)(2,1)S(1)}, u32[]{:S(2)}, u32[]{:S(2)}) collective-permute-start(bf16[128,128]{1,0:T(8,128)(2,1)S(1)} %get-tuple-element.94.own_ref), channel_id=1, source_target_pairs={{16,32},{17,33},{18,34},{19,35},{20,36},{21,37},{22,38},{23,39},{2... | collective-permute-start | bytes 98312 | tf_op jit(solution)/shard_map/ppermute | solution.py:244
  63.7 2.9 %all-to-all-done.3.mine_ref = bf16[8,32,512]{2,1,0:T(8,128)(2,1)S(1)} async-done(((bf16[8,32,512]{2,1,0:T(8,128)(2,1)}), bf16[8,32,512]{2,1,0:T(8,128)(2,1)S(1)}, u32[]{:S(2)}, u32[]{:S(2)}) %all-to-all-start.3) | async-done | bytes 262176 | tf_op jit(solution)/shard_map/all_to_all | solution.py:273
  66.6 3.3 %collective-permute-start.9 = (bf16[8,32,512]{2,1,0:T(8,128)(2,1)S(1)}, bf16[8,32,512]{2,1,0:T(8,128)(2,1)S(1)}, u32[]{:S(2)}, u32[]{:S(2)}) collective-permute-start(bf16[8,32,512]{2,1,0:T(8,128)(2,1)S(1)} %all-to-all-done.3.mine_ref), channel_id=1, source_target_pairs={{0,1},{2,3},{4,5},{6,7},{8,9},{10,11},{12,13},{14,15},{1,0},{3,2},... | collective-permute-start | bytes 786440 | tf_op jit(solution)/shard_map/ppermute | solution.py:244
  71.4 2.6 %shard_map.89 = (bf16[8,32,512]{2,1,0:T(8,128)(2,1)}, bf16[128,128]{1,0:T(8,128)(2,1)S(1)}, f32[128,128]{1,0:T(8,128)S(1)}) custom-call(bf16[1,1,64,8192]{3,2,1,0:T(8,128)(2,1)S(1)} %copy-done.7, bf16[6,1,2,64,1024]{4,3,2,1,0:T(8,128)(2,1)S(1)} %copy-done.1, s32[8,128]{1,0:T(8,128)S(1)} %get-tuple-element.69.index_ref, ...), custom_call_target="tpu_custom_call" | custom-call | flops 4294967296 | bytes 2097152 | tf_op jit(solution)/shard_map/pallas_call | solution.py:295
  74.1 3.4 %all-to-all-start.4 = ((bf16[8,32,512]{2,1,0:T(8,128)(2,1)}), bf16[8,32,512]{2,1,0:T(8,128)(2,1)S(1)}, u32[]{:S(2)}, u32[]{:S(2)}) async-start(bf16[8,32,512]{2,1,0:T(8,128)(2,1)} %get-tuple-element.102), calls=%async_computation.4 | async-start | bytes 524288 | tf_op jit(solution)/shard_map/all_to_all | solution.py:273
  77.6 2.0 %collective-permute-start.13 = (bf16[128,128]{1,0:T(8,128)(2,1)S(1)}, bf16[128,128]{1,0:T(8,128)(2,1)S(1)}, u32[]{:S(2)}, u32[]{:S(2)}) collective-permute-start(bf16[128,128]{1,0:T(8,128)(2,1)S(1)} %get-tuple-element.103.own_ref), channel_id=1, source_target_pairs={{16,32},{17,33},{18,34},{19,35},{20,36},{21,37},{22,38},{23,39},{2... | collective-permute-start | bytes 98312 | tf_op jit(solution)/shard_map/ppermute | solution.py:244
  79.5 0.9 shard_map.90.local_ref
  80.4 3.0 %all-to-all-done.4.mine_ref = bf16[8,32,512]{2,1,0:T(8,128)(2,1)S(1)} async-done(((bf16[8,32,512]{2,1,0:T(8,128)(2,1)}), bf16[8,32,512]{2,1,0:T(8,128)(2,1)S(1)}, u32[]{:S(2)}, u32[]{:S(2)}) %all-to-all-start.4) | async-done | bytes 262176 | tf_op jit(solution)/shard_map/all_to_all | solution.py:273
  83.5 3.5 %collective-permute-start.12 = (bf16[8,32,512]{2,1,0:T(8,128)(2,1)S(1)}, bf16[8,32,512]{2,1,0:T(8,128)(2,1)S(1)}, u32[]{:S(2)}, u32[]{:S(2)}) collective-permute-start(bf16[8,32,512]{2,1,0:T(8,128)(2,1)S(1)} %all-to-all-done.4.mine_ref), channel_id=1, source_target_pairs={{0,1},{2,3},{4,5},{6,7},{8,9},{10,11},{12,13},{14,15},{1,0},{3,2},... | collective-permute-start | bytes 786440 | tf_op jit(solution)/shard_map/ppermute | solution.py:244
  88.1 2.6 %shard_map.93 = (bf16[8,32,512]{2,1,0:T(8,128)(2,1)}, bf16[128,128]{1,0:T(8,128)(2,1)S(1)}, f32[128,128]{1,0:T(8,128)S(1)}, f32[128,128]{1,0:T(8,128)S(1)}) custom-call(bf16[1,1,64,8192]{3,2,1,0:T(8,128)(2,1)S(1)} %copy-done.7, bf16[6,1,2,64,1024]{4,3,2,1,0:T(8,128)(2,1)S(1)} %copy-done.1, s32[8,128]{1,0:T(8,128)S(1)} %get-tuple-element.69.index_ref, ...), custom_call_target="tpu_custom_call" | custom-call | flops 4294967296 | bytes 2097152 | tf_op jit(solution)/shard_map/pallas_call | solution.py:295
  90.8 3.4 %all-to-all-start.5 = ((bf16[8,32,512]{2,1,0:T(8,128)(2,1)}), bf16[8,32,512]{2,1,0:T(8,128)(2,1)S(1)}, u32[]{:S(2)}, u32[]{:S(2)}) async-start(bf16[8,32,512]{2,1,0:T(8,128)(2,1)} %get-tuple-element.108), calls=%async_computation.5 | async-start | bytes 524288 | tf_op jit(solution)/shard_map/all_to_all | solution.py:273
  94.3 2.0 %collective-permute-start.16 = (bf16[128,128]{1,0:T(8,128)(2,1)S(1)}, bf16[128,128]{1,0:T(8,128)(2,1)S(1)}, u32[]{:S(2)}, u32[]{:S(2)}) collective-permute-start(bf16[128,128]{1,0:T(8,128)(2,1)S(1)} %get-tuple-element.109.own_ref), channel_id=1, source_target_pairs={{16,32},{17,33},{18,34},{19,35},{20,36},{21,37},{22,38},{23,39},{2... | collective-permute-start | bytes 98312 | tf_op jit(solution)/shard_map/ppermute | solution.py:244
  96.3 0.9 shard_map.94.local_ref
  97.2 3.1 %all-to-all-done.5.mine_ref = bf16[8,32,512]{2,1,0:T(8,128)(2,1)S(1)} async-done(((bf16[8,32,512]{2,1,0:T(8,128)(2,1)}), bf16[8,32,512]{2,1,0:T(8,128)(2,1)S(1)}, u32[]{:S(2)}, u32[]{:S(2)}) %all-to-all-start.5) | async-done | bytes 262176 | tf_op jit(solution)/shard_map/all_to_all | solution.py:273
  100.2 3.3 %collective-permute-start.15 = (bf16[8,32,512]{2,1,0:T(8,128)(2,1)S(1)}, bf16[8,32,512]{2,1,0:T(8,128)(2,1)S(1)}, u32[]{:S(2)}, u32[]{:S(2)}) collective-permute-start(bf16[8,32,512]{2,1,0:T(8,128)(2,1)S(1)} %all-to-all-done.5.mine_ref), channel_id=1, source_target_pairs={{0,1},{2,3},{4,5},{6,7},{8,9},{10,11},{12,13},{14,15},{1,0},{3,2},... | collective-permute-start | bytes 786440 | tf_op jit(solution)/shard_map/ppermute | solution.py:244
  104.7 2.7 %shard_map.97 = (bf16[8,32,512]{2,1,0:T(8,128)(2,1)}, bf16[128,128]{1,0:T(8,128)(2,1)S(1)}, f32[128,128]{1,0:T(8,128)S(1)}, f32[128,128]{1,0:T(8,128)S(1)}) custom-call(bf16[1,1,64,8192]{3,2,1,0:T(8,128)(2,1)S(1)} %copy-done.7, bf16[6,1,2,64,1024]{4,3,2,1,0:T(8,128)(2,1)S(1)} %copy-done.1, s32[8,128]{1,0:T(8,128)S(1)} %get-tuple-element.69.index_ref, ...), custom_call_target="tpu_custom_call" | custom-call | flops 4294967296 | bytes 2097152 | tf_op jit(solution)/shard_map/pallas_call | solution.py:295
  107.3 3.4 %all-to-all-start.6 = ((bf16[8,32,512]{2,1,0:T(8,128)(2,1)}), bf16[8,32,512]{2,1,0:T(8,128)(2,1)S(1)}, u32[]{:S(2)}, u32[]{:S(2)}) async-start(bf16[8,32,512]{2,1,0:T(8,128)(2,1)} %get-tuple-element.116), calls=%async_computation.6 | async-start | bytes 524288 | tf_op jit(solution)/shard_map/all_to_all | solution.py:273
  110.9 2.0 %collective-permute-start.19 = (bf16[128,128]{1,0:T(8,128)(2,1)S(1)}, bf16[128,128]{1,0:T(8,128)(2,1)S(1)}, u32[]{:S(2)}, u32[]{:S(2)}) collective-permute-start(bf16[128,128]{1,0:T(8,128)(2,1)S(1)} %get-tuple-element.117.own_ref), channel_id=1, source_target_pairs={{16,32},{17,33},{18,34},{19,35},{20,36},{21,37},{22,38},{23,39},{2... | collective-permute-start | bytes 98312 | tf_op jit(solution)/shard_map/ppermute | solution.py:244
  113.7 3.0 %all-to-all-done.6.mine_ref = bf16[8,32,512]{2,1,0:T(8,128)(2,1)S(1)} async-done(((bf16[8,32,512]{2,1,0:T(8,128)(2,1)}), bf16[8,32,512]{2,1,0:T(8,128)(2,1)S(1)}, u32[]{:S(2)}, u32[]{:S(2)}) %all-to-all-start.6) | async-done | bytes 262176 | tf_op jit(solution)/shard_map/all_to_all | solution.py:273
  116.8 3.2 %collective-permute-start.18 = (bf16[8,32,512]{2,1,0:T(8,128)(2,1)S(1)}, bf16[8,32,512]{2,1,0:T(8,128)(2,1)S(1)}, u32[]{:S(2)}, u32[]{:S(2)}) collective-permute-start(bf16[8,32,512]{2,1,0:T(8,128)(2,1)S(1)} %all-to-all-done.6.mine_ref), channel_id=1, source_target_pairs={{0,1},{2,3},{4,5},{6,7},{8,9},{10,11},{12,13},{14,15},{1,0},{3,2},... | collective-permute-start | bytes 786440 | tf_op jit(solution)/shard_map/ppermute | solution.py:244
  121.4 2.6 %shard_map.101 = (bf16[8,32,512]{2,1,0:T(8,128)(2,1)}, bf16[128,128]{1,0:T(8,128)(2,1)S(1)}, f32[128,128]{1,0:T(8,128)S(1)}, f32[128,128]{1,0:T(8,128)S(1)}) custom-call(bf16[1,1,64,8192]{3,2,1,0:T(8,128)(2,1)S(1)} %copy-done.7, bf16[6,1,2,64,1024]{4,3,2,1,0:T(8,128)(2,1)S(1)} %copy-done.1, s32[8,128]{1,0:T(8,128)S(1)} %get-tuple-element.69.index_ref, ...), custom_call_target="tpu_custom_call" | custom-call | flops 4294967296 | bytes 2097152 | tf_op jit(solution)/shard_map/pallas_call | solution.py:295
  124.1 3.4 %all-to-all-start.7 = ((bf16[8,32,512]{2,1,0:T(8,128)(2,1)}), bf16[8,32,512]{2,1,0:T(8,128)(2,1)S(1)}, u32[]{:S(2)}, u32[]{:S(2)}) async-start(bf16[8,32,512]{2,1,0:T(8,128)(2,1)} %get-tuple-element.124), calls=%async_computation.7 | async-start | bytes 524288 | tf_op jit(solution)/shard_map/all_to_all | solution.py:273
  127.6 2.0 %collective-permute-start.22 = (bf16[128,128]{1,0:T(8,128)(2,1)S(1)}, bf16[128,128]{1,0:T(8,128)(2,1)S(1)}, u32[]{:S(2)}, u32[]{:S(2)}) collective-permute-start(bf16[128,128]{1,0:T(8,128)(2,1)S(1)} %get-tuple-element.125.own_ref), channel_id=1, source_target_pairs={{16,32},{17,33},{18,34},{19,35},{20,36},{21,37},{22,38},{23,39},{2... | collective-permute-start | bytes 98312 | tf_op jit(solution)/shard_map/ppermute | solution.py:244
  130.5 3.0 %all-to-all-done.7.mine_ref = bf16[8,32,512]{2,1,0:T(8,128)(2,1)S(1)} async-done(((bf16[8,32,512]{2,1,0:T(8,128)(2,1)}), bf16[8,32,512]{2,1,0:T(8,128)(2,1)S(1)}, u32[]{:S(2)}, u32[]{:S(2)}) %all-to-all-start.7) | async-done | bytes 262176 | tf_op jit(solution)/shard_map/all_to_all | solution.py:273
  133.5 3.3 %collective-permute-start.21 = (bf16[8,32,512]{2,1,0:T(8,128)(2,1)S(1)}, bf16[8,32,512]{2,1,0:T(8,128)(2,1)S(1)}, u32[]{:S(2)}, u32[]{:S(2)}) collective-permute-start(bf16[8,32,512]{2,1,0:T(8,128)(2,1)S(1)} %all-to-all-done.7.mine_ref), channel_id=1, source_target_pairs={{0,1},{2,3},{4,5},{6,7},{8,9},{10,11},{12,13},{14,15},{1,0},{3,2},... | collective-permute-start | bytes 786440 | tf_op jit(solution)/shard_map/ppermute | solution.py:244
  138.3 2.5 %shard_map.105 = f32[1,2,64,128]{3,2,1,0:T(8,128)} custom-call(bf16[1,1,64,8192]{3,2,1,0:T(8,128)(2,1)S(1)} %copy-done.7, bf16[6,1,2,64,1024]{4,3,2,1,0:T(8,128)(2,1)S(1)} %copy-done.1, s32[8,128]{1,0:T(8,128)S(1)} %get-tuple-element.69.index_ref, bf16[8,32,512]{2,1,0:T(8,128)(2,1)S(1)} %collective-permute-done.21.other_ref, ...), custom_call_target="tpu_custom_call" | custom-call | flops 4294967296 | bytes 2097152 | tf_op jit(solution)/shard_map/pallas_call | solution.py:295
  (89 shorter events, 16.6 us)
Async XLA Ops:
  0.7 0.8 copy-start.4
  4.0 5.8 %copy-start.8 = (f32[128,128]{1,0:T(8,128)}, f32[128,128]{1,0:T(8,128)S(1)}, u32[]{:S(2)}) copy-start(f32[128,128]{1,0:T(8,128)S(1)} %get-tuple-element.101.refs_1_) | copy-start | bytes 196612
  4.0 12.2 %all-to-all-start = ((bf16[8,32,512]{2,1,0:T(8,128)(2,1)}), bf16[8,32,512]{2,1,0:T(8,128)(2,1)S(1)}, u32[]{:S(2)}, u32[]{:S(2)}) async-start(bf16[8,32,512]{2,1,0:T(8,128)(2,1)} %get-tuple-element.70), calls=%async_computation | async-start | bytes 524288 | tf_op jit(solution)/shard_map/all_to_all | solution.py:273
  9.8 8.2 %collective-permute-start.2 = (bf16[128,128]{1,0:T(8,128)(2,1)S(1)}, bf16[128,128]{1,0:T(8,128)(2,1)S(1)}, u32[]{:S(2)}, u32[]{:S(2)}) collective-permute-start(bf16[128,128]{1,0:T(8,128)(2,1)S(1)} %get-tuple-element.71.own_ref), channel_id=1, source_target_pairs={{0,16},{32,48},{64,80},{96,112},{16,0},{48,32},{80,64},{112,96},{1... | collective-permute-start | bytes 98312 | tf_op jit(solution)/shard_map/ppermute | solution.py:244
  11.1 7.5 %collective-permute-start.1 = (bf16[128,128]{1,0:T(8,128)(2,1)S(1)}, bf16[128,128]{1,0:T(8,128)(2,1)S(1)}, u32[]{:S(2)}, u32[]{:S(2)}) collective-permute-start(bf16[128,128]{1,0:T(8,128)(2,1)S(1)} %get-tuple-element.71.own_ref), channel_id=1, source_target_pairs={{16,32},{17,33},{18,34},{19,35},{20,36},{21,37},{22,38},{23,39},{2... | collective-permute-start | bytes 98312 | tf_op jit(solution)/shard_map/ppermute | solution.py:244
  12.9 1.4 copy-start
  14.4 0.9 copy-start.2
  15.3 2.6 %copy-start.1 = (bf16[6,1,2,64,1024]{4,3,2,1,0:T(8,128)(2,1)S(1)}, bf16[6,1,2,64,1024]{4,3,2,1,0:T(8,128)(2,1)}, u32[]{:S(2)}) copy-start(bf16[6,1,2,64,1024]{4,3,2,1,0:T(8,128)(2,1)} %face_ref.63) | copy-start | bytes 4718596
  16.2 2.9 %collective-permute-start = (bf16[8,32,512]{2,1,0:T(8,128)(2,1)S(1)}, bf16[8,32,512]{2,1,0:T(8,128)(2,1)S(1)}, u32[]{:S(2)}, u32[]{:S(2)}) collective-permute-start(bf16[8,32,512]{2,1,0:T(8,128)(2,1)S(1)} %all-to-all-done.mine_ref), channel_id=1, source_target_pairs={{0,1},{2,3},{4,5},{6,7},{8,9},{10,11},{12,13},{14,15},{1,0},{3,2},... | collective-permute-start | bytes 786440 | tf_op jit(solution)/shard_map/ppermute | solution.py:244
  18.6 1.2 copy-start.7
  19.8 10.6 %copy-start.3 = (bf16[1,2,64,1024]{3,2,1,0:T(8,128)(2,1)S(1)}, bf16[1,2,64,1024]{3,2,1,0:T(8,128)(2,1)}, u32[]{:S(2)}) copy-start(bf16[1,2,64,1024]{3,2,1,0:T(8,128)(2,1)} %elem_ref.15) | copy-start | bytes 786436
  22.5 11.9 %all-to-all-start.1 = ((bf16[8,32,512]{2,1,0:T(8,128)(2,1)}), bf16[8,32,512]{2,1,0:T(8,128)(2,1)S(1)}, u32[]{:S(2)}, u32[]{:S(2)}) async-start(bf16[8,32,512]{2,1,0:T(8,128)(2,1)} %get-tuple-element.77), calls=%async_computation.1 | async-start | bytes 524288 | tf_op jit(solution)/shard_map/all_to_all | solution.py:273
  28.3 8.3 %collective-permute-start.5 = (bf16[128,128]{1,0:T(8,128)(2,1)S(1)}, bf16[128,128]{1,0:T(8,128)(2,1)S(1)}, u32[]{:S(2)}, u32[]{:S(2)}) collective-permute-start(bf16[128,128]{1,0:T(8,128)(2,1)S(1)} %get-tuple-element.78.own_ref), channel_id=1, source_target_pairs={{0,16},{32,48},{64,80},{96,112},{16,0},{48,32},{80,64},{112,96},{1... | collective-permute-start | bytes 98312 | tf_op jit(solution)/shard_map/ppermute | solution.py:244
  28.3 8.9 %collective-permute-start.4 = (bf16[128,128]{1,0:T(8,128)(2,1)S(1)}, bf16[128,128]{1,0:T(8,128)(2,1)S(1)}, u32[]{:S(2)}, u32[]{:S(2)}) collective-permute-start(bf16[128,128]{1,0:T(8,128)(2,1)S(1)} %get-tuple-element.78.own_ref), channel_id=1, source_target_pairs={{16,32},{17,33},{18,34},{19,35},{20,36},{21,37},{22,38},{23,39},{2... | collective-permute-start | bytes 98312 | tf_op jit(solution)/shard_map/ppermute | solution.py:244
  34.4 3.3 %collective-permute-start.3 = (bf16[8,32,512]{2,1,0:T(8,128)(2,1)S(1)}, bf16[8,32,512]{2,1,0:T(8,128)(2,1)S(1)}, u32[]{:S(2)}, u32[]{:S(2)}) collective-permute-start(bf16[8,32,512]{2,1,0:T(8,128)(2,1)S(1)} %all-to-all-done.1.mine_ref), channel_id=1, source_target_pairs={{0,1},{2,3},{4,5},{6,7},{8,9},{10,11},{12,13},{14,15},{1,0},{3,2},... | collective-permute-start | bytes 786440 | tf_op jit(solution)/shard_map/ppermute | solution.py:244
  40.4 3.5 %copy-start.16 = (f32[128,128]{1,0:T(8,128)}, f32[128,128]{1,0:T(8,128)S(1)}, u32[]{:S(2)}) copy-start(f32[128,128]{1,0:T(8,128)S(1)} %get-tuple-element.92.refs_0_) | copy-start | bytes 196612
  40.4 9.4 %all-to-all-start.2 = ((bf16[8,32,512]{2,1,0:T(8,128)(2,1)}), bf16[8,32,512]{2,1,0:T(8,128)(2,1)S(1)}, u32[]{:S(2)}, u32[]{:S(2)}) async-start(bf16[8,32,512]{2,1,0:T(8,128)(2,1)} %get-tuple-element.85), calls=%async_computation.2 | async-start | bytes 524288 | tf_op jit(solution)/shard_map/all_to_all | solution.py:273
  43.8 9.2 %collective-permute-start.8 = (bf16[128,128]{1,0:T(8,128)(2,1)S(1)}, bf16[128,128]{1,0:T(8,128)(2,1)S(1)}, u32[]{:S(2)}, u32[]{:S(2)}) collective-permute-start(bf16[128,128]{1,0:T(8,128)(2,1)S(1)} %get-tuple-element.86.own_ref), channel_id=1, source_target_pairs={{0,16},{32,48},{64,80},{96,112},{16,0},{48,32},{80,64},{112,96},{1... | collective-permute-start | bytes 98312 | tf_op jit(solution)/shard_map/ppermute | solution.py:244
  44.0 9.7 %collective-permute-start.7 = (bf16[128,128]{1,0:T(8,128)(2,1)S(1)}, bf16[128,128]{1,0:T(8,128)(2,1)S(1)}, u32[]{:S(2)}, u32[]{:S(2)}) collective-permute-start(bf16[128,128]{1,0:T(8,128)(2,1)S(1)} %get-tuple-element.86.own_ref), channel_id=1, source_target_pairs={{16,32},{17,33},{18,34},{19,35},{20,36},{21,37},{22,38},{23,39},{2... | collective-permute-start | bytes 98312 | tf_op jit(solution)/shard_map/ppermute | solution.py:244
  49.9 4.4 %collective-permute-start.6 = (bf16[8,32,512]{2,1,0:T(8,128)(2,1)S(1)}, bf16[8,32,512]{2,1,0:T(8,128)(2,1)S(1)}, u32[]{:S(2)}, u32[]{:S(2)}) collective-permute-start(bf16[8,32,512]{2,1,0:T(8,128)(2,1)S(1)} %all-to-all-done.2.mine_ref), channel_id=1, source_target_pairs={{0,1},{2,3},{4,5},{6,7},{8,9},{10,11},{12,13},{14,15},{1,0},{3,2},... | collective-permute-start | bytes 786440 | tf_op jit(solution)/shard_map/ppermute | solution.py:244
  53.7 0.8 copy-start.17
  57.2 3.5 %copy-start.14 = (f32[128,128]{1,0:T(8,128)}, f32[128,128]{1,0:T(8,128)S(1)}, u32[]{:S(2)}) copy-start(f32[128,128]{1,0:T(8,128)S(1)} %get-tuple-element.100.refs_0_) | copy-start | bytes 196612
  57.2 9.4 %all-to-all-start.3 = ((bf16[8,32,512]{2,1,0:T(8,128)(2,1)}), bf16[8,32,512]{2,1,0:T(8,128)(2,1)S(1)}, u32[]{:S(2)}, u32[]{:S(2)}) async-start(bf16[8,32,512]{2,1,0:T(8,128)(2,1)} %get-tuple-element.93), calls=%async_computation.3 | async-start | bytes 524288 | tf_op jit(solution)/shard_map/all_to_all | solution.py:273
  60.6 9.3 %collective-permute-start.11 = (bf16[128,128]{1,0:T(8,128)(2,1)S(1)}, bf16[128,128]{1,0:T(8,128)(2,1)S(1)}, u32[]{:S(2)}, u32[]{:S(2)}) collective-permute-start(bf16[128,128]{1,0:T(8,128)(2,1)S(1)} %get-tuple-element.94.own_ref), channel_id=1, source_target_pairs={{0,16},{32,48},{64,80},{96,112},{16,0},{48,32},{80,64},{112,96},{1... | collective-permute-start | bytes 98312 | tf_op jit(solution)/shard_map/ppermute | solution.py:244
  60.7 9.8 %collective-permute-start.10 = (bf16[128,128]{1,0:T(8,128)(2,1)S(1)}, bf16[128,128]{1,0:T(8,128)(2,1)S(1)}, u32[]{:S(2)}, u32[]{:S(2)}) collective-permute-start(bf16[128,128]{1,0:T(8,128)(2,1)S(1)} %get-tuple-element.94.own_ref), channel_id=1, source_target_pairs={{16,32},{17,33},{18,34},{19,35},{20,36},{21,37},{22,38},{23,39},{2... | collective-permute-start | bytes 98312 | tf_op jit(solution)/shard_map/ppermute | solution.py:244
  66.6 4.5 %collective-permute-start.9 = (bf16[8,32,512]{2,1,0:T(8,128)(2,1)S(1)}, bf16[8,32,512]{2,1,0:T(8,128)(2,1)S(1)}, u32[]{:S(2)}, u32[]{:S(2)}) collective-permute-start(bf16[8,32,512]{2,1,0:T(8,128)(2,1)S(1)} %all-to-all-done.3.mine_ref), channel_id=1, source_target_pairs={{0,1},{2,3},{4,5},{6,7},{8,9},{10,11},{12,13},{14,15},{1,0},{3,2},... | collective-permute-start | bytes 786440 | tf_op jit(solution)/shard_map/ppermute | solution.py:244
  70.5 0.9 copy-start.15
  74.0 3.4 %copy-start.10 = (f32[128,128]{1,0:T(8,128)}, f32[128,128]{1,0:T(8,128)S(1)}, u32[]{:S(2)}) copy-start(f32[128,128]{1,0:T(8,128)S(1)} %get-tuple-element.132.refs_1_) | copy-start | bytes 196612
  74.1 9.4 %all-to-all-start.4 = ((bf16[8,32,512]{2,1,0:T(8,128)(2,1)}), bf16[8,32,512]{2,1,0:T(8,128)(2,1)S(1)}, u32[]{:S(2)}, u32[]{:S(2)}) async-start(bf16[8,32,512]{2,1,0:T(8,128)(2,1)} %get-tuple-element.102), calls=%async_computation.4 | async-start | bytes 524288 | tf_op jit(solution)/shard_map/all_to_all | solution.py:273
  77.5 9.5 %collective-permute-start.14 = (bf16[128,128]{1,0:T(8,128)(2,1)S(1)}, bf16[128,128]{1,0:T(8,128)(2,1)S(1)}, u32[]{:S(2)}, u32[]{:S(2)}) collective-permute-start(bf16[128,128]{1,0:T(8,128)(2,1)S(1)} %get-tuple-element.103.own_ref), channel_id=1, source_target_pairs={{0,16},{32,48},{64,80},{96,112},{16,0},{48,32},{80,64},{112,96},{1... | collective-permute-start | bytes 98312 | tf_op jit(solution)/shard_map/ppermute | solution.py:244
  77.6 10.0 %collective-permute-start.13 = (bf16[128,128]{1,0:T(8,128)(2,1)S(1)}, bf16[128,128]{1,0:T(8,128)(2,1)S(1)}, u32[]{:S(2)}, u32[]{:S(2)}) collective-permute-start(bf16[128,128]{1,0:T(8,128)(2,1)S(1)} %get-tuple-element.103.own_ref), channel_id=1, source_target_pairs={{16,32},{17,33},{18,34},{19,35},{20,36},{21,37},{22,38},{23,39},{2... | collective-permute-start | bytes 98312 | tf_op jit(solution)/shard_map/ppermute | solution.py:244
  83.5 4.6 %collective-permute-start.12 = (bf16[8,32,512]{2,1,0:T(8,128)(2,1)S(1)}, bf16[8,32,512]{2,1,0:T(8,128)(2,1)S(1)}, u32[]{:S(2)}, u32[]{:S(2)}) collective-permute-start(bf16[8,32,512]{2,1,0:T(8,128)(2,1)S(1)} %all-to-all-done.4.mine_ref), channel_id=1, source_target_pairs={{0,1},{2,3},{4,5},{6,7},{8,9},{10,11},{12,13},{14,15},{1,0},{3,2},... | collective-permute-start | bytes 786440 | tf_op jit(solution)/shard_map/ppermute | solution.py:244
  90.8 9.4 %all-to-all-start.5 = ((bf16[8,32,512]{2,1,0:T(8,128)(2,1)}), bf16[8,32,512]{2,1,0:T(8,128)(2,1)S(1)}, u32[]{:S(2)}, u32[]{:S(2)}) async-start(bf16[8,32,512]{2,1,0:T(8,128)(2,1)} %get-tuple-element.108), calls=%async_computation.5 | async-start | bytes 524288 | tf_op jit(solution)/shard_map/all_to_all | solution.py:273
  94.2 9.3 %collective-permute-start.17 = (bf16[128,128]{1,0:T(8,128)(2,1)S(1)}, bf16[128,128]{1,0:T(8,128)(2,1)S(1)}, u32[]{:S(2)}, u32[]{:S(2)}) collective-permute-start(bf16[128,128]{1,0:T(8,128)(2,1)S(1)} %get-tuple-element.109.own_ref), channel_id=1, source_target_pairs={{0,16},{32,48},{64,80},{96,112},{16,0},{48,32},{80,64},{112,96},{1... | collective-permute-start | bytes 98312 | tf_op jit(solution)/shard_map/ppermute | solution.py:244
  94.3 9.8 %collective-permute-start.16 = (bf16[128,128]{1,0:T(8,128)(2,1)S(1)}, bf16[128,128]{1,0:T(8,128)(2,1)S(1)}, u32[]{:S(2)}, u32[]{:S(2)}) collective-permute-start(bf16[128,128]{1,0:T(8,128)(2,1)S(1)} %get-tuple-element.109.own_ref), channel_id=1, source_target_pairs={{16,32},{17,33},{18,34},{19,35},{20,36},{21,37},{22,38},{23,39},{2... | collective-permute-start | bytes 98312 | tf_op jit(solution)/shard_map/ppermute | solution.py:244
  100.2 4.4 %collective-permute-start.15 = (bf16[8,32,512]{2,1,0:T(8,128)(2,1)S(1)}, bf16[8,32,512]{2,1,0:T(8,128)(2,1)S(1)}, u32[]{:S(2)}, u32[]{:S(2)}) collective-permute-start(bf16[8,32,512]{2,1,0:T(8,128)(2,1)S(1)} %all-to-all-done.5.mine_ref), channel_id=1, source_target_pairs={{0,1},{2,3},{4,5},{6,7},{8,9},{10,11},{12,13},{14,15},{1,0},{3,2},... | collective-permute-start | bytes 786440 | tf_op jit(solution)/shard_map/ppermute | solution.py:244
  107.3 3.5 %copy-start.18 = (f32[128,128]{1,0:T(8,128)}, f32[128,128]{1,0:T(8,128)S(1)}, u32[]{:S(2)}) copy-start(f32[128,128]{1,0:T(8,128)S(1)} %get-tuple-element.123.refs_0_) | copy-start | bytes 196612
  107.3 9.4 %all-to-all-start.6 = ((bf16[8,32,512]{2,1,0:T(8,128)(2,1)}), bf16[8,32,512]{2,1,0:T(8,128)(2,1)S(1)}, u32[]{:S(2)}, u32[]{:S(2)}) async-start(bf16[8,32,512]{2,1,0:T(8,128)(2,1)} %get-tuple-element.116), calls=%async_computation.6 | async-start | bytes 524288 | tf_op jit(solution)/shard_map/all_to_all | solution.py:273
  110.8 9.2 %collective-permute-start.20 = (bf16[128,128]{1,0:T(8,128)(2,1)S(1)}, bf16[128,128]{1,0:T(8,128)(2,1)S(1)}, u32[]{:S(2)}, u32[]{:S(2)}) collective-permute-start(bf16[128,128]{1,0:T(8,128)(2,1)S(1)} %get-tuple-element.117.own_ref), channel_id=1, source_target_pairs={{0,16},{32,48},{64,80},{96,112},{16,0},{48,32},{80,64},{112,96},{1... | collective-permute-start | bytes 98312 | tf_op jit(solution)/shard_map/ppermute | solution.py:244
  110.9 9.7 %collective-permute-start.19 = (bf16[128,128]{1,0:T(8,128)(2,1)S(1)}, bf16[128,128]{1,0:T(8,128)(2,1)S(1)}, u32[]{:S(2)}, u32[]{:S(2)}) collective-permute-start(bf16[128,128]{1,0:T(8,128)(2,1)S(1)} %get-tuple-element.117.own_ref), channel_id=1, source_target_pairs={{16,32},{17,33},{18,34},{19,35},{20,36},{21,37},{22,38},{23,39},{2... | collective-permute-start | bytes 98312 | tf_op jit(solution)/shard_map/ppermute | solution.py:244
  116.8 4.4 %collective-permute-start.18 = (bf16[8,32,512]{2,1,0:T(8,128)(2,1)S(1)}, bf16[8,32,512]{2,1,0:T(8,128)(2,1)S(1)}, u32[]{:S(2)}, u32[]{:S(2)}) collective-permute-start(bf16[8,32,512]{2,1,0:T(8,128)(2,1)S(1)} %all-to-all-done.6.mine_ref), channel_id=1, source_target_pairs={{0,1},{2,3},{4,5},{6,7},{8,9},{10,11},{12,13},{14,15},{1,0},{3,2},... | collective-permute-start | bytes 786440 | tf_op jit(solution)/shard_map/ppermute | solution.py:244
  120.6 0.8 copy-start.19
  124.1 3.5 %copy-start.12 = (f32[128,128]{1,0:T(8,128)}, f32[128,128]{1,0:T(8,128)S(1)}, u32[]{:S(2)}) copy-start(f32[128,128]{1,0:T(8,128)S(1)} %get-tuple-element.131.refs_0_) | copy-start | bytes 196612
  124.1 9.4 %all-to-all-start.7 = ((bf16[8,32,512]{2,1,0:T(8,128)(2,1)}), bf16[8,32,512]{2,1,0:T(8,128)(2,1)S(1)}, u32[]{:S(2)}, u32[]{:S(2)}) async-start(bf16[8,32,512]{2,1,0:T(8,128)(2,1)} %get-tuple-element.124), calls=%async_computation.7 | async-start | bytes 524288 | tf_op jit(solution)/shard_map/all_to_all | solution.py:273
  127.5 9.3 %collective-permute-start.23 = (bf16[128,128]{1,0:T(8,128)(2,1)S(1)}, bf16[128,128]{1,0:T(8,128)(2,1)S(1)}, u32[]{:S(2)}, u32[]{:S(2)}) collective-permute-start(bf16[128,128]{1,0:T(8,128)(2,1)S(1)} %get-tuple-element.125.own_ref), channel_id=1, source_target_pairs={{0,16},{32,48},{64,80},{96,112},{16,0},{48,32},{80,64},{112,96},{1... | collective-permute-start | bytes 98312 | tf_op jit(solution)/shard_map/ppermute | solution.py:244
  127.6 9.8 %collective-permute-start.22 = (bf16[128,128]{1,0:T(8,128)(2,1)S(1)}, bf16[128,128]{1,0:T(8,128)(2,1)S(1)}, u32[]{:S(2)}, u32[]{:S(2)}) collective-permute-start(bf16[128,128]{1,0:T(8,128)(2,1)S(1)} %get-tuple-element.125.own_ref), channel_id=1, source_target_pairs={{16,32},{17,33},{18,34},{19,35},{20,36},{21,37},{22,38},{23,39},{2... | collective-permute-start | bytes 98312 | tf_op jit(solution)/shard_map/ppermute | solution.py:244
  133.5 4.5 %collective-permute-start.21 = (bf16[8,32,512]{2,1,0:T(8,128)(2,1)S(1)}, bf16[8,32,512]{2,1,0:T(8,128)(2,1)S(1)}, u32[]{:S(2)}, u32[]{:S(2)}) collective-permute-start(bf16[8,32,512]{2,1,0:T(8,128)(2,1)S(1)} %all-to-all-done.7.mine_ref), channel_id=1, source_target_pairs={{0,1},{2,3},{4,5},{6,7},{8,9},{10,11},{12,13},{14,15},{1,0},{3,2},... | collective-permute-start | bytes 786440 | tf_op jit(solution)/shard_map/ppermute | solution.py:244
  137.4 0.9 copy-start.13
  (4 other events, 3.2 us)

commit v5 on v4

--- a/solution.py
+++ b/solution.py
@@ -65,12 +65,11 @@
 
 
 def first_kernel(
-    count_ref, initial_ref, right_ref, faults_ref, spread_out, packed_out, solution_out, right_out, index_out, *scratch
+    count_ref, initial_ref, faults_ref, spread_out, packed_out, solution_out, index_out, *scratch
 ):
     field = initial_ref[0].reshape(2 * NODES, ROWS).T
     copy = send_field(field, spread_out, packed_out, scratch)
     solution_out[...] = field
-    right_out[...] = right_ref[0].reshape(2 * NODES, ROWS).T
     device = faults_ref[1, 0]
     column = (
         jnp.where(device % 2 == lax.axis_index("gy") % 2, 0, CHIPS * ELEMS)
@@ -148,7 +147,7 @@
         half_ref[...] = gathered(index_ref, 0, mine_ref)
         local = local_ref[...] + side_sum(even_ref, face_ref, lax.axis_index("gx") % 2 == 0)
         if turn == 0:
-            base_ref[...] = states[0][...] - local
+            base_ref[...] = states[0][0].reshape(2 * NODES, ROWS).T - local
         else:
             old, new = steps[turn - 1]
             base_ref[...] = old * states[1][...] + new * (states[0][...] - local)
@@ -259,14 +258,14 @@
     ]
     final_scratch = [pltpu.VMEM((RHS * NODES, PAIRS), F32), pltpu.VMEM((2, ROWS, NODES), F32)]
 
-    spread, packed, total, right, index = call(
+    spread, packed, total, index = call(
         first_kernel,
-        [SMEM] + [pl.BlockSpec()] * 3,
-        [spread_shape, packed_shape, state, state, shape((8, PAIRS), jnp.int32)],
-        [HBM] + [VMEM] * 4,
+        [SMEM] + [pl.BlockSpec()] * 2,
+        [spread_shape, packed_shape, state, shape((8, PAIRS), jnp.int32)],
+        [HBM] + [VMEM] * 3,
         send_scratch,
         room=ROOM,
-    )(fault_count, initial, right_side, faults)
+    )(fault_count, initial, faults)
     residual = step = correction = None
     for sweep in range(SWEEPS):
         for turn in range(DEGREE):
@@ -277,7 +276,7 @@
             mine, local = lax.optimization_barrier((mine, local))
             other = swap(mine, "gy", [(2 * chip, 2 * chip + 1) for chip in range(CHIPS)])
             last = sweep == SWEEPS - 1 and turn == DEGREE - 1
-            states = [right] if turn == 0 else [residual, step]
+            states = [right_side] if turn == 0 else [residual, step]
             late = ([correction] if turn > 0 else []) + ([total] if turn == DEGREE - 1 else [])
             base, half = call(
                 make_stage_kernel(turn),

time: 142 us -> 141 us (level)
  transfers between devices with their start and end apart: 32 -> 32, of which waited for: 7 -> 7; matrix products, arithmetic and copies ran while one was open for 0% -> 0% of each run, Pallas kernels for 11% -> 12%
where the time goes in v5:
time: 141 us; the launch traced here: 140 us
  starting transfers between devices  73.3 us (52%)
  Pallas kernels  38.3 us (27%)
  waiting for transfers between devices  21.3 us (15%)
  local copies, waits for them, and re-layouts  5.75 us (4%)
  between operations  1.51 us (1%)
    ppermute x24, starting transfers between devices, swap(): return lax.ppermute(value, axis, pairs + [(b, a) for a, b in pairs])  41.2 us
    all_to_all x8, starting transfers between devices, shards(): mine = lax.all_to_all(spread, 'gy', 0, 0, axis_index_groups=same_core)  32.1 us
    all_to_all x8, waiting for transfers between devices, shards(): mine = lax.all_to_all(spread, 'gy', 0, 0, axis_index_groups=same_core)  21.2 us
    pallas_call x8, Pallas kernels, shards(): call(make_final_kernel(turn, last), [VMEM] * (6 + len(late)), outs, out_s...  21 us
    pallas_call x8, Pallas kernels, shards(): call(local_kernel, [VMEM] * 3, state, VMEM, room=ROOM)  7.11 us
    unnamed x40, local copies, waits for them, and re-layouts  5.75 us
    pallas_call x8, Pallas kernels, shards(): call(make_stage_kernel(turn), [VMEM] * (5 + len(states)), [state, shape((...  4.89 us
    pallas_call x8, Pallas kernels, shards(): call(make_far_kernel(turn), [VMEM] * 3, state, VMEM, flops=FAR_FLOPS, roo...  4.29 us
  transfers between devices with their start and end apart: 32, of which 7 were waited for; matrix products, arithmetic and copies ran while one was open for 0% of the time, Pallas kernels for 12%

profile of v5, /device:TPU:17, one launch (start us, length us, event | category | flops | bytes accessed | tf_op | source)
XLA Modules:
  0.0 140.2 jit_solution(18432558385307627016)
XLA Ops:
  2.2 1.0 shard_map.73
  3.2 5.8 %all-to-all-start = ((bf16[8,32,512]{2,1,0:T(8,128)(2,1)}), bf16[8,32,512]{2,1,0:T(8,128)(2,1)S(1)}, u32[]{:S(2)}, u32[]{:S(2)}) async-start(bf16[8,32,512]{2,1,0:T(8,128)(2,1)} %get-tuple-element.69), calls=%async_computation | async-start | bytes 524288 | tf_op jit(solution)/shard_map/all_to_all | solution.py:272
  9.0 1.3 collective-permute-start.2
  10.3 1.9 %collective-permute-start.1 = (bf16[128,128]{1,0:T(8,128)(2,1)S(1)}, bf16[128,128]{1,0:T(8,128)(2,1)S(1)}, u32[]{:S(2)}, u32[]{:S(2)}) collective-permute-start(bf16[128,128]{1,0:T(8,128)(2,1)S(1)} %get-tuple-element.70.own_ref), channel_id=1, source_target_pairs={{16,32},{17,33},{18,34},{19,35},{20,36},{21,37},{22,38},{23,39},{2... | collective-permute-start | bytes 98312 | tf_op jit(solution)/shard_map/ppermute | solution.py:243
  12.1 1.4 %copy-done = bf16[6,1,2,64,1024]{4,3,2,1,0:T(8,128)(2,1)S(1)} copy-done((bf16[6,1,2,64,1024]{4,3,2,1,0:T(8,128)(2,1)S(1)}, bf16[6,1,2,64,1024]{4,3,2,1,0:T(8,128)(2,1)}, u32[]{:S(2)}) %copy-start) | copy-done | bytes 1572888
  13.6 0.9 copy-done.2
  15.4 1.7 %collective-permute-start = (bf16[8,32,512]{2,1,0:T(8,128)(2,1)S(1)}, bf16[8,32,512]{2,1,0:T(8,128)(2,1)S(1)}, u32[]{:S(2)}, u32[]{:S(2)}) collective-permute-start(bf16[8,32,512]{2,1,0:T(8,128)(2,1)S(1)} %all-to-all-done.mine_ref), channel_id=1, source_target_pairs={{0,1},{2,3},{4,5},{6,7},{8,9},{10,11},{12,13},{14,15},{1,0},{3,2},... | collective-permute-start | bytes 786440 | tf_op jit(solution)/shard_map/ppermute | solution.py:243
  19.0 2.6 %shard_map.77 = (bf16[8,32,512]{2,1,0:T(8,128)(2,1)}, bf16[128,128]{1,0:T(8,128)(2,1)S(1)}, f32[128,128]{1,0:T(8,128)S(1)}, f32[128,128]{1,0:T(8,128)S(1)}) custom-call(bf16[1,1,64,8192]{3,2,1,0:T(8,128)(2,1)S(1)} %copy-done.7, bf16[6,1,2,64,1024]{4,3,2,1,0:T(8,128)(2,1)S(1)} %copy-done.1, s32[8,128]{1,0:T(8,128)S(1)} %get-tuple-element.68.index_ref, ...), custom_call_target="tpu_custom_call" | custom-call | flops 4294967296 | bytes 2097152 | tf_op jit(solution)/shard_map/pallas_call | solution.py:294
  21.7 5.8 %all-to-all-start.1 = ((bf16[8,32,512]{2,1,0:T(8,128)(2,1)}), bf16[8,32,512]{2,1,0:T(8,128)(2,1)S(1)}, u32[]{:S(2)}, u32[]{:S(2)}) async-start(bf16[8,32,512]{2,1,0:T(8,128)(2,1)} %get-tuple-element.75), calls=%async_computation.1 | async-start | bytes 524288 | tf_op jit(solution)/shard_map/all_to_all | solution.py:272
  27.5 2.1 %collective-permute-start.4 = (bf16[128,128]{1,0:T(8,128)(2,1)S(1)}, bf16[128,128]{1,0:T(8,128)(2,1)S(1)}, u32[]{:S(2)}, u32[]{:S(2)}) collective-permute-start(bf16[128,128]{1,0:T(8,128)(2,1)S(1)} %get-tuple-element.76.own_ref), channel_id=1, source_target_pairs={{16,32},{17,33},{18,34},{19,35},{20,36},{21,37},{22,38},{23,39},{2... | collective-permute-start | bytes 98312 | tf_op jit(solution)/shard_map/ppermute | solution.py:243
  29.6 0.9 shard_map.78.local_ref
  30.5 3.1 %all-to-all-done.1.mine_ref = bf16[8,32,512]{2,1,0:T(8,128)(2,1)S(1)} async-done(((bf16[8,32,512]{2,1,0:T(8,128)(2,1)}), bf16[8,32,512]{2,1,0:T(8,128)(2,1)S(1)}, u32[]{:S(2)}, u32[]{:S(2)}) %all-to-all-start.1) | async-done | bytes 262176 | tf_op jit(solution)/shard_map/all_to_all | solution.py:272
  33.6 2.1 %collective-permute-start.3 = (bf16[8,32,512]{2,1,0:T(8,128)(2,1)S(1)}, bf16[8,32,512]{2,1,0:T(8,128)(2,1)S(1)}, u32[]{:S(2)}, u32[]{:S(2)}) collective-permute-start(bf16[8,32,512]{2,1,0:T(8,128)(2,1)S(1)} %all-to-all-done.1.mine_ref), channel_id=1, source_target_pairs={{0,1},{2,3},{4,5},{6,7},{8,9},{10,11},{12,13},{14,15},{1,0},{3,2},... | collective-permute-start | bytes 786440 | tf_op jit(solution)/shard_map/ppermute | solution.py:243
  36.9 2.7 %shard_map.81 = (bf16[8,32,512]{2,1,0:T(8,128)(2,1)}, bf16[128,128]{1,0:T(8,128)(2,1)S(1)}, f32[128,128]{1,0:T(8,128)S(1)}, f32[128,128]{1,0:T(8,128)S(1)}) custom-call(bf16[1,1,64,8192]{3,2,1,0:T(8,128)(2,1)S(1)} %copy-done.7, bf16[6,1,2,64,1024]{4,3,2,1,0:T(8,128)(2,1)S(1)} %copy-done.1, s32[8,128]{1,0:T(8,128)S(1)} %get-tuple-element.68.index_ref, ...), custom_call_target="tpu_custom_call" | custom-call | flops 4294967296 | bytes 2097152 | tf_op jit(solution)/shard_map/pallas_call | solution.py:294
  39.6 3.4 %all-to-all-start.2 = ((bf16[8,32,512]{2,1,0:T(8,128)(2,1)}), bf16[8,32,512]{2,1,0:T(8,128)(2,1)S(1)}, u32[]{:S(2)}, u32[]{:S(2)}) async-start(bf16[8,32,512]{2,1,0:T(8,128)(2,1)} %get-tuple-element.83), calls=%async_computation.2 | async-start | bytes 524288 | tf_op jit(solution)/shard_map/all_to_all | solution.py:272
  43.1 2.0 %collective-permute-start.7 = (bf16[128,128]{1,0:T(8,128)(2,1)S(1)}, bf16[128,128]{1,0:T(8,128)(2,1)S(1)}, u32[]{:S(2)}, u32[]{:S(2)}) collective-permute-start(bf16[128,128]{1,0:T(8,128)(2,1)S(1)} %get-tuple-element.84.own_ref), channel_id=1, source_target_pairs={{16,32},{17,33},{18,34},{19,35},{20,36},{21,37},{22,38},{23,39},{2... | collective-permute-start | bytes 98312 | tf_op jit(solution)/shard_map/ppermute | solution.py:243
  45.1 0.9 shard_map.82.local_ref
  46.0 3.0 %all-to-all-done.2.mine_ref = bf16[8,32,512]{2,1,0:T(8,128)(2,1)S(1)} async-done(((bf16[8,32,512]{2,1,0:T(8,128)(2,1)}), bf16[8,32,512]{2,1,0:T(8,128)(2,1)S(1)}, u32[]{:S(2)}, u32[]{:S(2)}) %all-to-all-start.2) | async-done | bytes 262176 | tf_op jit(solution)/shard_map/all_to_all | solution.py:272
  49.0 3.2 %collective-permute-start.6 = (bf16[8,32,512]{2,1,0:T(8,128)(2,1)S(1)}, bf16[8,32,512]{2,1,0:T(8,128)(2,1)S(1)}, u32[]{:S(2)}, u32[]{:S(2)}) collective-permute-start(bf16[8,32,512]{2,1,0:T(8,128)(2,1)S(1)} %all-to-all-done.2.mine_ref), channel_id=1, source_target_pairs={{0,1},{2,3},{4,5},{6,7},{8,9},{10,11},{12,13},{14,15},{1,0},{3,2},... | collective-permute-start | bytes 786440 | tf_op jit(solution)/shard_map/ppermute | solution.py:243
  53.7 2.6 %shard_map.85 = (bf16[8,32,512]{2,1,0:T(8,128)(2,1)}, bf16[128,128]{1,0:T(8,128)(2,1)S(1)}, f32[128,128]{1,0:T(8,128)S(1)}, f32[128,128]{1,0:T(8,128)S(1)}) custom-call(bf16[1,1,64,8192]{3,2,1,0:T(8,128)(2,1)S(1)} %copy-done.7, bf16[6,1,2,64,1024]{4,3,2,1,0:T(8,128)(2,1)S(1)} %copy-done.1, s32[8,128]{1,0:T(8,128)S(1)} %get-tuple-element.68.index_ref, ...), custom_call_target="tpu_custom_call" | custom-call | flops 4294967296 | bytes 2097152 | tf_op jit(solution)/shard_map/pallas_call | solution.py:294
  56.4 3.4 %all-to-all-start.3 = ((bf16[8,32,512]{2,1,0:T(8,128)(2,1)}), bf16[8,32,512]{2,1,0:T(8,128)(2,1)S(1)}, u32[]{:S(2)}, u32[]{:S(2)}) async-start(bf16[8,32,512]{2,1,0:T(8,128)(2,1)} %get-tuple-element.91), calls=%async_computation.3 | async-start | bytes 524288 | tf_op jit(solution)/shard_map/all_to_all | solution.py:272
  59.9 2.1 %collective-permute-start.10 = (bf16[128,128]{1,0:T(8,128)(2,1)S(1)}, bf16[128,128]{1,0:T(8,128)(2,1)S(1)}, u32[]{:S(2)}, u32[]{:S(2)}) collective-permute-start(bf16[128,128]{1,0:T(8,128)(2,1)S(1)} %get-tuple-element.92.own_ref), channel_id=1, source_target_pairs={{16,32},{17,33},{18,34},{19,35},{20,36},{21,37},{22,38},{23,39},{2... | collective-permute-start | bytes 98312 | tf_op jit(solution)/shard_map/ppermute | solution.py:243
  62.9 2.9 %all-to-all-done.3.mine_ref = bf16[8,32,512]{2,1,0:T(8,128)(2,1)S(1)} async-done(((bf16[8,32,512]{2,1,0:T(8,128)(2,1)}), bf16[8,32,512]{2,1,0:T(8,128)(2,1)S(1)}, u32[]{:S(2)}, u32[]{:S(2)}) %all-to-all-start.3) | async-done | bytes 262176 | tf_op jit(solution)/shard_map/all_to_all | solution.py:272
  65.8 3.3 %collective-permute-start.9 = (bf16[8,32,512]{2,1,0:T(8,128)(2,1)S(1)}, bf16[8,32,512]{2,1,0:T(8,128)(2,1)S(1)}, u32[]{:S(2)}, u32[]{:S(2)}) collective-permute-start(bf16[8,32,512]{2,1,0:T(8,128)(2,1)S(1)} %all-to-all-done.3.mine_ref), channel_id=1, source_target_pairs={{0,1},{2,3},{4,5},{6,7},{8,9},{10,11},{12,13},{14,15},{1,0},{3,2},... | collective-permute-start | bytes 786440 | tf_op jit(solution)/shard_map/ppermute | solution.py:243
  70.6 2.6 %shard_map.89 = (bf16[8,32,512]{2,1,0:T(8,128)(2,1)}, bf16[128,128]{1,0:T(8,128)(2,1)S(1)}, f32[128,128]{1,0:T(8,128)S(1)}) custom-call(bf16[1,1,64,8192]{3,2,1,0:T(8,128)(2,1)S(1)} %copy-done.7, bf16[6,1,2,64,1024]{4,3,2,1,0:T(8,128)(2,1)S(1)} %copy-done.1, s32[8,128]{1,0:T(8,128)S(1)} %get-tuple-element.68.index_ref, ...), custom_call_target="tpu_custom_call" | custom-call | flops 4294967296 | bytes 2097152 | tf_op jit(solution)/shard_map/pallas_call | solution.py:294
  73.2 3.4 %all-to-all-start.4 = ((bf16[8,32,512]{2,1,0:T(8,128)(2,1)}), bf16[8,32,512]{2,1,0:T(8,128)(2,1)S(1)}, u32[]{:S(2)}, u32[]{:S(2)}) async-start(bf16[8,32,512]{2,1,0:T(8,128)(2,1)} %get-tuple-element.100), calls=%async_computation.4 | async-start | bytes 524288 | tf_op jit(solution)/shard_map/all_to_all | solution.py:272
  76.8 2.0 %collective-permute-start.13 = (bf16[128,128]{1,0:T(8,128)(2,1)S(1)}, bf16[128,128]{1,0:T(8,128)(2,1)S(1)}, u32[]{:S(2)}, u32[]{:S(2)}) collective-permute-start(bf16[128,128]{1,0:T(8,128)(2,1)S(1)} %get-tuple-element.101.own_ref), channel_id=1, source_target_pairs={{16,32},{17,33},{18,34},{19,35},{20,36},{21,37},{22,38},{23,39},{2... | collective-permute-start | bytes 98312 | tf_op jit(solution)/shard_map/ppermute | solution.py:243
  78.7 0.9 shard_map.90.local_ref
  79.6 3.0 %all-to-all-done.4.mine_ref = bf16[8,32,512]{2,1,0:T(8,128)(2,1)S(1)} async-done(((bf16[8,32,512]{2,1,0:T(8,128)(2,1)}), bf16[8,32,512]{2,1,0:T(8,128)(2,1)S(1)}, u32[]{:S(2)}, u32[]{:S(2)}) %all-to-all-start.4) | async-done | bytes 262176 | tf_op jit(solution)/shard_map/all_to_all | solution.py:272
  82.7 3.5 %collective-permute-start.12 = (bf16[8,32,512]{2,1,0:T(8,128)(2,1)S(1)}, bf16[8,32,512]{2,1,0:T(8,128)(2,1)S(1)}, u32[]{:S(2)}, u32[]{:S(2)}) collective-permute-start(bf16[8,32,512]{2,1,0:T(8,128)(2,1)S(1)} %all-to-all-done.4.mine_ref), channel_id=1, source_target_pairs={{0,1},{2,3},{4,5},{6,7},{8,9},{10,11},{12,13},{14,15},{1,0},{3,2},... | collective-permute-start | bytes 786440 | tf_op jit(solution)/shard_map/ppermute | solution.py:243
  87.4 2.7 %shard_map.93 = (bf16[8,32,512]{2,1,0:T(8,128)(2,1)}, bf16[128,128]{1,0:T(8,128)(2,1)S(1)}, f32[128,128]{1,0:T(8,128)S(1)}, f32[128,128]{1,0:T(8,128)S(1)}) custom-call(bf16[1,1,64,8192]{3,2,1,0:T(8,128)(2,1)S(1)} %copy-done.7, bf16[6,1,2,64,1024]{4,3,2,1,0:T(8,128)(2,1)S(1)} %copy-done.1, s32[8,128]{1,0:T(8,128)S(1)} %get-tuple-element.68.index_ref, ...), custom_call_target="tpu_custom_call" | custom-call | flops 4294967296 | bytes 2097152 | tf_op jit(solution)/shard_map/pallas_call | solution.py:294
  90.0 3.4 %all-to-all-start.5 = ((bf16[8,32,512]{2,1,0:T(8,128)(2,1)}), bf16[8,32,512]{2,1,0:T(8,128)(2,1)S(1)}, u32[]{:S(2)}, u32[]{:S(2)}) async-start(bf16[8,32,512]{2,1,0:T(8,128)(2,1)} %get-tuple-element.106), calls=%async_computation.5 | async-start | bytes 524288 | tf_op jit(solution)/shard_map/all_to_all | solution.py:272
  93.5 2.0 %collective-permute-start.16 = (bf16[128,128]{1,0:T(8,128)(2,1)S(1)}, bf16[128,128]{1,0:T(8,128)(2,1)S(1)}, u32[]{:S(2)}, u32[]{:S(2)}) collective-permute-start(bf16[128,128]{1,0:T(8,128)(2,1)S(1)} %get-tuple-element.107.own_ref), channel_id=1, source_target_pairs={{16,32},{17,33},{18,34},{19,35},{20,36},{21,37},{22,38},{23,39},{2... | collective-permute-start | bytes 98312 | tf_op jit(solution)/shard_map/ppermute | solution.py:243
  96.4 3.1 %all-to-all-done.5.mine_ref = bf16[8,32,512]{2,1,0:T(8,128)(2,1)S(1)} async-done(((bf16[8,32,512]{2,1,0:T(8,128)(2,1)}), bf16[8,32,512]{2,1,0:T(8,128)(2,1)S(1)}, u32[]{:S(2)}, u32[]{:S(2)}) %all-to-all-start.5) | async-done | bytes 262176 | tf_op jit(solution)/shard_map/all_to_all | solution.py:272
  99.5 3.2 %collective-permute-start.15 = (bf16[8,32,512]{2,1,0:T(8,128)(2,1)S(1)}, bf16[8,32,512]{2,1,0:T(8,128)(2,1)S(1)}, u32[]{:S(2)}, u32[]{:S(2)}) collective-permute-start(bf16[8,32,512]{2,1,0:T(8,128)(2,1)S(1)} %all-to-all-done.5.mine_ref), channel_id=1, source_target_pairs={{0,1},{2,3},{4,5},{6,7},{8,9},{10,11},{12,13},{14,15},{1,0},{3,2},... | collective-permute-start | bytes 786440 | tf_op jit(solution)/shard_map/ppermute | solution.py:243
  103.9 2.7 %shard_map.97 = (bf16[8,32,512]{2,1,0:T(8,128)(2,1)}, bf16[128,128]{1,0:T(8,128)(2,1)S(1)}, f32[128,128]{1,0:T(8,128)S(1)}, f32[128,128]{1,0:T(8,128)S(1)}) custom-call(bf16[1,1,64,8192]{3,2,1,0:T(8,128)(2,1)S(1)} %copy-done.7, bf16[6,1,2,64,1024]{4,3,2,1,0:T(8,128)(2,1)S(1)} %copy-done.1, s32[8,128]{1,0:T(8,128)S(1)} %get-tuple-element.68.index_ref, ...), custom_call_target="tpu_custom_call" | custom-call | flops 4294967296 | bytes 2097152 | tf_op jit(solution)/shard_map/pallas_call | solution.py:294
  106.5 3.4 %all-to-all-start.6 = ((bf16[8,32,512]{2,1,0:T(8,128)(2,1)}), bf16[8,32,512]{2,1,0:T(8,128)(2,1)S(1)}, u32[]{:S(2)}, u32[]{:S(2)}) async-start(bf16[8,32,512]{2,1,0:T(8,128)(2,1)} %get-tuple-element.114), calls=%async_computation.6 | async-start | bytes 524288 | tf_op jit(solution)/shard_map/all_to_all | solution.py:272
  110.1 2.0 %collective-permute-start.19 = (bf16[128,128]{1,0:T(8,128)(2,1)S(1)}, bf16[128,128]{1,0:T(8,128)(2,1)S(1)}, u32[]{:S(2)}, u32[]{:S(2)}) collective-permute-start(bf16[128,128]{1,0:T(8,128)(2,1)S(1)} %get-tuple-element.115.own_ref), channel_id=1, source_target_pairs={{16,32},{17,33},{18,34},{19,35},{20,36},{21,37},{22,38},{23,39},{2... | collective-permute-start | bytes 98312 | tf_op jit(solution)/shard_map/ppermute | solution.py:243
  112.0 0.9 shard_map.98.local_ref
  112.9 3.0 %all-to-all-done.6.mine_ref = bf16[8,32,512]{2,1,0:T(8,128)(2,1)S(1)} async-done(((bf16[8,32,512]{2,1,0:T(8,128)(2,1)}), bf16[8,32,512]{2,1,0:T(8,128)(2,1)S(1)}, u32[]{:S(2)}, u32[]{:S(2)}) %all-to-all-start.6) | async-done | bytes 262176 | tf_op jit(solution)/shard_map/all_to_all | solution.py:272
  116.0 3.2 %collective-permute-start.18 = (bf16[8,32,512]{2,1,0:T(8,128)(2,1)S(1)}, bf16[8,32,512]{2,1,0:T(8,128)(2,1)S(1)}, u32[]{:S(2)}, u32[]{:S(2)}) collective-permute-start(bf16[8,32,512]{2,1,0:T(8,128)(2,1)S(1)} %all-to-all-done.6.mine_ref), channel_id=1, source_target_pairs={{0,1},{2,3},{4,5},{6,7},{8,9},{10,11},{12,13},{14,15},{1,0},{3,2},... | collective-permute-start | bytes 786440 | tf_op jit(solution)/shard_map/ppermute | solution.py:243
  120.6 2.6 %shard_map.101 = (bf16[8,32,512]{2,1,0:T(8,128)(2,1)}, bf16[128,128]{1,0:T(8,128)(2,1)S(1)}, f32[128,128]{1,0:T(8,128)S(1)}, f32[128,128]{1,0:T(8,128)S(1)}) custom-call(bf16[1,1,64,8192]{3,2,1,0:T(8,128)(2,1)S(1)} %copy-done.7, bf16[6,1,2,64,1024]{4,3,2,1,0:T(8,128)(2,1)S(1)} %copy-done.1, s32[8,128]{1,0:T(8,128)S(1)} %get-tuple-element.68.index_ref, ...), custom_call_target="tpu_custom_call" | custom-call | flops 4294967296 | bytes 2097152 | tf_op jit(solution)/shard_map/pallas_call | solution.py:294
  123.3 3.4 %all-to-all-start.7 = ((bf16[8,32,512]{2,1,0:T(8,128)(2,1)}), bf16[8,32,512]{2,1,0:T(8,128)(2,1)S(1)}, u32[]{:S(2)}, u32[]{:S(2)}) async-start(bf16[8,32,512]{2,1,0:T(8,128)(2,1)} %get-tuple-element.122), calls=%async_computation.7 | async-start | bytes 524288 | tf_op jit(solution)/shard_map/all_to_all | solution.py:272
  126.8 2.0 %collective-permute-start.22 = (bf16[128,128]{1,0:T(8,128)(2,1)S(1)}, bf16[128,128]{1,0:T(8,128)(2,1)S(1)}, u32[]{:S(2)}, u32[]{:S(2)}) collective-permute-start(bf16[128,128]{1,0:T(8,128)(2,1)S(1)} %get-tuple-element.123.own_ref), channel_id=1, source_target_pairs={{16,32},{17,33},{18,34},{19,35},{20,36},{21,37},{22,38},{23,39},{2... | collective-permute-start | bytes 98312 | tf_op jit(solution)/shard_map/ppermute | solution.py:243
  128.8 0.9 shard_map.102.local_ref
  129.7 3.0 %all-to-all-done.7.mine_ref = bf16[8,32,512]{2,1,0:T(8,128)(2,1)S(1)} async-done(((bf16[8,32,512]{2,1,0:T(8,128)(2,1)}), bf16[8,32,512]{2,1,0:T(8,128)(2,1)S(1)}, u32[]{:S(2)}, u32[]{:S(2)}) %all-to-all-start.7) | async-done | bytes 262176 | tf_op jit(solution)/shard_map/all_to_all | solution.py:272
  132.7 3.3 %collective-permute-start.21 = (bf16[8,32,512]{2,1,0:T(8,128)(2,1)S(1)}, bf16[8,32,512]{2,1,0:T(8,128)(2,1)S(1)}, u32[]{:S(2)}, u32[]{:S(2)}) collective-permute-start(bf16[8,32,512]{2,1,0:T(8,128)(2,1)S(1)} %all-to-all-done.7.mine_ref), channel_id=1, source_target_pairs={{0,1},{2,3},{4,5},{6,7},{8,9},{10,11},{12,13},{14,15},{1,0},{3,2},... | collective-permute-start | bytes 786440 | tf_op jit(solution)/shard_map/ppermute | solution.py:243
  137.5 2.5 %shard_map.105 = f32[1,2,64,128]{3,2,1,0:T(8,128)} custom-call(bf16[1,1,64,8192]{3,2,1,0:T(8,128)(2,1)S(1)} %copy-done.7, bf16[6,1,2,64,1024]{4,3,2,1,0:T(8,128)(2,1)S(1)} %copy-done.1, s32[8,128]{1,0:T(8,128)S(1)} %get-tuple-element.68.index_ref, bf16[8,32,512]{2,1,0:T(8,128)(2,1)S(1)} %collective-permute-done.21.other_ref, ...), custom_call_target="tpu_custom_call" | custom-call | flops 4294967296 | bytes 2097152 | tf_op jit(solution)/shard_map/pallas_call | solution.py:294
  (89 shorter events, 15.8 us)
Async XLA Ops:
  0.0 17.2 %copy-start.4 = (f32[1,2,64,128]{3,2,1,0:T(8,128)S(1)}, f32[1,2,64,128]{3,2,1,0:T(8,128)}, u32[]{:S(2)}) copy-start(f32[1,2,64,128]{3,2,1,0:T(8,128)} %refs_0_.3) | copy-start | bytes 196612
  3.2 5.8 %copy-start.8 = (f32[128,128]{1,0:T(8,128)}, f32[128,128]{1,0:T(8,128)S(1)}, u32[]{:S(2)}) copy-start(f32[128,128]{1,0:T(8,128)S(1)} %get-tuple-element.99.refs_1_) | copy-start | bytes 196612
  3.2 12.2 %all-to-all-start = ((bf16[8,32,512]{2,1,0:T(8,128)(2,1)}), bf16[8,32,512]{2,1,0:T(8,128)(2,1)S(1)}, u32[]{:S(2)}, u32[]{:S(2)}) async-start(bf16[8,32,512]{2,1,0:T(8,128)(2,1)} %get-tuple-element.69), calls=%async_computation | async-start | bytes 524288 | tf_op jit(solution)/shard_map/all_to_all | solution.py:272
  9.0 8.2 %collective-permute-start.2 = (bf16[128,128]{1,0:T(8,128)(2,1)S(1)}, bf16[128,128]{1,0:T(8,128)(2,1)S(1)}, u32[]{:S(2)}, u32[]{:S(2)}) collective-permute-start(bf16[128,128]{1,0:T(8,128)(2,1)S(1)} %get-tuple-element.70.own_ref), channel_id=1, source_target_pairs={{0,16},{32,48},{64,80},{96,112},{16,0},{48,32},{80,64},{112,96},{1... | collective-permute-start | bytes 98312 | tf_op jit(solution)/shard_map/ppermute | solution.py:243
  10.3 7.5 %collective-permute-start.1 = (bf16[128,128]{1,0:T(8,128)(2,1)S(1)}, bf16[128,128]{1,0:T(8,128)(2,1)S(1)}, u32[]{:S(2)}, u32[]{:S(2)}) collective-permute-start(bf16[128,128]{1,0:T(8,128)(2,1)S(1)} %get-tuple-element.70.own_ref), channel_id=1, source_target_pairs={{16,32},{17,33},{18,34},{19,35},{20,36},{21,37},{22,38},{23,39},{2... | collective-permute-start | bytes 98312 | tf_op jit(solution)/shard_map/ppermute | solution.py:243
  12.1 1.4 %copy-start = (bf16[6,1,2,64,1024]{4,3,2,1,0:T(8,128)(2,1)S(1)}, bf16[6,1,2,64,1024]{4,3,2,1,0:T(8,128)(2,1)}, u32[]{:S(2)}) copy-start(bf16[6,1,2,64,1024]{4,3,2,1,0:T(8,128)(2,1)} %face_ref.63) | copy-start | bytes 4718596
  13.6 0.9 copy-start.2
  14.5 2.7 %copy-start.1 = (bf16[6,1,2,64,1024]{4,3,2,1,0:T(8,128)(2,1)S(1)}, bf16[6,1,2,64,1024]{4,3,2,1,0:T(8,128)(2,1)}, u32[]{:S(2)}) copy-start(bf16[6,1,2,64,1024]{4,3,2,1,0:T(8,128)(2,1)} %face_ref.63) | copy-start | bytes 4718596
  15.4 3.0 %collective-permute-start = (bf16[8,32,512]{2,1,0:T(8,128)(2,1)S(1)}, bf16[8,32,512]{2,1,0:T(8,128)(2,1)S(1)}, u32[]{:S(2)}, u32[]{:S(2)}) collective-permute-start(bf16[8,32,512]{2,1,0:T(8,128)(2,1)S(1)} %all-to-all-done.mine_ref), channel_id=1, source_target_pairs={{0,1},{2,3},{4,5},{6,7},{8,9},{10,11},{12,13},{14,15},{1,0},{3,2},... | collective-permute-start | bytes 786440 | tf_op jit(solution)/shard_map/ppermute | solution.py:243
  17.8 1.2 copy-start.7
  19.0 10.6 %copy-start.3 = (bf16[1,2,64,1024]{3,2,1,0:T(8,128)(2,1)S(1)}, bf16[1,2,64,1024]{3,2,1,0:T(8,128)(2,1)}, u32[]{:S(2)}) copy-start(bf16[1,2,64,1024]{3,2,1,0:T(8,128)(2,1)} %elem_ref.15) | copy-start | bytes 786436
  21.7 11.9 %all-to-all-start.1 = ((bf16[8,32,512]{2,1,0:T(8,128)(2,1)}), bf16[8,32,512]{2,1,0:T(8,128)(2,1)S(1)}, u32[]{:S(2)}, u32[]{:S(2)}) async-start(bf16[8,32,512]{2,1,0:T(8,128)(2,1)} %get-tuple-element.75), calls=%async_computation.1 | async-start | bytes 524288 | tf_op jit(solution)/shard_map/all_to_all | solution.py:272
  27.5 8.3 %collective-permute-start.5 = (bf16[128,128]{1,0:T(8,128)(2,1)S(1)}, bf16[128,128]{1,0:T(8,128)(2,1)S(1)}, u32[]{:S(2)}, u32[]{:S(2)}) collective-permute-start(bf16[128,128]{1,0:T(8,128)(2,1)S(1)} %get-tuple-element.76.own_ref), channel_id=1, source_target_pairs={{0,16},{32,48},{64,80},{96,112},{16,0},{48,32},{80,64},{112,96},{1... | collective-permute-start | bytes 98312 | tf_op jit(solution)/shard_map/ppermute | solution.py:243
  27.5 8.8 %collective-permute-start.4 = (bf16[128,128]{1,0:T(8,128)(2,1)S(1)}, bf16[128,128]{1,0:T(8,128)(2,1)S(1)}, u32[]{:S(2)}, u32[]{:S(2)}) collective-permute-start(bf16[128,128]{1,0:T(8,128)(2,1)S(1)} %get-tuple-element.76.own_ref), channel_id=1, source_target_pairs={{16,32},{17,33},{18,34},{19,35},{20,36},{21,37},{22,38},{23,39},{2... | collective-permute-start | bytes 98312 | tf_op jit(solution)/shard_map/ppermute | solution.py:243
  33.6 3.3 %collective-permute-start.3 = (bf16[8,32,512]{2,1,0:T(8,128)(2,1)S(1)}, bf16[8,32,512]{2,1,0:T(8,128)(2,1)S(1)}, u32[]{:S(2)}, u32[]{:S(2)}) collective-permute-start(bf16[8,32,512]{2,1,0:T(8,128)(2,1)S(1)} %all-to-all-done.1.mine_ref), channel_id=1, source_target_pairs={{0,1},{2,3},{4,5},{6,7},{8,9},{10,11},{12,13},{14,15},{1,0},{3,2},... | collective-permute-start | bytes 786440 | tf_op jit(solution)/shard_map/ppermute | solution.py:243
  39.6 3.5 %copy-start.16 = (f32[128,128]{1,0:T(8,128)}, f32[128,128]{1,0:T(8,128)S(1)}, u32[]{:S(2)}) copy-start(f32[128,128]{1,0:T(8,128)S(1)} %get-tuple-element.90.refs_0_) | copy-start | bytes 196612
  39.6 9.4 %all-to-all-start.2 = ((bf16[8,32,512]{2,1,0:T(8,128)(2,1)}), bf16[8,32,512]{2,1,0:T(8,128)(2,1)S(1)}, u32[]{:S(2)}, u32[]{:S(2)}) async-start(bf16[8,32,512]{2,1,0:T(8,128)(2,1)} %get-tuple-element.83), calls=%async_computation.2 | async-start | bytes 524288 | tf_op jit(solution)/shard_map/all_to_all | solution.py:272
  43.0 9.2 %collective-permute-start.8 = (bf16[128,128]{1,0:T(8,128)(2,1)S(1)}, bf16[128,128]{1,0:T(8,128)(2,1)S(1)}, u32[]{:S(2)}, u32[]{:S(2)}) collective-permute-start(bf16[128,128]{1,0:T(8,128)(2,1)S(1)} %get-tuple-element.84.own_ref), channel_id=1, source_target_pairs={{0,16},{32,48},{64,80},{96,112},{16,0},{48,32},{80,64},{112,96},{1... | collective-permute-start | bytes 98312 | tf_op jit(solution)/shard_map/ppermute | solution.py:243
  43.1 9.7 %collective-permute-start.7 = (bf16[128,128]{1,0:T(8,128)(2,1)S(1)}, bf16[128,128]{1,0:T(8,128)(2,1)S(1)}, u32[]{:S(2)}, u32[]{:S(2)}) collective-permute-start(bf16[128,128]{1,0:T(8,128)(2,1)S(1)} %get-tuple-element.84.own_ref), channel_id=1, source_target_pairs={{16,32},{17,33},{18,34},{19,35},{20,36},{21,37},{22,38},{23,39},{2... | collective-permute-start | bytes 98312 | tf_op jit(solution)/shard_map/ppermute | solution.py:243
  49.0 4.4 %collective-permute-start.6 = (bf16[8,32,512]{2,1,0:T(8,128)(2,1)S(1)}, bf16[8,32,512]{2,1,0:T(8,128)(2,1)S(1)}, u32[]{:S(2)}, u32[]{:S(2)}) collective-permute-start(bf16[8,32,512]{2,1,0:T(8,128)(2,1)S(1)} %all-to-all-done.2.mine_ref), channel_id=1, source_target_pairs={{0,1},{2,3},{4,5},{6,7},{8,9},{10,11},{12,13},{14,15},{1,0},{3,2},... | collective-permute-start | bytes 786440 | tf_op jit(solution)/shard_map/ppermute | solution.py:243
  52.9 0.8 copy-start.17
  56.4 3.5 %copy-start.14 = (f32[128,128]{1,0:T(8,128)}, f32[128,128]{1,0:T(8,128)S(1)}, u32[]{:S(2)}) copy-start(f32[128,128]{1,0:T(8,128)S(1)} %get-tuple-element.98.refs_0_) | copy-start | bytes 196612
  56.4 9.4 %all-to-all-start.3 = ((bf16[8,32,512]{2,1,0:T(8,128)(2,1)}), bf16[8,32,512]{2,1,0:T(8,128)(2,1)S(1)}, u32[]{:S(2)}, u32[]{:S(2)}) async-start(bf16[8,32,512]{2,1,0:T(8,128)(2,1)} %get-tuple-element.91), calls=%async_computation.3 | async-start | bytes 524288 | tf_op jit(solution)/shard_map/all_to_all | solution.py:272
  59.8 9.3 %collective-permute-start.11 = (bf16[128,128]{1,0:T(8,128)(2,1)S(1)}, bf16[128,128]{1,0:T(8,128)(2,1)S(1)}, u32[]{:S(2)}, u32[]{:S(2)}) collective-permute-start(bf16[128,128]{1,0:T(8,128)(2,1)S(1)} %get-tuple-element.92.own_ref), channel_id=1, source_target_pairs={{0,16},{32,48},{64,80},{96,112},{16,0},{48,32},{80,64},{112,96},{1... | collective-permute-start | bytes 98312 | tf_op jit(solution)/shard_map/ppermute | solution.py:243
  59.9 9.8 %collective-permute-start.10 = (bf16[128,128]{1,0:T(8,128)(2,1)S(1)}, bf16[128,128]{1,0:T(8,128)(2,1)S(1)}, u32[]{:S(2)}, u32[]{:S(2)}) collective-permute-start(bf16[128,128]{1,0:T(8,128)(2,1)S(1)} %get-tuple-element.92.own_ref), channel_id=1, source_target_pairs={{16,32},{17,33},{18,34},{19,35},{20,36},{21,37},{22,38},{23,39},{2... | collective-permute-start | bytes 98312 | tf_op jit(solution)/shard_map/ppermute | solution.py:243
  65.8 4.5 %collective-permute-start.9 = (bf16[8,32,512]{2,1,0:T(8,128)(2,1)S(1)}, bf16[8,32,512]{2,1,0:T(8,128)(2,1)S(1)}, u32[]{:S(2)}, u32[]{:S(2)}) collective-permute-start(bf16[8,32,512]{2,1,0:T(8,128)(2,1)S(1)} %all-to-all-done.3.mine_ref), channel_id=1, source_target_pairs={{0,1},{2,3},{4,5},{6,7},{8,9},{10,11},{12,13},{14,15},{1,0},{3,2},... | collective-permute-start | bytes 786440 | tf_op jit(solution)/shard_map/ppermute | solution.py:243
  69.7 0.9 copy-start.15
  73.2 3.4 %copy-start.10 = (f32[128,128]{1,0:T(8,128)}, f32[128,128]{1,0:T(8,128)S(1)}, u32[]{:S(2)}) copy-start(f32[128,128]{1,0:T(8,128)S(1)} %get-tuple-element.130.refs_1_) | copy-start | bytes 196612
  73.2 9.4 %all-to-all-start.4 = ((bf16[8,32,512]{2,1,0:T(8,128)(2,1)}), bf16[8,32,512]{2,1,0:T(8,128)(2,1)S(1)}, u32[]{:S(2)}, u32[]{:S(2)}) async-start(bf16[8,32,512]{2,1,0:T(8,128)(2,1)} %get-tuple-element.100), calls=%async_computation.4 | async-start | bytes 524288 | tf_op jit(solution)/shard_map/all_to_all | solution.py:272
  76.7 9.5 %collective-permute-start.14 = (bf16[128,128]{1,0:T(8,128)(2,1)S(1)}, bf16[128,128]{1,0:T(8,128)(2,1)S(1)}, u32[]{:S(2)}, u32[]{:S(2)}) collective-permute-start(bf16[128,128]{1,0:T(8,128)(2,1)S(1)} %get-tuple-element.101.own_ref), channel_id=1, source_target_pairs={{0,16},{32,48},{64,80},{96,112},{16,0},{48,32},{80,64},{112,96},{1... | collective-permute-start | bytes 98312 | tf_op jit(solution)/shard_map/ppermute | solution.py:243
  76.8 10.0 %collective-permute-start.13 = (bf16[128,128]{1,0:T(8,128)(2,1)S(1)}, bf16[128,128]{1,0:T(8,128)(2,1)S(1)}, u32[]{:S(2)}, u32[]{:S(2)}) collective-permute-start(bf16[128,128]{1,0:T(8,128)(2,1)S(1)} %get-tuple-element.101.own_ref), channel_id=1, source_target_pairs={{16,32},{17,33},{18,34},{19,35},{20,36},{21,37},{22,38},{23,39},{2... | collective-permute-start | bytes 98312 | tf_op jit(solution)/shard_map/ppermute | solution.py:243
  82.7 4.7 %collective-permute-start.12 = (bf16[8,32,512]{2,1,0:T(8,128)(2,1)S(1)}, bf16[8,32,512]{2,1,0:T(8,128)(2,1)S(1)}, u32[]{:S(2)}, u32[]{:S(2)}) collective-permute-start(bf16[8,32,512]{2,1,0:T(8,128)(2,1)S(1)} %all-to-all-done.4.mine_ref), channel_id=1, source_target_pairs={{0,1},{2,3},{4,5},{6,7},{8,9},{10,11},{12,13},{14,15},{1,0},{3,2},... | collective-permute-start | bytes 786440 | tf_op jit(solution)/shard_map/ppermute | solution.py:243
  90.0 9.4 %all-to-all-start.5 = ((bf16[8,32,512]{2,1,0:T(8,128)(2,1)}), bf16[8,32,512]{2,1,0:T(8,128)(2,1)S(1)}, u32[]{:S(2)}, u32[]{:S(2)}) async-start(bf16[8,32,512]{2,1,0:T(8,128)(2,1)} %get-tuple-element.106), calls=%async_computation.5 | async-start | bytes 524288 | tf_op jit(solution)/shard_map/all_to_all | solution.py:272
  93.4 9.2 %collective-permute-start.17 = (bf16[128,128]{1,0:T(8,128)(2,1)S(1)}, bf16[128,128]{1,0:T(8,128)(2,1)S(1)}, u32[]{:S(2)}, u32[]{:S(2)}) collective-permute-start(bf16[128,128]{1,0:T(8,128)(2,1)S(1)} %get-tuple-element.107.own_ref), channel_id=1, source_target_pairs={{0,16},{32,48},{64,80},{96,112},{16,0},{48,32},{80,64},{112,96},{1... | collective-permute-start | bytes 98312 | tf_op jit(solution)/shard_map/ppermute | solution.py:243
  93.5 9.8 %collective-permute-start.16 = (bf16[128,128]{1,0:T(8,128)(2,1)S(1)}, bf16[128,128]{1,0:T(8,128)(2,1)S(1)}, u32[]{:S(2)}, u32[]{:S(2)}) collective-permute-start(bf16[128,128]{1,0:T(8,128)(2,1)S(1)} %get-tuple-element.107.own_ref), channel_id=1, source_target_pairs={{16,32},{17,33},{18,34},{19,35},{20,36},{21,37},{22,38},{23,39},{2... | collective-permute-start | bytes 98312 | tf_op jit(solution)/shard_map/ppermute | solution.py:243
  99.5 4.4 %collective-permute-start.15 = (bf16[8,32,512]{2,1,0:T(8,128)(2,1)S(1)}, bf16[8,32,512]{2,1,0:T(8,128)(2,1)S(1)}, u32[]{:S(2)}, u32[]{:S(2)}) collective-permute-start(bf16[8,32,512]{2,1,0:T(8,128)(2,1)S(1)} %all-to-all-done.5.mine_ref), channel_id=1, source_target_pairs={{0,1},{2,3},{4,5},{6,7},{8,9},{10,11},{12,13},{14,15},{1,0},{3,2},... | collective-permute-start | bytes 786440 | tf_op jit(solution)/shard_map/ppermute | solution.py:243
  106.5 3.5 %copy-start.18 = (f32[128,128]{1,0:T(8,128)}, f32[128,128]{1,0:T(8,128)S(1)}, u32[]{:S(2)}) copy-start(f32[128,128]{1,0:T(8,128)S(1)} %get-tuple-element.121.refs_0_) | copy-start | bytes 196612
  106.5 9.4 %all-to-all-start.6 = ((bf16[8,32,512]{2,1,0:T(8,128)(2,1)}), bf16[8,32,512]{2,1,0:T(8,128)(2,1)S(1)}, u32[]{:S(2)}, u32[]{:S(2)}) async-start(bf16[8,32,512]{2,1,0:T(8,128)(2,1)} %get-tuple-element.114), calls=%async_computation.6 | async-start | bytes 524288 | tf_op jit(solution)/shard_map/all_to_all | solution.py:272
  110.0 9.2 %collective-permute-start.20 = (bf16[128,128]{1,0:T(8,128)(2,1)S(1)}, bf16[128,128]{1,0:T(8,128)(2,1)S(1)}, u32[]{:S(2)}, u32[]{:S(2)}) collective-permute-start(bf16[128,128]{1,0:T(8,128)(2,1)S(1)} %get-tuple-element.115.own_ref), channel_id=1, source_target_pairs={{0,16},{32,48},{64,80},{96,112},{16,0},{48,32},{80,64},{112,96},{1... | collective-permute-start | bytes 98312 | tf_op jit(solution)/shard_map/ppermute | solution.py:243
  110.1 9.7 %collective-permute-start.19 = (bf16[128,128]{1,0:T(8,128)(2,1)S(1)}, bf16[128,128]{1,0:T(8,128)(2,1)S(1)}, u32[]{:S(2)}, u32[]{:S(2)}) collective-permute-start(bf16[128,128]{1,0:T(8,128)(2,1)S(1)} %get-tuple-element.115.own_ref), channel_id=1, source_target_pairs={{16,32},{17,33},{18,34},{19,35},{20,36},{21,37},{22,38},{23,39},{2... | collective-permute-start | bytes 98312 | tf_op jit(solution)/shard_map/ppermute | solution.py:243
  116.0 4.4 %collective-permute-start.18 = (bf16[8,32,512]{2,1,0:T(8,128)(2,1)S(1)}, bf16[8,32,512]{2,1,0:T(8,128)(2,1)S(1)}, u32[]{:S(2)}, u32[]{:S(2)}) collective-permute-start(bf16[8,32,512]{2,1,0:T(8,128)(2,1)S(1)} %all-to-all-done.6.mine_ref), channel_id=1, source_target_pairs={{0,1},{2,3},{4,5},{6,7},{8,9},{10,11},{12,13},{14,15},{1,0},{3,2},... | collective-permute-start | bytes 786440 | tf_op jit(solution)/shard_map/ppermute | solution.py:243
  119.8 0.8 copy-start.19
  123.3 3.5 %copy-start.12 = (f32[128,128]{1,0:T(8,128)}, f32[128,128]{1,0:T(8,128)S(1)}, u32[]{:S(2)}) copy-start(f32[128,128]{1,0:T(8,128)S(1)} %get-tuple-element.129.refs_0_) | copy-start | bytes 196612
  123.3 9.4 %all-to-all-start.7 = ((bf16[8,32,512]{2,1,0:T(8,128)(2,1)}), bf16[8,32,512]{2,1,0:T(8,128)(2,1)S(1)}, u32[]{:S(2)}, u32[]{:S(2)}) async-start(bf16[8,32,512]{2,1,0:T(8,128)(2,1)} %get-tuple-element.122), calls=%async_computation.7 | async-start | bytes 524288 | tf_op jit(solution)/shard_map/all_to_all | solution.py:272
  126.7 9.3 %collective-permute-start.23 = (bf16[128,128]{1,0:T(8,128)(2,1)S(1)}, bf16[128,128]{1,0:T(8,128)(2,1)S(1)}, u32[]{:S(2)}, u32[]{:S(2)}) collective-permute-start(bf16[128,128]{1,0:T(8,128)(2,1)S(1)} %get-tuple-element.123.own_ref), channel_id=1, source_target_pairs={{0,16},{32,48},{64,80},{96,112},{16,0},{48,32},{80,64},{112,96},{1... | collective-permute-start | bytes 98312 | tf_op jit(solution)/shard_map/ppermute | solution.py:243
  126.8 9.8 %collective-permute-start.22 = (bf16[128,128]{1,0:T(8,128)(2,1)S(1)}, bf16[128,128]{1,0:T(8,128)(2,1)S(1)}, u32[]{:S(2)}, u32[]{:S(2)}) collective-permute-start(bf16[128,128]{1,0:T(8,128)(2,1)S(1)} %get-tuple-element.123.own_ref), channel_id=1, source_target_pairs={{16,32},{17,33},{18,34},{19,35},{20,36},{21,37},{22,38},{23,39},{2... | collective-permute-start | bytes 98312 | tf_op jit(solution)/shard_map/ppermute | solution.py:243
  132.7 4.5 %collective-permute-start.21 = (bf16[8,32,512]{2,1,0:T(8,128)(2,1)S(1)}, bf16[8,32,512]{2,1,0:T(8,128)(2,1)S(1)}, u32[]{:S(2)}, u32[]{:S(2)}) collective-permute-start(bf16[8,32,512]{2,1,0:T(8,128)(2,1)S(1)} %all-to-all-done.7.mine_ref), channel_id=1, source_target_pairs={{0,1},{2,3},{4,5},{6,7},{8,9},{10,11},{12,13},{14,15},{1,0},{3,2},... | collective-permute-start | bytes 786440 | tf_op jit(solution)/shard_map/ppermute | solution.py:243
  136.6 0.9 copy-start.13
  (4 other events, 3.2 us)

commit v6 on v5

--- a/solution.py
+++ b/solution.py
@@ -64,12 +64,14 @@
     return copy
 
 
-def first_kernel(
-    count_ref, initial_ref, faults_ref, spread_out, packed_out, solution_out, index_out, *scratch
-):
+def first_kernel(initial_ref, spread_out, packed_out, solution_out, *scratch):
     field = initial_ref[0].reshape(2 * NODES, ROWS).T
     copy = send_field(field, spread_out, packed_out, scratch)
     solution_out[...] = field
+    copy.wait()
+
+
+def index_kernel(count_ref, faults_ref, index_out):
     device = faults_ref[1, 0]
     column = (
         jnp.where(device % 2 == lax.axis_index("gy") % 2, 0, CHIPS * ELEMS)
@@ -78,7 +80,6 @@
     )
     owner = jnp.where(iota((1, PAIRS), 1) < count_ref[0, 0], faults_ref[0, 0], -1)
     index_out[...] = jnp.concatenate([column, owner, jnp.zeros((6, PAIRS), jnp.int32)], axis=0)
-    copy.wait()
 
 
 def one_hot(hit):
@@ -258,14 +259,15 @@
     ]
     final_scratch = [pltpu.VMEM((RHS * NODES, PAIRS), F32), pltpu.VMEM((2, ROWS, NODES), F32)]
 
-    spread, packed, total, index = call(
+    spread, packed, total = call(
         first_kernel,
-        [SMEM] + [pl.BlockSpec()] * 2,
-        [spread_shape, packed_shape, state, shape((8, PAIRS), jnp.int32)],
-        [HBM] + [VMEM] * 3,
+        [pl.BlockSpec()],
+        [spread_shape, packed_shape, state],
+        [HBM] + [VMEM] * 2,
         send_scratch,
         room=ROOM,
-    )(fault_count, initial, faults)
+    )(initial)
+    index = call(index_kernel, [SMEM, pl.BlockSpec()], shape((8, PAIRS), jnp.int32), pl.BlockSpec())(fault_count, faults)
     residual = step = correction = None
     for sweep in range(SWEEPS):
         for turn in range(DEGREE):

time: 141 us -> 142 us (level)
  transfers between devices with their start and end apart: 32 -> 32, of which waited for: 7 -> 7; matrix products, arithmetic and copies ran while one was open for 0% -> 0% of each run, Pallas kernels for 12% -> 13%
where the time goes in v6:
time: 142 us; the launch traced here: 140 us
  starting transfers between devices  73.4 us (52%)
  Pallas kernels  39.6 us (28%)
  waiting for transfers between devices  20.8 us (15%)
  local copies, waits for them, and re-layouts  5.12 us (4%)
  between operations  1.48 us (1%)
    ppermute x24, starting transfers between devices, swap(): return lax.ppermute(value, axis, pairs + [(b, a) for a, b in pairs])  41.2 us
    all_to_all x8, starting transfers between devices, shards(): mine = lax.all_to_all(spread, 'gy', 0, 0, axis_index_groups=same_core)  32.3 us
    pallas_call x8, Pallas kernels, shards(): call(make_final_kernel(turn, last), [VMEM] * (6 + len(late)), outs, out_s...  21 us
    all_to_all x8, waiting for transfers between devices, shards(): mine = lax.all_to_all(spread, 'gy', 0, 0, axis_index_groups=same_core)  20.8 us
    pallas_call x8, Pallas kernels, shards(): call(local_kernel, [VMEM] * 3, state, VMEM, room=ROOM)  7.11 us
    unnamed x40, local copies, waits for them, and re-layouts  5.12 us
    pallas_call x8, Pallas kernels, shards(): call(make_stage_kernel(turn), [VMEM] * (5 + len(states)), [state, shape((...  4.89 us
    pallas_call x8, Pallas kernels, shards(): call(make_far_kernel(turn), [VMEM] * 3, state, VMEM, flops=FAR_FLOPS, roo...  4.29 us
  transfers between devices with their start and end apart: 32, of which 7 were waited for; matrix products, arithmetic and copies ran while one was open for 0% of the time, Pallas kernels for 13%

profile of v6, /device:TPU:17, one launch (start us, length us, event | category | flops | bytes accessed | tf_op | source)
XLA Modules:
  0.0 140.4 jit_solution(4423130740187757923)
XLA Ops:
  0.9 1.0 shard_map.74
  1.9 5.8 %all-to-all-start = ((bf16[8,32,512]{2,1,0:T(8,128)(2,1)}), bf16[8,32,512]{2,1,0:T(8,128)(2,1)S(1)}, u32[]{:S(2)}, u32[]{:S(2)}) async-start(bf16[8,32,512]{2,1,0:T(8,128)(2,1)} %get-tuple-element.67), calls=%async_computation | async-start | bytes 524288 | tf_op jit(solution)/shard_map/all_to_all | solution.py:274
  7.6 1.3 collective-permute-start.2
  8.9 1.9 %collective-permute-start.1 = (bf16[128,128]{1,0:T(8,128)(2,1)S(1)}, bf16[128,128]{1,0:T(8,128)(2,1)S(1)}, u32[]{:S(2)}, u32[]{:S(2)}) collective-permute-start(bf16[128,128]{1,0:T(8,128)(2,1)S(1)} %get-tuple-element.68.own_ref), channel_id=1, source_target_pairs={{16,32},{17,33},{18,34},{19,35},{20,36},{21,37},{22,38},{23,39},{2... | collective-permute-start | bytes 98312 | tf_op jit(solution)/shard_map/ppermute | solution.py:244
  11.5 1.3 shard_map.73.index_ref
  12.8 1.4 %copy-done = bf16[6,1,2,64,1024]{4,3,2,1,0:T(8,128)(2,1)S(1)} copy-done((bf16[6,1,2,64,1024]{4,3,2,1,0:T(8,128)(2,1)S(1)}, bf16[6,1,2,64,1024]{4,3,2,1,0:T(8,128)(2,1)}, u32[]{:S(2)}) %copy-start) | copy-done | bytes 1572888
  14.2 0.9 copy-done.2
  16.0 1.6 %collective-permute-start = (bf16[8,32,512]{2,1,0:T(8,128)(2,1)S(1)}, bf16[8,32,512]{2,1,0:T(8,128)(2,1)S(1)}, u32[]{:S(2)}, u32[]{:S(2)}) collective-permute-start(bf16[8,32,512]{2,1,0:T(8,128)(2,1)S(1)} %all-to-all-done.mine_ref), channel_id=1, source_target_pairs={{0,1},{2,3},{4,5},{6,7},{8,9},{10,11},{12,13},{14,15},{1,0},{3,2},... | collective-permute-start | bytes 786440 | tf_op jit(solution)/shard_map/ppermute | solution.py:244
  19.5 2.6 %shard_map.78 = (bf16[8,32,512]{2,1,0:T(8,128)(2,1)}, bf16[128,128]{1,0:T(8,128)(2,1)S(1)}, f32[128,128]{1,0:T(8,128)S(1)}, f32[128,128]{1,0:T(8,128)S(1)}) custom-call(bf16[1,1,64,8192]{3,2,1,0:T(8,128)(2,1)S(1)} %copy-done.7, bf16[6,1,2,64,1024]{4,3,2,1,0:T(8,128)(2,1)S(1)} %copy-done.1, s32[8,128]{1,0:T(8,128)S(1)} %copy-done.4, ...), custom_call_target="tpu_custom_call" | custom-call | flops 4294967296 | bytes 2097152 | tf_op jit(solution)/shard_map/pallas_call | solution.py:296
  22.2 6.0 %all-to-all-start.1 = ((bf16[8,32,512]{2,1,0:T(8,128)(2,1)}), bf16[8,32,512]{2,1,0:T(8,128)(2,1)S(1)}, u32[]{:S(2)}, u32[]{:S(2)}) async-start(bf16[8,32,512]{2,1,0:T(8,128)(2,1)} %get-tuple-element.73), calls=%async_computation.1 | async-start | bytes 524288 | tf_op jit(solution)/shard_map/all_to_all | solution.py:274
  28.1 2.1 %collective-permute-start.4 = (bf16[128,128]{1,0:T(8,128)(2,1)S(1)}, bf16[128,128]{1,0:T(8,128)(2,1)S(1)}, u32[]{:S(2)}, u32[]{:S(2)}) collective-permute-start(bf16[128,128]{1,0:T(8,128)(2,1)S(1)} %get-tuple-element.74.own_ref), channel_id=1, source_target_pairs={{16,32},{17,33},{18,34},{19,35},{20,36},{21,37},{22,38},{23,39},{2... | collective-permute-start | bytes 98312 | tf_op jit(solution)/shard_map/ppermute | solution.py:244
  31.1 3.2 %all-to-all-done.1.mine_ref = bf16[8,32,512]{2,1,0:T(8,128)(2,1)S(1)} async-done(((bf16[8,32,512]{2,1,0:T(8,128)(2,1)}), bf16[8,32,512]{2,1,0:T(8,128)(2,1)S(1)}, u32[]{:S(2)}, u32[]{:S(2)}) %all-to-all-start.1) | async-done | bytes 262176 | tf_op jit(solution)/shard_map/all_to_all | solution.py:274
  34.3 2.0 %collective-permute-start.3 = (bf16[8,32,512]{2,1,0:T(8,128)(2,1)S(1)}, bf16[8,32,512]{2,1,0:T(8,128)(2,1)S(1)}, u32[]{:S(2)}, u32[]{:S(2)}) collective-permute-start(bf16[8,32,512]{2,1,0:T(8,128)(2,1)S(1)} %all-to-all-done.1.mine_ref), channel_id=1, source_target_pairs={{0,1},{2,3},{4,5},{6,7},{8,9},{10,11},{12,13},{14,15},{1,0},{3,2},... | collective-permute-start | bytes 786440 | tf_op jit(solution)/shard_map/ppermute | solution.py:244
  37.5 2.7 %shard_map.82 = (bf16[8,32,512]{2,1,0:T(8,128)(2,1)}, bf16[128,128]{1,0:T(8,128)(2,1)S(1)}, f32[128,128]{1,0:T(8,128)S(1)}, f32[128,128]{1,0:T(8,128)S(1)}) custom-call(bf16[1,1,64,8192]{3,2,1,0:T(8,128)(2,1)S(1)} %copy-done.7, bf16[6,1,2,64,1024]{4,3,2,1,0:T(8,128)(2,1)S(1)} %copy-done.1, s32[8,128]{1,0:T(8,128)S(1)} %copy-done.4, ...), custom_call_target="tpu_custom_call" | custom-call | flops 4294967296 | bytes 2097152 | tf_op jit(solution)/shard_map/pallas_call | solution.py:296
  40.2 3.4 %all-to-all-start.2 = ((bf16[8,32,512]{2,1,0:T(8,128)(2,1)}), bf16[8,32,512]{2,1,0:T(8,128)(2,1)S(1)}, u32[]{:S(2)}, u32[]{:S(2)}) async-start(bf16[8,32,512]{2,1,0:T(8,128)(2,1)} %get-tuple-element.81), calls=%async_computation.2 | async-start | bytes 524288 | tf_op jit(solution)/shard_map/all_to_all | solution.py:274
  43.7 2.1 %collective-permute-start.7 = (bf16[128,128]{1,0:T(8,128)(2,1)S(1)}, bf16[128,128]{1,0:T(8,128)(2,1)S(1)}, u32[]{:S(2)}, u32[]{:S(2)}) collective-permute-start(bf16[128,128]{1,0:T(8,128)(2,1)S(1)} %get-tuple-element.82.own_ref), channel_id=1, source_target_pairs={{16,32},{17,33},{18,34},{19,35},{20,36},{21,37},{22,38},{23,39},{2... | collective-permute-start | bytes 98312 | tf_op jit(solution)/shard_map/ppermute | solution.py:244
  46.7 2.9 %all-to-all-done.2.mine_ref = bf16[8,32,512]{2,1,0:T(8,128)(2,1)S(1)} async-done(((bf16[8,32,512]{2,1,0:T(8,128)(2,1)}), bf16[8,32,512]{2,1,0:T(8,128)(2,1)S(1)}, u32[]{:S(2)}, u32[]{:S(2)}) %all-to-all-start.2) | async-done | bytes 262176 | tf_op jit(solution)/shard_map/all_to_all | solution.py:274
  49.6 2.9 %collective-permute-start.6 = (bf16[8,32,512]{2,1,0:T(8,128)(2,1)S(1)}, bf16[8,32,512]{2,1,0:T(8,128)(2,1)S(1)}, u32[]{:S(2)}, u32[]{:S(2)}) collective-permute-start(bf16[8,32,512]{2,1,0:T(8,128)(2,1)S(1)} %all-to-all-done.2.mine_ref), channel_id=1, source_target_pairs={{0,1},{2,3},{4,5},{6,7},{8,9},{10,11},{12,13},{14,15},{1,0},{3,2},... | collective-permute-start | bytes 786440 | tf_op jit(solution)/shard_map/ppermute | solution.py:244
  54.0 2.6 %shard_map.86 = (bf16[8,32,512]{2,1,0:T(8,128)(2,1)}, bf16[128,128]{1,0:T(8,128)(2,1)S(1)}, f32[128,128]{1,0:T(8,128)S(1)}, f32[128,128]{1,0:T(8,128)S(1)}) custom-call(bf16[1,1,64,8192]{3,2,1,0:T(8,128)(2,1)S(1)} %copy-done.7, bf16[6,1,2,64,1024]{4,3,2,1,0:T(8,128)(2,1)S(1)} %copy-done.1, s32[8,128]{1,0:T(8,128)S(1)} %copy-done.4, ...), custom_call_target="tpu_custom_call" | custom-call | flops 4294967296 | bytes 2097152 | tf_op jit(solution)/shard_map/pallas_call | solution.py:296
  56.6 3.4 %all-to-all-start.3 = ((bf16[8,32,512]{2,1,0:T(8,128)(2,1)}), bf16[8,32,512]{2,1,0:T(8,128)(2,1)S(1)}, u32[]{:S(2)}, u32[]{:S(2)}) async-start(bf16[8,32,512]{2,1,0:T(8,128)(2,1)} %get-tuple-element.89), calls=%async_computation.3 | async-start | bytes 524288 | tf_op jit(solution)/shard_map/all_to_all | solution.py:274
  60.2 2.2 %collective-permute-start.10 = (bf16[128,128]{1,0:T(8,128)(2,1)S(1)}, bf16[128,128]{1,0:T(8,128)(2,1)S(1)}, u32[]{:S(2)}, u32[]{:S(2)}) collective-permute-start(bf16[128,128]{1,0:T(8,128)(2,1)S(1)} %get-tuple-element.90.own_ref), channel_id=1, source_target_pairs={{16,32},{17,33},{18,34},{19,35},{20,36},{21,37},{22,38},{23,39},{2... | collective-permute-start | bytes 98312 | tf_op jit(solution)/shard_map/ppermute | solution.py:244
  62.4 0.9 shard_map.87.local_ref
  63.3 2.8 %all-to-all-done.3.mine_ref = bf16[8,32,512]{2,1,0:T(8,128)(2,1)S(1)} async-done(((bf16[8,32,512]{2,1,0:T(8,128)(2,1)}), bf16[8,32,512]{2,1,0:T(8,128)(2,1)S(1)}, u32[]{:S(2)}, u32[]{:S(2)}) %all-to-all-start.3) | async-done | bytes 262176 | tf_op jit(solution)/shard_map/all_to_all | solution.py:274
  66.1 3.3 %collective-permute-start.9 = (bf16[8,32,512]{2,1,0:T(8,128)(2,1)S(1)}, bf16[8,32,512]{2,1,0:T(8,128)(2,1)S(1)}, u32[]{:S(2)}, u32[]{:S(2)}) collective-permute-start(bf16[8,32,512]{2,1,0:T(8,128)(2,1)S(1)} %all-to-all-done.3.mine_ref), channel_id=1, source_target_pairs={{0,1},{2,3},{4,5},{6,7},{8,9},{10,11},{12,13},{14,15},{1,0},{3,2},... | collective-permute-start | bytes 786440 | tf_op jit(solution)/shard_map/ppermute | solution.py:244
  70.9 2.6 %shard_map.90 = (bf16[8,32,512]{2,1,0:T(8,128)(2,1)}, bf16[128,128]{1,0:T(8,128)(2,1)S(1)}, f32[128,128]{1,0:T(8,128)S(1)}) custom-call(bf16[1,1,64,8192]{3,2,1,0:T(8,128)(2,1)S(1)} %copy-done.7, bf16[6,1,2,64,1024]{4,3,2,1,0:T(8,128)(2,1)S(1)} %copy-done.1, s32[8,128]{1,0:T(8,128)S(1)} %copy-done.4, ...), custom_call_target="tpu_custom_call" | custom-call | flops 4294967296 | bytes 2097152 | tf_op jit(solution)/shard_map/pallas_call | solution.py:296
  73.5 3.4 %all-to-all-start.4 = ((bf16[8,32,512]{2,1,0:T(8,128)(2,1)}), bf16[8,32,512]{2,1,0:T(8,128)(2,1)S(1)}, u32[]{:S(2)}, u32[]{:S(2)}) async-start(bf16[8,32,512]{2,1,0:T(8,128)(2,1)} %get-tuple-element.98), calls=%async_computation.4 | async-start | bytes 524288 | tf_op jit(solution)/shard_map/all_to_all | solution.py:274
  77.1 2.1 %collective-permute-start.13 = (bf16[128,128]{1,0:T(8,128)(2,1)S(1)}, bf16[128,128]{1,0:T(8,128)(2,1)S(1)}, u32[]{:S(2)}, u32[]{:S(2)}) collective-permute-start(bf16[128,128]{1,0:T(8,128)(2,1)S(1)} %get-tuple-element.99.own_ref), channel_id=1, source_target_pairs={{16,32},{17,33},{18,34},{19,35},{20,36},{21,37},{22,38},{23,39},{2... | collective-permute-start | bytes 98312 | tf_op jit(solution)/shard_map/ppermute | solution.py:244
  79.1 0.9 shard_map.91.local_ref
  80.0 2.9 %all-to-all-done.4.mine_ref = bf16[8,32,512]{2,1,0:T(8,128)(2,1)S(1)} async-done(((bf16[8,32,512]{2,1,0:T(8,128)(2,1)}), bf16[8,32,512]{2,1,0:T(8,128)(2,1)S(1)}, u32[]{:S(2)}, u32[]{:S(2)}) %all-to-all-start.4) | async-done | bytes 262176 | tf_op jit(solution)/shard_map/all_to_all | solution.py:274
  83.0 3.5 %collective-permute-start.12 = (bf16[8,32,512]{2,1,0:T(8,128)(2,1)S(1)}, bf16[8,32,512]{2,1,0:T(8,128)(2,1)S(1)}, u32[]{:S(2)}, u32[]{:S(2)}) collective-permute-start(bf16[8,32,512]{2,1,0:T(8,128)(2,1)S(1)} %all-to-all-done.4.mine_ref), channel_id=1, source_target_pairs={{0,1},{2,3},{4,5},{6,7},{8,9},{10,11},{12,13},{14,15},{1,0},{3,2},... | collective-permute-start | bytes 786440 | tf_op jit(solution)/shard_map/ppermute | solution.py:244
  87.6 2.7 %shard_map.94 = (bf16[8,32,512]{2,1,0:T(8,128)(2,1)}, bf16[128,128]{1,0:T(8,128)(2,1)S(1)}, f32[128,128]{1,0:T(8,128)S(1)}, f32[128,128]{1,0:T(8,128)S(1)}) custom-call(bf16[1,1,64,8192]{3,2,1,0:T(8,128)(2,1)S(1)} %copy-done.7, bf16[6,1,2,64,1024]{4,3,2,1,0:T(8,128)(2,1)S(1)} %copy-done.1, s32[8,128]{1,0:T(8,128)S(1)} %copy-done.4, ...), custom_call_target="tpu_custom_call" | custom-call | flops 4294967296 | bytes 2097152 | tf_op jit(solution)/shard_map/pallas_call | solution.py:296
  90.3 3.4 %all-to-all-start.5 = ((bf16[8,32,512]{2,1,0:T(8,128)(2,1)}), bf16[8,32,512]{2,1,0:T(8,128)(2,1)S(1)}, u32[]{:S(2)}, u32[]{:S(2)}) async-start(bf16[8,32,512]{2,1,0:T(8,128)(2,1)} %get-tuple-element.104), calls=%async_computation.5 | async-start | bytes 524288 | tf_op jit(solution)/shard_map/all_to_all | solution.py:274
  93.8 2.1 %collective-permute-start.16 = (bf16[128,128]{1,0:T(8,128)(2,1)S(1)}, bf16[128,128]{1,0:T(8,128)(2,1)S(1)}, u32[]{:S(2)}, u32[]{:S(2)}) collective-permute-start(bf16[128,128]{1,0:T(8,128)(2,1)S(1)} %get-tuple-element.105.own_ref), channel_id=1, source_target_pairs={{16,32},{17,33},{18,34},{19,35},{20,36},{21,37},{22,38},{23,39},{2... | collective-permute-start | bytes 98312 | tf_op jit(solution)/shard_map/ppermute | solution.py:244
  95.9 0.9 shard_map.95.local_ref
  96.8 3.0 %all-to-all-done.5.mine_ref = bf16[8,32,512]{2,1,0:T(8,128)(2,1)S(1)} async-done(((bf16[8,32,512]{2,1,0:T(8,128)(2,1)}), bf16[8,32,512]{2,1,0:T(8,128)(2,1)S(1)}, u32[]{:S(2)}, u32[]{:S(2)}) %all-to-all-start.5) | async-done | bytes 262176 | tf_op jit(solution)/shard_map/all_to_all | solution.py:274
  99.7 3.2 %collective-permute-start.15 = (bf16[8,32,512]{2,1,0:T(8,128)(2,1)S(1)}, bf16[8,32,512]{2,1,0:T(8,128)(2,1)S(1)}, u32[]{:S(2)}, u32[]{:S(2)}) collective-permute-start(bf16[8,32,512]{2,1,0:T(8,128)(2,1)S(1)} %all-to-all-done.5.mine_ref), channel_id=1, source_target_pairs={{0,1},{2,3},{4,5},{6,7},{8,9},{10,11},{12,13},{14,15},{1,0},{3,2},... | collective-permute-start | bytes 786440 | tf_op jit(solution)/shard_map/ppermute | solution.py:244
  104.1 2.7 %shard_map.98 = (bf16[8,32,512]{2,1,0:T(8,128)(2,1)}, bf16[128,128]{1,0:T(8,128)(2,1)S(1)}, f32[128,128]{1,0:T(8,128)S(1)}, f32[128,128]{1,0:T(8,128)S(1)}) custom-call(bf16[1,1,64,8192]{3,2,1,0:T(8,128)(2,1)S(1)} %copy-done.7, bf16[6,1,2,64,1024]{4,3,2,1,0:T(8,128)(2,1)S(1)} %copy-done.1, s32[8,128]{1,0:T(8,128)S(1)} %copy-done.4, ...), custom_call_target="tpu_custom_call" | custom-call | flops 4294967296 | bytes 2097152 | tf_op jit(solution)/shard_map/pallas_call | solution.py:296
  106.8 3.4 %all-to-all-start.6 = ((bf16[8,32,512]{2,1,0:T(8,128)(2,1)}), bf16[8,32,512]{2,1,0:T(8,128)(2,1)S(1)}, u32[]{:S(2)}, u32[]{:S(2)}) async-start(bf16[8,32,512]{2,1,0:T(8,128)(2,1)} %get-tuple-element.112), calls=%async_computation.6 | async-start | bytes 524288 | tf_op jit(solution)/shard_map/all_to_all | solution.py:274
  110.3 2.0 %collective-permute-start.19 = (bf16[128,128]{1,0:T(8,128)(2,1)S(1)}, bf16[128,128]{1,0:T(8,128)(2,1)S(1)}, u32[]{:S(2)}, u32[]{:S(2)}) collective-permute-start(bf16[128,128]{1,0:T(8,128)(2,1)S(1)} %get-tuple-element.113.own_ref), channel_id=1, source_target_pairs={{16,32},{17,33},{18,34},{19,35},{20,36},{21,37},{22,38},{23,39},{2... | collective-permute-start | bytes 98312 | tf_op jit(solution)/shard_map/ppermute | solution.py:244
  112.4 0.9 shard_map.99.local_ref
  113.3 3.0 %all-to-all-done.6.mine_ref = bf16[8,32,512]{2,1,0:T(8,128)(2,1)S(1)} async-done(((bf16[8,32,512]{2,1,0:T(8,128)(2,1)}), bf16[8,32,512]{2,1,0:T(8,128)(2,1)S(1)}, u32[]{:S(2)}, u32[]{:S(2)}) %all-to-all-start.6) | async-done | bytes 262176 | tf_op jit(solution)/shard_map/all_to_all | solution.py:274
  116.2 3.2 %collective-permute-start.18 = (bf16[8,32,512]{2,1,0:T(8,128)(2,1)S(1)}, bf16[8,32,512]{2,1,0:T(8,128)(2,1)S(1)}, u32[]{:S(2)}, u32[]{:S(2)}) collective-permute-start(bf16[8,32,512]{2,1,0:T(8,128)(2,1)S(1)} %all-to-all-done.6.mine_ref), channel_id=1, source_target_pairs={{0,1},{2,3},{4,5},{6,7},{8,9},{10,11},{12,13},{14,15},{1,0},{3,2},... | collective-permute-start | bytes 786440 | tf_op jit(solution)/shard_map/ppermute | solution.py:244
  120.9 2.6 %shard_map.102 = (bf16[8,32,512]{2,1,0:T(8,128)(2,1)}, bf16[128,128]{1,0:T(8,128)(2,1)S(1)}, f32[128,128]{1,0:T(8,128)S(1)}, f32[128,128]{1,0:T(8,128)S(1)}) custom-call(bf16[1,1,64,8192]{3,2,1,0:T(8,128)(2,1)S(1)} %copy-done.7, bf16[6,1,2,64,1024]{4,3,2,1,0:T(8,128)(2,1)S(1)} %copy-done.1, s32[8,128]{1,0:T(8,128)S(1)} %copy-done.4, ...), custom_call_target="tpu_custom_call" | custom-call | flops 4294967296 | bytes 2097152 | tf_op jit(solution)/shard_map/pallas_call | solution.py:296
  123.6 3.4 %all-to-all-start.7 = ((bf16[8,32,512]{2,1,0:T(8,128)(2,1)}), bf16[8,32,512]{2,1,0:T(8,128)(2,1)S(1)}, u32[]{:S(2)}, u32[]{:S(2)}) async-start(bf16[8,32,512]{2,1,0:T(8,128)(2,1)} %get-tuple-element.120), calls=%async_computation.7 | async-start | bytes 524288 | tf_op jit(solution)/shard_map/all_to_all | solution.py:274
  127.1 2.1 %collective-permute-start.22 = (bf16[128,128]{1,0:T(8,128)(2,1)S(1)}, bf16[128,128]{1,0:T(8,128)(2,1)S(1)}, u32[]{:S(2)}, u32[]{:S(2)}) collective-permute-start(bf16[128,128]{1,0:T(8,128)(2,1)S(1)} %get-tuple-element.121.own_ref), channel_id=1, source_target_pairs={{16,32},{17,33},{18,34},{19,35},{20,36},{21,37},{22,38},{23,39},{2... | collective-permute-start | bytes 98312 | tf_op jit(solution)/shard_map/ppermute | solution.py:244
  130.0 3.0 %all-to-all-done.7.mine_ref = bf16[8,32,512]{2,1,0:T(8,128)(2,1)S(1)} async-done(((bf16[8,32,512]{2,1,0:T(8,128)(2,1)}), bf16[8,32,512]{2,1,0:T(8,128)(2,1)S(1)}, u32[]{:S(2)}, u32[]{:S(2)}) %all-to-all-start.7) | async-done | bytes 262176 | tf_op jit(solution)/shard_map/all_to_all | solution.py:274
  133.0 3.3 %collective-permute-start.21 = (bf16[8,32,512]{2,1,0:T(8,128)(2,1)S(1)}, bf16[8,32,512]{2,1,0:T(8,128)(2,1)S(1)}, u32[]{:S(2)}, u32[]{:S(2)}) collective-permute-start(bf16[8,32,512]{2,1,0:T(8,128)(2,1)S(1)} %all-to-all-done.7.mine_ref), channel_id=1, source_target_pairs={{0,1},{2,3},{4,5},{6,7},{8,9},{10,11},{12,13},{14,15},{1,0},{3,2},... | collective-permute-start | bytes 786440 | tf_op jit(solution)/shard_map/ppermute | solution.py:244
  137.8 2.5 %shard_map.106 = f32[1,2,64,128]{3,2,1,0:T(8,128)} custom-call(bf16[1,1,64,8192]{3,2,1,0:T(8,128)(2,1)S(1)} %copy-done.7, bf16[6,1,2,64,1024]{4,3,2,1,0:T(8,128)(2,1)S(1)} %copy-done.1, s32[8,128]{1,0:T(8,128)S(1)} %copy-done.4, bf16[8,32,512]{2,1,0:T(8,128)(2,1)S(1)} %collective-permute-done.21.other_ref, f32[128,128]{1,0:T(8,128)S(1)} %shard_map.105.base_ref, ...), custom_call_target="tpu_custom_call" | custom-call | flops 4294967296 | bytes 2097152 | tf_op jit(solution)/shard_map/pallas_call | solution.py:296
  (90 shorter events, 16.1 us)
Async XLA Ops:
  0.0 17.6 %copy-start.5 = (f32[1,2,64,128]{3,2,1,0:T(8,128)S(1)}, f32[1,2,64,128]{3,2,1,0:T(8,128)}, u32[]{:S(2)}) copy-start(f32[1,2,64,128]{3,2,1,0:T(8,128)} %refs_0_.3) | copy-start | bytes 196612
  0.0 0.9 copy-start.6
  1.9 5.8 %copy-start.8 = (f32[128,128]{1,0:T(8,128)}, f32[128,128]{1,0:T(8,128)S(1)}, u32[]{:S(2)}) copy-start(f32[128,128]{1,0:T(8,128)S(1)} %get-tuple-element.97.refs_1_) | copy-start | bytes 196612
  1.9 14.1 %all-to-all-start = ((bf16[8,32,512]{2,1,0:T(8,128)(2,1)}), bf16[8,32,512]{2,1,0:T(8,128)(2,1)S(1)}, u32[]{:S(2)}, u32[]{:S(2)}) async-start(bf16[8,32,512]{2,1,0:T(8,128)(2,1)} %get-tuple-element.67), calls=%async_computation | async-start | bytes 524288 | tf_op jit(solution)/shard_map/all_to_all | solution.py:274
  7.6 10.0 %collective-permute-start.2 = (bf16[128,128]{1,0:T(8,128)(2,1)S(1)}, bf16[128,128]{1,0:T(8,128)(2,1)S(1)}, u32[]{:S(2)}, u32[]{:S(2)}) collective-permute-start(bf16[128,128]{1,0:T(8,128)(2,1)S(1)} %get-tuple-element.68.own_ref), channel_id=1, source_target_pairs={{0,16},{32,48},{64,80},{96,112},{16,0},{48,32},{80,64},{112,96},{1... | collective-permute-start | bytes 98312 | tf_op jit(solution)/shard_map/ppermute | solution.py:244
  8.9 9.4 %collective-permute-start.1 = (bf16[128,128]{1,0:T(8,128)(2,1)S(1)}, bf16[128,128]{1,0:T(8,128)(2,1)S(1)}, u32[]{:S(2)}, u32[]{:S(2)}) collective-permute-start(bf16[128,128]{1,0:T(8,128)(2,1)S(1)} %get-tuple-element.68.own_ref), channel_id=1, source_target_pairs={{16,32},{17,33},{18,34},{19,35},{20,36},{21,37},{22,38},{23,39},{2... | collective-permute-start | bytes 98312 | tf_op jit(solution)/shard_map/ppermute | solution.py:244
  12.7 1.4 %copy-start = (bf16[6,1,2,64,1024]{4,3,2,1,0:T(8,128)(2,1)S(1)}, bf16[6,1,2,64,1024]{4,3,2,1,0:T(8,128)(2,1)}, u32[]{:S(2)}) copy-start(bf16[6,1,2,64,1024]{4,3,2,1,0:T(8,128)(2,1)} %face_ref.63) | copy-start | bytes 4718596
  14.2 0.9 copy-start.2
  15.1 2.5 %copy-start.1 = (bf16[6,1,2,64,1024]{4,3,2,1,0:T(8,128)(2,1)S(1)}, bf16[6,1,2,64,1024]{4,3,2,1,0:T(8,128)(2,1)}, u32[]{:S(2)}) copy-start(bf16[6,1,2,64,1024]{4,3,2,1,0:T(8,128)(2,1)} %face_ref.63) | copy-start | bytes 4718596
  15.1 2.5 %copy-start.4 = (s32[8,128]{1,0:T(8,128)S(1)}, s32[8,128]{1,0:T(8,128)}, u32[]{:S(2)}) copy-start(s32[8,128]{1,0:T(8,128)} %shard_map.73.index_ref) | copy-start | bytes 12292
  16.0 2.8 %collective-permute-start = (bf16[8,32,512]{2,1,0:T(8,128)(2,1)S(1)}, bf16[8,32,512]{2,1,0:T(8,128)(2,1)S(1)}, u32[]{:S(2)}, u32[]{:S(2)}) collective-permute-start(bf16[8,32,512]{2,1,0:T(8,128)(2,1)S(1)} %all-to-all-done.mine_ref), channel_id=1, source_target_pairs={{0,1},{2,3},{4,5},{6,7},{8,9},{10,11},{12,13},{14,15},{1,0},{3,2},... | collective-permute-start | bytes 786440 | tf_op jit(solution)/shard_map/ppermute | solution.py:244
  18.3 1.2 copy-start.7
  19.5 10.7 %copy-start.3 = (bf16[1,2,64,1024]{3,2,1,0:T(8,128)(2,1)S(1)}, bf16[1,2,64,1024]{3,2,1,0:T(8,128)(2,1)}, u32[]{:S(2)}) copy-start(bf16[1,2,64,1024]{3,2,1,0:T(8,128)(2,1)} %elem_ref.15) | copy-start | bytes 786436
  22.2 12.2 %all-to-all-start.1 = ((bf16[8,32,512]{2,1,0:T(8,128)(2,1)}), bf16[8,32,512]{2,1,0:T(8,128)(2,1)S(1)}, u32[]{:S(2)}, u32[]{:S(2)}) async-start(bf16[8,32,512]{2,1,0:T(8,128)(2,1)} %get-tuple-element.73), calls=%async_computation.1 | async-start | bytes 524288 | tf_op jit(solution)/shard_map/all_to_all | solution.py:274
  28.1 8.2 %collective-permute-start.5 = (bf16[128,128]{1,0:T(8,128)(2,1)S(1)}, bf16[128,128]{1,0:T(8,128)(2,1)S(1)}, u32[]{:S(2)}, u32[]{:S(2)}) collective-permute-start(bf16[128,128]{1,0:T(8,128)(2,1)S(1)} %get-tuple-element.74.own_ref), channel_id=1, source_target_pairs={{0,16},{32,48},{64,80},{96,112},{16,0},{48,32},{80,64},{112,96},{1... | collective-permute-start | bytes 98312 | tf_op jit(solution)/shard_map/ppermute | solution.py:244
  28.1 8.8 %collective-permute-start.4 = (bf16[128,128]{1,0:T(8,128)(2,1)S(1)}, bf16[128,128]{1,0:T(8,128)(2,1)S(1)}, u32[]{:S(2)}, u32[]{:S(2)}) collective-permute-start(bf16[128,128]{1,0:T(8,128)(2,1)S(1)} %get-tuple-element.74.own_ref), channel_id=1, source_target_pairs={{16,32},{17,33},{18,34},{19,35},{20,36},{21,37},{22,38},{23,39},{2... | collective-permute-start | bytes 98312 | tf_op jit(solution)/shard_map/ppermute | solution.py:244
  34.3 3.1 %collective-permute-start.3 = (bf16[8,32,512]{2,1,0:T(8,128)(2,1)S(1)}, bf16[8,32,512]{2,1,0:T(8,128)(2,1)S(1)}, u32[]{:S(2)}, u32[]{:S(2)}) collective-permute-start(bf16[8,32,512]{2,1,0:T(8,128)(2,1)S(1)} %all-to-all-done.1.mine_ref), channel_id=1, source_target_pairs={{0,1},{2,3},{4,5},{6,7},{8,9},{10,11},{12,13},{14,15},{1,0},{3,2},... | collective-permute-start | bytes 786440 | tf_op jit(solution)/shard_map/ppermute | solution.py:244
  40.1 3.5 %copy-start.16 = (f32[128,128]{1,0:T(8,128)}, f32[128,128]{1,0:T(8,128)S(1)}, u32[]{:S(2)}) copy-start(f32[128,128]{1,0:T(8,128)S(1)} %get-tuple-element.88.refs_0_) | copy-start | bytes 196612
  40.2 9.4 %all-to-all-start.2 = ((bf16[8,32,512]{2,1,0:T(8,128)(2,1)}), bf16[8,32,512]{2,1,0:T(8,128)(2,1)S(1)}, u32[]{:S(2)}, u32[]{:S(2)}) async-start(bf16[8,32,512]{2,1,0:T(8,128)(2,1)} %get-tuple-element.81), calls=%async_computation.2 | async-start | bytes 524288 | tf_op jit(solution)/shard_map/all_to_all | solution.py:274
  43.6 8.9 %collective-permute-start.8 = (bf16[128,128]{1,0:T(8,128)(2,1)S(1)}, bf16[128,128]{1,0:T(8,128)(2,1)S(1)}, u32[]{:S(2)}, u32[]{:S(2)}) collective-permute-start(bf16[128,128]{1,0:T(8,128)(2,1)S(1)} %get-tuple-element.82.own_ref), channel_id=1, source_target_pairs={{0,16},{32,48},{64,80},{96,112},{16,0},{48,32},{80,64},{112,96},{1... | collective-permute-start | bytes 98312 | tf_op jit(solution)/shard_map/ppermute | solution.py:244
  43.7 9.4 %collective-permute-start.7 = (bf16[128,128]{1,0:T(8,128)(2,1)S(1)}, bf16[128,128]{1,0:T(8,128)(2,1)S(1)}, u32[]{:S(2)}, u32[]{:S(2)}) collective-permute-start(bf16[128,128]{1,0:T(8,128)(2,1)S(1)} %get-tuple-element.82.own_ref), channel_id=1, source_target_pairs={{16,32},{17,33},{18,34},{19,35},{20,36},{21,37},{22,38},{23,39},{2... | collective-permute-start | bytes 98312 | tf_op jit(solution)/shard_map/ppermute | solution.py:244
  49.6 4.1 %collective-permute-start.6 = (bf16[8,32,512]{2,1,0:T(8,128)(2,1)S(1)}, bf16[8,32,512]{2,1,0:T(8,128)(2,1)S(1)}, u32[]{:S(2)}, u32[]{:S(2)}) collective-permute-start(bf16[8,32,512]{2,1,0:T(8,128)(2,1)S(1)} %all-to-all-done.2.mine_ref), channel_id=1, source_target_pairs={{0,1},{2,3},{4,5},{6,7},{8,9},{10,11},{12,13},{14,15},{1,0},{3,2},... | collective-permute-start | bytes 786440 | tf_op jit(solution)/shard_map/ppermute | solution.py:244
  56.6 3.5 %copy-start.14 = (f32[128,128]{1,0:T(8,128)}, f32[128,128]{1,0:T(8,128)S(1)}, u32[]{:S(2)}) copy-start(f32[128,128]{1,0:T(8,128)S(1)} %get-tuple-element.96.refs_0_) | copy-start | bytes 196612
  56.6 9.4 %all-to-all-start.3 = ((bf16[8,32,512]{2,1,0:T(8,128)(2,1)}), bf16[8,32,512]{2,1,0:T(8,128)(2,1)S(1)}, u32[]{:S(2)}, u32[]{:S(2)}) async-start(bf16[8,32,512]{2,1,0:T(8,128)(2,1)} %get-tuple-element.89), calls=%async_computation.3 | async-start | bytes 524288 | tf_op jit(solution)/shard_map/all_to_all | solution.py:274
  60.1 9.3 %collective-permute-start.11 = (bf16[128,128]{1,0:T(8,128)(2,1)S(1)}, bf16[128,128]{1,0:T(8,128)(2,1)S(1)}, u32[]{:S(2)}, u32[]{:S(2)}) collective-permute-start(bf16[128,128]{1,0:T(8,128)(2,1)S(1)} %get-tuple-element.90.own_ref), channel_id=1, source_target_pairs={{0,16},{32,48},{64,80},{96,112},{16,0},{48,32},{80,64},{112,96},{1... | collective-permute-start | bytes 98312 | tf_op jit(solution)/shard_map/ppermute | solution.py:244
  60.2 9.8 %collective-permute-start.10 = (bf16[128,128]{1,0:T(8,128)(2,1)S(1)}, bf16[128,128]{1,0:T(8,128)(2,1)S(1)}, u32[]{:S(2)}, u32[]{:S(2)}) collective-permute-start(bf16[128,128]{1,0:T(8,128)(2,1)S(1)} %get-tuple-element.90.own_ref), channel_id=1, source_target_pairs={{16,32},{17,33},{18,34},{19,35},{20,36},{21,37},{22,38},{23,39},{2... | collective-permute-start | bytes 98312 | tf_op jit(solution)/shard_map/ppermute | solution.py:244
  66.1 4.5 %collective-permute-start.9 = (bf16[8,32,512]{2,1,0:T(8,128)(2,1)S(1)}, bf16[8,32,512]{2,1,0:T(8,128)(2,1)S(1)}, u32[]{:S(2)}, u32[]{:S(2)}) collective-permute-start(bf16[8,32,512]{2,1,0:T(8,128)(2,1)S(1)} %all-to-all-done.3.mine_ref), channel_id=1, source_target_pairs={{0,1},{2,3},{4,5},{6,7},{8,9},{10,11},{12,13},{14,15},{1,0},{3,2},... | collective-permute-start | bytes 786440 | tf_op jit(solution)/shard_map/ppermute | solution.py:244
  70.0 0.9 copy-start.15
  73.5 3.4 %copy-start.10 = (f32[128,128]{1,0:T(8,128)}, f32[128,128]{1,0:T(8,128)S(1)}, u32[]{:S(2)}) copy-start(f32[128,128]{1,0:T(8,128)S(1)} %get-tuple-element.128.refs_1_) | copy-start | bytes 196612
  73.5 9.4 %all-to-all-start.4 = ((bf16[8,32,512]{2,1,0:T(8,128)(2,1)}), bf16[8,32,512]{2,1,0:T(8,128)(2,1)S(1)}, u32[]{:S(2)}, u32[]{:S(2)}) async-start(bf16[8,32,512]{2,1,0:T(8,128)(2,1)} %get-tuple-element.98), calls=%async_computation.4 | async-start | bytes 524288 | tf_op jit(solution)/shard_map/all_to_all | solution.py:274
  77.0 9.5 %collective-permute-start.14 = (bf16[128,128]{1,0:T(8,128)(2,1)S(1)}, bf16[128,128]{1,0:T(8,128)(2,1)S(1)}, u32[]{:S(2)}, u32[]{:S(2)}) collective-permute-start(bf16[128,128]{1,0:T(8,128)(2,1)S(1)} %get-tuple-element.99.own_ref), channel_id=1, source_target_pairs={{0,16},{32,48},{64,80},{96,112},{16,0},{48,32},{80,64},{112,96},{1... | collective-permute-start | bytes 98312 | tf_op jit(solution)/shard_map/ppermute | solution.py:244
  77.1 10.0 %collective-permute-start.13 = (bf16[128,128]{1,0:T(8,128)(2,1)S(1)}, bf16[128,128]{1,0:T(8,128)(2,1)S(1)}, u32[]{:S(2)}, u32[]{:S(2)}) collective-permute-start(bf16[128,128]{1,0:T(8,128)(2,1)S(1)} %get-tuple-element.99.own_ref), channel_id=1, source_target_pairs={{16,32},{17,33},{18,34},{19,35},{20,36},{21,37},{22,38},{23,39},{2... | collective-permute-start | bytes 98312 | tf_op jit(solution)/shard_map/ppermute | solution.py:244
  83.0 4.7 %collective-permute-start.12 = (bf16[8,32,512]{2,1,0:T(8,128)(2,1)S(1)}, bf16[8,32,512]{2,1,0:T(8,128)(2,1)S(1)}, u32[]{:S(2)}, u32[]{:S(2)}) collective-permute-start(bf16[8,32,512]{2,1,0:T(8,128)(2,1)S(1)} %all-to-all-done.4.mine_ref), channel_id=1, source_target_pairs={{0,1},{2,3},{4,5},{6,7},{8,9},{10,11},{12,13},{14,15},{1,0},{3,2},... | collective-permute-start | bytes 786440 | tf_op jit(solution)/shard_map/ppermute | solution.py:244
  90.3 9.4 %all-to-all-start.5 = ((bf16[8,32,512]{2,1,0:T(8,128)(2,1)}), bf16[8,32,512]{2,1,0:T(8,128)(2,1)S(1)}, u32[]{:S(2)}, u32[]{:S(2)}) async-start(bf16[8,32,512]{2,1,0:T(8,128)(2,1)} %get-tuple-element.104), calls=%async_computation.5 | async-start | bytes 524288 | tf_op jit(solution)/shard_map/all_to_all | solution.py:274
  93.7 9.2 %collective-permute-start.17 = (bf16[128,128]{1,0:T(8,128)(2,1)S(1)}, bf16[128,128]{1,0:T(8,128)(2,1)S(1)}, u32[]{:S(2)}, u32[]{:S(2)}) collective-permute-start(bf16[128,128]{1,0:T(8,128)(2,1)S(1)} %get-tuple-element.105.own_ref), channel_id=1, source_target_pairs={{0,16},{32,48},{64,80},{96,112},{16,0},{48,32},{80,64},{112,96},{1... | collective-permute-start | bytes 98312 | tf_op jit(solution)/shard_map/ppermute | solution.py:244
  93.8 9.8 %collective-permute-start.16 = (bf16[128,128]{1,0:T(8,128)(2,1)S(1)}, bf16[128,128]{1,0:T(8,128)(2,1)S(1)}, u32[]{:S(2)}, u32[]{:S(2)}) collective-permute-start(bf16[128,128]{1,0:T(8,128)(2,1)S(1)} %get-tuple-element.105.own_ref), channel_id=1, source_target_pairs={{16,32},{17,33},{18,34},{19,35},{20,36},{21,37},{22,38},{23,39},{2... | collective-permute-start | bytes 98312 | tf_op jit(solution)/shard_map/ppermute | solution.py:244
  99.7 4.4 %collective-permute-start.15 = (bf16[8,32,512]{2,1,0:T(8,128)(2,1)S(1)}, bf16[8,32,512]{2,1,0:T(8,128)(2,1)S(1)}, u32[]{:S(2)}, u32[]{:S(2)}) collective-permute-start(bf16[8,32,512]{2,1,0:T(8,128)(2,1)S(1)} %all-to-all-done.5.mine_ref), channel_id=1, source_target_pairs={{0,1},{2,3},{4,5},{6,7},{8,9},{10,11},{12,13},{14,15},{1,0},{3,2},... | collective-permute-start | bytes 786440 | tf_op jit(solution)/shard_map/ppermute | solution.py:244
  106.8 3.5 %copy-start.18 = (f32[128,128]{1,0:T(8,128)}, f32[128,128]{1,0:T(8,128)S(1)}, u32[]{:S(2)}) copy-start(f32[128,128]{1,0:T(8,128)S(1)} %get-tuple-element.119.refs_0_) | copy-start | bytes 196612
  106.8 9.4 %all-to-all-start.6 = ((bf16[8,32,512]{2,1,0:T(8,128)(2,1)}), bf16[8,32,512]{2,1,0:T(8,128)(2,1)S(1)}, u32[]{:S(2)}, u32[]{:S(2)}) async-start(bf16[8,32,512]{2,1,0:T(8,128)(2,1)} %get-tuple-element.112), calls=%async_computation.6 | async-start | bytes 524288 | tf_op jit(solution)/shard_map/all_to_all | solution.py:274
  110.2 9.2 %collective-permute-start.20 = (bf16[128,128]{1,0:T(8,128)(2,1)S(1)}, bf16[128,128]{1,0:T(8,128)(2,1)S(1)}, u32[]{:S(2)}, u32[]{:S(2)}) collective-permute-start(bf16[128,128]{1,0:T(8,128)(2,1)S(1)} %get-tuple-element.113.own_ref), channel_id=1, source_target_pairs={{0,16},{32,48},{64,80},{96,112},{16,0},{48,32},{80,64},{112,96},{1... | collective-permute-start | bytes 98312 | tf_op jit(solution)/shard_map/ppermute | solution.py:244
  110.3 9.7 %collective-permute-start.19 = (bf16[128,128]{1,0:T(8,128)(2,1)S(1)}, bf16[128,128]{1,0:T(8,128)(2,1)S(1)}, u32[]{:S(2)}, u32[]{:S(2)}) collective-permute-start(bf16[128,128]{1,0:T(8,128)(2,1)S(1)} %get-tuple-element.113.own_ref), channel_id=1, source_target_pairs={{16,32},{17,33},{18,34},{19,35},{20,36},{21,37},{22,38},{23,39},{2... | collective-permute-start | bytes 98312 | tf_op jit(solution)/shard_map/ppermute | solution.py:244
  116.2 4.4 %collective-permute-start.18 = (bf16[8,32,512]{2,1,0:T(8,128)(2,1)S(1)}, bf16[8,32,512]{2,1,0:T(8,128)(2,1)S(1)}, u32[]{:S(2)}, u32[]{:S(2)}) collective-permute-start(bf16[8,32,512]{2,1,0:T(8,128)(2,1)S(1)} %all-to-all-done.6.mine_ref), channel_id=1, source_target_pairs={{0,1},{2,3},{4,5},{6,7},{8,9},{10,11},{12,13},{14,15},{1,0},{3,2},... | collective-permute-start | bytes 786440 | tf_op jit(solution)/shard_map/ppermute | solution.py:244
  123.5 3.5 %copy-start.12 = (f32[128,128]{1,0:T(8,128)}, f32[128,128]{1,0:T(8,128)S(1)}, u32[]{:S(2)}) copy-start(f32[128,128]{1,0:T(8,128)S(1)} %get-tuple-element.127.refs_0_) | copy-start | bytes 196612
  123.6 9.4 %all-to-all-start.7 = ((bf16[8,32,512]{2,1,0:T(8,128)(2,1)}), bf16[8,32,512]{2,1,0:T(8,128)(2,1)S(1)}, u32[]{:S(2)}, u32[]{:S(2)}) async-start(bf16[8,32,512]{2,1,0:T(8,128)(2,1)} %get-tuple-element.120), calls=%async_computation.7 | async-start | bytes 524288 | tf_op jit(solution)/shard_map/all_to_all | solution.py:274
  127.0 9.3 %collective-permute-start.23 = (bf16[128,128]{1,0:T(8,128)(2,1)S(1)}, bf16[128,128]{1,0:T(8,128)(2,1)S(1)}, u32[]{:S(2)}, u32[]{:S(2)}) collective-permute-start(bf16[128,128]{1,0:T(8,128)(2,1)S(1)} %get-tuple-element.121.own_ref), channel_id=1, source_target_pairs={{0,16},{32,48},{64,80},{96,112},{16,0},{48,32},{80,64},{112,96},{1... | collective-permute-start | bytes 98312 | tf_op jit(solution)/shard_map/ppermute | solution.py:244
  127.1 9.8 %collective-permute-start.22 = (bf16[128,128]{1,0:T(8,128)(2,1)S(1)}, bf16[128,128]{1,0:T(8,128)(2,1)S(1)}, u32[]{:S(2)}, u32[]{:S(2)}) collective-permute-start(bf16[128,128]{1,0:T(8,128)(2,1)S(1)} %get-tuple-element.121.own_ref), channel_id=1, source_target_pairs={{16,32},{17,33},{18,34},{19,35},{20,36},{21,37},{22,38},{23,39},{2... | collective-permute-start | bytes 98312 | tf_op jit(solution)/shard_map/ppermute | solution.py:244
  133.0 4.5 %collective-permute-start.21 = (bf16[8,32,512]{2,1,0:T(8,128)(2,1)S(1)}, bf16[8,32,512]{2,1,0:T(8,128)(2,1)S(1)}, u32[]{:S(2)}, u32[]{:S(2)}) collective-permute-start(bf16[8,32,512]{2,1,0:T(8,128)(2,1)S(1)} %all-to-all-done.7.mine_ref), channel_id=1, source_target_pairs={{0,1},{2,3},{4,5},{6,7},{8,9},{10,11},{12,13},{14,15},{1,0},{3,2},... | collective-permute-start | bytes 786440 | tf_op jit(solution)/shard_map/ppermute | solution.py:244
  136.9 0.9 copy-start.13
  (4 other events, 3.4 us)
